TPU v7x, 32 devices: a whole 2x2x4 slice. The times are simulated.
32 devices in a mesh: dp: 4 (over z), seq: 8 (over y, x, core).
Axes of the slice: x: 2, y: 2, z: 4, core: 2. Of those that a mesh axis runs over, the one named last changes fastest.
Arguments:
- query: bfloat16 [4, 2048, 1024], P('dp', 'seq'), may hold values from -150 to 150
- key: bfloat16 [4, 2048, 128], P('dp', 'seq'), may hold values from -5 to 5
- value: bfloat16 [4, 2048, 128], P('dp', 'seq'), may hold values from -6 to 6
- ssm_input: bfloat16 [4, 2048, 1024], P('dp', 'seq'), may hold values from -9 to 9
- in_b: bfloat16 [4, 2048, 128], P('dp', 'seq'), may hold values from -0.625 to 0.625
- in_c: bfloat16 [4, 2048, 128], P('dp', 'seq'), may hold values from -0.625 to 0.625
- step: float32 [4, 2048, 8], P('dp', 'seq'), may hold values from 0.3 to 6144
- rate_log: float32 [8], replicated, may hold values from -20 to 0
- skip: float32 [8], replicated, may hold values from 0.5 to 1.5
- block_mask: int32 [4, 16, 16], P('dp'), may hold values from 0 to 1, as said below
- grad_out: bfloat16 [4, 2048, 1024], P('dp', 'seq'), may hold values from -10 to 10
Outputs:
- layer_out: bfloat16 [4, 2048, 1024], P('dp', 'seq')
- query_gradient: bfloat16 [4, 2048, 1024], P('dp', 'seq')
- key_gradient: bfloat16 [4, 2048, 128], P('dp', 'seq')
- value_gradient: bfloat16 [4, 2048, 128], P('dp', 'seq')
- grad_input: bfloat16 [4, 2048, 1024], P('dp', 'seq')
- grad_in_b: bfloat16 [4, 2048, 128], P('dp', 'seq')
- grad_in_c: bfloat16 [4, 2048, 128], P('dp', 'seq')
- grad_rate_log: float32 [8], replicated
- grad_skip: float32 [8], replicated
Inputs may be any that keep to these rules, and one draw needn't show every extreme that they name: block_mask[b, i, i] = 1; every row holds at most 6 ones, and the last row of every sequence's mask holds exactly 6.
All inputs are finite; a program needn't handle non-finite values.
Results may differ from a plain program's by a relative error of at most 0.02.
Values may be sent and summed in bfloat16 or wider, within the bound.
No kernel may reach another device: no remote copies, remote signals or barrier semaphores. Data moves between devices by JAX's collectives and lax.ppermute only.
A program may use at most 192 MiB of HBM per device.

v0:
```python
import jax
import jax.numpy as jnp
from jax import lax
from jax.sharding import PartitionSpec as P

HEAD_WIDTH = 128
QUERY_HEADS = 8
KEY_VALUE_HEADS = 1
HS = 8
P_SIZE = 128
NS = 128
BLOCK_TOKENS = 128


HIGH = lax.Precision.HIGHEST


def entering(value, axis, combine, identity, reverse):
    devices, mine = (lax.axis_size(axis), lax.axis_index(axis))
    everything = jax.tree.map(
        lambda part, kind: lax.all_gather(part.astype(kind), axis),
        value,
        (jnp.bfloat16, jnp.bfloat16),
    )
    start = jax.tree.map(
        lambda part, zero: jnp.broadcast_to(jnp.asarray(zero, part.dtype), part.shape),
        value,
        identity,
    )

    def lap(k, before):
        at = devices - 1 - k if reverse else k
        reached = at > mine if reverse else at < mine
        new = combine(
            before, jax.tree.map(lambda part, own: part[at].astype(own.dtype), everything, value)
        )
        return jax.tree.map(lambda a, b: jnp.where(reached, a, b), new, before)

    return lax.fori_loop(0, devices, lap, start)


def ssm_blocks(h_start, x_seq, b_seq, c_seq, rate_log, skip, step_sizes):
    heads = rate_log.shape[0]
    length = x_seq.shape[0]
    width = x_seq.shape[1] // heads
    count_of_blocks = length // BLOCK_TOKENS
    decay_log = -step_sizes * jnp.exp(rate_log)[None, :]
    lower = jnp.arange(BLOCK_TOKENS)[:, None] >= jnp.arange(BLOCK_TOKENS)[None, :]

    def one_block(state, pieces):
        x_block, b_block, c_block, log_block = pieces
        running = jnp.cumsum(log_block, axis=0)
        spread = running.T[:, :, None] - running.T[:, None, :]
        decay = jnp.exp(jnp.where(lower[None, :, :], spread, -jnp.inf))
        inner = jnp.dot(c_block, b_block.T, precision=HIGH)
        y_inner = jnp.einsum("hij,jhp->ihp", decay * inner[None, :, :], x_block, precision=HIGH)
        carried = jnp.einsum("in,hpn->ihp", c_block, state, precision=HIGH)
        y_block = y_inner + jnp.exp(running)[:, :, None] * carried + skip[None, :, None] * x_block
        tail = jnp.exp(running[-1][None, :] - running)
        fresh = jnp.einsum("jh,jhp,jn->hpn", tail, x_block, b_block, precision=HIGH)
        new_state = jnp.exp(running[-1])[:, None, None] * state + fresh
        return (new_state, y_block)

    pieces = (
        x_seq.reshape(count_of_blocks, BLOCK_TOKENS, heads, width),
        b_seq.reshape(count_of_blocks, BLOCK_TOKENS, -1),
        c_seq.reshape(count_of_blocks, BLOCK_TOKENS, -1),
        decay_log.reshape(count_of_blocks, BLOCK_TOKENS, heads),
    )
    h_end, y_all = lax.scan(one_block, h_start, pieces)
    return (y_all.reshape(length, heads * width), h_end)


def chain(earlier, later):
    decay_one, state_one = earlier
    decay_two, state_two = later
    return (decay_one * decay_two, decay_two[:, None, None] * state_one + state_two)


def block_attention(
    query_block, block_gradient, mask_row, every_key_row, every_value_row, holding_array
):
    block_piece = query_block.shape[0]
    head_groups = QUERY_HEADS // KEY_VALUE_HEADS
    factor = HEAD_WIDTH ** (-0.5)
    count_of_blocks = mask_row.shape[0]
    query_rows = query_block.reshape(block_piece, KEY_VALUE_HEADS, head_groups, HEAD_WIDTH)
    gradient_list = block_gradient.reshape(block_piece, KEY_VALUE_HEADS, head_groups, HEAD_WIDTH)
    ranking = jnp.argsort(
        (1 - mask_row) * count_of_blocks + jnp.arange(count_of_blocks, dtype=jnp.int32)
    )
    allowed = jnp.sum(mask_row)

    def fetch(step_index):
        first = ranking[step_index] * block_piece
        return (
            lax.dynamic_slice_in_dim(every_key_row, first, block_piece, 0),
            lax.dynamic_slice_in_dim(every_value_row, first, block_piece, 0),
            first,
        )

    def scores_of(k_tile):
        return (
            jnp.einsum("qhgd,khd->hgqk", query_rows, k_tile, preferred_element_type=jnp.float32)
            * factor
        )

    def online_step(step_index, carry):
        best, total, accum = carry
        k_tile, v_tile, first = fetch(step_index)
        scores = scores_of(k_tile)
        raised = jnp.maximum(best, jnp.max(scores, axis=-1))
        rescale = jnp.exp(best - raised)
        weights = jnp.exp(scores - raised[..., None])
        total = total * rescale + jnp.sum(weights, axis=-1)
        accum = accum * rescale[..., None] + jnp.einsum(
            "hgqk,khd->hgqd",
            weights.astype(jnp.bfloat16),
            v_tile,
            preferred_element_type=jnp.float32,
        )
        return (raised, total, accum)

    best, total, accum = lax.fori_loop(
        0,
        allowed,
        online_step,
        (
            jnp.full((KEY_VALUE_HEADS, head_groups, block_piece), -jnp.inf, jnp.float32),
            jnp.zeros((KEY_VALUE_HEADS, head_groups, block_piece), jnp.float32),
            jnp.zeros((KEY_VALUE_HEADS, head_groups, block_piece, HEAD_WIDTH), jnp.float32),
        ),
    )
    output = accum / total[..., None]
    delta = jnp.sum(
        output * jnp.transpose(gradient_list, (1, 2, 0, 3)).astype(jnp.float32), axis=-1
    )

    def tile_grads(k_tile, v_tile):
        probs = jnp.exp(scores_of(k_tile) - best[..., None]) / total[..., None]
        dprobs = jnp.einsum(
            "qhgd,khd->hgqk", gradient_list, v_tile, preferred_element_type=jnp.float32
        )
        dscores = (probs * (dprobs - delta[..., None])).astype(jnp.bfloat16)
        return (probs, dscores)

    def key_parts(probs, dscores):
        key_gradient_part = (
            jnp.einsum("hgqk,qhgd->khd", dscores, query_rows, preferred_element_type=jnp.float32)
            * factor
        )
        value_gradient_part = jnp.einsum(
            "hgqk,qhgd->khd",
            probs.astype(jnp.bfloat16),
            gradient_list,
            preferred_element_type=jnp.float32,
        )
        return jnp.concatenate(
            [
                key_gradient_part.reshape(block_piece, KEY_VALUE_HEADS * HEAD_WIDTH),
                value_gradient_part.reshape(block_piece, KEY_VALUE_HEADS * HEAD_WIDTH),
            ],
            axis=1,
        )

    def query_part(dscores, k_tile):
        return (
            jnp.einsum("hgqk,khd->qhgd", dscores, k_tile, preferred_element_type=jnp.float32)
            * factor
        )

    blank_query_rows = jnp.zeros(
        (block_piece, KEY_VALUE_HEADS, head_groups, HEAD_WIDTH), jnp.float32
    )

    def query_step(step_index, carry):
        query_gradient_part, terms = carry
        k_tile, v_tile, first = fetch(step_index)
        probs, dscores = tile_grads(k_tile, v_tile)
        query_gradient_part = query_gradient_part + query_part(dscores, k_tile)
        fresh = key_parts(probs, dscores)
        terms = lax.dynamic_update_slice_in_dim(
            terms, lax.dynamic_slice_in_dim(terms, first, block_piece, 0) + fresh, first, 0
        )
        return (query_gradient_part, terms)

    query_gradient_part, holding_array = lax.fori_loop(
        0, allowed, query_step, (blank_query_rows, holding_array)
    )

    def add_terms(start, term):
        span_rows = term.shape[0]

        def add_one(step_index, term):
            k_tile, v_tile, first = fetch(step_index)
            offset = first - start
            inside = jnp.logical_and(offset >= 0, offset < span_rows)

            def place(term):
                fresh = key_parts(*tile_grads(k_tile, v_tile))
                return lax.dynamic_update_slice_in_dim(
                    term, lax.dynamic_slice_in_dim(term, offset, block_piece, 0) + fresh, offset, 0
                )

            return lax.cond(inside, place, lambda same: same, term)

        return lax.fori_loop(0, allowed, add_one, term)

    output_rows = jnp.transpose(output, (2, 0, 1, 3)).reshape(block_piece, QUERY_HEADS * HEAD_WIDTH)
    return (
        output_rows,
        query_gradient_part.reshape(block_piece, QUERY_HEADS * HEAD_WIDTH),
        holding_array,
        add_terms,
    )


def body(query, key, value, ssm_input, in_b, in_c, step, rate_log, skip, block_mask, grad_out):
    local_rows = query.shape[1]
    per_device = local_rows // BLOCK_TOKENS
    collected_keys, collected_values = (
        lax.all_gather(key, "seq", axis=1, tiled=True),
        lax.all_gather(value, "seq", axis=1, tiled=True),
    )
    every_key_row = collected_keys[0].reshape(-1, KEY_VALUE_HEADS, HEAD_WIDTH)
    every_value_row = collected_values[0].reshape(-1, KEY_VALUE_HEADS, HEAD_WIDTH)
    complete_rows = every_key_row.shape[0]
    position = lax.axis_index("seq")
    q_local = query[0]
    g_local = grad_out[0]
    mask_all = block_mask[0]
    homes = [position * per_device + block for block in range(per_device)]
    holding_array = jnp.zeros((complete_rows, 2 * KEY_VALUE_HEADS * HEAD_WIDTH), jnp.float32)
    outputs = []
    query_grads = []
    adders = []
    for block in range(per_device):
        mask_row = lax.dynamic_index_in_dim(mask_all, homes[block], 0, keepdims=False)
        output_rows, grad_rows, holding_array, adder = block_attention(
            q_local[block * BLOCK_TOKENS : (block + 1) * BLOCK_TOKENS],
            g_local[block * BLOCK_TOKENS : (block + 1) * BLOCK_TOKENS],
            mask_row,
            every_key_row,
            every_value_row,
            holding_array,
        )
        outputs.append(output_rows)
        query_grads.append(grad_rows)
        adders.append(adder)
    attention = jnp.concatenate(outputs, axis=0)
    query_gradient = jnp.concatenate(query_grads, axis=0)
    summed_total = lax.psum_scatter(
        holding_array.astype(jnp.bfloat16), "seq", scatter_dimension=0, tiled=True
    ).astype(jnp.float32)
    x_float = ssm_input[0].astype(jnp.float32)
    b_float = in_b[0].astype(jnp.float32)
    c_float = in_c[0].astype(jnp.float32)
    step_local = step[0]
    down = g_local.astype(jnp.float32)
    zero_state = jnp.zeros((HS, P_SIZE, NS), jnp.float32)
    decay_log = -step_local * jnp.exp(rate_log)[None, :]
    running = jnp.cumsum(decay_log, axis=0)
    decay_total = jnp.exp(running[-1])
    x_heads = x_float.reshape(local_rows, HS, P_SIZE)
    end_state = jnp.einsum(
        "th,thp,tn->hpn", jnp.exp(running[-1][None, :] - running), x_heads, b_float, precision=HIGH
    )
    identity = (jnp.ones_like(decay_total), zero_state)
    start_decay, start_state = entering((decay_total, end_state), "seq", chain, identity, False)
    start_grad = jnp.einsum(
        "th,thp,tn->hpn",
        jnp.exp(running),
        down.reshape(local_rows, HS, P_SIZE),
        c_float,
        precision=HIGH,
    )
    later_decay, later_state = entering((decay_total, start_grad), "seq", chain, identity, True)
    (ssm_out, state_out), pullback = jax.vjp(
        ssm_blocks, start_state, x_float, b_float, c_float, rate_log, skip, step_local
    )
    gradient_list = pullback((down, later_state))
    rate_sum, skip_sum = lax.psum((gradient_list[4], gradient_list[5]), ("dp", "seq"))
    tokens_all = lax.axis_size("dp") * lax.axis_size("seq") * local_rows
    grad_rate_log = rate_sum / tokens_all
    grad_skip = skip_sum / (tokens_all * P_SIZE)
    layer_out = (attention + ssm_out).astype(jnp.bfloat16)[None]
    key_gradient = summed_total[:, : KEY_VALUE_HEADS * HEAD_WIDTH].astype(jnp.bfloat16)[None]
    value_gradient = summed_total[:, KEY_VALUE_HEADS * HEAD_WIDTH :].astype(jnp.bfloat16)[None]
    return (
        layer_out,
        query_gradient.astype(jnp.bfloat16)[None],
        key_gradient,
        value_gradient,
        gradient_list[1].astype(jnp.bfloat16)[None],
        gradient_list[2].astype(jnp.bfloat16)[None],
        gradient_list[3].astype(jnp.bfloat16)[None],
        grad_rate_log,
        grad_skip,
    )


def solution(mesh):
    in_specs = (
        P("dp", "seq", None),
        P("dp", "seq", None),
        P("dp", "seq", None),
        P("dp", "seq", None),
        P("dp", "seq", None),
        P("dp", "seq", None),
        P("dp", "seq", None),
        P(),
        P(),
        P("dp", None, None),
        P("dp", "seq", None),
    )
    out_specs = (
        P("dp", "seq", None),
        P("dp", "seq", None),
        P("dp", "seq", None),
        P("dp", "seq", None),
        P("dp", "seq", None),
        P("dp", "seq", None),
        P("dp", "seq", None),
        P(),
        P(),
    )
    return jax.shard_map(body, mesh=mesh, in_specs=in_specs, out_specs=out_specs, check_vma=False)
```

profile of v0, /device:TPU:0, one launch (start us, length us, event | category | flops | bytes accessed | tf_op | source)
XLA Modules:
  0.0 349.7 jit_solution(3028856755081038883)
XLA Ops:
  9.4 11.6 %all_gather.24 = bf16[1,2048,128]{2,1,0:T(8,128)(2,1)S(1)} all-gather(bf16[1,256,128]{2,1,0:T(8,128)(2,1)} %param.28), channel_id=1, replica_groups=mesh['dp'=4,'seq'=8] {'seq'}, dimensions={1}, use_global_device_ids=true | all-gather | bytes 589824 | tf_op jit(solution)/shard_map/all_gather | solution.py:222
  21.0 9.5 %all_gather.25 = bf16[1,2048,128]{2,1,0:T(8,128)(2,1)S(1)} all-gather(bf16[1,256,128]{2,1,0:T(8,128)(2,1)} %param.29), channel_id=1, replica_groups=mesh['dp'=4,'seq'=8] {'seq'}, dimensions={1}, use_global_device_ids=true | all-gather | bytes 589824 | tf_op jit(solution)/shard_map/all_gather | solution.py:223
  34.0 3.4 while.146
  39.8 6.1 %while.148 = (s32[]{:T(128)}, f32[128,1,8,128]{0,3,2,1:T(8,128)S(1)}, f32[2048,256]{0,1:T(8,128)S(1)}, s32[]{:T(128)}, s32[16]{0:T(128)S(1)}, /*index=5*/bf16[20...) while((s32[]{:T(128)}, ...), condition=%wide.region_21.22_spmd, body=%wide.region_20.21_spmd.sunk | while | flops 169033728 | bytes 5091593 | solution.py:187
  49.5 5.1 %while.147 = (s32[]{:T(128)}, f32[1,8,128]{2,1,0:T(8,128)S(1)}, f32[1,8,128]{2,1,0:T(8,128)S(1)}, f32[1,8,128,128]{3,2,1,0:T(8,128)S(1)}, s32[]{:T(128)}, /*inde...) while((s32[]{:T(128)}, f32[1,8,128]{2,1,0:T(8,128)S(1)}, ...), condition=%wide.region_11.12_spmd, body=%wide.region_8.0_spmd.sunk | while | flops 68160520 | bytes 3014889 | solution.py:124
  56.8 7.7 %while.149 = (s32[]{:T(128)}, f32[128,1,8,128]{0,3,2,1:T(8,128)S(1)}, f32[2048,256]{0,1:T(8,128)}, s32[]{:T(128)}, s32[16]{0:T(128)S(1)}, /*index=5*/bf16[2048,1...) while((s32[]{:T(128)}, ...), condition=%wide.region_24.25_spmd, body=%wide.region_23.24_spmd.sunk | while | flops 169033728 | bytes 5091593 | solution.py:187
  64.5 2.6 copy.222
  69.6 2.6 convolution_convert_fusion.1
  73.5 2.5 convolution_convert_fusion
  79.6 81.6 %all-gather.2 = bf16[8,1,8]{2,1,0:T(2,128)(2,1)S(1)} all-gather(bf16[1,1,8]{2,1,0:T(2,128)(2,1)S(1)} %bitcast.791), channel_id=1, replica_groups=mesh['dp'=4,'seq'=8] {'seq'}, dimensions={0}, use_global_device_ids=true | all-gather | bytes 144 | tf_op jit(solution)/shard_map/all_gather | solution.py:21
  162.5 2.4 copy.282
  171.1 21.8 %reduce-scatter.2.cloned.1.call-done = bf16[256,256]{1,0:T(8,128)(2,1)} async-done(((bf16[2048,256]{1,0:T(8,128)(2,1)}), bf16[256,256]{1,0:T(8,128)(2,1)}) %reduce-scatter.2.cloned.1.call-update) | async-done | bytes 131088 | tf_op jit(solution)/shard_map/reduce_scatter | solution.py:252
  194.5 28.3 %all-gather.6.cloned.1.call-done = bf16[64,128,128]{2,1,0:T(8,128)(2,1)} async-done(((bf16[8,128,128]{2,1,0:T(8,128)(2,1)}), bf16[64,128,128]{2,1,0:T(8,128)(2,1)}) %all-gather.6.cloned.1.call-update) | async-done | bytes 2097168 | tf_op jit(solution)/shard_map/all_gather | solution.py:21
  222.8 9.1 %while.151 = (s32[]{:T(128)}, f32[8,128,128]{2,1,0:T(8,128)S(1)}, s32[]{:T(128)}, bf16[8,8]{1,0:T(8,128)(2,1)S(1)}, bf16[8,8,128,128]{3,2,1,0:T(8,128)(2,1)}, /*index=5*/s32[]{:T(128)}, s32[]{:T(128)}) while((s32[]{:T(128)}, f32[8,128,128]{2,1,0:T(8,128)S(1)}, s32[]{:T(128)}, bf16[8,8]{1,0:T(8,128)(2,1)S(1)}, ...), condition=%wide.region_15.16_spmd.clone, body=%wide.region_14.15_spmd.clone.sunk | while | flops 655372 | bytes 1310905 | solution.py:39
  233.0 20.3 %while.150 = (s32[]{:T(128)}, f32[8,128,128]{2,1,0:T(8,128)S(1)}, f32[2,128,8,128]{3,2,1,0:T(8,128)}, f32[2,8,128,128]{3,2,1,0:T(8,128)}, f32[2,128,128]{1,2,0:T...) while((s32[]{:T(128)}, f32[8,128,128]{2,1,0:T(8,128)S(1)}, ...), condition=%wide.region_18.19_spmd.clone.clone, body=%wide.region_16.18_spmd.clone.clone.sunk | while | flops 631112704 | bytes 22333552 | solution.py:70
  253.3 9.2 %while.152 = (s32[]{:T(128)}, f32[8,128,128]{2,1,0:T(8,128)S(1)}, s32[]{:T(128)}, bf16[8,8]{1,0:T(8,128)(2,1)S(1)}, bf16[8,8,128,128]{3,2,1,0:T(8,128)(2,1)}, /*index=5*/s32[]{:T(128)}, s32[]{:T(128)}, s32[]{:T(128)}, s32[]{:T(128)}) while((s32[]{:T(128)}, f32[8,128,128]{2,1,0:T(8,128)S(1)}, s32[]{:T(128)}, ...), condition=%wide.region_27.28_spmd.clone, body=%wide.region_26.27_spmd.clone.sunk | while | flops 655376 | bytes 1310967 | solution.py:39
  264.5 34.0 %while.153 = (s32[]{:T(128)}, f32[8]{0:T(128)S(1)}, f32[8,128,128]{2,1,0:T(8,128)S(1)}, bf16[2,128,8,128]{3,1,2,0:T(8,128)(2,1)}, bf16[2,128,128]{2,1,0:T(8,128)...) while((s32[]{:T(128)}, f32[8]{0:T(128)S(1)}, ...), condition=%wide.region_37.38_spmd.clone, body=%wide.region_28.37_spmd.clone.sunk | while | flops 1261459456 | bytes 24430788 | solution.py:70
  268.0 2.1 multiply_reduce_fusion.5
  273.0 1.9 convolution_bitcast_fusion.19
  276.0 2.9 fusion.349
  285.0 2.1 multiply_reduce_fusion.5
  290.0 1.9 convolution_bitcast_fusion.19
  293.0 2.9 fusion.349
  302.3 39.3 %all-reduce.2 = (f32[8]{0:T(128)S(1)}, f32[8]{0:T(128)S(1)}) all-reduce(f32[8]{0:T(128)S(1)} %exponential_multiply_fusion, f32[8]{0:T(128)S(1)} %get-tuple-element.1173), channel_id=1, replica_groups=mesh['dp'=4,'seq'=8] {'dp','seq'}, use_global_device_ids=true, to_apply=%region_39.40 | all-reduce | flops 16 | bytes 128 | tf_op jit(solution)/shard_map/psum | solution.py:282
  (345 shorter events, 110.1 us)
Async XLA Ops:
  7.2 185.8 %reduce-scatter.2.cloned.1.call-start = ((), (), s32[]{:S(2)}) async-start(), calls=%async_computation.1 | async-start | bytes 1179648 | tf_op jit(solution)/shard_map/reduce_scatter | solution.py:252
  67.2 155.5 %all-gather.6.cloned.1.call-start = ((), (), s32[]{:S(2)}) async-start(), calls=%async_computation.2 | async-start | bytes 2359296 | tf_op jit(solution)/shard_map/all_gather | solution.py:21
  72.2 181.1 %all-gather.8.cloned.1.call-start = ((), (), s32[]{:S(2)}) async-start(), calls=%async_computation.3 | async-start | bytes 2359296 | tf_op jit(solution)/shard_map/all_gather | solution.py:21
  78.7 86.3 %copy-start.8 = (f32[32,8,8,128]{3,1,2,0:T(8,128)S(1)}, f32[32,8,8,128]{3,1,2,0:T(8,128)}, u32[]{:S(2)}) copy-start(f32[32,8,8,128]{3,1,2,0:T(8,128)} %convert_bitcast_fusion) | copy-start | bytes 3145732
  168.1 54.7 %copy-start.33 = (bf16[8,1,8]{2,0,1:T(8,128)(2,1)S(1)}, bf16[8,1,8]{2,0,1:T(8,128)(2,1)}, u32[]{:S(2)}) copy-start(bf16[8,1,8]{2,0,1:T(8,128)(2,1)} %copy.313) | copy-start | bytes 388
  222.7 10.3 %copy-start.16 = (f32[2,128,8]{2,1,0:T(8,128)S(1)}, f32[2,128,8]{2,1,0:T(8,128)}, u32[]{:S(2)}) copy-start(f32[2,128,8]{2,1,0:T(8,128)} %broadcast_multiply_fusion) | copy-start | bytes 24580
  222.7 10.3 %copy-start.27 = (f32[8]{0:T(128)S(1)}, f32[8]{0:T(128)}, u32[]{:S(2)}) copy-start(f32[8]{0:T(128)} %param.35) | copy-start | bytes 100
  222.7 10.3 %copy-start.28 = (f32[2,128,8]{1,2,0:T(8,128)S(1)}, f32[2,128,8]{1,2,0:T(8,128)}, u32[]{:S(2)}) copy-start(f32[2,128,8]{1,2,0:T(8,128)} %custom-call.9) | copy-start | bytes 24580
  222.7 10.3 %copy-start.29 = (f32[2,128,8,1]{1,2,3,0:T(8,128)S(1)}, f32[2,128,8,1]{1,2,3,0:T(8,128)}, u32[]{:S(2)}) copy-start(f32[2,128,8,1]{1,2,3,0:T(8,128)} %custom-call.10) | copy-start | bytes 24580
  222.7 10.2 %copy-start.30 = (f32[2,128,8]{1,2,0:T(8,128)S(1)}, f32[2,128,8]{1,2,0:T(8,128)}, u32[]{:S(2)}) copy-start(f32[2,128,8]{1,2,0:T(8,128)} %custom-call.11) | copy-start | bytes 24580
  222.7 10.2 %copy-start.34 = (f32[2,8]{1,0:T(2,128)S(1)}, f32[2,8]{1,0:T(2,128)}, u32[]{:S(2)}) copy-start(f32[2,8]{1,0:T(2,128)} %custom-call.13) | copy-start | bytes 196
  222.8 10.2 %copy-start.37 = (f32[2,8,1,1]{1,3,2,0:T(1,128)S(1)}, f32[2,8,1,1]{1,3,2,0:T(1,128)}, u32[]{:S(2)}) copy-start(f32[2,8,1,1]{1,3,2,0:T(1,128)} %custom-call.14) | copy-start | bytes 196
  253.3 11.1 %copy-start = (f32[2,128,8,128]{3,2,1,0:T(8,128)S(1)}, f32[2,128,8,128]{3,2,1,0:T(8,128)}, u32[]{:S(2)}) copy-start(f32[2,128,8,128]{3,2,1,0:T(8,128)} %get-tuple-element.2952) | copy-start | bytes 3145732
  253.3 11.1 %copy-start.32 = (f32[8]{0:T(128)S(1)}, f32[8]{0:T(128)}, u32[]{:S(2)}) copy-start(f32[8]{0:T(128)} %custom-call.2) | copy-start | bytes 100
  264.5 35.1 %copy-start.36 = (f32[8]{0:T(128)S(1)}, f32[8]{0:T(128)}, u32[]{:S(2)}) copy-start(f32[8]{0:T(128)} %param.34) | copy-start | bytes 100
  268.0 7.0 %copy-start.25 = (bf16[2,128,128]{2,1,0:T(8,128)(2,1)S(1)}, bf16[2,128,128]{2,1,0:T(8,128)(2,1)}, u32[]{:S(2)}) copy-start(bf16[2,128,128]{2,1,0:T(8,128)(2,1)} %get-tuple-element.2898) | copy-start | bytes 196612 | tf_op jit(solution)/shard_map/transpose(jvp())/while
  273.0 5.9 %copy-start.4 = (f32[2,128,8,128]{1,3,2,0:T(8,128)S(1)}, f32[2,128,8,128]{1,3,2,0:T(8,128)}, u32[]{:S(2)}) copy-start(f32[2,128,8,128]{1,3,2,0:T(8,128)} %get-tuple-element.2937) | copy-start | bytes 3145732 | tf_op jit(solution)/shard_map/transpose(jvp())/while
  273.0 6.9 %copy-start.20 = (f32[2,128,8]{2,1,0:T(8,128)}, f32[2,128,8]{2,1,0:T(8,128)S(1)}, u32[]{:S(2)}) copy-start(f32[2,128,8]{2,1,0:T(8,128)S(1)} %constant_dynamic-update-slice_fusion.15) | copy-start | bytes 24580 | tf_op jit(solution)/shard_map/transpose(jvp())/while
  273.0 6.9 %copy-start.23 = (bf16[2,128,128]{2,1,0:T(8,128)(2,1)S(1)}, bf16[2,128,128]{2,1,0:T(8,128)(2,1)}, u32[]{:S(2)}) copy-start(bf16[2,128,128]{2,1,0:T(8,128)(2,1)} %get-tuple-element.2897) | copy-start | bytes 196612 | tf_op jit(solution)/shard_map/transpose(jvp())/while
  285.0 6.9 %copy-start.25 = (bf16[2,128,128]{2,1,0:T(8,128)(2,1)S(1)}, bf16[2,128,128]{2,1,0:T(8,128)(2,1)}, u32[]{:S(2)}) copy-start(bf16[2,128,128]{2,1,0:T(8,128)(2,1)} %get-tuple-element.2898) | copy-start | bytes 196612 | tf_op jit(solution)/shard_map/transpose(jvp())/while
  290.0 6.9 %copy-start.20 = (f32[2,128,8]{2,1,0:T(8,128)}, f32[2,128,8]{2,1,0:T(8,128)S(1)}, u32[]{:S(2)}) copy-start(f32[2,128,8]{2,1,0:T(8,128)S(1)} %constant_dynamic-update-slice_fusion.15) | copy-start | bytes 24580 | tf_op jit(solution)/shard_map/transpose(jvp())/while
  290.0 6.9 %copy-start.23 = (bf16[2,128,128]{2,1,0:T(8,128)(2,1)S(1)}, bf16[2,128,128]{2,1,0:T(8,128)(2,1)}, u32[]{:S(2)}) copy-start(bf16[2,128,128]{2,1,0:T(8,128)(2,1)} %get-tuple-element.2897) | copy-start | bytes 196612 | tf_op jit(solution)/shard_map/transpose(jvp())/while
  299.7 42.5 %copy-start.12 = (f32[1,128,1024]{2,1,0:T(8,128)S(1)}, f32[1,128,1024]{2,1,0:T(8,128)}, u32[]{:S(2)}) copy-start(f32[1,128,1024]{2,1,0:T(8,128)} %copy.256) | copy-start | bytes 1572868
  299.7 42.5 %copy-start.13 = (f32[1,128,1024]{2,1,0:T(8,128)S(1)}, f32[1,128,1024]{2,1,0:T(8,128)}, u32[]{:S(2)}) copy-start(f32[1,128,1024]{2,1,0:T(8,128)} %copy.257) | copy-start | bytes 1572868
  (27 other events, 86.0 us)
Sparse Core Ops, SparseCore 0:
  67.3 125.5 reduce-scatter.1
  194.8 27.8 all-gather.5
  224.6 27.9 all-gather.7
where the time goes:
time: 350 us
  blocking collectives  142 us (41%)
  waiting for transfers between devices  50.1 us (14%)
  matrix products  47.6 us (14%)
  other arithmetic  43.6 us (12%)
  local copies, waits for them, and re-layouts  42.5 us (12%)
  between operations  14.4 us (4%)
  loops' own time  9.29 us (3%)
    all_gather x1, blocking collectives, entering(): lax.all_gather(part.astype(kind), axis)  81.6 us
    psum x1, blocking collectives, body(): lax.psum((gradient_list[4], gradient_list[5]), ('dp', 'seq'))  39.3 us
    all_gather x2, waiting for transfers between devices, entering(): lax.all_gather(part.astype(kind), axis)  28.3 us
    reduce_scatter x1, waiting for transfers between devices, body(): lax.psum_scatter(holding_array.astype(jnp.bfloat16), 'seq', scatter_dimen...  21.8 us
    select_n x16, other arithmetic, lap(): return jax.tree.map(lambda a, b: jnp.where(reached, a, b), new, before)  17.6 us
    all_gather x1, blocking collectives, body(): lax.all_gather(key, 'seq', axis=1, tiled=True)  11.6 us
    dot_general x6, matrix products, one_block(): jnp.einsum('hij,jhp->ihp', decay * inner[None, :, :], x_block, precision=...  11.1 us
    all_gather x1, blocking collectives, body(): lax.all_gather(value, 'seq', axis=1, tiled=True)  9.53 us
  transfers between devices with their start and end apart: 3, of which 2 were waited for; matrix products, arithmetic and copies ran while one was open for 15% of the time, Pallas kernels for 0%

commit v1 on v0

v1 whole, which is shorter than its diff:
```python
import jax
import jax.numpy as jnp
from jax import lax
from jax.experimental import pallas as pl
from jax.experimental.pallas import tpu as pltpu
from jax.sharding import PartitionSpec as P

HEAD_WIDTH = 128
QUERY_HEADS = 8
HS = 8
P_SIZE = 128
NS = 128
BLOCK = 128
WIDE = HS * P_SIZE
LANES = 128
FACTOR = HEAD_WIDTH ** (-0.5)
LOG2E = 1.4426950408889634
NEG = -1e30
HIGH = lax.Precision.HIGHEST
F32 = jnp.float32
BF16 = jnp.bfloat16

VMEM = pl.BlockSpec(memory_space=pltpu.VMEM)
SMEM = pl.BlockSpec(memory_space=pltpu.SMEM)


def params(limit=56 << 20):
    return pltpu.CompilerParams(vmem_limit_bytes=limit)


def dot(a, b, ca, cb, precision=None):
    return lax.dot_general(
        a, b, (((ca,), (cb,)), ((), ())), preferred_element_type=F32, precision=precision
    )


def head(h):
    return slice(h * LANES, (h + 1) * LANES)


def running_logs(step_ref, rate_ref, pad_ref):
    pad_ref[...] = jnp.zeros_like(pad_ref)
    pad_ref[:, :HS] = -step_ref[...] * jnp.exp(rate_ref[...])
    row = lax.broadcasted_iota(jnp.int32, (BLOCK, BLOCK), 0)
    col = lax.broadcasted_iota(jnp.int32, (BLOCK, BLOCK), 1)
    lower = jnp.where(row >= col, 1.0, 0.0).astype(F32)
    run0 = dot(lower, pad_ref[:BLOCK], 1, 0, HIGH)
    run1 = dot(lower, pad_ref[BLOCK:], 1, 0, HIGH)
    return run0, run1


def scaled(x_ref, column, out_ref):
    for h in range(HS):
        out_ref[:, head(h)] = (x_ref[:, head(h)].astype(F32) * column[:, h : h + 1]).astype(BF16)


def local_states_kernel(
    x_ref, g_ref, b_ref, c_ref, step_ref, rate_ref, out_ref, pad_ref, xt_ref, gt_ref
):
    run0, run1 = running_logs(step_ref, rate_ref, pad_ref)
    t0, t1 = run0[BLOCK - 1 :, :], run1[BLOCK - 1 :, :]
    enter = jnp.exp(jnp.concatenate([run0, run1 + t0], axis=0))
    tail = jnp.exp(jnp.concatenate([(t0 - run0) + t1, t1 - run1], axis=0))
    scaled(x_ref, tail, xt_ref)
    scaled(g_ref, enter, gt_ref)
    out_ref[0, :, :WIDE] = dot(b_ref[...], xt_ref[...], 0, 0).astype(BF16)
    out_ref[1, :, :WIDE] = dot(c_ref[...], gt_ref[...], 0, 0).astype(BF16)
    total = t0 + t1
    high = total.astype(BF16).astype(F32)
    middle = (total - high).astype(BF16).astype(F32)
    low = total - high - middle
    place = lax.broadcasted_iota(jnp.int32, (NS, LANES), 0) % 4
    logs = jnp.where(place == 0, high, jnp.where(place == 1, middle, low)).astype(BF16)
    out_ref[0, :, WIDE:] = logs
    out_ref[1, :, WIDE:] = logs


def chain_kernel(n, rows, in_ref, out_ref):
    decays = []
    for e in range(n):
        logs = in_ref[0, e * rows : (e + 1) * rows, WIDE:].astype(F32)
        total = logs[0:1, :] + logs[1:2, :] + logs[2:3, :]
        factor = jnp.exp(total)
        decays.append([factor[:, h : h + 1] for h in range(HS)])
    for direction in range(2):
        for h in range(HS):
            state = jnp.zeros((rows, LANES), F32)
            for e in range(n) if direction == 0 else range(n - 1, -1, -1):
                at = slice(e * rows, (e + 1) * rows)
                out_ref[direction, at, head(h)] = state.astype(BF16)
                state = state * decays[e][h] + in_ref[direction, at, head(h)].astype(F32)


def attention_kernel(
    mask_ref, first_ref, q_ref, g_ref, kv_ref, out_ref, dq_ref, dkv_ref,
    index_ref, s_ref, acc_ref, qs_ref, gs_ref, ds_ref, pr_ref, o_ref, dqt_ref, rows_ref,
):
    count = mask_ref.shape[0]
    columns = QUERY_HEADS * BLOCK
    acc_ref[...] = jnp.zeros_like(acc_ref)
    scale = FACTOR * LOG2E
    for block in range(q_ref.shape[0] // BLOCK):
        at = slice(block * BLOCK, (block + 1) * BLOCK)
        row = first_ref[0] + block

        def note(j, n):
            @pl.when(mask_ref[row, j] == 1)
            def _():
                index_ref[n] = j

            return n + mask_ref[row, j]

        allowed = lax.fori_loop(0, count, note, 0)
        index_ref[allowed] = row
        pairs = (allowed + 1) // 2
        for h in range(QUERY_HEADS):
            qs_ref[head(h), :] = q_ref[at, head(h)]
            gs_ref[head(h), :] = g_ref[at, head(h)]

        def spans(t):
            first = pl.multiple_of(index_ref[2 * t] * BLOCK, BLOCK)
            second = pl.multiple_of(index_ref[2 * t + 1] * BLOCK, BLOCK)
            return pl.ds(first, BLOCK), pl.ds(second, BLOCK)

        def tile(t, lanes):
            one, two = spans(t)
            return jnp.concatenate([kv_ref[one, lanes], kv_ref[two, lanes]], axis=0)

        def scores_step(t, best):
            k_tile = tile(t, slice(0, LANES))
            live = 2 * t + 1 < allowed
            outs = []
            for part in range(columns // 256):
                lanes = slice(part * 256, (part + 1) * 256)
                s = dot(k_tile, qs_ref[lanes, :], 1, 1)
                low = s[:BLOCK]
                high = jnp.where(live, s[BLOCK:], NEG)
                s_ref[t, :BLOCK, lanes] = low
                s_ref[t, BLOCK:, lanes] = high
                both = jnp.maximum(low, high).reshape(BLOCK // 8, 8, 256)
                outs.append(jnp.maximum(best[part], jnp.max(both, axis=0)))
            return tuple(outs)

        best = lax.fori_loop(
            0, pairs, scores_step, tuple(jnp.full((8, 256), NEG, F32) for _ in range(columns // 256))
        )
        for part in range(columns // 256):
            lanes = slice(part * 256, (part + 1) * 256)
            rows_ref[0:1, lanes] = jnp.max(best[part], axis=0, keepdims=True) * scale
        o_ref[...] = jnp.zeros_like(o_ref)

        def weights_step(t, total):
            v_tile = tile(t, slice(LANES, 2 * LANES))
            outs = []
            for part in range(columns // 256):
                lanes = slice(part * 256, (part + 1) * 256)
                w = jnp.exp2(s_ref[t, :, lanes] * scale - rows_ref[0:1, lanes])
                s_ref[t, :, lanes] = w
                outs.append(total[part] + jnp.sum(w.reshape(32, 8, 256), axis=0))
                o_ref[:, lanes] += dot(v_tile, w.astype(BF16), 0, 0)
            return tuple(outs)

        total = lax.fori_loop(
            0, pairs, weights_step, tuple(jnp.zeros((8, 256), F32) for _ in range(columns // 256))
        )
        for part in range(columns // 256):
            lanes = slice(part * 256, (part + 1) * 256)
            inverse = 1.0 / jnp.sum(total[part], axis=0, keepdims=True)
            rows_ref[1:2, lanes] = inverse
            o = o_ref[:, lanes] * inverse
            o_ref[:, lanes] = o
            g_t = gs_ref[lanes, :].astype(F32).T
            rows_ref[2:3, lanes] = jnp.sum(o * g_t, axis=0, keepdims=True)
        for h in range(QUERY_HEADS):
            out_ref[at, head(h)] = o_ref[:, head(h)].T
        dqt_ref[...] = jnp.zeros_like(dqt_ref)

        def grads_step(t, carry):
            k_tile = tile(t, slice(0, LANES))
            v_tile = tile(t, slice(LANES, 2 * LANES))
            for part in range(columns // 256):
                lanes = slice(part * 256, (part + 1) * 256)
                dp = dot(v_tile, gs_ref[lanes, :], 1, 1)
                probs = s_ref[t, :, lanes] * rows_ref[1:2, lanes]
                ds = (probs * (dp - rows_ref[2:3, lanes])).astype(BF16)
                ds_ref[:, lanes] = ds
                pr_ref[:, lanes] = probs.astype(BF16)
                dqt_ref[:, lanes] += dot(k_tile, ds, 0, 0)
            dk = dot(ds_ref[...], qs_ref[...], 1, 0) * FACTOR
            dv = dot(pr_ref[...], gs_ref[...], 1, 0)
            one, two = spans(t)
            acc_ref[one, :LANES] += dk[:BLOCK]
            acc_ref[one, LANES:] += dv[:BLOCK]
            acc_ref[two, :LANES] += dk[BLOCK:]
            acc_ref[two, LANES:] += dv[BLOCK:]
            return carry

        lax.fori_loop(0, pairs, grads_step, 0)
        for h in range(QUERY_HEADS):
            dq_ref[at, head(h)] = (dqt_ref[:, head(h)].T * FACTOR).astype(BF16)
    dkv_ref[...] = acc_ref[...].astype(BF16)


def ssm_kernel(
    x_ref, g_ref, b_ref, c_ref, step_ref, rate_ref, skip_ref, ent_ref, att_ref,
    y_ref, dx_ref, db_ref, dc_ref, sums_ref,
    pad_ref, xt_ref, gt_ref, inner_ref, dinner_ref, m_ref, runt_ref,
):
    tokens = 2 * BLOCK
    run0, run1 = running_logs(step_ref, rate_ref, pad_ref)
    t0, t1 = run0[BLOCK - 1 :, :], run1[BLOCK - 1 :, :]
    enter_log = jnp.concatenate([run0, run1 + t0], axis=0)
    tail_log = jnp.concatenate([(t0 - run0) + t1, t1 - run1], axis=0)
    enter, tail = jnp.exp(enter_log), jnp.exp(tail_log)
    scaled(x_ref, tail, xt_ref)
    scaled(g_ref, enter, gt_ref)
    own = jnp.concatenate([run0, run1], axis=0)
    runt_ref[:, :tokens] = own.T
    runt_ref[:, tokens:] = jnp.concatenate([run0 - t0, run1], axis=0).T
    b = b_ref[...]
    c = c_ref[...]
    inner_ref[...] = dot(c, b, 1, 1)
    dinner_ref[...] = jnp.zeros_like(dinner_ref)
    row0 = lax.broadcasted_iota(jnp.int32, (BLOCK, BLOCK), 0)
    col0 = lax.broadcasted_iota(jnp.int32, (BLOCK, BLOCK), 1)
    row1 = lax.broadcasted_iota(jnp.int32, (BLOCK, tokens), 0)
    col1 = lax.broadcasted_iota(jnp.int32, (BLOCK, tokens), 1)
    seen0 = row0 >= col0
    seen1 = row1 + BLOCK >= col1
    m_ref[:BLOCK, BLOCK:] = jnp.zeros((BLOCK, BLOCK), BF16)
    both = t0 + t1
    for h in range(HS):
        lanes = head(h)
        x = x_ref[:, lanes]
        g = g_ref[:, lanes]
        xf, gf = x.astype(F32), g.astype(F32)
        gain = skip_ref[0, h]
        spread0 = jnp.where(seen0, own[:BLOCK, h : h + 1] - runt_ref[h : h + 1, :BLOCK], NEG)
        spread1 = jnp.where(seen1, own[BLOCK:, h : h + 1] - runt_ref[h : h + 1, tokens:], NEG)
        decay0, decay1 = jnp.exp(spread0), jnp.exp(spread1)
        dm = dot(g, x, 1, 1)
        e0, e1 = decay0 * dm[:BLOCK, :BLOCK], decay1 * dm[BLOCK:, :]
        m_ref[:BLOCK, :BLOCK] = (decay0 * inner_ref[:BLOCK, :BLOCK]).astype(BF16)
        m_ref[BLOCK:, :] = (decay1 * inner_ref[BLOCK:, :]).astype(BF16)
        dinner_ref[:BLOCK, :BLOCK] += e0
        dinner_ref[BLOCK:, :] += e1
        w0 = jnp.sum(spread0 * (e0 * inner_ref[:BLOCK, :BLOCK]), axis=0, keepdims=True)
        w1 = jnp.sum(spread1 * (e1 * inner_ref[BLOCK:, :]), axis=0, keepdims=True)
        rate = w0 + w1[:, :BLOCK] + w1[:, BLOCK:]
        h0 = ent_ref[0, :, lanes]
        later = ent_ref[1, :, lanes]
        carried = dot(c, h0, 1, 0) * enter[:, h : h + 1]
        back = dot(b, later, 1, 0) * tail[:, h : h + 1]
        m = m_ref[...]
        y = dot(m, x, 1, 0) + carried + gain * xf
        y_ref[:, lanes] = (y + att_ref[:, lanes]).astype(BF16)
        dx_ref[:, lanes] = (dot(m, g, 0, 0) + back + gain * gf).astype(BF16)
        rate += jnp.sum(
            gf * carried * enter_log[:, h : h + 1] + xf * back * tail_log[:, h : h + 1],
            axis=0,
            keepdims=True,
        )
        cross = jnp.sum(h0.astype(F32) * later.astype(F32), axis=0, keepdims=True)
        whole = both[:, h : h + 1]
        rate += cross * (whole * jnp.exp(whole))
        sums_ref[h : h + 1, :] = rate
        sums_ref[HS + h : HS + h + 1, :] = jnp.sum(gf * xf, axis=0, keepdims=True)
    dinner = dinner_ref[...].astype(BF16)
    dc = dot(dinner, b, 1, 0) + dot(gt_ref[...], ent_ref[0], 1, 1)
    db = dot(dinner, c, 0, 0) + dot(xt_ref[...], ent_ref[1], 1, 1)
    dc_ref[...] = dc.astype(BF16)
    db_ref[...] = db.astype(BF16)


def body(query, key, value, ssm_input, in_b, in_c, step, rate_log, skip, block_mask, grad_out):
    n = lax.axis_size("seq")
    tokens = query.shape[1]
    per_device = tokens // BLOCK
    blocks = block_mask.shape[1]
    most = 3 * blocks // 8
    every = blocks * BLOCK
    q, g, x = query[0], grad_out[0], ssm_input[0]
    b, c = in_b[0], in_c[0]
    rate_row, skip_row = rate_log.reshape(1, HS), skip.reshape(1, HS)
    shape = jax.ShapeDtypeStruct

    kv = jnp.concatenate([key[0], value[0]], axis=1)
    kv_all = lax.all_gather(kv, "seq", axis=0, tiled=True)

    states = pl.pallas_call(
        local_states_kernel,
        out_shape=shape((2, NS, WIDE + LANES), BF16),
        in_specs=[VMEM] * 6,
        out_specs=VMEM,
        scratch_shapes=[
            pltpu.VMEM((tokens, LANES), F32),
            pltpu.VMEM((tokens, WIDE), BF16),
            pltpu.VMEM((tokens, WIDE), BF16),
        ],
        compiler_params=params(),
        name="local_states",
    )(x, g, b, c, step[0], rate_row)
    rows = NS // n
    swapped = lax.all_to_all(states, "seq", split_axis=1, concat_axis=1, tiled=True)
    chained = pl.pallas_call(
        lambda *refs: chain_kernel(n, rows, *refs),
        out_shape=shape((2, NS, WIDE), BF16),
        in_specs=[VMEM],
        out_specs=VMEM,
        compiler_params=params(),
        name="chain_states",
    )(swapped)
    entering = lax.all_to_all(chained, "seq", split_axis=1, concat_axis=1, tiled=True)

    first = (lax.axis_index("seq") * per_device).astype(jnp.int32).reshape(1)
    columns = QUERY_HEADS * BLOCK
    attention, dq, dkv = pl.pallas_call(
        attention_kernel,
        out_shape=(
            shape((tokens, columns), F32),
            shape((tokens, columns), BF16),
            shape((every, 2 * LANES), BF16),
        ),
        in_specs=[SMEM, SMEM, VMEM, VMEM, VMEM],
        out_specs=(VMEM, VMEM, VMEM),
        scratch_shapes=[
            pltpu.SMEM((blocks + 1,), jnp.int32),
            pltpu.VMEM(((most + 1) // 2, 2 * BLOCK, columns), F32),
            pltpu.VMEM((every, 2 * LANES), F32),
            pltpu.VMEM((columns, LANES), BF16),
            pltpu.VMEM((columns, LANES), BF16),
            pltpu.VMEM((2 * BLOCK, columns), BF16),
            pltpu.VMEM((2 * BLOCK, columns), BF16),
            pltpu.VMEM((LANES, columns), F32),
            pltpu.VMEM((LANES, columns), F32),
            pltpu.VMEM((8, columns), F32),
        ],
        compiler_params=params(),
        name="attention",
    )(block_mask[0], first, q, g, kv_all)
    parts = lax.all_to_all(
        dkv.reshape(n, tokens, 2 * LANES), "seq", split_axis=0, concat_axis=0, tiled=True
    )

    y, dx, db, dc, sums = pl.pallas_call(
        ssm_kernel,
        out_shape=(
            shape((tokens, WIDE), BF16),
            shape((tokens, WIDE), BF16),
            shape((tokens, NS), BF16),
            shape((tokens, NS), BF16),
            shape((2 * HS, LANES), F32),
        ),
        in_specs=[VMEM] * 6 + [SMEM] + [VMEM] * 2,
        out_specs=(VMEM,) * 5,
        scratch_shapes=[
            pltpu.VMEM((tokens, LANES), F32),
            pltpu.VMEM((tokens, WIDE), BF16),
            pltpu.VMEM((tokens, WIDE), BF16),
            pltpu.VMEM((tokens, tokens), F32),
            pltpu.VMEM((tokens, tokens), F32),
            pltpu.VMEM((tokens, tokens), BF16),
            pltpu.VMEM((LANES, 2 * tokens), F32),
        ],
        compiler_params=params(),
        name="ssm",
    )(x, g, b, c, step[0], rate_row, skip_row, entering, attention)

    summed = lax.all_gather(jnp.sum(sums, axis=1), ("dp", "seq"), axis=0)
    totals = jnp.sum(summed, axis=0)
    tokens_all = lax.axis_size("dp") * n * tokens
    grad_rate_log = totals[:HS] / tokens_all
    grad_skip = totals[HS:] / (tokens_all * P_SIZE)
    owned = jnp.sum(parts.astype(F32), axis=0).astype(BF16)
    return (
        y[None],
        dq[None],
        owned[:, :LANES][None],
        owned[:, LANES:][None],
        dx[None],
        db[None],
        dc[None],
        grad_rate_log,
        grad_skip,
    )


def solution(mesh):
    split = P("dp", "seq", None)
    in_specs = (split,) * 7 + (P(), P(), P("dp", None, None), split)
    out_specs = (split,) * 7 + (P(), P())
    return jax.shard_map(body, mesh=mesh, in_specs=in_specs, out_specs=out_specs, check_vma=False)
```

time: 350 us -> 117 us (0.33)
  blocking collectives: 142 us -> 59.2 us
  waiting for transfers between devices: 50.1 us -> 1.11 us
  matrix products: 47.6 us -> 0 us
  other arithmetic: 43.6 us -> 3.12 us
  local copies, waits for them, and re-layouts: 42.5 us -> 8.28 us
  Pallas kernels: 0 us -> 20.1 us
  starting transfers between devices: 0.12 us -> 10.2 us
  loops' own time: 9.29 us -> 0 us
    all_gather x3 -> x0, blocking collectives: 103 us -> none  [the longest x1 81.6 us: entering(): lax.all_gather(part.astype(kind), axis)]
    dot_general x40 -> x0, matrix products: 47.6 us -> none  [the longest x6 11.1 us: one_block(): jnp.einsum('hij,jhp->ihp', decay * inner[None, :, :], x_block, precision=...]
    unnamed x0 -> x1, blocking collectives: none -> 42.7 us
    psum x1 -> x0, blocking collectives: 39.3 us -> none  [body(): lax.psum((gradient_list[4], gradient_list[5]), ('dp', 'seq'))]
    all_gather x2 -> x1, waiting for transfers between devices: 28.3 us -> 0.02 us  [body(): kv_all = lax.all_gather(kv, 'seq', axis=0, tiled=True)]
    reduce_scatter x1 -> x0, waiting for transfers between devices: 21.8 us -> none  [body(): lax.psum_scatter(holding_array.astype(jnp.bfloat16), 'seq', scatter_dimen...]
    pallas_call x0 -> x4, Pallas kernels: none -> 20.1 us  [the longest x1 8.57 us: body(): pl.pallas_call(attention_kernel, out_shape=(shape((tokens, columns), F32)...]
    select_n x16 -> x0, other arithmetic: 17.6 us -> none  [lap(): return jax.tree.map(lambda a, b: jnp.where(reached, a, b), new, before)]
  transfers between devices with their start and end apart: 3 -> 3, of which waited for: 2 -> 1; matrix products, arithmetic and copies ran while one was open for 15% -> 7% of each run, Pallas kernels for 0% -> 17%
where the time goes in v1:
time: 117 us; the launch traced here: 116 us
  blocking collectives  59.2 us (51%)
  Pallas kernels  20.1 us (17%)
  between operations  14.1 us (12%)
  starting transfers between devices  10.2 us (9%)
  local copies, waits for them, and re-layouts  8.28 us (7%)
  other arithmetic  3.12 us (3%)
    unnamed x1, blocking collectives  42.7 us
    all_to_all x1, blocking collectives, body(): lax.all_to_all(states, 'seq', split_axis=1, concat_axis=1, tiled=True)  16.5 us
    pallas_call x1, Pallas kernels, body(): pl.pallas_call(attention_kernel, out_shape=(shape((tokens, columns), F32)...  8.57 us
    all_to_all x1, starting transfers between devices, body(): lax.all_to_all(dkv.reshape(n, tokens, 2 * LANES), 'seq', split_axis=0, co...  6.67 us
    pallas_call x1, Pallas kernels, body(): pl.pallas_call(ssm_kernel, out_shape=(shape((tokens, WIDE), BF16), shape(...  6.02 us
    all_to_all x1, starting transfers between devices, body(): lax.all_to_all(chained, 'seq', split_axis=1, concat_axis=1, tiled=True)  3.49 us
    pallas_call x1, Pallas kernels, body(): pl.pallas_call(local_states_kernel, out_shape=shape((2, NS, WIDE + LANES)...  3.38 us
    pallas_call x1, local copies, waits for them, and re-layouts, body(): pl.pallas_call(lambda *refs: chain_kernel(n, rows, *refs), out_shape=shap...  2.37 us
  transfers between devices with their start and end apart: 3, of which 1 were waited for; matrix products, arithmetic and copies ran while one was open for 7% of the time, Pallas kernels for 17%

profile of v1, /device:TPU:0, one launch (start us, length us, event | category | flops | bytes accessed | tf_op | source)
XLA Modules:
  0.0 116.1 jit_solution(10059102950798031795)
XLA Ops:
  7.2 0.0 all-gather.3.cloned.1.call-start
  7.2 1.5 %pad_maximum_fusion = bf16[256,256]{1,0:T(8,128)(2,1)} fusion(bf16[256,128]{1,0:T(8,128)(2,1)} %bitcast.35, bf16[256,128]{1,0:T(8,128)(2,1)} %bitcast.36), kind=kLoop, calls=%fused_computation | loop fusion | flops 262144 | bytes 262144 | tf_op jit(solution)/shard_map/concatenate | solution.py:287
  8.8 0.7 copy-done
  9.5 0.8 copy.22
  10.2 3.4 %local_states.1 = bf16[2,128,1152]{2,1,0:T(8,128)(2,1)} custom-call(bf16[256,1024]{1,0:T(8,128)(2,1)} %bitcast.25, bf16[256,1024]{1,0:T(8,128)(2,1)} %bitcast.22, bf16[256,128]{1,0:T(8,128)(2,1)} %bitcast.31, bf16[256,128]{1,0:T(8,128)(2,1)} %bitcast.33, f32[256,8]{1,0:T(8,128)} %bitcast.27, f32[1,8]{1,0:T(1,128)} %bitcast.38), custom_call_target="tpu_custom_call" | custom-call | tf_op jit(solution)/shard_map/local_states/pallas_call | solution.py:290
  13.6 1.7 %copy.23 = bf16[2,128,1152]{2,0,1:T(2,128)(2,1)S(1)} copy(bf16[2,128,1152]{2,1,0:T(8,128)(2,1)} %local_states.1) | data formatting | bytes 1179648 | tf_op jit(solution)/shard_map/local_states/pallas_call | solution.py:290
  15.3 16.5 %all_to_all.15 = bf16[2,128,1152]{2,0,1:T(2,128)(2,1)S(1)} all-to-all(bf16[2,128,1152]{2,0,1:T(2,128)(2,1)S(1)} %copy.23), channel_id=1, replica_groups=mesh['dp'=4,'seq'=8] {'seq'}, dimensions={1} | all-to-all | bytes 1179648 | tf_op jit(solution)/shard_map/all_to_all | solution.py:304
  31.8 0.9 copy.24.refs_0_
  32.7 2.2 %chain_states.1 = bf16[2,128,1024]{2,1,0:T(8,128)(2,1)} custom-call(bf16[2,128,1152]{2,1,0:T(8,128)(2,1)} %copy.24.refs_0_), custom_call_target="tpu_custom_call" | custom-call | tf_op jit(solution)/shard_map/chain_states/pallas_call | solution.py:305
  34.9 2.4 %copy.25 = bf16[2,128,1024]{2,0,1:T(2,128)(2,1)} copy(bf16[2,128,1024]{2,1,0:T(8,128)(2,1)} %chain_states.1) | data formatting | bytes 1048576 | tf_op jit(solution)/shard_map/chain_states/pallas_call | solution.py:305
  37.2 3.5 %all-to-all-start.1 = ((bf16[2,128,1024]{2,0,1:T(2,128)(2,1)}), bf16[2,128,1024]{2,0,1:T(2,128)(2,1)S(1)}, u32[]{:S(2)}, u32[]{:S(2)}) async-start(bf16[2,128,1024]{2,0,1:T(2,128)(2,1)} %copy.25), calls=%async_computation.1 | async-start | bytes 1048576 | tf_op jit(solution)/shard_map/all_to_all | solution.py:313
  40.8 0.0 all-gather.3.cloned.1.call-done.kv_ref
  40.8 8.6 %attention.1 = (f32[256,1024]{1,0:T(8,128)}, bf16[256,1024]{1,0:T(8,128)(2,1)}, bf16[2048,256]{1,0:T(8,128)(2,1)}) custom-call(s32[16,16]{1,0:T(8,128)} %bitcast.37, s32[1]{0:T(128)} %bitcast.8.first_ref, bf16[256,1024]{1,0:T(8,128)(2,1)} %bitcast.30, bf16[256,1024]{1,0:T(8,128)(2,1)} %bitcast.23, bf16[2048,256]{1,0:T(8,128)(2,1)} %all-gather.3.cloned.1.call-done.kv_ref), custom_call_target="tpu_custom_call" | custom-call | tf_op jit(solution)/shard_map/attention/pallas_call | solution.py:317
  49.4 1.1 all-to-all-done.1
  50.4 6.7 %all-to-all-start.2 = ((bf16[8,256,256]{2,1,0:T(8,128)(2,1)}), bf16[8,256,256]{2,1,0:T(8,128)(2,1)S(1)}, u32[]{:S(2)}, u32[]{:S(2)}) async-start(bf16[8,256,256]{2,1,0:T(8,128)(2,1)} %bitcast.29), calls=%async_computation.2 | async-start | bytes 2097152 | tf_op jit(solution)/shard_map/all_to_all | solution.py:341
  57.1 0.9 copy.26.ent_ref
  58.0 6.0 %ssm.1 = (bf16[256,1024]{1,0:T(8,128)(2,1)}, bf16[256,1024]{1,0:T(8,128)(2,1)}, bf16[256,128]{1,0:T(8,128)(2,1)}, bf16[256,128]{1,0:T(8,128)(2,1)}, f32[16,128]{1,0:T(8,128)}) custom-call(bf16[256,1024]{1,0:T(8,128)(2,1)} %bitcast.26, bf16[256,1024]{1,0:T(8,128)(2,1)} %bitcast.24, bf16[256,128]{1,0:T(8,128)(2,1)} %bitcast.32, bf16[256,128]{1,0:T(8,128)(2,1)} %bitcast.34, ...), custom_call_target="tpu_custom_call" | custom-call | tf_op jit(solution)/shard_map/ssm/pallas_call | solution.py:345
  64.0 0.8 reduce_sum.31
  64.8 0.2 dynamic-update-slice
  65.1 42.7 %all-reduce = f32[512]{0:T(512)S(1)} all-reduce(f32[512]{0:T(512)S(1)} %dynamic-update-slice), channel_id=2, replica_groups=mesh['dp'=4,'seq'=8] {'dp','seq'}, use_global_device_ids=true, to_apply=%add | all-reduce | flops 512 | bytes 4096
  107.8 0.1 reshape.34
  107.9 0.6 slice_multiply_fusion
  108.5 0.1 reduce_sum.30
  108.6 0.7 slice_bitcast_fusion
  (5 shorter events, 0.0 us)
Async XLA Ops:
  7.2 33.6 %all-gather.3.cloned.1.call-start = ((), (), s32[]{:S(2)}) async-start(), calls=%async_computation.3 | async-start | bytes 1179648 | tf_op jit(solution)/shard_map/all_gather | solution.py:288
  8.8 0.7 copy-start
  37.2 13.2 %all-to-all-start.1 = ((bf16[2,128,1024]{2,0,1:T(2,128)(2,1)}), bf16[2,128,1024]{2,0,1:T(2,128)(2,1)S(1)}, u32[]{:S(2)}, u32[]{:S(2)}) async-start(bf16[2,128,1024]{2,0,1:T(2,128)(2,1)} %copy.25), calls=%async_computation.1 | async-start | bytes 1048576 | tf_op jit(solution)/shard_map/all_to_all | solution.py:313
  50.4 58.0 %all-to-all-start.2 = ((bf16[8,256,256]{2,1,0:T(8,128)(2,1)}), bf16[8,256,256]{2,1,0:T(8,128)(2,1)S(1)}, u32[]{:S(2)}, u32[]{:S(2)}) async-start(bf16[8,256,256]{2,1,0:T(8,128)(2,1)} %bitcast.29), calls=%async_computation.2 | async-start | bytes 2097152 | tf_op jit(solution)/shard_map/all_to_all | solution.py:341
Sparse Core Ops, SparseCore 0:
  10.5 29.5 all-gather.2

commit v2 on v1

--- a/solution.py
+++ b/solution.py
@@ -28,6 +28,12 @@
     return pltpu.CompilerParams(vmem_limit_bytes=limit)
 
 
+def cost(microseconds):
+    return pl.CostEstimate(
+        flops=int(microseconds * 1.1e9), bytes_accessed=1 << 20, transcendentals=0
+    )
+
+
 def dot(a, b, ca, cb, precision=None):
     return lax.dot_general(
         a, b, (((ca,), (cb,)), ((), ())), preferred_element_type=F32, precision=precision
@@ -40,13 +46,15 @@
 
 def running_logs(step_ref, rate_ref, pad_ref):
     pad_ref[...] = jnp.zeros_like(pad_ref)
-    pad_ref[:, :HS] = -step_ref[...] * jnp.exp(rate_ref[...])
+    for h in range(HS):
+        rate = jnp.exp(jnp.full((1, 2 * BLOCK), rate_ref[h], F32))
+        pad_ref[h : h + 1, :] = -step_ref[h : h + 1, :] * rate
     row = lax.broadcasted_iota(jnp.int32, (BLOCK, BLOCK), 0)
     col = lax.broadcasted_iota(jnp.int32, (BLOCK, BLOCK), 1)
-    lower = jnp.where(row >= col, 1.0, 0.0).astype(F32)
-    run0 = dot(lower, pad_ref[:BLOCK], 1, 0, HIGH)
-    run1 = dot(lower, pad_ref[BLOCK:], 1, 0, HIGH)
-    return run0, run1
+    upper = jnp.where(row <= col, 1.0, 0.0).astype(F32)
+    flat0 = dot(pad_ref[:, :BLOCK], upper, 1, 0, HIGH)
+    flat1 = dot(pad_ref[:, BLOCK:], upper, 1, 0, HIGH)
+    return flat0, flat1, flat0.T, flat1.T
 
 
 def scaled(x_ref, column, out_ref):
@@ -54,54 +62,94 @@
         out_ref[:, head(h)] = (x_ref[:, head(h)].astype(F32) * column[:, h : h + 1]).astype(BF16)
 
 
+def pieces(n):
+    groups = max(1, (n * 16) // NS)
+    return NS * groups // n, groups
+
+
 def local_states_kernel(
-    x_ref, g_ref, b_ref, c_ref, step_ref, rate_ref, out_ref, pad_ref, xt_ref, gt_ref
+    n, x_ref, g_ref, b_ref, c_ref, step_ref, rate_ref, out_ref, pad_ref, high_ref, rest_ref
 ):
-    run0, run1 = running_logs(step_ref, rate_ref, pad_ref)
+    rows, groups = pieces(n)
+    heads = HS // groups
+    width = heads * LANES
+    _, _, run0, run1 = running_logs(step_ref, rate_ref, pad_ref)
     t0, t1 = run0[BLOCK - 1 :, :], run1[BLOCK - 1 :, :]
     enter = jnp.exp(jnp.concatenate([run0, run1 + t0], axis=0))
     tail = jnp.exp(jnp.concatenate([(t0 - run0) + t1, t1 - run1], axis=0))
-    scaled(x_ref, tail, xt_ref)
-    scaled(g_ref, enter, gt_ref)
-    out_ref[0, :, :WIDE] = dot(b_ref[...], xt_ref[...], 0, 0).astype(BF16)
-    out_ref[1, :, :WIDE] = dot(c_ref[...], gt_ref[...], 0, 0).astype(BF16)
     total = t0 + t1
     high = total.astype(BF16).astype(F32)
     middle = (total - high).astype(BF16).astype(F32)
     low = total - high - middle
-    place = lax.broadcasted_iota(jnp.int32, (NS, LANES), 0) % 4
-    logs = jnp.where(place == 0, high, jnp.where(place == 1, middle, low)).astype(BF16)
-    out_ref[0, :, WIDE:] = logs
-    out_ref[1, :, WIDE:] = logs
-
-
-def chain_kernel(n, rows, in_ref, out_ref):
-    decays = []
+    place = lax.broadcasted_iota(jnp.int32, (rows, LANES), 0) % 4
+    logs = jnp.where(place == 0, high, jnp.where(place == 1, middle, low))
+    for direction, (left, right, column) in enumerate(((b_ref, x_ref, tail), (c_ref, g_ref, enter))):
+        for h in range(HS):
+            product = right[:, head(h)].astype(F32) * column[:, h : h + 1]
+            rounded = product.astype(BF16)
+            high_ref[:, head(h)] = rounded
+            rest_ref[:, head(h)] = (product - rounded.astype(F32)).astype(BF16)
+        state = (
+            dot(left[...], high_ref[...], 0, 0) + dot(left[...], rest_ref[...], 0, 0)
+        ).astype(BF16)
+        for d in range(n):
+            at = (d // groups) * rows
+            shift = (d % groups) * heads
+            out_ref[d, direction, :, :width] = state[
+                at : at + rows, shift * LANES : shift * LANES + width
+            ]
+            own = logs if shift == 0 else pltpu.roll(logs, LANES - shift, 1)
+            out_ref[d, direction, :, width:] = own.astype(BF16)
+
+
+def chain_kernel(n, in_ref, out_ref, cross_ref, held_ref):
+    rows, groups = pieces(n)
+    heads = HS // groups
+    width = heads * LANES
+    logs = []
     for e in range(n):
-        logs = in_ref[0, e * rows : (e + 1) * rows, WIDE:].astype(F32)
-        total = logs[0:1, :] + logs[1:2, :] + logs[2:3, :]
-        factor = jnp.exp(total)
-        decays.append([factor[:, h : h + 1] for h in range(HS)])
-    for direction in range(2):
-        for h in range(HS):
-            state = jnp.zeros((rows, LANES), F32)
-            for e in range(n) if direction == 0 else range(n - 1, -1, -1):
-                at = slice(e * rows, (e + 1) * rows)
-                out_ref[direction, at, head(h)] = state.astype(BF16)
-                state = state * decays[e][h] + in_ref[direction, at, head(h)].astype(F32)
+        parts = in_ref[e, 0, :, width:].astype(F32)
+        logs.append(parts[0:1, :] + parts[1:2, :] + parts[2:3, :])
+    decays = [jnp.exp(log) for log in logs]
+    cross_ref[...] = jnp.zeros_like(cross_ref)
+    for h in range(heads):
+        state = jnp.zeros((rows, LANES), F32)
+        for e in range(n):
+            held_ref[e] = state
+            out_ref[e, 0, :, head(h)] = state.astype(BF16)
+            state = state * decays[e][:, h : h + 1] + in_ref[e, 0, :, head(h)].astype(F32)
+        state = jnp.zeros((rows, LANES), F32)
+        cross = jnp.zeros((1, LANES), F32)
+        for e in range(n - 1, -1, -1):
+            out_ref[e, 1, :, head(h)] = state.astype(BF16)
+            weight = (logs[e] * decays[e])[:, h : h + 1]
+            cross += jnp.sum(state * held_ref[e], axis=0, keepdims=True) * weight
+            state = state * decays[e][:, h : h + 1] + in_ref[e, 1, :, head(h)].astype(F32)
+        cross_ref[h : h + 1, :] = cross
 
 
 def attention_kernel(
-    mask_ref, first_ref, q_ref, g_ref, kv_ref, out_ref, dq_ref, dkv_ref,
-    index_ref, s_ref, acc_ref, qs_ref, gs_ref, ds_ref, pr_ref, o_ref, dqt_ref, rows_ref,
+    n, mask_ref, place_ref, q_ref, g_ref, *refs
 ):
+    key_parts, value_parts = refs[:n], refs[n : 2 * n]
+    out_ref, dq_ref = refs[2 * n : 2 * n + 2]
+    dkv_parts = refs[2 * n + 2 : 3 * n + 2]
+    (
+        index_ref, kv_ref, s_ref, acc_ref, qs_ref, gs_ref, ds_ref, pr_ref, o_ref, dqt_ref, rows_ref,
+    ) = refs[3 * n + 2 :]
     count = mask_ref.shape[0]
     columns = QUERY_HEADS * BLOCK
+    tokens = q_ref.shape[0]
+    me = place_ref[0]
     acc_ref[...] = jnp.zeros_like(acc_ref)
+    for k in range(n):
+        source = pl.ds(pl.multiple_of(lax.rem(me + n - k, n) * tokens, tokens), tokens)
+        kv_ref[source, :LANES] = key_parts[k][...]
+        kv_ref[source, LANES:] = value_parts[k][...]
     scale = FACTOR * LOG2E
-    for block in range(q_ref.shape[0] // BLOCK):
+    for block in range(tokens // BLOCK):
         at = slice(block * BLOCK, (block + 1) * BLOCK)
-        row = first_ref[0] + block
+        row = me * (tokens // BLOCK) + block
 
         def note(j, n):
             @pl.when(mask_ref[row, j] == 1)
@@ -198,16 +246,32 @@
         lax.fori_loop(0, pairs, grads_step, 0)
         for h in range(QUERY_HEADS):
             dq_ref[at, head(h)] = (dqt_ref[:, head(h)].T * FACTOR).astype(BF16)
-    dkv_ref[...] = acc_ref[...].astype(BF16)
+    for k in range(n):
+        target = pl.ds(pl.multiple_of(lax.rem(me + k, n) * tokens, tokens), tokens)
+        dkv_parts[k][...] = acc_ref[target, :].astype(BF16)
+
+
+def owner_sum_kernel(*refs):
+    parts, (dk_ref, dv_ref) = refs[:-2], refs[-2:]
+    for out_ref, lanes in ((dk_ref, slice(0, LANES)), (dv_ref, slice(LANES, 2 * LANES))):
+        total = parts[0][:, lanes].astype(F32)
+        for part in parts[1:]:
+            total += part[:, lanes].astype(F32)
+        out_ref[...] = total.astype(BF16)
 
 
 def ssm_kernel(
-    x_ref, g_ref, b_ref, c_ref, step_ref, rate_ref, skip_ref, ent_ref, att_ref,
+    n, x_ref, g_ref, b_ref, c_ref, step_ref, rate_ref, skip_ref, pieces_ref, cross_ref, att_ref,
     y_ref, dx_ref, db_ref, dc_ref, sums_ref,
-    pad_ref, xt_ref, gt_ref, inner_ref, dinner_ref, m_ref, runt_ref,
+    pad_ref, xt_ref, gt_ref, inner_ref, dinner_ref, m_ref, runt_ref, ent_ref,
 ):
     tokens = 2 * BLOCK
-    run0, run1 = running_logs(step_ref, rate_ref, pad_ref)
+    rows, groups = pieces(n)
+    width = HS // groups * LANES
+    for d in range(n):
+        at, lanes = (d // groups) * rows, (d % groups) * width
+        ent_ref[:, at : at + rows, lanes : lanes + width] = pieces_ref[d]
+    flat0, flat1, run0, run1 = running_logs(step_ref, rate_ref, pad_ref)
     t0, t1 = run0[BLOCK - 1 :, :], run1[BLOCK - 1 :, :]
     enter_log = jnp.concatenate([run0, run1 + t0], axis=0)
     tail_log = jnp.concatenate([(t0 - run0) + t1, t1 - run1], axis=0)
@@ -215,8 +279,9 @@
     scaled(x_ref, tail, xt_ref)
     scaled(g_ref, enter, gt_ref)
     own = jnp.concatenate([run0, run1], axis=0)
-    runt_ref[:, :tokens] = own.T
-    runt_ref[:, tokens:] = jnp.concatenate([run0 - t0, run1], axis=0).T
+    runt_ref[:, :BLOCK] = flat0
+    runt_ref[:, tokens : tokens + BLOCK] = flat0 - flat0[:, BLOCK - 1 :]
+    runt_ref[:, tokens + BLOCK :] = flat1
     b = b_ref[...]
     c = c_ref[...]
     inner_ref[...] = dot(c, b, 1, 1)
@@ -228,13 +293,12 @@
     seen0 = row0 >= col0
     seen1 = row1 + BLOCK >= col1
     m_ref[:BLOCK, BLOCK:] = jnp.zeros((BLOCK, BLOCK), BF16)
-    both = t0 + t1
     for h in range(HS):
         lanes = head(h)
         x = x_ref[:, lanes]
         g = g_ref[:, lanes]
         xf, gf = x.astype(F32), g.astype(F32)
-        gain = skip_ref[0, h]
+        gain = skip_ref[h]
         spread0 = jnp.where(seen0, own[:BLOCK, h : h + 1] - runt_ref[h : h + 1, :BLOCK], NEG)
         spread1 = jnp.where(seen1, own[BLOCK:, h : h + 1] - runt_ref[h : h + 1, tokens:], NEG)
         decay0, decay1 = jnp.exp(spread0), jnp.exp(spread1)
@@ -260,10 +324,7 @@
             axis=0,
             keepdims=True,
         )
-        cross = jnp.sum(h0.astype(F32) * later.astype(F32), axis=0, keepdims=True)
-        whole = both[:, h : h + 1]
-        rate += cross * (whole * jnp.exp(whole))
-        sums_ref[h : h + 1, :] = rate
+        sums_ref[h : h + 1, :] = rate + cross_ref[h : h + 1, :]
         sums_ref[HS + h : HS + h + 1, :] = jnp.sum(gf * xf, axis=0, keepdims=True)
     dinner = dinner_ref[...].astype(BF16)
     dc = dot(dinner, b, 1, 0) + dot(gt_ref[...], ent_ref[0], 1, 1)
@@ -272,59 +333,75 @@
     db_ref[...] = db.astype(BF16)
 
 
+def turned(array, axis, k):
+    n = lax.axis_size(axis)
+    return lax.ppermute(array, axis, [(i, (i + k) % n) for i in range(n)])
+
+
+def everywhere(array, axis):
+    return [array] + [turned(array, axis, k) for k in range(1, lax.axis_size(axis))]
+
+
+def total_over(array, axis):
+    return sum(everywhere(array, axis))
+
+
 def body(query, key, value, ssm_input, in_b, in_c, step, rate_log, skip, block_mask, grad_out):
     n = lax.axis_size("seq")
     tokens = query.shape[1]
-    per_device = tokens // BLOCK
     blocks = block_mask.shape[1]
     most = 3 * blocks // 8
     every = blocks * BLOCK
+    rows, groups = pieces(n)
+    heads = HS // groups
     q, g, x = query[0], grad_out[0], ssm_input[0]
-    b, c = in_b[0], in_c[0]
-    rate_row, skip_row = rate_log.reshape(1, HS), skip.reshape(1, HS)
+    b, c, steps = in_b[0], in_c[0], step[0].T
     shape = jax.ShapeDtypeStruct
 
-    kv = jnp.concatenate([key[0], value[0]], axis=1)
-    kv_all = lax.all_gather(kv, "seq", axis=0, tiled=True)
+    key_parts = everywhere(key[0], "seq")
+    value_parts = everywhere(value[0], "seq")
 
     states = pl.pallas_call(
-        local_states_kernel,
-        out_shape=shape((2, NS, WIDE + LANES), BF16),
-        in_specs=[VMEM] * 6,
+        lambda *refs: local_states_kernel(n, *refs),
+        out_shape=shape((n, 2, rows, (heads + 1) * LANES), BF16),
+        in_specs=[VMEM] * 5 + [SMEM],
         out_specs=VMEM,
         scratch_shapes=[
-            pltpu.VMEM((tokens, LANES), F32),
+            pltpu.VMEM((LANES, tokens), F32),
             pltpu.VMEM((tokens, WIDE), BF16),
             pltpu.VMEM((tokens, WIDE), BF16),
         ],
         compiler_params=params(),
+        cost_estimate=cost(3),
         name="local_states",
-    )(x, g, b, c, step[0], rate_row)
-    rows = NS // n
-    swapped = lax.all_to_all(states, "seq", split_axis=1, concat_axis=1, tiled=True)
-    chained = pl.pallas_call(
-        lambda *refs: chain_kernel(n, rows, *refs),
-        out_shape=shape((2, NS, WIDE), BF16),
+    )(x, g, b, c, steps, rate_log)
+    swapped = lax.all_to_all(states, "seq", split_axis=0, concat_axis=0, tiled=True)
+    chained, cross = pl.pallas_call(
+        lambda *refs: chain_kernel(n, *refs),
+        out_shape=(shape((n, 2, rows, heads * LANES), BF16), shape((HS, LANES), F32)),
         in_specs=[VMEM],
-        out_specs=VMEM,
+        out_specs=(VMEM, VMEM),
+        scratch_shapes=[pltpu.VMEM((n, rows, LANES), F32)],
         compiler_params=params(),
+        cost_estimate=cost(2),
         name="chain_states",
     )(swapped)
-    entering = lax.all_to_all(chained, "seq", split_axis=1, concat_axis=1, tiled=True)
-
-    first = (lax.axis_index("seq") * per_device).astype(jnp.int32).reshape(1)
+    if groups > 1:
+        at = (lax.axis_index("seq") % groups) * heads
+        cross = lax.dynamic_update_slice_in_dim(jnp.zeros_like(cross), cross[:heads], at, 0)
+    entering = lax.all_to_all(chained, "seq", split_axis=0, concat_axis=0, tiled=True)
+
+    place = lax.axis_index("seq").astype(jnp.int32).reshape(1)
     columns = QUERY_HEADS * BLOCK
-    attention, dq, dkv = pl.pallas_call(
-        attention_kernel,
-        out_shape=(
-            shape((tokens, columns), F32),
-            shape((tokens, columns), BF16),
-            shape((every, 2 * LANES), BF16),
-        ),
-        in_specs=[SMEM, SMEM, VMEM, VMEM, VMEM],
-        out_specs=(VMEM, VMEM, VMEM),
+    attention, dq, *dkv_parts = pl.pallas_call(
+        lambda *refs: attention_kernel(n, *refs),
+        out_shape=(shape((tokens, columns), F32), shape((tokens, columns), BF16))
+        + (shape((tokens, 2 * LANES), BF16),) * n,
+        in_specs=[SMEM, SMEM] + [VMEM] * (2 + 2 * n),
+        out_specs=(VMEM,) * (2 + n),
         scratch_shapes=[
             pltpu.SMEM((blocks + 1,), jnp.int32),
+            pltpu.VMEM((every, 2 * LANES), BF16),
             pltpu.VMEM(((most + 1) // 2, 2 * BLOCK, columns), F32),
             pltpu.VMEM((every, 2 * LANES), F32),
             pltpu.VMEM((columns, LANES), BF16),
@@ -336,14 +413,13 @@
             pltpu.VMEM((8, columns), F32),
         ],
         compiler_params=params(),
+        cost_estimate=cost(10),
         name="attention",
-    )(block_mask[0], first, q, g, kv_all)
-    parts = lax.all_to_all(
-        dkv.reshape(n, tokens, 2 * LANES), "seq", split_axis=0, concat_axis=0, tiled=True
-    )
+    )(block_mask[0], place, q, g, *key_parts, *value_parts)
+    owned = [dkv_parts[0]] + [turned(dkv_parts[k], "seq", k) for k in range(1, n)]
 
     y, dx, db, dc, sums = pl.pallas_call(
-        ssm_kernel,
+        lambda *refs: ssm_kernel(n, *refs),
         out_shape=(
             shape((tokens, WIDE), BF16),
             shape((tokens, WIDE), BF16),
@@ -351,32 +427,41 @@
             shape((tokens, NS), BF16),
             shape((2 * HS, LANES), F32),
         ),
-        in_specs=[VMEM] * 6 + [SMEM] + [VMEM] * 2,
+        in_specs=[VMEM] * 5 + [SMEM] * 2 + [VMEM] * 3,
         out_specs=(VMEM,) * 5,
         scratch_shapes=[
-            pltpu.VMEM((tokens, LANES), F32),
+            pltpu.VMEM((LANES, tokens), F32),
             pltpu.VMEM((tokens, WIDE), BF16),
             pltpu.VMEM((tokens, WIDE), BF16),
             pltpu.VMEM((tokens, tokens), F32),
             pltpu.VMEM((tokens, tokens), F32),
             pltpu.VMEM((tokens, tokens), BF16),
             pltpu.VMEM((LANES, 2 * tokens), F32),
+            pltpu.VMEM((2, NS, WIDE), BF16),
         ],
         compiler_params=params(),
+        cost_estimate=cost(6),
         name="ssm",
-    )(x, g, b, c, step[0], rate_row, skip_row, entering, attention)
-
-    summed = lax.all_gather(jnp.sum(sums, axis=1), ("dp", "seq"), axis=0)
-    totals = jnp.sum(summed, axis=0)
+    )(x, g, b, c, steps, rate_log, skip, entering, cross, attention)
+
+    totals = jnp.sum(total_over(total_over(sums, "seq"), "dp"), axis=1)
     tokens_all = lax.axis_size("dp") * n * tokens
     grad_rate_log = totals[:HS] / tokens_all
     grad_skip = totals[HS:] / (tokens_all * P_SIZE)
-    owned = jnp.sum(parts.astype(F32), axis=0).astype(BF16)
+    dk, dv = pl.pallas_call(
+        owner_sum_kernel,
+        out_shape=(shape((tokens, LANES), BF16),) * 2,
+        in_specs=[VMEM] * n,
+        out_specs=(VMEM, VMEM),
+        compiler_params=params(),
+        cost_estimate=cost(1),
+        name="owner_sum",
+    )(*owned)
     return (
         y[None],
         dq[None],
-        owned[:, :LANES][None],
-        owned[:, LANES:][None],
+        dk[None],
+        dv[None],
         dx[None],
         db[None],
         dc[None],

time: 117 us -> 89.4 us (0.76)
  the two profiles are of different devices: /device:TPU:0 before, /device:TPU:2 now
where the time goes in v2:
time: 89.4 us; the launch traced here: 88 us
  starting transfers between devices  51.6 us (58%)
  Pallas kernels  22.5 us (25%)
  waiting for transfers between devices  9.13 us (10%)
  local copies, waits for them, and re-layouts  3.01 us (3%)
  between operations  0.95 us (1%)
    ppermute x31, starting transfers between devices, turned(): return lax.ppermute(array, axis, [(i, (i + k) % n) for i in range(n)])  42.8 us
    ppermute x31, waiting for transfers between devices, turned(): return lax.ppermute(array, axis, [(i, (i + k) % n) for i in range(n)])  9.12 us
    pallas_call x1, Pallas kernels, body(): pl.pallas_call(lambda *refs: attention_kernel(n, *refs), out_shape=(shape...  8.72 us
    pallas_call x1, Pallas kernels, body(): pl.pallas_call(lambda *refs: ssm_kernel(n, *refs), out_shape=(shape((toke...  6 us
    all_to_all x1, starting transfers between devices, body(): lax.all_to_all(chained, 'seq', split_axis=0, concat_axis=0, tiled=True)  4.39 us
    all_to_all x1, starting transfers between devices, body(): lax.all_to_all(states, 'seq', split_axis=0, concat_axis=0, tiled=True)  4.38 us
    pallas_call x1, Pallas kernels, body(): pl.pallas_call(lambda *refs: local_states_kernel(n, *refs), out_shape=sha...  3.57 us
    unnamed x62, local copies, waits for them, and re-layouts  3.01 us
  transfers between devices with their start and end apart: 33, of which 6 were waited for; matrix products, arithmetic and copies ran while one was open for 0% of the time, Pallas kernels for 22%

profile of v2, /device:TPU:2, one launch (start us, length us, event | category | flops | bytes accessed | tf_op | source)
XLA Modules:
  0.0 88.0 jit_solution(6175133965704276244)
XLA Ops:
  0.6 3.6 %local_states.1 = bf16[8,2,16,1152]{3,2,1,0:T(8,128)(2,1)} custom-call(bf16[256,1024]{1,0:T(8,128)(2,1)} %bitcast.20, bf16[256,1024]{1,0:T(8,128)(2,1)} %bitcast.22, bf16[256,128]{1,0:T(8,128)(2,1)} %bitcast.41, bf16[256,128]{1,0:T(8,128)(2,1)} %bitcast.43, f32[8,256]{1,0:T(8,128)} %bitcast.46, f32[8]{0:T(128)} %refs_5_.3), custom_call_target="tpu_custom_call" | custom-call | flops 3300000000 | bytes 1048576 | tf_op jit(solution)/shard_map/local_states/pallas_call | solution.py:364
  4.2 4.4 %all-to-all-start = ((bf16[8,2,16,1152]{3,2,1,0:T(8,128)(2,1)}), bf16[8,2,16,1152]{3,2,1,0:T(8,128)(2,1)S(1)}, u32[]{:S(2)}, u32[]{:S(2)}) async-start(bf16[8,2,16,1152]{3,2,1,0:T(8,128)(2,1)} %local_states.1), calls=%async_computation | async-start | bytes 1179648 | tf_op jit(solution)/shard_map/all_to_all | solution.py:378
  8.7 2.6 %collective-permute-start.5 = (bf16[256,128]{1,0:T(8,128)(2,1)S(1)}, bf16[256,128]{1,0:T(8,128)(2,1)S(1)}, u32[]{:S(2)}, u32[]{:S(2)}) collective-permute-start(bf16[256,128]{1,0:T(8,128)(2,1)S(1)} %bitcast.27), channel_id=1, source_target_pairs={{0,6},{1,7},{2,0},{3,1},{4,2},{5,3},{6,4},{7,5},{8,14},{9,15},{10,... | collective-permute-start | bytes 196616 | tf_op jit(solution)/shard_map/ppermute | solution.py:338
  11.8 2.4 %collective-permute-start.2 = (bf16[256,128]{1,0:T(8,128)(2,1)S(1)}, bf16[256,128]{1,0:T(8,128)(2,1)S(1)}, u32[]{:S(2)}, u32[]{:S(2)}) collective-permute-start(bf16[256,128]{1,0:T(8,128)(2,1)S(1)} %bitcast.30), channel_id=1, source_target_pairs={{0,3},{1,4},{2,5},{3,6},{4,7},{5,0},{6,1},{7,2},{8,11},{9,12},{10,... | collective-permute-start | bytes 196616 | tf_op jit(solution)/shard_map/ppermute | solution.py:338
  14.2 3.3 %collective-permute-done.6.refs_11_ = bf16[256,128]{1,0:T(8,128)(2,1)S(1)} collective-permute-done((bf16[256,128]{1,0:T(8,128)(2,1)S(1)}, bf16[256,128]{1,0:T(8,128)(2,1)S(1)}, u32[]{:S(2)}, u32[]{:S(2)}) %collective-permute-start.6) | collective-permute-done | bytes 65568 | tf_op jit(solution)/shard_map/ppermute | solution.py:338
  17.5 1.5 %collective-permute-start.1 = (bf16[256,128]{1,0:T(8,128)(2,1)S(1)}, bf16[256,128]{1,0:T(8,128)(2,1)S(1)}, u32[]{:S(2)}, u32[]{:S(2)}) collective-permute-start(bf16[256,128]{1,0:T(8,128)(2,1)S(1)} %bitcast.31), channel_id=1, source_target_pairs={{0,2},{1,3},{2,4},{3,5},{4,6},{5,7},{6,0},{7,1},{8,10},{9,11},{10,... | collective-permute-start | bytes 196616 | tf_op jit(solution)/shard_map/ppermute | solution.py:338
  19.1 1.4 %collective-permute-done.5.refs_10_ = bf16[256,128]{1,0:T(8,128)(2,1)S(1)} collective-permute-done((bf16[256,128]{1,0:T(8,128)(2,1)S(1)}, bf16[256,128]{1,0:T(8,128)(2,1)S(1)}, u32[]{:S(2)}, u32[]{:S(2)}) %collective-permute-start.5) | collective-permute-done | bytes 65568 | tf_op jit(solution)/shard_map/ppermute | solution.py:338
  20.8 1.5 %collective-permute-start.13 = (bf16[256,128]{1,0:T(8,128)(2,1)S(1)}, bf16[256,128]{1,0:T(8,128)(2,1)S(1)}, u32[]{:S(2)}, u32[]{:S(2)}) collective-permute-start(bf16[256,128]{1,0:T(8,128)(2,1)S(1)} %bitcast.34), channel_id=1, source_target_pairs={{0,7},{1,0},{2,1},{3,2},{4,3},{5,4},{6,5},{7,6},{8,15},{9,8},{10,9... | collective-permute-start | bytes 196616 | tf_op jit(solution)/shard_map/ppermute | solution.py:338
  23.7 1.5 %collective-permute-start.10 = (bf16[256,128]{1,0:T(8,128)(2,1)S(1)}, bf16[256,128]{1,0:T(8,128)(2,1)S(1)}, u32[]{:S(2)}, u32[]{:S(2)}) collective-permute-start(bf16[256,128]{1,0:T(8,128)(2,1)S(1)} %bitcast.37), channel_id=1, source_target_pairs={{0,4},{1,5},{2,6},{3,7},{4,0},{5,1},{6,2},{7,3},{8,12},{9,13},{10,... | collective-permute-start | bytes 196616 | tf_op jit(solution)/shard_map/ppermute | solution.py:338
  25.2 2.3 %collective-permute-start.9 = (bf16[256,128]{1,0:T(8,128)(2,1)S(1)}, bf16[256,128]{1,0:T(8,128)(2,1)S(1)}, u32[]{:S(2)}, u32[]{:S(2)}) collective-permute-start(bf16[256,128]{1,0:T(8,128)(2,1)S(1)} %bitcast.38), channel_id=1, source_target_pairs={{0,3},{1,4},{2,5},{3,6},{4,7},{5,0},{6,1},{7,2},{8,11},{9,12},{10,... | collective-permute-start | bytes 196616 | tf_op jit(solution)/shard_map/ppermute | solution.py:338
  29.9 2.2 %chain_states.1 = (bf16[8,2,16,1024]{3,2,1,0:T(8,128)(2,1)}, f32[8,128]{1,0:T(8,128)}) custom-call(bf16[8,2,16,1152]{3,2,1,0:T(8,128)(2,1)} %copy-done), custom_call_target="tpu_custom_call" | custom-call | flops 2200000000 | bytes 1048576 | tf_op jit(solution)/shard_map/chain_states/pallas_call | solution.py:379
  32.2 4.4 %all-to-all-start.1 = ((bf16[8,2,16,1024]{3,2,1,0:T(8,128)(2,1)}), bf16[8,2,16,1024]{3,2,1,0:T(8,128)(2,1)S(1)}, u32[]{:S(2)}, u32[]{:S(2)}) async-start(bf16[8,2,16,1024]{3,2,1,0:T(8,128)(2,1)} %get-tuple-element.28), calls=%async_computation.1 | async-start | bytes 1048576 | tf_op jit(solution)/shard_map/all_to_all | solution.py:392
  37.3 8.7 %attention.1 = (f32[256,1024]{1,0:T(8,128)}, bf16[256,1024]{1,0:T(8,128)(2,1)}, bf16[256,256]{1,0:T(8,128)(2,1)}, bf16[256,256]{1,0:T(8,128)(2,1)}, bf16[256,256...) custom-call(s32[16,16]{1,0:T(8,128)} %bitcast.45, ...), custom_call_target="tpu_custom_call" | custom-call | flops 11000000512 | bytes 1048576 | tf_op jit(solution)/shard_map/attention/pallas_call | solution.py:396
  46.2 1.5 %collective-permute-start.15 = (bf16[256,256]{1,0:T(8,128)(2,1)}, bf16[256,256]{1,0:T(8,128)(2,1)S(1)}, u32[]{:S(2)}, u32[]{:S(2)}) collective-permute-start(bf16[256,256]{1,0:T(8,128)(2,1)} %get-tuple-element.35), channel_id=1, source_target_pairs={{0,2},{1,3},{2,4},{3,5},{4,6},{5,7},{6,0},{7,1},{8,10},{9,11},{10,... | collective-permute-start | bytes 393224 | tf_op jit(solution)/shard_map/ppermute | solution.py:338
  48.5 6.0 %ssm.1 = (bf16[256,1024]{1,0:T(8,128)(2,1)}, bf16[256,1024]{1,0:T(8,128)(2,1)}, bf16[256,128]{1,0:T(8,128)(2,1)}, bf16[256,128]{1,0:T(8,128)(2,1)}, f32[16,128]{1,0:T(8,128)}) custom-call(bf16[256,1024]{1,0:T(8,128)(2,1)} %bitcast.21, bf16[256,1024]{1,0:T(8,128)(2,1)} %bitcast.24, bf16[256,128]{1,0:T(8,128)(2,1)} %bitcast.42, bf16[256,128]{1,0:T(8,128)(2,1)} %bitcast.44, ...), custom_call_target="tpu_custom_call" | custom-call | flops 6600000000 | bytes 1048576 | tf_op jit(solution)/shard_map/ssm/pallas_call | solution.py:421
  55.9 3.7 %collective-permute-start.26 = (f32[16,128]{1,0:T(8,128)}, f32[16,128]{1,0:T(8,128)S(1)}, u32[]{:S(2)}, u32[]{:S(2)}) collective-permute-start(f32[16,128]{1,0:T(8,128)} %get-tuple-element.46), channel_id=1, source_target_pairs={{0,6},{1,7},{2,0},{3,1},{4,2},{5,3},{6,4},{7,5},{8,14},{9,15},{10,... | collective-permute-start | bytes 24584 | tf_op jit(solution)/shard_map/ppermute | solution.py:338
  60.6 2.3 %collective-permute-start.23 = (f32[16,128]{1,0:T(8,128)}, f32[16,128]{1,0:T(8,128)S(1)}, u32[]{:S(2)}, u32[]{:S(2)}) collective-permute-start(f32[16,128]{1,0:T(8,128)} %get-tuple-element.46), channel_id=1, source_target_pairs={{0,3},{1,4},{2,5},{3,6},{4,7},{5,0},{6,1},{7,2},{8,11},{9,12},{10,... | collective-permute-start | bytes 24584 | tf_op jit(solution)/shard_map/ppermute | solution.py:338
  64.3 1.6 %collective-permute-start.16 = (bf16[256,256]{1,0:T(8,128)(2,1)S(1)}, bf16[256,256]{1,0:T(8,128)(2,1)S(1)}, u32[]{:S(2)}, u32[]{:S(2)}) collective-permute-start(bf16[256,256]{1,0:T(8,128)(2,1)S(1)} %copy-done.9), channel_id=1, source_target_pairs={{0,3},{1,4},{2,5},{3,6},{4,7},{5,0},{6,1},{7,2},{8,11},{9,12},{10,... | collective-permute-start | bytes 393224 | tf_op jit(solution)/shard_map/ppermute | solution.py:338
  65.9 1.6 %collective-permute-start.17 = (bf16[256,256]{1,0:T(8,128)(2,1)S(1)}, bf16[256,256]{1,0:T(8,128)(2,1)S(1)}, u32[]{:S(2)}, u32[]{:S(2)}) collective-permute-start(bf16[256,256]{1,0:T(8,128)(2,1)S(1)} %copy-done.7), channel_id=1, source_target_pairs={{0,4},{1,5},{2,6},{3,7},{4,0},{5,1},{6,2},{7,3},{8,12},{9,13},{10,... | collective-permute-start | bytes 393224 | tf_op jit(solution)/shard_map/ppermute | solution.py:338
  68.3 1.9 %collective-permute-start.20 = (bf16[256,256]{1,0:T(8,128)(2,1)S(1)}, bf16[256,256]{1,0:T(8,128)(2,1)S(1)}, u32[]{:S(2)}, u32[]{:S(2)}) collective-permute-start(bf16[256,256]{1,0:T(8,128)(2,1)S(1)} %copy-done.3), channel_id=1, source_target_pairs={{0,7},{1,0},{2,1},{3,2},{4,3},{5,4},{6,5},{7,6},{8,15},{9,8},{10,9... | collective-permute-start | bytes 393224 | tf_op jit(solution)/shard_map/ppermute | solution.py:338
  70.2 5.6 %collective-permute-start.30 = (f32[16,128]{1,0:T(8,128)S(1)}, f32[16,128]{1,0:T(8,128)S(1)}, u32[]{:S(2)}, u32[]{:S(2)}) collective-permute-start(f32[16,128]{1,0:T(8,128)S(1)} %add_add_fusion), channel_id=1, source_target_pairs={{0,24},{8,0},{16,8},{24,16},{1,25},{9,1},{17,9},{25,17},{2,26},{10... | collective-permute-start | bytes 24584 | tf_op jit(solution)/shard_map/ppermute | solution.py:338
  77.2 4.6 %collective-permute-start.29 = (f32[16,128]{1,0:T(8,128)S(1)}, f32[16,128]{1,0:T(8,128)S(1)}, u32[]{:S(2)}, u32[]{:S(2)}) collective-permute-start(f32[16,128]{1,0:T(8,128)S(1)} %add_add_fusion), channel_id=1, source_target_pairs={{0,16},{8,24},{16,0},{24,8},{1,17},{9,25},{17,1},{25,9},{2,18},{10... | collective-permute-start | bytes 24584 | tf_op jit(solution)/shard_map/ppermute | solution.py:338
  81.8 1.8 %collective-permute-start.28 = (f32[16,128]{1,0:T(8,128)S(1)}, f32[16,128]{1,0:T(8,128)S(1)}, u32[]{:S(2)}, u32[]{:S(2)}) collective-permute-start(f32[16,128]{1,0:T(8,128)S(1)} %add_add_fusion), channel_id=1, source_target_pairs={{0,8},{8,16},{16,24},{24,0},{1,9},{9,17},{17,25},{25,1},{2,10},{10... | collective-permute-start | bytes 24584 | tf_op jit(solution)/shard_map/ppermute | solution.py:338
  84.3 2.0 %owner_sum.1 = (bf16[256,128]{1,0:T(8,128)(2,1)}, bf16[256,128]{1,0:T(8,128)(2,1)}) custom-call(bf16[256,256]{1,0:T(8,128)(2,1)} %get-tuple-element.33.refs_0_, bf16[256,256]{1,0:T(8,128)(2,1)} %copy-done.6, bf16[256,256]{1,0:T(8,128)(2,1)} %copy-done.8, bf16[256,256]{1,0:T(8,128)(2,1)} %copy-done.10, bf16[256,256]{1,0:T(8,128)(2,1)} %copy-done.11, ...), custom_call_target="tpu_custom_call" | custom-call | flops 1100000000 | bytes 1048576 | tf_op jit(solution)/shard_map/owner_sum/pallas_call | solution.py:451
  (112 shorter events, 14.6 us)
Async XLA Ops:
  4.2 24.9 %all-to-all-start = ((bf16[8,2,16,1152]{3,2,1,0:T(8,128)(2,1)}), bf16[8,2,16,1152]{3,2,1,0:T(8,128)(2,1)S(1)}, u32[]{:S(2)}, u32[]{:S(2)}) async-start(bf16[8,2,16,1152]{3,2,1,0:T(8,128)(2,1)} %local_states.1), calls=%async_computation | async-start | bytes 1179648 | tf_op jit(solution)/shard_map/all_to_all | solution.py:378
  8.6 8.9 %collective-permute-start.6 = (bf16[256,128]{1,0:T(8,128)(2,1)S(1)}, bf16[256,128]{1,0:T(8,128)(2,1)S(1)}, u32[]{:S(2)}, u32[]{:S(2)}) collective-permute-start(bf16[256,128]{1,0:T(8,128)(2,1)S(1)} %bitcast.26), channel_id=1, source_target_pairs={{0,7},{1,0},{2,1},{3,2},{4,3},{5,4},{6,5},{7,6},{8,15},{9,8},{10,9... | collective-permute-start | bytes 196616 | tf_op jit(solution)/shard_map/ppermute | solution.py:338
  8.7 11.8 %collective-permute-start.5 = (bf16[256,128]{1,0:T(8,128)(2,1)S(1)}, bf16[256,128]{1,0:T(8,128)(2,1)S(1)}, u32[]{:S(2)}, u32[]{:S(2)}) collective-permute-start(bf16[256,128]{1,0:T(8,128)(2,1)S(1)} %bitcast.27), channel_id=1, source_target_pairs={{0,6},{1,7},{2,0},{3,1},{4,2},{5,3},{6,4},{7,5},{8,14},{9,15},{10,... | collective-permute-start | bytes 196616 | tf_op jit(solution)/shard_map/ppermute | solution.py:338
  11.3 9.5 %collective-permute-start.4 = (bf16[256,128]{1,0:T(8,128)(2,1)S(1)}, bf16[256,128]{1,0:T(8,128)(2,1)S(1)}, u32[]{:S(2)}, u32[]{:S(2)}) collective-permute-start(bf16[256,128]{1,0:T(8,128)(2,1)S(1)} %bitcast.28), channel_id=1, source_target_pairs={{0,5},{1,6},{2,7},{3,0},{4,1},{5,2},{6,3},{7,4},{8,13},{9,14},{10,... | collective-permute-start | bytes 196616 | tf_op jit(solution)/shard_map/ppermute | solution.py:338
  11.3 11.9 %collective-permute-start.3 = (bf16[256,128]{1,0:T(8,128)(2,1)S(1)}, bf16[256,128]{1,0:T(8,128)(2,1)S(1)}, u32[]{:S(2)}, u32[]{:S(2)}) collective-permute-start(bf16[256,128]{1,0:T(8,128)(2,1)S(1)} %bitcast.29), channel_id=1, source_target_pairs={{0,4},{1,5},{2,6},{3,7},{4,0},{5,1},{6,2},{7,3},{8,12},{9,13},{10,... | collective-permute-start | bytes 196616 | tf_op jit(solution)/shard_map/ppermute | solution.py:338
  11.8 11.8 %collective-permute-start.2 = (bf16[256,128]{1,0:T(8,128)(2,1)S(1)}, bf16[256,128]{1,0:T(8,128)(2,1)S(1)}, u32[]{:S(2)}, u32[]{:S(2)}) collective-permute-start(bf16[256,128]{1,0:T(8,128)(2,1)S(1)} %bitcast.30), channel_id=1, source_target_pairs={{0,3},{1,4},{2,5},{3,6},{4,7},{5,0},{6,1},{7,2},{8,11},{9,12},{10,... | collective-permute-start | bytes 196616 | tf_op jit(solution)/shard_map/ppermute | solution.py:338
  20.8 6.7 %collective-permute-start.13 = (bf16[256,128]{1,0:T(8,128)(2,1)S(1)}, bf16[256,128]{1,0:T(8,128)(2,1)S(1)}, u32[]{:S(2)}, u32[]{:S(2)}) collective-permute-start(bf16[256,128]{1,0:T(8,128)(2,1)S(1)} %bitcast.34), channel_id=1, source_target_pairs={{0,7},{1,0},{2,1},{3,2},{4,3},{5,4},{6,5},{7,6},{8,15},{9,8},{10,9... | collective-permute-start | bytes 196616 | tf_op jit(solution)/shard_map/ppermute | solution.py:338
  23.7 12.9 %collective-permute-start.11 = (bf16[256,128]{1,0:T(8,128)(2,1)S(1)}, bf16[256,128]{1,0:T(8,128)(2,1)S(1)}, u32[]{:S(2)}, u32[]{:S(2)}) collective-permute-start(bf16[256,128]{1,0:T(8,128)(2,1)S(1)} %bitcast.36), channel_id=1, source_target_pairs={{0,5},{1,6},{2,7},{3,0},{4,1},{5,2},{6,3},{7,4},{8,13},{9,14},{10,... | collective-permute-start | bytes 196616 | tf_op jit(solution)/shard_map/ppermute | solution.py:338
  23.7 12.9 %collective-permute-start.10 = (bf16[256,128]{1,0:T(8,128)(2,1)S(1)}, bf16[256,128]{1,0:T(8,128)(2,1)S(1)}, u32[]{:S(2)}, u32[]{:S(2)}) collective-permute-start(bf16[256,128]{1,0:T(8,128)(2,1)S(1)} %bitcast.37), channel_id=1, source_target_pairs={{0,4},{1,5},{2,6},{3,7},{4,0},{5,1},{6,2},{7,3},{8,12},{9,13},{10,... | collective-permute-start | bytes 196616 | tf_op jit(solution)/shard_map/ppermute | solution.py:338
  25.2 11.4 %collective-permute-start.9 = (bf16[256,128]{1,0:T(8,128)(2,1)S(1)}, bf16[256,128]{1,0:T(8,128)(2,1)S(1)}, u32[]{:S(2)}, u32[]{:S(2)}) collective-permute-start(bf16[256,128]{1,0:T(8,128)(2,1)S(1)} %bitcast.38), channel_id=1, source_target_pairs={{0,3},{1,4},{2,5},{3,6},{4,7},{5,0},{6,1},{7,2},{8,11},{9,12},{10,... | collective-permute-start | bytes 196616 | tf_op jit(solution)/shard_map/ppermute | solution.py:338
  27.5 9.1 %collective-permute-start.8 = (bf16[256,128]{1,0:T(8,128)(2,1)S(1)}, bf16[256,128]{1,0:T(8,128)(2,1)S(1)}, u32[]{:S(2)}, u32[]{:S(2)}) collective-permute-start(bf16[256,128]{1,0:T(8,128)(2,1)S(1)} %bitcast.39), channel_id=1, source_target_pairs={{0,2},{1,3},{2,4},{3,5},{4,6},{5,7},{6,0},{7,1},{8,10},{9,11},{10,... | collective-permute-start | bytes 196616 | tf_op jit(solution)/shard_map/ppermute | solution.py:338
  29.1 7.6 %collective-permute-start.7 = (bf16[256,128]{1,0:T(8,128)(2,1)S(1)}, bf16[256,128]{1,0:T(8,128)(2,1)S(1)}, u32[]{:S(2)}, u32[]{:S(2)}) collective-permute-start(bf16[256,128]{1,0:T(8,128)(2,1)S(1)} %bitcast.40), channel_id=1, source_target_pairs={{0,1},{1,2},{2,3},{3,4},{4,5},{5,6},{6,7},{7,0},{8,9},{9,10},{10,1... | collective-permute-start | bytes 196616 | tf_op jit(solution)/shard_map/ppermute | solution.py:338
  32.2 15.5 %all-to-all-start.1 = ((bf16[8,2,16,1024]{3,2,1,0:T(8,128)(2,1)}), bf16[8,2,16,1024]{3,2,1,0:T(8,128)(2,1)S(1)}, u32[]{:S(2)}, u32[]{:S(2)}) async-start(bf16[8,2,16,1024]{3,2,1,0:T(8,128)(2,1)} %get-tuple-element.28), calls=%async_computation.1 | async-start | bytes 1048576 | tf_op jit(solution)/shard_map/all_to_all | solution.py:392
  46.0 14.3 %collective-permute-start.14 = (bf16[256,256]{1,0:T(8,128)(2,1)}, bf16[256,256]{1,0:T(8,128)(2,1)S(1)}, u32[]{:S(2)}, u32[]{:S(2)}) collective-permute-start(bf16[256,256]{1,0:T(8,128)(2,1)} %get-tuple-element.34), channel_id=1, source_target_pairs={{0,1},{1,2},{2,3},{3,4},{4,5},{5,6},{6,7},{7,0},{8,9},{9,10},{10,1... | collective-permute-start | bytes 393224 | tf_op jit(solution)/shard_map/ppermute | solution.py:338
  46.2 14.4 %collective-permute-start.15 = (bf16[256,256]{1,0:T(8,128)(2,1)}, bf16[256,256]{1,0:T(8,128)(2,1)S(1)}, u32[]{:S(2)}, u32[]{:S(2)}) collective-permute-start(bf16[256,256]{1,0:T(8,128)(2,1)} %get-tuple-element.35), channel_id=1, source_target_pairs={{0,2},{1,3},{2,4},{3,5},{4,6},{5,7},{6,0},{7,1},{8,10},{9,11},{10,... | collective-permute-start | bytes 393224 | tf_op jit(solution)/shard_map/ppermute | solution.py:338
  54.5 8.4 %collective-permute-start.27 = (f32[16,128]{1,0:T(8,128)}, f32[16,128]{1,0:T(8,128)S(1)}, u32[]{:S(2)}, u32[]{:S(2)}) collective-permute-start(f32[16,128]{1,0:T(8,128)} %get-tuple-element.46), channel_id=1, source_target_pairs={{0,7},{1,0},{2,1},{3,2},{4,3},{5,4},{6,5},{7,6},{8,15},{9,8},{10,9... | collective-permute-start | bytes 24584 | tf_op jit(solution)/shard_map/ppermute | solution.py:338
  55.9 8.4 %collective-permute-start.26 = (f32[16,128]{1,0:T(8,128)}, f32[16,128]{1,0:T(8,128)S(1)}, u32[]{:S(2)}, u32[]{:S(2)}) collective-permute-start(f32[16,128]{1,0:T(8,128)} %get-tuple-element.46), channel_id=1, source_target_pairs={{0,6},{1,7},{2,0},{3,1},{4,2},{5,3},{6,4},{7,5},{8,14},{9,15},{10,... | collective-permute-start | bytes 24584 | tf_op jit(solution)/shard_map/ppermute | solution.py:338
  60.6 6.9 %collective-permute-start.23 = (f32[16,128]{1,0:T(8,128)}, f32[16,128]{1,0:T(8,128)S(1)}, u32[]{:S(2)}, u32[]{:S(2)}) collective-permute-start(f32[16,128]{1,0:T(8,128)} %get-tuple-element.46), channel_id=1, source_target_pairs={{0,3},{1,4},{2,5},{3,6},{4,7},{5,0},{6,1},{7,2},{8,11},{9,12},{10,... | collective-permute-start | bytes 24584 | tf_op jit(solution)/shard_map/ppermute | solution.py:338
  65.9 11.4 %collective-permute-start.17 = (bf16[256,256]{1,0:T(8,128)(2,1)S(1)}, bf16[256,256]{1,0:T(8,128)(2,1)S(1)}, u32[]{:S(2)}, u32[]{:S(2)}) collective-permute-start(bf16[256,256]{1,0:T(8,128)(2,1)S(1)} %copy-done.7), channel_id=1, source_target_pairs={{0,4},{1,5},{2,6},{3,7},{4,0},{5,1},{6,2},{7,3},{8,12},{9,13},{10,... | collective-permute-start | bytes 393224 | tf_op jit(solution)/shard_map/ppermute | solution.py:338
  67.5 14.3 %collective-permute-start.18 = (bf16[256,256]{1,0:T(8,128)(2,1)S(1)}, bf16[256,256]{1,0:T(8,128)(2,1)S(1)}, u32[]{:S(2)}, u32[]{:S(2)}) collective-permute-start(bf16[256,256]{1,0:T(8,128)(2,1)S(1)} %copy-done.5), channel_id=1, source_target_pairs={{0,5},{1,6},{2,7},{3,0},{4,1},{5,2},{6,3},{7,4},{8,13},{9,14},{10,... | collective-permute-start | bytes 393224 | tf_op jit(solution)/shard_map/ppermute | solution.py:338
  67.5 16.0 %collective-permute-start.19 = (bf16[256,256]{1,0:T(8,128)(2,1)S(1)}, bf16[256,256]{1,0:T(8,128)(2,1)S(1)}, u32[]{:S(2)}, u32[]{:S(2)}) collective-permute-start(bf16[256,256]{1,0:T(8,128)(2,1)S(1)} %copy-done.4), channel_id=1, source_target_pairs={{0,6},{1,7},{2,0},{3,1},{4,2},{5,3},{6,4},{7,5},{8,14},{9,15},{10,... | collective-permute-start | bytes 393224 | tf_op jit(solution)/shard_map/ppermute | solution.py:338
  68.3 15.3 %collective-permute-start.20 = (bf16[256,256]{1,0:T(8,128)(2,1)S(1)}, bf16[256,256]{1,0:T(8,128)(2,1)S(1)}, u32[]{:S(2)}, u32[]{:S(2)}) collective-permute-start(bf16[256,256]{1,0:T(8,128)(2,1)S(1)} %copy-done.3), channel_id=1, source_target_pairs={{0,7},{1,0},{2,1},{3,2},{4,3},{5,4},{6,5},{7,6},{8,15},{9,8},{10,9... | collective-permute-start | bytes 393224 | tf_op jit(solution)/shard_map/ppermute | solution.py:338
  70.2 16.1 %collective-permute-start.30 = (f32[16,128]{1,0:T(8,128)S(1)}, f32[16,128]{1,0:T(8,128)S(1)}, u32[]{:S(2)}, u32[]{:S(2)}) collective-permute-start(f32[16,128]{1,0:T(8,128)S(1)} %add_add_fusion), channel_id=1, source_target_pairs={{0,24},{8,0},{16,8},{24,16},{1,25},{9,1},{17,9},{25,17},{2,26},{10... | collective-permute-start | bytes 24584 | tf_op jit(solution)/shard_map/ppermute | solution.py:338
  77.2 9.1 %collective-permute-start.29 = (f32[16,128]{1,0:T(8,128)S(1)}, f32[16,128]{1,0:T(8,128)S(1)}, u32[]{:S(2)}, u32[]{:S(2)}) collective-permute-start(f32[16,128]{1,0:T(8,128)S(1)} %add_add_fusion), channel_id=1, source_target_pairs={{0,16},{8,24},{16,0},{24,8},{1,17},{9,25},{17,1},{25,9},{2,18},{10... | collective-permute-start | bytes 24584 | tf_op jit(solution)/shard_map/ppermute | solution.py:338
  (40 other events, 326.8 us)

commit v3 on v2

v3 whole, which is shorter than its diff:
```python
import jax
import jax.numpy as jnp
from jax import lax
from jax.experimental import pallas as pl
from jax.experimental.pallas import tpu as pltpu
from jax.sharding import PartitionSpec as P

HEAD_WIDTH = 128
QUERY_HEADS = 8
HS = 8
P_SIZE = 128
NS = 128
BLOCK = 128
WIDE = HS * P_SIZE
LANES = 128
FACTOR = HEAD_WIDTH ** (-0.5)
LOG2E = 1.4426950408889634
NEG = -1e30
HALF = NS // 2
HIGH = lax.Precision.HIGHEST
F32 = jnp.float32
BF16 = jnp.bfloat16

VMEM = pl.BlockSpec(memory_space=pltpu.VMEM)
SMEM = pl.BlockSpec(memory_space=pltpu.SMEM)


def params(limit=56 << 20):
    return pltpu.CompilerParams(vmem_limit_bytes=limit)


def cost(microseconds):
    return pl.CostEstimate(
        flops=int(microseconds * 1.1e9), bytes_accessed=1 << 20, transcendentals=0
    )


def dot(a, b, ca, cb, precision=None):
    return lax.dot_general(
        a, b, (((ca,), (cb,)), ((), ())), preferred_element_type=F32, precision=precision
    )


def head(h):
    return slice(h * LANES, (h + 1) * LANES)


def running_logs(step_ref, rate_ref, pad_ref):
    pad_ref[...] = jnp.zeros_like(pad_ref)
    for h in range(HS):
        rate = jnp.exp(jnp.full((1, 2 * BLOCK), rate_ref[h], F32))
        pad_ref[h : h + 1, :] = -step_ref[h : h + 1, :] * rate
    row = lax.broadcasted_iota(jnp.int32, (BLOCK, BLOCK), 0)
    col = lax.broadcasted_iota(jnp.int32, (BLOCK, BLOCK), 1)
    upper = jnp.where(row <= col, 1.0, 0.0).astype(F32)
    flat0 = dot(pad_ref[:, :BLOCK], upper, 1, 0, HIGH)
    flat1 = dot(pad_ref[:, BLOCK:], upper, 1, 0, HIGH)
    return flat0, flat1, flat0.T, flat1.T


def scaled(x_ref, column, out_ref):
    for h in range(HS):
        out_ref[:, head(h)] = (x_ref[:, head(h)].astype(F32) * column[:, h : h + 1]).astype(BF16)


def pack_kernel(key_ref, value_ref, out_ref):
    out_ref[:, :LANES] = key_ref[...]
    out_ref[:, LANES:] = value_ref[...]


def enter_and_tail(run0, run1):
    t0, t1 = run0[BLOCK - 1 :, :], run1[BLOCK - 1 :, :]
    enter = jnp.concatenate([run0, run1 + t0], axis=0)
    tail = jnp.concatenate([(t0 - run0) + t1, t1 - run1], axis=0)
    return enter, tail, t0 + t1


def local_states_kernel(
    place_ref, x_ref, g_ref, b_ref, c_ref, step_ref, rate_ref, keep_ref, give_ref,
    pad_ref, high_ref, rest_ref, log_ref, state_ref,
):
    core = place_ref[1]
    _, _, run0, run1 = running_logs(step_ref, rate_ref, pad_ref)
    enter_log, tail_log, total = enter_and_tail(run0, run1)
    enter, tail = jnp.exp(enter_log), jnp.exp(tail_log)
    high = total.astype(BF16).astype(F32)
    middle = (total - high).astype(BF16).astype(F32)
    low = total - high - middle
    index = lax.broadcasted_iota(jnp.int32, (HALF, LANES), 0)
    logs = jnp.where(index == 0, high, jnp.where(index == 1, middle, low)).astype(BF16)
    mine = pl.ds(pl.multiple_of(core * HALF, HALF), HALF)
    other = pl.ds(pl.multiple_of((1 - core) * HALF, HALF), HALF)
    cases = ((b_ref, x_ref, tail, tail_log), (c_ref, g_ref, enter, enter_log))
    for direction, (left, right, factor, weight) in enumerate(cases):
        for h in range(HS):
            product = right[:, head(h)].astype(F32) * factor[:, h : h + 1]
            rounded = product.astype(BF16)
            high_ref[:, head(h)] = rounded
            rest_ref[:, head(h)] = (product - rounded.astype(F32)).astype(BF16)
            log_ref[:, head(h)] = (product * weight[:, h : h + 1]).astype(BF16)
        turned_left = left[...].astype(F32).T.astype(BF16)
        state_ref[direction, :, :WIDE] = (
            dot(turned_left, high_ref[...], 1, 0) + dot(turned_left, rest_ref[...], 1, 0)
        ).astype(BF16)
        state_ref[3 - direction, :, :WIDE] = dot(turned_left, log_ref[...], 1, 0).astype(BF16)
    for kind in range(4):
        keep_ref[kind, :, :WIDE] = state_ref[kind, mine, :]
        keep_ref[kind, :, WIDE:] = logs
        give_ref[kind, :, :WIDE] = state_ref[kind, other, :]
        give_ref[kind, :, WIDE:] = logs


def log_row(ref, at):
    parts = ref[at + (slice(0, 16), slice(WIDE, WIDE + LANES))].astype(F32)
    return parts[0:1, :] + parts[1:2, :] + parts[2:3, :]


def combine_kernel(chips, place_ref, keep_ref, recv_ref, *message_refs):
    chip, core = place_ref[0], place_ref[1]
    is0 = core == 0
    log_mine, log_other = log_row(keep_ref, (0,)), log_row(recv_ref, (0,))
    log0, log1 = jnp.where(is0, log_mine, log_other), jnp.where(is0, log_other, log_mine)
    total = log0 + log1
    high = total.astype(BF16).astype(F32)
    middle = (total - high).astype(BF16).astype(F32)
    low = total - high - middle
    index = lax.broadcasted_iota(jnp.int32, (HALF, LANES), 0)
    logs = jnp.where(index == 0, high, jnp.where(index == 1, middle, low)).astype(BF16)
    decay0, decay1 = jnp.exp(log0), jnp.exp(log1)
    for h in range(HS):
        mine, other = keep_ref[0, :, head(h)].astype(F32), recv_ref[0, :, head(h)].astype(F32)
        first, second = jnp.where(is0, mine, other), jnp.where(is0, other, mine)
        state = (first * decay1[:, h : h + 1] + second).astype(BF16)
        mine, other = keep_ref[1, :, head(h)].astype(F32), recv_ref[1, :, head(h)].astype(F32)
        first, second = jnp.where(is0, mine, other), jnp.where(is0, other, mine)
        grad = (second * decay0[:, h : h + 1] + first).astype(BF16)
        for k in range(1, chips):
            later = chip + k < chips
            message_refs[k - 1][:, head(h)] = jnp.where(later, state, grad)
    for k in range(1, chips):
        message_refs[k - 1][:, WIDE:] = logs


def chain_kernel(chips, place_ref, keep_ref, recv_ref, sums_ref, *refs):
    message_refs = refs[: chips - 1]
    own_ref, give_ref, total_ref = refs[chips - 1 :]
    chip, core = place_ref[0], place_ref[1]
    is0 = core == 0
    log_mine, log_other = log_row(keep_ref, (0,)), log_row(recv_ref, (0,))
    log0, log1 = jnp.where(is0, log_mine, log_other), jnp.where(is0, log_other, log_mine)
    decay0, decay1 = jnp.exp(log0), jnp.exp(log1)
    weight0, weight1 = log0 * decay0, log1 * decay1
    factors = [None] + [jnp.exp(log_row(ref, ())) for ref in message_refs]
    total_ref[...] = sums_ref[...]
    for h in range(HS):
        column = slice(h, h + 1)
        states = [
            (keep_ref[kind, :, head(h)].astype(F32), recv_ref[kind, :, head(h)].astype(F32))
            for kind in range(4)
        ]
        (s0, s1), (g0, g1), (qs0, qs1), (qg0, qg1) = [
            (jnp.where(is0, mine, other), jnp.where(is0, other, mine)) for mine, other in states
        ]
        state = jnp.zeros((HALF, LANES), F32)
        for k in range(chips - 1, 0, -1):
            new = state * factors[k][:, column] + message_refs[k - 1][:, head(h)].astype(F32)
            state = jnp.where(k <= chip, new, state)
        grad = jnp.zeros((HALF, LANES), F32)
        for k in range(1, chips):
            new = grad * factors[k][:, column] + message_refs[k - 1][:, head(h)].astype(F32)
            grad = jnp.where(k > chip, new, grad)
        h0, l1 = state, grad
        h1 = h0 * decay0[:, column] + s0
        l0 = l1 * decay1[:, column] + g1
        cross = h0 * (l0 * weight0[:, column] + qs0) + h1 * (l1 * weight1[:, column] + qs1)
        cross += l0 * qg0 + l1 * qg1
        total_ref[h : h + 1, :] += jnp.sum(cross, axis=0, keepdims=True)
        h0, h1, l0, l1 = (value.astype(BF16) for value in (h0, h1, l0, l1))
        own_ref[0, :, head(h)] = jnp.where(is0, h0, h1)
        own_ref[1, :, head(h)] = jnp.where(is0, l0, l1)
        give_ref[0, :, head(h)] = jnp.where(is0, h1, h0)
        give_ref[1, :, head(h)] = jnp.where(is0, l1, l0)


def attention_kernel(
    chips, mask_ref, place_ref, after_ref, q_ref, g_ref, *refs
):
    kv_parts = refs[: 2 * chips]
    (
        out_ref, dq_ref, keep_ref, give_ref,
        index_ref, kv_ref, s_ref, acc_ref, qs_ref, gs_ref, ds_ref, pr_ref, o_ref, dqt_ref, rows_ref,
    ) = refs[2 * chips :]
    count = mask_ref.shape[0]
    columns = QUERY_HEADS * BLOCK
    tokens = q_ref.shape[0]
    chip, core = place_ref[0], place_ref[1]
    me = 2 * chip + core
    acc_ref[...] = jnp.zeros_like(acc_ref)
    for k in range(chips):
        for other in range(2):
            source = 2 * lax.rem(chip + chips - k, chips) + lax.rem(core + other, 2)
            at = pl.ds(pl.multiple_of(source * tokens, tokens), tokens)
            kv_ref[at, :] = kv_parts[2 * k + other][...]
    scale = FACTOR * LOG2E
    for block in range(tokens // BLOCK):
        at = slice(block * BLOCK, (block + 1) * BLOCK)
        row = me * (tokens // BLOCK) + block

        def note(j, n):
            @pl.when(mask_ref[row, j] == 1)
            def _():
                index_ref[n] = j

            return n + mask_ref[row, j]

        allowed = lax.fori_loop(0, count, note, 0)
        index_ref[allowed] = row
        pairs = (allowed + 1) // 2
        for h in range(QUERY_HEADS):
            qs_ref[head(h), :] = q_ref[at, head(h)]
            gs_ref[head(h), :] = g_ref[at, head(h)]

        def spans(t):
            first = pl.multiple_of(index_ref[2 * t] * BLOCK, BLOCK)
            second = pl.multiple_of(index_ref[2 * t + 1] * BLOCK, BLOCK)
            return pl.ds(first, BLOCK), pl.ds(second, BLOCK)

        def tile(t, lanes):
            one, two = spans(t)
            return jnp.concatenate([kv_ref[one, lanes], kv_ref[two, lanes]], axis=0)

        def scores_step(t, best):
            k_tile = tile(t, slice(0, LANES))
            live = 2 * t + 1 < allowed
            outs = []
            for part in range(columns // 256):
                lanes = slice(part * 256, (part + 1) * 256)
                s = dot(k_tile, qs_ref[lanes, :], 1, 1)
                low = s[:BLOCK]
                high = jnp.where(live, s[BLOCK:], NEG)
                s_ref[t, :BLOCK, lanes] = low
                s_ref[t, BLOCK:, lanes] = high
                both = jnp.maximum(low, high).reshape(BLOCK // 8, 8, 256)
                outs.append(jnp.maximum(best[part], jnp.max(both, axis=0)))
            return tuple(outs)

        best = lax.fori_loop(
            0, pairs, scores_step, tuple(jnp.full((8, 256), NEG, F32) for _ in range(columns // 256))
        )
        for part in range(columns // 256):
            lanes = slice(part * 256, (part + 1) * 256)
            rows_ref[0:1, lanes] = jnp.max(best[part], axis=0, keepdims=True) * scale
        o_ref[...] = jnp.zeros_like(o_ref)

        def weights_step(t, total):
            v_tile = tile(t, slice(LANES, 2 * LANES))
            outs = []
            for part in range(columns // 256):
                lanes = slice(part * 256, (part + 1) * 256)
                w = jnp.exp2(s_ref[t, :, lanes] * scale - rows_ref[0:1, lanes])
                s_ref[t, :, lanes] = w
                outs.append(total[part] + jnp.sum(w.reshape(32, 8, 256), axis=0))
                o_ref[:, lanes] += dot(v_tile, w.astype(BF16), 0, 0)
            return tuple(outs)

        total = lax.fori_loop(
            0, pairs, weights_step, tuple(jnp.zeros((8, 256), F32) for _ in range(columns // 256))
        )
        for part in range(columns // 256):
            lanes = slice(part * 256, (part + 1) * 256)
            inverse = 1.0 / jnp.sum(total[part], axis=0, keepdims=True)
            rows_ref[1:2, lanes] = inverse
            o = o_ref[:, lanes] * inverse
            o_ref[:, lanes] = o
            g_t = gs_ref[lanes, :].astype(F32).T
            rows_ref[2:3, lanes] = jnp.sum(o * g_t, axis=0, keepdims=True)
        for h in range(QUERY_HEADS):
            out_ref[at, head(h)] = o_ref[:, head(h)].T
        dqt_ref[...] = jnp.zeros_like(dqt_ref)

        def grads_step(t, carry):
            k_tile = tile(t, slice(0, LANES))
            v_tile = tile(t, slice(LANES, 2 * LANES))
            for part in range(columns // 256):
                lanes = slice(part * 256, (part + 1) * 256)
                dp = dot(v_tile, gs_ref[lanes, :], 1, 1)
                probs = s_ref[t, :, lanes] * rows_ref[1:2, lanes]
                ds = (probs * (dp - rows_ref[2:3, lanes])).astype(BF16)
                ds_ref[:, lanes] = ds
                pr_ref[:, lanes] = probs.astype(BF16)
                dqt_ref[:, lanes] += dot(k_tile, ds, 0, 0)
            dk = dot(ds_ref[...], qs_ref[...], 1, 0) * FACTOR
            dv = dot(pr_ref[...], gs_ref[...], 1, 0)
            one, two = spans(t)
            acc_ref[one, :LANES] += dk[:BLOCK]
            acc_ref[one, LANES:] += dv[:BLOCK]
            acc_ref[two, :LANES] += dk[BLOCK:]
            acc_ref[two, LANES:] += dv[BLOCK:]
            return carry

        lax.fori_loop(0, pairs, grads_step, 0)
        for h in range(QUERY_HEADS):
            dq_ref[at, head(h)] = (dqt_ref[:, head(h)].T * FACTOR).astype(BF16)
    for k in range(chips):
        mine = pl.multiple_of((2 * k + core) * tokens, tokens)
        other = pl.multiple_of((2 * k + 1 - core) * tokens, tokens)
        keep_ref[k] = acc_ref[pl.ds(mine, tokens), :].astype(BF16)
        give_ref[k] = acc_ref[pl.ds(other, tokens), :].astype(BF16)


def pair_sum_kernel(chips, place_ref, keep_ref, recv_ref, own_ref, *message_refs):
    chip = place_ref[0]
    own_ref[...] = keep_ref[chip].astype(F32) + recv_ref[chip].astype(F32)
    for k in range(1, chips):
        target = lax.rem(chip + k, chips)
        both = keep_ref[target].astype(F32) + recv_ref[target].astype(F32)
        message_refs[k - 1][...] = both.astype(BF16)


def owner_sum_kernel(*refs):
    parts, (dk_ref, dv_ref) = refs[:-2], refs[-2:]
    for out_ref, lanes in ((dk_ref, slice(0, LANES)), (dv_ref, slice(LANES, 2 * LANES))):
        total = parts[0][:, lanes].astype(F32)
        for part in parts[1:]:
            total += part[:, lanes].astype(F32)
        out_ref[...] = total.astype(BF16)


def inner_kernel(
    x_ref, g_ref, b_ref, c_ref, step_ref, rate_ref, skip_ref,
    y_ref, dx_ref, db_ref, dc_ref, sums_ref,
    pad_ref, inner_ref, dinner_ref, m_ref, runt_ref,
):
    tokens = 2 * BLOCK
    flat0, flat1, run0, run1 = running_logs(step_ref, rate_ref, pad_ref)
    own = jnp.concatenate([run0, run1], axis=0)
    runt_ref[:, :BLOCK] = flat0
    runt_ref[:, tokens : tokens + BLOCK] = flat0 - flat0[:, BLOCK - 1 :]
    runt_ref[:, tokens + BLOCK :] = flat1
    b = b_ref[...]
    c = c_ref[...]
    inner_ref[...] = dot(c, b, 1, 1)
    dinner_ref[...] = jnp.zeros_like(dinner_ref)
    row0 = lax.broadcasted_iota(jnp.int32, (BLOCK, BLOCK), 0)
    col0 = lax.broadcasted_iota(jnp.int32, (BLOCK, BLOCK), 1)
    row1 = lax.broadcasted_iota(jnp.int32, (BLOCK, tokens), 0)
    col1 = lax.broadcasted_iota(jnp.int32, (BLOCK, tokens), 1)
    seen0 = row0 >= col0
    seen1 = row1 + BLOCK >= col1
    m_ref[:BLOCK, BLOCK:] = jnp.zeros((BLOCK, BLOCK), BF16)
    for h in range(HS):
        lanes = head(h)
        x = x_ref[:, lanes]
        g = g_ref[:, lanes]
        xf, gf = x.astype(F32), g.astype(F32)
        gain = skip_ref[h]
        spread0 = jnp.where(seen0, own[:BLOCK, h : h + 1] - runt_ref[h : h + 1, :BLOCK], NEG)
        spread1 = jnp.where(seen1, own[BLOCK:, h : h + 1] - runt_ref[h : h + 1, tokens:], NEG)
        decay0, decay1 = jnp.exp(spread0), jnp.exp(spread1)
        dm = dot(g, x, 1, 1)
        e0, e1 = decay0 * dm[:BLOCK, :BLOCK], decay1 * dm[BLOCK:, :]
        m_ref[:BLOCK, :BLOCK] = (decay0 * inner_ref[:BLOCK, :BLOCK]).astype(BF16)
        m_ref[BLOCK:, :] = (decay1 * inner_ref[BLOCK:, :]).astype(BF16)
        dinner_ref[:BLOCK, :BLOCK] += e0
        dinner_ref[BLOCK:, :] += e1
        w0 = jnp.sum(spread0 * (e0 * inner_ref[:BLOCK, :BLOCK]), axis=0, keepdims=True)
        w1 = jnp.sum(spread1 * (e1 * inner_ref[BLOCK:, :]), axis=0, keepdims=True)
        m = m_ref[...]
        y_ref[:, lanes] = dot(m, x, 1, 0) + gain * xf
        dx_ref[:, lanes] = dot(m, g, 0, 0) + gain * gf
        sums_ref[h : h + 1, :] = w0 + w1[:, :BLOCK] + w1[:, BLOCK:]
        sums_ref[HS + h : HS + h + 1, :] = jnp.sum(gf * xf, axis=0, keepdims=True)
    dinner = dinner_ref[...].astype(BF16)
    dc_ref[...] = dot(dinner, b, 1, 0)
    db_ref[...] = dot(dinner, c, 0, 0)


def outer_kernel(
    place_ref, x_ref, g_ref, b_ref, c_ref, step_ref, rate_ref, own_ref, other_ref, att_ref,
    inner_y_ref, inner_dx_ref, inner_db_ref, inner_dc_ref,
    y_ref, dx_ref, db_ref, dc_ref,
    pad_ref, xt_ref, gt_ref, ent_ref,
):
    core = place_ref[1]
    ent_ref[:, pl.ds(pl.multiple_of(core * HALF, HALF), HALF), :] = own_ref[...]
    ent_ref[:, pl.ds(pl.multiple_of((1 - core) * HALF, HALF), HALF), :] = other_ref[...]
    _, _, run0, run1 = running_logs(step_ref, rate_ref, pad_ref)
    enter_log, tail_log, _ = enter_and_tail(run0, run1)
    enter, tail = jnp.exp(enter_log), jnp.exp(tail_log)
    scaled(x_ref, tail, xt_ref)
    scaled(g_ref, enter, gt_ref)
    b = b_ref[...]
    c = c_ref[...]
    for h in range(HS):
        lanes = head(h)
        carried = dot(c, ent_ref[0, :, lanes], 1, 0) * enter[:, h : h + 1]
        back = dot(b, ent_ref[1, :, lanes], 1, 0) * tail[:, h : h + 1]
        y_ref[:, lanes] = (inner_y_ref[:, lanes] + carried + att_ref[:, lanes]).astype(BF16)
        dx_ref[:, lanes] = (inner_dx_ref[:, lanes] + back).astype(BF16)
    dc_ref[...] = (inner_dc_ref[...] + dot(gt_ref[...], ent_ref[0], 1, 1)).astype(BF16)
    db_ref[...] = (inner_db_ref[...] + dot(xt_ref[...], ent_ref[1], 1, 1)).astype(BF16)


def swapped(array):
    return lax.ppermute(array, "seq", [(i, i ^ 1) for i in range(lax.axis_size("seq"))])


def from_chip(array, k):
    n = lax.axis_size("seq")
    return lax.ppermute(array, "seq", [(i, (i + 2 * k) % n) for i in range(n)])


def turned(array, k):
    n = lax.axis_size("dp")
    return lax.ppermute(array, "dp", [(i, (i + k) % n) for i in range(n)])


def call(kernel, outs, ins, scratch, microseconds, name):
    return pl.pallas_call(
        kernel,
        out_shape=tuple(jax.ShapeDtypeStruct(*out) for out in outs),
        in_specs=[SMEM if small else VMEM for small in ins],
        out_specs=(VMEM,) * len(outs),
        scratch_shapes=scratch,
        compiler_params=params(),
        cost_estimate=cost(microseconds),
        name=name,
    )


def body(query, key, value, ssm_input, in_b, in_c, step, rate_log, skip, block_mask, grad_out):
    n = lax.axis_size("seq")
    chips = n // 2
    tokens = query.shape[1]
    blocks = block_mask.shape[1]
    most = 3 * blocks // 8
    every = blocks * BLOCK
    q, g, x = query[0], grad_out[0], ssm_input[0]
    b, c, steps = in_b[0], in_c[0], step[0].T
    me = lax.axis_index("seq").astype(jnp.int32)
    place = jnp.stack([me // 2, me % 2])

    (kv,) = call(pack_kernel, [((tokens, 2 * LANES), BF16)], [0] * 2, [], 1, "pack_kv")(key[0], value[0])
    kv_parts = [kv, swapped(kv)]
    for k in range(1, chips):
        part = from_chip(kv, k)
        kv_parts += [part, swapped(part)]

    half = (4, HALF, WIDE + LANES)
    keep, give = call(
        local_states_kernel,
        [(half, BF16), (half, BF16)],
        [1] + [0] * 5 + [1],
        [
            pltpu.VMEM((LANES, tokens), F32),
            pltpu.VMEM((tokens, WIDE), BF16),
            pltpu.VMEM((tokens, WIDE), BF16),
            pltpu.VMEM((tokens, WIDE), BF16),
            pltpu.VMEM((4, NS, WIDE), BF16),
        ],
        4,
        "local_states",
    )(place, x, g, b, c, steps, rate_log)
    received = swapped(give)

    inner_y, inner_dx, inner_db, inner_dc, sums = call(
        inner_kernel,
        [((tokens, WIDE), F32)] * 2 + [((tokens, NS), F32)] * 2 + [((2 * HS, LANES), F32)],
        [0] * 5 + [1] * 2,
        [
            pltpu.VMEM((LANES, tokens), F32),
            pltpu.VMEM((tokens, tokens), F32),
            pltpu.VMEM((tokens, tokens), F32),
            pltpu.VMEM((tokens, tokens), BF16),
            pltpu.VMEM((LANES, 2 * tokens), F32),
        ],
        5,
        "chunk_inner",
    )(x, g, b, c, steps, rate_log, skip)

    messages = call(
        lambda *refs: combine_kernel(chips, *refs),
        [((HALF, WIDE + LANES), BF16)] * (chips - 1),
        [1, 0, 0],
        [],
        1,
        "combine_states",
    )(place, keep, received)
    arrived = [from_chip(messages[k - 1], k) for k in range(1, chips)]
    entering = ((2, HALF, WIDE), BF16)
    own, give, totals = call(
        lambda *refs: chain_kernel(chips, *refs),
        [entering, entering, ((2 * HS, LANES), F32)],
        [1] + [0] * (2 + chips),
        [],
        2,
        "chain_states",
    )(place, keep, received, sums, *arrived)
    other = swapped(give)

    totals = totals + swapped(totals)
    totals = totals + sum(from_chip(totals, k) for k in range(1, chips))
    totals = totals + sum(turned(totals, k) for k in range(1, lax.axis_size("dp")))
    totals = jnp.sum(totals, axis=1)
    tokens_all = lax.axis_size("dp") * n * tokens
    grad_rate_log = totals[:HS] / tokens_all
    grad_skip = totals[HS:] / (tokens_all * P_SIZE)

    columns = QUERY_HEADS * BLOCK
    split = ((chips, tokens, 2 * LANES), BF16)
    attention, dq, keep, give = call(
        lambda *refs: attention_kernel(chips, *refs),
        [((tokens, columns), F32), ((tokens, columns), BF16), split, split],
        [1, 1] + [0] * (3 + n),
        [
            pltpu.SMEM((blocks + 1,), jnp.int32),
            pltpu.VMEM((every, 2 * LANES), BF16),
            pltpu.VMEM(((most + 1) // 2, 2 * BLOCK, columns), F32),
            pltpu.VMEM((every, 2 * LANES), F32),
            pltpu.VMEM((columns, LANES), BF16),
            pltpu.VMEM((columns, LANES), BF16),
            pltpu.VMEM((2 * BLOCK, columns), BF16),
            pltpu.VMEM((2 * BLOCK, columns), BF16),
            pltpu.VMEM((LANES, columns), F32),
            pltpu.VMEM((LANES, columns), F32),
            pltpu.VMEM((8, columns), F32),
        ],
        10,
        "attention",
    )(block_mask[0], place, sums, q, g, *kv_parts)
    partial, *messages = call(
        lambda *refs: pair_sum_kernel(chips, *refs),
        [((tokens, 2 * LANES), F32)] + [((tokens, 2 * LANES), BF16)] * (chips - 1),
        [1, 0, 0],
        [],
        1,
        "pair_sum",
    )(place, keep, swapped(give))
    owned = [partial] + [from_chip(messages[k - 1], k) for k in range(1, chips)]

    y, dx, db, dc = call(
        outer_kernel,
        [((tokens, WIDE), BF16)] * 2 + [((tokens, NS), BF16)] * 2,
        [1] + [0] * 5 + [1] + [0] * 7,
        [
            pltpu.VMEM((LANES, tokens), F32),
            pltpu.VMEM((tokens, WIDE), BF16),
            pltpu.VMEM((tokens, WIDE), BF16),
            pltpu.VMEM((2, NS, WIDE), BF16),
        ],
        3,
        "chunk_outer",
    )(place, x, g, b, c, steps, rate_log, own, other, attention, inner_y, inner_dx, inner_db, inner_dc)

    dk, dv = call(
        owner_sum_kernel, [((tokens, LANES), BF16)] * 2, [0] * chips, [], 1, "owner_sum"
    )(*owned)
    return (
        y[None],
        dq[None],
        dk[None],
        dv[None],
        dx[None],
        db[None],
        dc[None],
        grad_rate_log,
        grad_skip,
    )


def solution(mesh):
    split = P("dp", "seq", None)
    in_specs = (split,) * 7 + (P(), P(), P("dp", None, None), split)
    out_specs = (split,) * 7 + (P(), P())
    return jax.shard_map(body, mesh=mesh, in_specs=in_specs, out_specs=out_specs, check_vma=False)
```

time: 89.4 us -> 79.5 us (0.89)
  the two profiles are of different devices: /device:TPU:2 before, /device:TPU:0 now
where the time goes in v3:
time: 79.5 us; the launch traced here: 80.1 us
  Pallas kernels  32.7 us (41%)
  starting transfers between devices  27.9 us (35%)
  waiting for transfers between devices  11.5 us (14%)
  local copies, waits for them, and re-layouts  5.09 us (6%)
  other arithmetic  2.05 us (3%)
  between operations  0.8 us (1%)
    ppermute x12, starting transfers between devices, from_chip(): return lax.ppermute(array, 'seq', [(i, (i + 2 * k) % n) for i in range(n)])  17.6 us
    ppermute x12, waiting for transfers between devices, from_chip(): return lax.ppermute(array, 'seq', [(i, (i + 2 * k) % n) for i in range(n)])  9.09 us
    ppermute x3, starting transfers between devices, turned(): return lax.ppermute(array, 'dp', [(i, (i + k) % n) for i in range(n)])  8.85 us
    pallas_call x1, Pallas kernels, body(): call(lambda *refs: attention_kernel(chips, *refs), [((tokens, columns), F...  8.54 us
    unnamed x34, local copies, waits for them, and re-layouts  5.09 us
    pallas_call x1, Pallas kernels, body(): call(inner_kernel, [((tokens, WIDE), F32)] * 2 + [((tokens, NS), F32)] *...  4.62 us
    pallas_call x1, Pallas kernels, body(): call(outer_kernel, [((tokens, WIDE), BF16)] * 2 + [((tokens, NS), BF16)]...  4.58 us
    pallas_call x1, Pallas kernels, body(): call(local_states_kernel, [(half, BF16), (half, BF16)], [1] + [0] * 5 + [...  4.44 us
  transfers between devices with their start and end apart: 23, of which 8 were waited for; matrix products, arithmetic and copies ran while one was open for 3% of the time, Pallas kernels for 33%

profile of v3, /device:TPU:0, one launch (start us, length us, event | category | flops | bytes accessed | tf_op | source)
XLA Modules:
  0.0 80.1 jit_solution(14244481365204442634)
XLA Ops:
  0.6 1.6 %pack_kv.1.refs_5_ = bf16[256,256]{1,0:T(8,128)(2,1)} custom-call(bf16[256,128]{1,0:T(8,128)(2,1)} %bitcast.28, bf16[256,128]{1,0:T(8,128)(2,1)} %bitcast.29), custom_call_target="tpu_custom_call" | custom-call | flops 1100000000 | bytes 1048576 | tf_op jit(solution)/shard_map/pack_kv/pallas_call | solution.py:443
  2.2 3.9 %collective-permute-start.10 = (bf16[256,256]{1,0:T(8,128)(2,1)}, bf16[256,256]{1,0:T(8,128)(2,1)S(1)}, u32[]{:S(2)}, u32[]{:S(2)}) collective-permute-start(bf16[256,256]{1,0:T(8,128)(2,1)} %pack_kv.1.refs_5_), channel_id=1, source_target_pairs={{0,6},{1,7},{2,0},{3,1},{4,2},{5,3},{6,4},{7,5},{8,14},{9,15},{10,... | collective-permute-start | bytes 393224 | tf_op jit(solution)/shard_map/ppermute | solution.py:410
  6.1 1.1 %collective-permute-start.8 = (bf16[256,256]{1,0:T(8,128)(2,1)}, bf16[256,256]{1,0:T(8,128)(2,1)S(1)}, u32[]{:S(2)}, u32[]{:S(2)}) collective-permute-start(bf16[256,256]{1,0:T(8,128)(2,1)} %pack_kv.1.refs_5_), channel_id=1, source_target_pairs={{0,4},{1,5},{2,6},{3,7},{4,0},{5,1},{6,2},{7,3},{8,12},{9,13},{10,... | collective-permute-start | bytes 393224 | tf_op jit(solution)/shard_map/ppermute | solution.py:410
  7.9 4.4 %local_states.1 = (bf16[4,64,1152]{2,1,0:T(8,128)(2,1)}, bf16[4,64,1152]{2,1,0:T(8,128)(2,1)}) custom-call(s32[2]{0:T(128)} %pad_add_fusion.place_ref.refs_0_.refs_1_, bf16[256,1024]{1,0:T(8,128)(2,1)} %bitcast.21, bf16[256,1024]{1,0:T(8,128)(2,1)} %bitcast.24, bf16[256,128]{1,0:T(8,128)(2,1)} %bitcast.30, bf16[256,128]{1,0:T(8,128)(2,1)} %bitcast.33, ...), custom_call_target="tpu_custom_call" | custom-call | flops 4400000000 | bytes 1048576 | tf_op jit(solution)/shard_map/local_states/pallas_call | solution.py:450
  14.1 4.6 %chunk_inner.1 = (f32[256,1024]{1,0:T(8,128)}, f32[256,1024]{1,0:T(8,128)}, f32[256,128]{1,0:T(8,128)}, f32[256,128]{1,0:T(8,128)}, f32[16,128]{1,0:T(8,128)}) custom-call(bf16[256,1024]{1,0:T(8,128)(2,1)} %bitcast.22, bf16[256,1024]{1,0:T(8,128)(2,1)} %bitcast.25, bf16[256,128]{1,0:T(8,128)(2,1)} %bitcast.31, bf16[256,128]{1,0:T(8,128)(2,1)} %bitcast.34, ...), custom_call_target="tpu_custom_call" | custom-call | flops 5500000256 | bytes 1048576 | tf_op jit(solution)/shard_map/chunk_inner/pallas_call | solution.py:466
  19.6 2.3 %combine_states.1 = (bf16[64,1152]{1,0:T(8,128)(2,1)}, bf16[64,1152]{1,0:T(8,128)(2,1)}, bf16[64,1152]{1,0:T(8,128)(2,1)}) custom-call(s32[2]{0:T(128)} %pad_add_fusion.place_ref.refs_0_.refs_1_, bf16[4,64,1152]{2,1,0:T(8,128)(2,1)} %get-tuple-element.36.refs_1_, bf16[4,64,1152]{2,1,0:T(8,128)(2,1)} %copy-done), custom_call_target="tpu_custom_call" | custom-call | flops 1100000000 | bytes 1048576 | tf_op jit(solution)/shard_map/combine_states/pallas_call | solution.py:481
  21.8 1.7 %collective-permute-start.1 = (bf16[64,1152]{1,0:T(8,128)(2,1)}, bf16[64,1152]{1,0:T(8,128)(2,1)S(1)}, u32[]{:S(2)}, u32[]{:S(2)}) collective-permute-start(bf16[64,1152]{1,0:T(8,128)(2,1)} %get-tuple-element.39), channel_id=1, source_target_pairs={{0,2},{1,3},{2,4},{3,5},{4,6},{5,7},{6,0},{7,1},{8,10},{9,11},{10,... | collective-permute-start | bytes 442376 | tf_op jit(solution)/shard_map/ppermute | solution.py:410
  24.0 1.6 %collective-permute-start.3 = (bf16[64,1152]{1,0:T(8,128)(2,1)}, bf16[64,1152]{1,0:T(8,128)(2,1)S(1)}, u32[]{:S(2)}, u32[]{:S(2)}) collective-permute-start(bf16[64,1152]{1,0:T(8,128)(2,1)} %get-tuple-element.41), channel_id=1, source_target_pairs={{0,6},{1,7},{2,0},{3,1},{4,2},{5,3},{6,4},{7,5},{8,14},{9,15},{10,... | collective-permute-start | bytes 442376 | tf_op jit(solution)/shard_map/ppermute | solution.py:410
  26.3 8.5 %attention.1 = (f32[256,1024]{1,0:T(8,128)}, bf16[256,1024]{1,0:T(8,128)(2,1)}, bf16[4,256,256]{2,1,0:T(8,128)(2,1)}, bf16[4,256,256]{2,1,0:T(8,128)(2,1)}) custom-call(s32[16,16]{1,0:T(8,128)} %bitcast.36, s32[2]{0:T(128)} %pad_add_fusion.place_ref.refs_0_.refs_1_, f32[16,128]{1,0:T(8,128)} %get-tuple-element.38.refs_3_.refs_2_, ...), custom_call_target="tpu_custom_call" | custom-call | flops 11000000512 | bytes 1048576 | tf_op jit(solution)/shard_map/attention/pallas_call | solution.py:511
  36.2 2.8 %chain_states.1 = (bf16[2,64,1024]{2,1,0:T(8,128)(2,1)}, bf16[2,64,1024]{2,1,0:T(8,128)(2,1)}, f32[16,128]{1,0:T(8,128)}) custom-call(s32[2]{0:T(128)} %pad_add_fusion.place_ref.refs_0_.refs_1_, bf16[4,64,1152]{2,1,0:T(8,128)(2,1)} %get-tuple-element.36.refs_1_, bf16[4,64,1152]{2,1,0:T(8,128)(2,1)} %copy-done, f32[16,128]{1,0:T(8,128)} %get-tuple-element.38.refs_3_.refs_2_, ...), custom_call_target="tpu_custom_call" | custom-call | flops 2200000000 | bytes 1048576 | tf_op jit(solution)/shard_map/chain_states/pallas_call | solution.py:491
  39.5 1.0 %collective-permute-done.16 = f32[16,128]{1,0:T(8,128)S(1)} collective-permute-done((f32[16,128]{1,0:T(8,128)}, f32[16,128]{1,0:T(8,128)S(1)}, u32[]{:S(2)}, u32[]{:S(2)}) %collective-permute-start.16) | collective-permute-done | bytes 8224 | tf_op jit(solution)/shard_map/ppermute | solution.py:405
  41.7 5.4 %collective-permute-start.18 = (f32[16,128]{1,0:T(8,128)S(1)}, f32[16,128]{1,0:T(8,128)S(1)}, u32[]{:S(2)}, u32[]{:S(2)}) collective-permute-start(f32[16,128]{1,0:T(8,128)S(1)} %add.27), channel_id=1, source_target_pairs={{0,4},{1,5},{2,6},{3,7},{4,0},{5,1},{6,2},{7,3},{8,12},{9,13},{10,... | collective-permute-start | bytes 24584 | tf_op jit(solution)/shard_map/ppermute | solution.py:410
  47.1 1.1 %collective-permute-done.17 = f32[16,128]{1,0:T(8,128)S(1)} collective-permute-done((f32[16,128]{1,0:T(8,128)S(1)}, f32[16,128]{1,0:T(8,128)S(1)}, u32[]{:S(2)}, u32[]{:S(2)}) %collective-permute-start.17) | collective-permute-done | bytes 8224 | tf_op jit(solution)/shard_map/ppermute | solution.py:410
  48.8 2.0 %collective-permute-done.19 = f32[16,128]{1,0:T(8,128)S(1)} collective-permute-done((f32[16,128]{1,0:T(8,128)S(1)}, f32[16,128]{1,0:T(8,128)S(1)}, u32[]{:S(2)}, u32[]{:S(2)}) %collective-permute-start.19) | collective-permute-done | bytes 8224 | tf_op jit(solution)/shard_map/ppermute | solution.py:410
  50.8 3.0 %collective-permute-start.20 = (f32[16,128]{1,0:T(8,128)S(1)}, f32[16,128]{1,0:T(8,128)S(1)}, u32[]{:S(2)}, u32[]{:S(2)}) collective-permute-start(f32[16,128]{1,0:T(8,128)S(1)} %add_add_fusion), channel_id=1, source_target_pairs={{0,8},{8,16},{16,24},{24,0},{1,9},{9,17},{17,25},{25,1},{2,10},{10... | collective-permute-start | bytes 24584 | tf_op jit(solution)/shard_map/ppermute | solution.py:415
  53.7 3.0 %collective-permute-start.21 = (f32[16,128]{1,0:T(8,128)S(1)}, f32[16,128]{1,0:T(8,128)S(1)}, u32[]{:S(2)}, u32[]{:S(2)}) collective-permute-start(f32[16,128]{1,0:T(8,128)S(1)} %add_add_fusion), channel_id=1, source_target_pairs={{0,16},{8,24},{16,0},{24,8},{1,17},{9,25},{17,1},{25,9},{2,18},{10... | collective-permute-start | bytes 24584 | tf_op jit(solution)/shard_map/ppermute | solution.py:415
  56.8 2.9 %collective-permute-start.22 = (f32[16,128]{1,0:T(8,128)S(1)}, f32[16,128]{1,0:T(8,128)S(1)}, u32[]{:S(2)}, u32[]{:S(2)}) collective-permute-start(f32[16,128]{1,0:T(8,128)S(1)} %add_add_fusion), channel_id=1, source_target_pairs={{0,24},{8,0},{16,8},{24,16},{1,25},{9,1},{17,9},{25,17},{2,26},{10... | collective-permute-start | bytes 24584 | tf_op jit(solution)/shard_map/ppermute | solution.py:415
  59.6 1.4 %collective-permute-done.22 = f32[16,128]{1,0:T(8,128)S(1)} collective-permute-done((f32[16,128]{1,0:T(8,128)S(1)}, f32[16,128]{1,0:T(8,128)S(1)}, u32[]{:S(2)}, u32[]{:S(2)}) %collective-permute-start.22) | collective-permute-done | bytes 8224 | tf_op jit(solution)/shard_map/ppermute | solution.py:415
  61.9 2.1 %pair_sum.1 = (f32[256,256]{1,0:T(8,128)}, bf16[256,256]{1,0:T(8,128)(2,1)}, bf16[256,256]{1,0:T(8,128)(2,1)}, bf16[256,256]{1,0:T(8,128)(2,1)}) custom-call(s32[2]{0:T(128)} %pad_add_fusion.place_ref.refs_0_.refs_1_, bf16[4,256,256]{2,1,0:T(8,128)(2,1)} %get-tuple-element.51.refs_1_, bf16[4,256,256]{2,1,0:T(8,128)(2,1)} %copy-done.1), custom_call_target="tpu_custom_call" | custom-call | flops 1100000000 | bytes 1048576 | tf_op jit(solution)/shard_map/pair_sum/pallas_call | solution.py:531
  65.5 1.5 %collective-permute-start.15 = (bf16[256,256]{1,0:T(8,128)(2,1)}, bf16[256,256]{1,0:T(8,128)(2,1)S(1)}, u32[]{:S(2)}, u32[]{:S(2)}) collective-permute-start(bf16[256,256]{1,0:T(8,128)(2,1)} %get-tuple-element.56), channel_id=1, source_target_pairs={{0,6},{1,7},{2,0},{3,1},{4,2},{5,3},{6,4},{7,5},{8,14},{9,15},{10,... | collective-permute-start | bytes 393224 | tf_op jit(solution)/shard_map/ppermute | solution.py:410
  67.6 3.6 %collective-permute-done.13.refs_1_ = bf16[256,256]{1,0:T(8,128)(2,1)S(1)} collective-permute-done((bf16[256,256]{1,0:T(8,128)(2,1)}, bf16[256,256]{1,0:T(8,128)(2,1)S(1)}, u32[]{:S(2)}, u32[]{:S(2)}) %collective-permute-start.13) | collective-permute-done | bytes 131104 | tf_op jit(solution)/shard_map/ppermute | solution.py:410
  71.2 1.0 %collective-permute-done.14.refs_2_ = bf16[256,256]{1,0:T(8,128)(2,1)S(1)} collective-permute-done((bf16[256,256]{1,0:T(8,128)(2,1)}, bf16[256,256]{1,0:T(8,128)(2,1)S(1)}, u32[]{:S(2)}, u32[]{:S(2)}) %collective-permute-start.14) | collective-permute-done | bytes 131104 | tf_op jit(solution)/shard_map/ppermute | solution.py:410
  73.0 1.8 %owner_sum.1 = (bf16[256,128]{1,0:T(8,128)(2,1)}, bf16[256,128]{1,0:T(8,128)(2,1)}) custom-call(f32[256,256]{1,0:T(8,128)} %get-tuple-element.53.refs_0_, bf16[256,256]{1,0:T(8,128)(2,1)} %copy-done.14, bf16[256,256]{1,0:T(8,128)(2,1)} %copy-done.15, bf16[256,256]{1,0:T(8,128)(2,1)} %copy-done.16), custom_call_target="tpu_custom_call" | custom-call | flops 1100000000 | bytes 1048576 | tf_op jit(solution)/shard_map/owner_sum/pallas_call | solution.py:555
  75.5 4.6 %chunk_outer.1 = (bf16[256,1024]{1,0:T(8,128)(2,1)}, bf16[256,1024]{1,0:T(8,128)(2,1)}, bf16[256,128]{1,0:T(8,128)(2,1)}, bf16[256,128]{1,0:T(8,128)(2,1)}) custom-call(s32[2]{0:T(128)} %pad_add_fusion.place_ref.refs_0_.refs_1_, bf16[256,1024]{1,0:T(8,128)(2,1)} %bitcast.23, bf16[256,1024]{1,0:T(8,128)(2,1)} %bitcast.27, bf16[256,128]{1,0:T(8,128)(2,1)} %bitcast.32, ...), custom_call_target="tpu_custom_call" | custom-call | flops 3300000000 | bytes 1048576 | tf_op jit(solution)/shard_map/chunk_outer/pallas_call | solution.py:541
  (70 shorter events, 12.4 us)
Async XLA Ops:
  2.2 10.6 %collective-permute-start.10 = (bf16[256,256]{1,0:T(8,128)(2,1)}, bf16[256,256]{1,0:T(8,128)(2,1)S(1)}, u32[]{:S(2)}, u32[]{:S(2)}) collective-permute-start(bf16[256,256]{1,0:T(8,128)(2,1)} %pack_kv.1.refs_5_), channel_id=1, source_target_pairs={{0,6},{1,7},{2,0},{3,1},{4,2},{5,3},{6,4},{7,5},{8,14},{9,15},{10,... | collective-permute-start | bytes 393224 | tf_op jit(solution)/shard_map/ppermute | solution.py:410
  6.1 6.8 %collective-permute-start.6 = (bf16[256,256]{1,0:T(8,128)(2,1)}, bf16[256,256]{1,0:T(8,128)(2,1)S(1)}, u32[]{:S(2)}, u32[]{:S(2)}) collective-permute-start(bf16[256,256]{1,0:T(8,128)(2,1)} %pack_kv.1.refs_5_), channel_id=1, source_target_pairs={{0,2},{1,3},{2,4},{3,5},{4,6},{5,7},{6,0},{7,1},{8,10},{9,11},{10,... | collective-permute-start | bytes 393224 | tf_op jit(solution)/shard_map/ppermute | solution.py:410
  6.1 8.0 %collective-permute-start.8 = (bf16[256,256]{1,0:T(8,128)(2,1)}, bf16[256,256]{1,0:T(8,128)(2,1)S(1)}, u32[]{:S(2)}, u32[]{:S(2)}) collective-permute-start(bf16[256,256]{1,0:T(8,128)(2,1)} %pack_kv.1.refs_5_), channel_id=1, source_target_pairs={{0,4},{1,5},{2,6},{3,7},{4,0},{5,1},{6,2},{7,3},{8,12},{9,13},{10,... | collective-permute-start | bytes 393224 | tf_op jit(solution)/shard_map/ppermute | solution.py:410
  12.3 6.4 %collective-permute-start = (bf16[4,64,1152]{2,1,0:T(8,128)(2,1)}, bf16[4,64,1152]{2,1,0:T(8,128)(2,1)S(1)}, u32[]{:S(2)}, u32[]{:S(2)}) collective-permute-start(bf16[4,64,1152]{2,1,0:T(8,128)(2,1)} %get-tuple-element.37), channel_id=1, source_target_pairs={{0,1},{1,0},{2,3},{3,2},{4,5},{5,4},{6,7},{7,6},{8,9},{9,8},{10,11... | collective-permute-start | bytes 1769480 | tf_op jit(solution)/shard_map/ppermute | solution.py:405
  12.3 11.2 %collective-permute-start.5 = (bf16[256,256]{1,0:T(8,128)(2,1)S(1)}, bf16[256,256]{1,0:T(8,128)(2,1)S(1)}, u32[]{:S(2)}, u32[]{:S(2)}) collective-permute-start(bf16[256,256]{1,0:T(8,128)(2,1)S(1)} %copy-done.6), channel_id=1, source_target_pairs={{0,1},{1,0},{2,3},{3,2},{4,5},{5,4},{6,7},{7,6},{8,9},{9,8},{10,11... | collective-permute-start | bytes 393224 | tf_op jit(solution)/shard_map/ppermute | solution.py:405
  12.8 5.9 %copy-start.7 = (bf16[256,256]{1,0:T(8,128)(2,1)}, bf16[256,256]{1,0:T(8,128)(2,1)S(1)}, u32[]{:S(2)}) copy-start(bf16[256,256]{1,0:T(8,128)(2,1)S(1)} %collective-permute-done.10.refs_11_) | copy-start | bytes 393220
  12.8 11.2 %collective-permute-start.11 = (bf16[256,256]{1,0:T(8,128)(2,1)S(1)}, bf16[256,256]{1,0:T(8,128)(2,1)S(1)}, u32[]{:S(2)}, u32[]{:S(2)}) collective-permute-start(bf16[256,256]{1,0:T(8,128)(2,1)S(1)} %collective-permute-done.10.refs_11_), channel_id=1, source_target_pairs={{0,1},{1,0},{2,3},{3,2},{4,5},{5,4},{6,7},{7,6},{8,9},{9,8},{10,11... | collective-permute-start | bytes 393224 | tf_op jit(solution)/shard_map/ppermute | solution.py:405
  12.9 12.7 %collective-permute-start.7 = (bf16[256,256]{1,0:T(8,128)(2,1)S(1)}, bf16[256,256]{1,0:T(8,128)(2,1)S(1)}, u32[]{:S(2)}, u32[]{:S(2)}) collective-permute-start(bf16[256,256]{1,0:T(8,128)(2,1)S(1)} %collective-permute-done.6.refs_7_), channel_id=1, source_target_pairs={{0,1},{1,0},{2,3},{3,2},{4,5},{5,4},{6,7},{7,6},{8,9},{9,8},{10,11... | collective-permute-start | bytes 393224 | tf_op jit(solution)/shard_map/ppermute | solution.py:405
  14.1 11.5 %collective-permute-start.9 = (bf16[256,256]{1,0:T(8,128)(2,1)S(1)}, bf16[256,256]{1,0:T(8,128)(2,1)S(1)}, u32[]{:S(2)}, u32[]{:S(2)}) collective-permute-start(bf16[256,256]{1,0:T(8,128)(2,1)S(1)} %collective-permute-done.8.refs_9_), channel_id=1, source_target_pairs={{0,1},{1,0},{2,3},{3,2},{4,5},{5,4},{6,7},{7,6},{8,9},{9,8},{10,11... | collective-permute-start | bytes 393224 | tf_op jit(solution)/shard_map/ppermute | solution.py:405
  21.8 13.0 %collective-permute-start.1 = (bf16[64,1152]{1,0:T(8,128)(2,1)}, bf16[64,1152]{1,0:T(8,128)(2,1)S(1)}, u32[]{:S(2)}, u32[]{:S(2)}) collective-permute-start(bf16[64,1152]{1,0:T(8,128)(2,1)} %get-tuple-element.39), channel_id=1, source_target_pairs={{0,2},{1,3},{2,4},{3,5},{4,6},{5,7},{6,0},{7,1},{8,10},{9,11},{10,... | collective-permute-start | bytes 442376 | tf_op jit(solution)/shard_map/ppermute | solution.py:410
  23.5 11.3 %collective-permute-start.2 = (bf16[64,1152]{1,0:T(8,128)(2,1)}, bf16[64,1152]{1,0:T(8,128)(2,1)S(1)}, u32[]{:S(2)}, u32[]{:S(2)}) collective-permute-start(bf16[64,1152]{1,0:T(8,128)(2,1)} %get-tuple-element.40), channel_id=1, source_target_pairs={{0,4},{1,5},{2,6},{3,7},{4,0},{5,1},{6,2},{7,3},{8,12},{9,13},{10,... | collective-permute-start | bytes 442376 | tf_op jit(solution)/shard_map/ppermute | solution.py:410
  24.0 10.9 %collective-permute-start.3 = (bf16[64,1152]{1,0:T(8,128)(2,1)}, bf16[64,1152]{1,0:T(8,128)(2,1)S(1)}, u32[]{:S(2)}, u32[]{:S(2)}) collective-permute-start(bf16[64,1152]{1,0:T(8,128)(2,1)} %get-tuple-element.41), channel_id=1, source_target_pairs={{0,6},{1,7},{2,0},{3,1},{4,2},{5,3},{6,4},{7,5},{8,14},{9,15},{10,... | collective-permute-start | bytes 442376 | tf_op jit(solution)/shard_map/ppermute | solution.py:410
  34.8 26.3 %collective-permute-start.12 = (bf16[4,256,256]{2,1,0:T(8,128)(2,1)}, bf16[4,256,256]{2,1,0:T(8,128)(2,1)S(1)}, u32[]{:S(2)}, u32[]{:S(2)}) collective-permute-start(bf16[4,256,256]{2,1,0:T(8,128)(2,1)} %get-tuple-element.52), channel_id=1, source_target_pairs={{0,1},{1,0},{2,3},{3,2},{4,5},{5,4},{6,7},{7,6},{8,9},{9,8},{10,11... | collective-permute-start | bytes 1572872 | tf_op jit(solution)/shard_map/ppermute | solution.py:405
  39.0 1.5 %collective-permute-start.16 = (f32[16,128]{1,0:T(8,128)}, f32[16,128]{1,0:T(8,128)S(1)}, u32[]{:S(2)}, u32[]{:S(2)}) collective-permute-start(f32[16,128]{1,0:T(8,128)} %get-tuple-element.62), channel_id=1, source_target_pairs={{0,1},{1,0},{2,3},{3,2},{4,5},{5,4},{6,7},{7,6},{8,9},{9,8},{10,11... | collective-permute-start | bytes 24584 | tf_op jit(solution)/shard_map/ppermute | solution.py:405
  41.2 7.0 %collective-permute-start.17 = (f32[16,128]{1,0:T(8,128)S(1)}, f32[16,128]{1,0:T(8,128)S(1)}, u32[]{:S(2)}, u32[]{:S(2)}) collective-permute-start(f32[16,128]{1,0:T(8,128)S(1)} %add.27), channel_id=1, source_target_pairs={{0,2},{1,3},{2,4},{3,5},{4,6},{5,7},{6,0},{7,1},{8,10},{9,11},{10,... | collective-permute-start | bytes 24584 | tf_op jit(solution)/shard_map/ppermute | solution.py:410
  41.7 7.1 %collective-permute-start.18 = (f32[16,128]{1,0:T(8,128)S(1)}, f32[16,128]{1,0:T(8,128)S(1)}, u32[]{:S(2)}, u32[]{:S(2)}) collective-permute-start(f32[16,128]{1,0:T(8,128)S(1)} %add.27), channel_id=1, source_target_pairs={{0,4},{1,5},{2,6},{3,7},{4,0},{5,1},{6,2},{7,3},{8,12},{9,13},{10,... | collective-permute-start | bytes 24584 | tf_op jit(solution)/shard_map/ppermute | solution.py:410
  47.1 3.7 %collective-permute-start.19 = (f32[16,128]{1,0:T(8,128)S(1)}, f32[16,128]{1,0:T(8,128)S(1)}, u32[]{:S(2)}, u32[]{:S(2)}) collective-permute-start(f32[16,128]{1,0:T(8,128)S(1)} %add.27), channel_id=1, source_target_pairs={{0,6},{1,7},{2,0},{3,1},{4,2},{5,3},{6,4},{7,5},{8,14},{9,15},{10,... | collective-permute-start | bytes 24584 | tf_op jit(solution)/shard_map/ppermute | solution.py:410
  50.8 8.9 %collective-permute-start.20 = (f32[16,128]{1,0:T(8,128)S(1)}, f32[16,128]{1,0:T(8,128)S(1)}, u32[]{:S(2)}, u32[]{:S(2)}) collective-permute-start(f32[16,128]{1,0:T(8,128)S(1)} %add_add_fusion), channel_id=1, source_target_pairs={{0,8},{8,16},{16,24},{24,0},{1,9},{9,17},{17,25},{25,1},{2,10},{10... | collective-permute-start | bytes 24584 | tf_op jit(solution)/shard_map/ppermute | solution.py:415
  53.7 5.9 %collective-permute-start.21 = (f32[16,128]{1,0:T(8,128)S(1)}, f32[16,128]{1,0:T(8,128)S(1)}, u32[]{:S(2)}, u32[]{:S(2)}) collective-permute-start(f32[16,128]{1,0:T(8,128)S(1)} %add_add_fusion), channel_id=1, source_target_pairs={{0,16},{8,24},{16,0},{24,8},{1,17},{9,25},{17,1},{25,9},{2,18},{10... | collective-permute-start | bytes 24584 | tf_op jit(solution)/shard_map/ppermute | solution.py:415
  56.8 4.2 %collective-permute-start.22 = (f32[16,128]{1,0:T(8,128)S(1)}, f32[16,128]{1,0:T(8,128)S(1)}, u32[]{:S(2)}, u32[]{:S(2)}) collective-permute-start(f32[16,128]{1,0:T(8,128)S(1)} %add_add_fusion), channel_id=1, source_target_pairs={{0,24},{8,0},{16,8},{24,16},{1,25},{9,1},{17,9},{25,17},{2,26},{10... | collective-permute-start | bytes 24584 | tf_op jit(solution)/shard_map/ppermute | solution.py:415
  59.6 15.1 %collective-permute-start.4 = (bf16[2,64,1024]{2,1,0:T(8,128)(2,1)}, bf16[2,64,1024]{2,1,0:T(8,128)(2,1)S(1)}, u32[]{:S(2)}, u32[]{:S(2)}) collective-permute-start(bf16[2,64,1024]{2,1,0:T(8,128)(2,1)} %get-tuple-element.43), channel_id=1, source_target_pairs={{0,1},{1,0},{2,3},{3,2},{4,5},{5,4},{6,7},{7,6},{8,9},{9,8},{10,11... | collective-permute-start | bytes 786440 | tf_op jit(solution)/shard_map/ppermute | solution.py:405
  64.0 7.2 %collective-permute-start.13 = (bf16[256,256]{1,0:T(8,128)(2,1)}, bf16[256,256]{1,0:T(8,128)(2,1)S(1)}, u32[]{:S(2)}, u32[]{:S(2)}) collective-permute-start(bf16[256,256]{1,0:T(8,128)(2,1)} %get-tuple-element.54), channel_id=1, source_target_pairs={{0,2},{1,3},{2,4},{3,5},{4,6},{5,7},{6,0},{7,1},{8,10},{9,11},{10,... | collective-permute-start | bytes 393224 | tf_op jit(solution)/shard_map/ppermute | solution.py:410
  64.9 7.3 %collective-permute-start.14 = (bf16[256,256]{1,0:T(8,128)(2,1)}, bf16[256,256]{1,0:T(8,128)(2,1)S(1)}, u32[]{:S(2)}, u32[]{:S(2)}) collective-permute-start(bf16[256,256]{1,0:T(8,128)(2,1)} %get-tuple-element.55), channel_id=1, source_target_pairs={{0,4},{1,5},{2,6},{3,7},{4,0},{5,1},{6,2},{7,3},{8,12},{9,13},{10,... | collective-permute-start | bytes 393224 | tf_op jit(solution)/shard_map/ppermute | solution.py:410
  65.5 6.7 %collective-permute-start.15 = (bf16[256,256]{1,0:T(8,128)(2,1)}, bf16[256,256]{1,0:T(8,128)(2,1)S(1)}, u32[]{:S(2)}, u32[]{:S(2)}) collective-permute-start(bf16[256,256]{1,0:T(8,128)(2,1)} %get-tuple-element.56), channel_id=1, source_target_pairs={{0,6},{1,7},{2,0},{3,1},{4,2},{5,3},{6,4},{7,5},{8,14},{9,15},{10,... | collective-permute-start | bytes 393224 | tf_op jit(solution)/shard_map/ppermute | solution.py:410
  (16 other events, 26.7 us)

commit v4 on v3

v4 whole, which is shorter than its diff:
```python
import jax
import jax.numpy as jnp
from jax import lax
from jax.experimental import pallas as pl
from jax.experimental.pallas import tpu as pltpu
from jax.sharding import PartitionSpec as P

HEAD_WIDTH = 128
QUERY_HEADS = 8
HS = 8
P_SIZE = 128
NS = 128
BLOCK = 128
WIDE = HS * P_SIZE
LANES = 128
FACTOR = HEAD_WIDTH ** (-0.5)
LOG2E = 1.4426950408889634
NEG = -1e30
HALF = NS // 2
HIGH = lax.Precision.HIGHEST
F32 = jnp.float32
BF16 = jnp.bfloat16

VMEM = pl.BlockSpec(memory_space=pltpu.VMEM)
SMEM = pl.BlockSpec(memory_space=pltpu.SMEM)
AFTER = pl.BlockSpec(memory_space=pl.ANY)


def params(limit=56 << 20):
    return pltpu.CompilerParams(vmem_limit_bytes=limit)


def cost(microseconds):
    return pl.CostEstimate(
        flops=int(microseconds * 1.1e9), bytes_accessed=1 << 20, transcendentals=0
    )


def dot(a, b, ca, cb, precision=None):
    return lax.dot_general(
        a, b, (((ca,), (cb,)), ((), ())), preferred_element_type=F32, precision=precision
    )


def head(h):
    return slice(h * LANES, (h + 1) * LANES)


def running_logs(step_ref, rate_ref, pad_ref):
    pad_ref[...] = jnp.zeros_like(pad_ref)
    for h in range(HS):
        rate = jnp.exp(jnp.full((1, 2 * BLOCK), rate_ref[h], F32))
        pad_ref[h : h + 1, :] = -step_ref[h : h + 1, :] * rate
    row = lax.broadcasted_iota(jnp.int32, (BLOCK, BLOCK), 0)
    col = lax.broadcasted_iota(jnp.int32, (BLOCK, BLOCK), 1)
    upper = jnp.where(row <= col, 1.0, 0.0).astype(F32)
    flat0 = dot(pad_ref[:, :BLOCK], upper, 1, 0, HIGH)
    flat1 = dot(pad_ref[:, BLOCK:], upper, 1, 0, HIGH)
    return flat0, flat1, flat0.T, flat1.T


def scaled(x_ref, column, out_ref):
    for h in range(HS):
        out_ref[:, head(h)] = (x_ref[:, head(h)].astype(F32) * column[:, h : h + 1]).astype(BF16)


def chip_and_core():
    me = lax.axis_index("seq")
    return me // 2, me % 2


def pack_kernel(key_ref, value_ref, out_ref):
    out_ref[:, :LANES] = key_ref[...]
    out_ref[:, LANES:] = value_ref[...]


def enter_and_tail(run0, run1):
    t0, t1 = run0[BLOCK - 1 :, :], run1[BLOCK - 1 :, :]
    enter = jnp.concatenate([run0, run1 + t0], axis=0)
    tail = jnp.concatenate([(t0 - run0) + t1, t1 - run1], axis=0)
    return enter, tail, t0 + t1


def local_states_kernel(
    x_ref, g_ref, b_ref, c_ref, step_ref, rate_ref, keep_ref, give_ref,
    pad_ref, high_ref, rest_ref, log_ref, state_ref,
):
    _, core = chip_and_core()
    _, _, run0, run1 = running_logs(step_ref, rate_ref, pad_ref)
    enter_log, tail_log, total = enter_and_tail(run0, run1)
    enter, tail = jnp.exp(enter_log), jnp.exp(tail_log)
    logs = jnp.broadcast_to(total, (HALF, LANES))
    mine = pl.ds(pl.multiple_of(core * HALF, HALF), HALF)
    other = pl.ds(pl.multiple_of((1 - core) * HALF, HALF), HALF)
    cases = ((b_ref, x_ref, tail, tail_log), (c_ref, g_ref, enter, enter_log))
    for direction, (left, right, factor, weight) in enumerate(cases):
        for h in range(HS):
            product = right[:, head(h)].astype(F32) * factor[:, h : h + 1]
            rounded = product.astype(BF16)
            high_ref[:, head(h)] = rounded
            rest_ref[:, head(h)] = (product - rounded.astype(F32)).astype(BF16)
            log_ref[:, head(h)] = (product * weight[:, h : h + 1]).astype(BF16)
        turned_left = left[...].astype(F32).T.astype(BF16)
        state_ref[direction] = dot(turned_left, high_ref[...], 1, 0) + dot(
            turned_left, rest_ref[...], 1, 0
        )
        state_ref[3 - direction] = dot(turned_left, log_ref[...], 1, 0)
    for kind in range(4):
        keep_ref[kind, :, :WIDE] = state_ref[kind, mine, :]
        keep_ref[kind, :, WIDE:] = logs
        give_ref[kind, :, :WIDE] = state_ref[kind, other, :]
        give_ref[kind, :, WIDE:] = logs


def three_parts(value, rows):
    high = value.astype(BF16).astype(F32)
    middle = (value - high).astype(BF16).astype(F32)
    low = value - high - middle
    index = lax.broadcasted_iota(jnp.int32, (rows, LANES), 0)
    return jnp.where(index == 0, high, jnp.where(index == 1, middle, low)).astype(BF16)


def pair_logs(keep_ref, recv_ref, is0):
    mine, other = keep_ref[0, 0:1, WIDE:], recv_ref[0, 0:1, WIDE:]
    return jnp.where(is0, mine, other), jnp.where(is0, other, mine)


def combine_kernel(chips, keep_ref, recv_ref, *message_refs):
    chip, core = chip_and_core()
    is0 = core == 0
    log0, log1 = pair_logs(keep_ref, recv_ref, is0)
    logs = three_parts(log0 + log1, HALF)
    decay0, decay1 = jnp.exp(log0), jnp.exp(log1)
    for h in range(HS):
        mine, other = keep_ref[0, :, head(h)], recv_ref[0, :, head(h)]
        first, second = jnp.where(is0, mine, other), jnp.where(is0, other, mine)
        state = (first * decay1[:, h : h + 1] + second).astype(BF16)
        mine, other = keep_ref[1, :, head(h)], recv_ref[1, :, head(h)]
        first, second = jnp.where(is0, mine, other), jnp.where(is0, other, mine)
        grad = (second * decay0[:, h : h + 1] + first).astype(BF16)
        for k in range(1, chips):
            later = chip + k < chips
            message_refs[k - 1][:, head(h)] = jnp.where(later, state, grad)
    for k in range(1, chips):
        message_refs[k - 1][:, WIDE:] = logs


def chain_kernel(chips, keep_ref, recv_ref, sums_ref, *refs):
    message_refs = refs[: chips - 1]
    own_ref, give_ref, total_ref = refs[chips - 1 :]
    chip, core = chip_and_core()
    is0 = core == 0
    log0, log1 = pair_logs(keep_ref, recv_ref, is0)
    decay0, decay1 = jnp.exp(log0), jnp.exp(log1)
    weight0, weight1 = log0 * decay0, log1 * decay1
    factors = [None]
    for ref in message_refs:
        parts = ref[:16, WIDE:].astype(F32)
        factors.append(jnp.exp(parts[0:1, :] + parts[1:2, :] + parts[2:3, :]))
    total_ref[...] = sums_ref[...]
    for h in range(HS):
        column = slice(h, h + 1)
        states = [(keep_ref[kind, :, head(h)], recv_ref[kind, :, head(h)]) for kind in range(4)]
        (s0, s1), (g0, g1), (qs0, qs1), (qg0, qg1) = [
            (jnp.where(is0, mine, other), jnp.where(is0, other, mine)) for mine, other in states
        ]
        state = jnp.zeros((HALF, LANES), F32)
        for k in range(chips - 1, 0, -1):
            new = state * factors[k][:, column] + message_refs[k - 1][:, head(h)].astype(F32)
            state = jnp.where(k <= chip, new, state)
        grad = jnp.zeros((HALF, LANES), F32)
        for k in range(1, chips):
            new = grad * factors[k][:, column] + message_refs[k - 1][:, head(h)].astype(F32)
            grad = jnp.where(k > chip, new, grad)
        h0, l1 = state, grad
        h1 = h0 * decay0[:, column] + s0
        l0 = l1 * decay1[:, column] + g1
        cross = h0 * (l0 * weight0[:, column] + qs0) + h1 * (l1 * weight1[:, column] + qs1)
        cross += l0 * qg0 + l1 * qg1
        total_ref[h : h + 1, :] += jnp.sum(cross, axis=0, keepdims=True)
        h0, h1, l0, l1 = (value.astype(BF16) for value in (h0, h1, l0, l1))
        own_ref[0, :, head(h)] = jnp.where(is0, h0, h1)
        own_ref[1, :, head(h)] = jnp.where(is0, l0, l1)
        give_ref[0, :, head(h)] = jnp.where(is0, h1, h0)
        give_ref[1, :, head(h)] = jnp.where(is0, l1, l0)


def attention_kernel(chips, most, mask_ref, q_ref, g_ref, *refs):
    kv_parts = refs[: 2 * chips]
    (
        _, out_ref, dq_ref, keep_ref, give_ref,
        kv_ref, acc_ref, k_ref, k_live_ref, v_ref, q_turned_ref, g_turned_ref, ds_ref, pr_ref,
    ) = refs[2 * chips :]
    count = mask_ref.shape[0]
    columns = QUERY_HEADS * BLOCK
    tokens = q_ref.shape[0]
    chip, core = chip_and_core()
    me = 2 * chip + core
    scale = FACTOR * LOG2E
    acc_ref[...] = jnp.zeros_like(acc_ref)
    for k in range(chips):
        for other in range(2):
            source = 2 * lax.rem(chip + chips - k, chips) + lax.rem(core + other, 2)
            at = pl.ds(pl.multiple_of(source * tokens, tokens), tokens)
            kv_ref[at, :] = kv_parts[2 * k + other][...]

    def nth(row, slot):
        def look(j, carry):
            found, seen = carry
            hit = (mask_ref[row, j] == 1) & (seen == slot)
            return jnp.where(hit, j, found), seen + mask_ref[row, j]

        return lax.fori_loop(0, count, look, (row, 0))

    lower, upper = slice(0, LANES), slice(LANES, 2 * LANES)
    for block in range(tokens // BLOCK):
        at = slice(block * BLOCK, (block + 1) * BLOCK)
        row = me * (tokens // BLOCK) + block
        slots = []
        for slot in range(most):
            index, allowed = nth(row, slot)
            live = slot < allowed
            slots.append((index, live))
            source = pl.ds(pl.multiple_of(index * BLOCK, BLOCK), BLOCK)
            target = slice(slot * BLOCK, (slot + 1) * BLOCK)
            k_tile, v_tile = kv_ref[source, lower], kv_ref[source, upper]
            k_ref[target, :] = k_tile
            k_live_ref[target, :] = jnp.where(live, k_tile, jnp.zeros_like(k_tile))
            v_ref[target, lower] = jnp.where(live, v_tile, jnp.zeros_like(v_tile))
            v_ref[target, upper] = jnp.full((BLOCK, LANES), jnp.where(live, 1.0, 0.0), F32).astype(BF16)
        for h in range(QUERY_HEADS):
            rows = slice(h * BLOCK, (h + 1) * BLOCK)
            q_turned_ref[:, rows] = q_ref[at, head(h)].T
            g_turned_ref[:, rows] = g_ref[at, head(h)].T
        group = 2
        for first in range(0, QUERY_HEADS, group):
            heads = range(first, first + group)
            rows = slice(first * BLOCK, (first + group) * BLOCK)
            q = jnp.concatenate([q_ref[at, head(h)] for h in heads], axis=0)
            g = jnp.concatenate([g_ref[at, head(h)] for h in heads], axis=0)
            scores = dot(q, k_ref[...], 1, 1)
            best = jnp.max(scores, axis=1, keepdims=True)
            weights = jnp.exp2((scores - best) * scale)
            both = dot(weights.astype(BF16), v_ref[...], 1, 0)
            inverse = 1.0 / both[:, upper]
            out = both[:, lower] * inverse
            delta = jnp.sum(out * g.astype(F32), axis=1, keepdims=True)
            probs = weights * jnp.concatenate([inverse] * most, axis=1)
            dprobs = dot(g, v_ref[:, lower], 1, 1)
            ds = (probs * (dprobs - delta)).astype(BF16)
            pr_ref[rows, :] = probs.astype(BF16)
            ds_ref[rows, :] = ds
            dq = (dot(ds, k_live_ref[...], 1, 0) * FACTOR).astype(BF16)
            for place, h in enumerate(heads):
                part = slice(place * BLOCK, (place + 1) * BLOCK)
                out_ref[at, head(h)] = out[part]
                dq_ref[at, head(h)] = dq[part]
        dk = dot(q_turned_ref[...], ds_ref[...], 1, 0)
        dv = dot(g_turned_ref[...], pr_ref[...], 1, 0)
        for slot, (index, live) in enumerate(slots):
            source = slice(slot * BLOCK, (slot + 1) * BLOCK)

            @pl.when(live)
            def _():
                target = pl.ds(pl.multiple_of(index * BLOCK, BLOCK), BLOCK)
                acc_ref[lower, target] += dk[:, source]
                acc_ref[upper, target] += dv[:, source]

    for k in range(chips):
        mine = pl.multiple_of((2 * k + core) * tokens, tokens)
        other = pl.multiple_of((2 * k + 1 - core) * tokens, tokens)
        keep_ref[k] = acc_ref[:, pl.ds(mine, tokens)].astype(BF16)
        give_ref[k] = acc_ref[:, pl.ds(other, tokens)].astype(BF16)


def pair_sum_kernel(chips, keep_ref, recv_ref, sums_ref, other_ref, own_ref, total_ref, *message_refs):
    chip, _ = chip_and_core()
    rows = own_ref.shape[0]
    own_ref[...] = keep_ref[chip].astype(F32) + recv_ref[chip].astype(F32)
    total = sums_ref[...] + other_ref[...]
    total_ref[...] = total
    high = total.astype(BF16)
    middle = (total - high.astype(F32)).astype(BF16)
    low = (total - high.astype(F32) - middle.astype(F32)).astype(BF16)
    tail = jnp.concatenate(
        [
            jnp.concatenate([high, middle], axis=1),
            jnp.concatenate([low, jnp.zeros_like(low)], axis=1),
        ],
        axis=0,
    )
    for k in range(1, chips):
        target = lax.rem(chip + k, chips)
        both = keep_ref[target].astype(F32) + recv_ref[target].astype(F32)
        message_refs[k - 1][:rows, :] = both.astype(BF16)
        message_refs[k - 1][rows:, :] = tail


def owner_sum_kernel(chips, tokens_all, own_ref, sums_ref, *refs):
    parts, (dk_ref, dv_ref, rate_ref, skip_ref) = refs[: chips - 1], refs[chips - 1 :]
    rows = own_ref.shape[0]
    total = own_ref[...]
    sums = sums_ref[...]
    for part in parts:
        total += part[:rows, :].astype(F32)
        tail = part[rows:, :].astype(F32)
        sums += tail[:16, :LANES] + tail[:16, LANES:] + tail[16:, :LANES]
    dk_ref[...] = (total[:LANES].T * FACTOR).astype(BF16)
    dv_ref[...] = total[LANES:].T.astype(BF16)
    ones = jnp.ones((8, LANES), F32)
    rate = dot(ones, sums[:HS], 1, 1, HIGH) * (1.0 / tokens_all)
    skip = dot(ones, sums[HS:], 1, 1, HIGH) * (1.0 / (tokens_all * P_SIZE))
    rate_ref[...] = rate[0:1, :]
    skip_ref[...] = skip[0:1, :]


def inner_kernel(
    x_ref, g_ref, b_ref, c_ref, step_ref, rate_ref, skip_ref, _,
    y_ref, dx_ref, db_ref, dc_ref, sums_ref,
    pad_ref, inner_ref, dinner_ref, m_ref, runt_ref,
):
    tokens = 2 * BLOCK
    flat0, flat1, run0, run1 = running_logs(step_ref, rate_ref, pad_ref)
    own = jnp.concatenate([run0, run1], axis=0)
    runt_ref[:, :BLOCK] = flat0
    runt_ref[:, tokens : tokens + BLOCK] = flat0 - flat0[:, BLOCK - 1 :]
    runt_ref[:, tokens + BLOCK :] = flat1
    b = b_ref[...]
    c = c_ref[...]
    inner_ref[...] = dot(c, b, 1, 1)
    dinner_ref[...] = jnp.zeros_like(dinner_ref)
    row0 = lax.broadcasted_iota(jnp.int32, (BLOCK, BLOCK), 0)
    col0 = lax.broadcasted_iota(jnp.int32, (BLOCK, BLOCK), 1)
    row1 = lax.broadcasted_iota(jnp.int32, (BLOCK, tokens), 0)
    col1 = lax.broadcasted_iota(jnp.int32, (BLOCK, tokens), 1)
    seen0 = row0 >= col0
    seen1 = row1 + BLOCK >= col1
    m_ref[:BLOCK, BLOCK:] = jnp.zeros((BLOCK, BLOCK), BF16)
    for h in range(HS):
        lanes = head(h)
        x = x_ref[:, lanes]
        g = g_ref[:, lanes]
        xf, gf = x.astype(F32), g.astype(F32)
        gain = skip_ref[h]
        spread0 = jnp.where(seen0, own[:BLOCK, h : h + 1] - runt_ref[h : h + 1, :BLOCK], NEG)
        spread1 = jnp.where(seen1, own[BLOCK:, h : h + 1] - runt_ref[h : h + 1, tokens:], NEG)
        decay0, decay1 = jnp.exp(spread0), jnp.exp(spread1)
        dm = dot(g, x, 1, 1)
        e0, e1 = decay0 * dm[:BLOCK, :BLOCK], decay1 * dm[BLOCK:, :]
        m_ref[:BLOCK, :BLOCK] = (decay0 * inner_ref[:BLOCK, :BLOCK]).astype(BF16)
        m_ref[BLOCK:, :] = (decay1 * inner_ref[BLOCK:, :]).astype(BF16)
        dinner_ref[:BLOCK, :BLOCK] += e0
        dinner_ref[BLOCK:, :] += e1
        w0 = jnp.sum(spread0 * (e0 * inner_ref[:BLOCK, :BLOCK]), axis=0, keepdims=True)
        w1 = jnp.sum(spread1 * (e1 * inner_ref[BLOCK:, :]), axis=0, keepdims=True)
        m = m_ref[...]
        y_ref[:, lanes] = dot(m, x, 1, 0) + gain * xf
        dx_ref[:, lanes] = dot(m, g, 0, 0) + gain * gf
        sums_ref[h : h + 1, :] = w0 + w1[:, :BLOCK] + w1[:, BLOCK:]
        sums_ref[HS + h : HS + h + 1, :] = jnp.sum(gf * xf, axis=0, keepdims=True)
    dinner = dinner_ref[...].astype(BF16)
    dc_ref[...] = dot(dinner, b, 1, 0)
    db_ref[...] = dot(dinner, c, 0, 0)


def outer_kernel(
    x_ref, g_ref, b_ref, c_ref, step_ref, rate_ref, own_ref, other_ref, att_ref,
    inner_y_ref, inner_dx_ref, inner_db_ref, inner_dc_ref, _,
    y_ref, dx_ref, db_ref, dc_ref,
    pad_ref, xt_ref, gt_ref, ent_ref,
):
    _, core = chip_and_core()
    ent_ref[:, pl.ds(pl.multiple_of(core * HALF, HALF), HALF), :] = own_ref[...]
    ent_ref[:, pl.ds(pl.multiple_of((1 - core) * HALF, HALF), HALF), :] = other_ref[...]
    _, _, run0, run1 = running_logs(step_ref, rate_ref, pad_ref)
    enter_log, tail_log, _ = enter_and_tail(run0, run1)
    enter, tail = jnp.exp(enter_log), jnp.exp(tail_log)
    scaled(x_ref, tail, xt_ref)
    scaled(g_ref, enter, gt_ref)
    b = b_ref[...]
    c = c_ref[...]
    for h in range(HS):
        lanes = head(h)
        carried = dot(c, ent_ref[0, :, lanes], 1, 0) * enter[:, h : h + 1]
        back = dot(b, ent_ref[1, :, lanes], 1, 0) * tail[:, h : h + 1]
        y_ref[:, lanes] = (inner_y_ref[:, lanes] + carried + att_ref[:, lanes]).astype(BF16)
        dx_ref[:, lanes] = (inner_dx_ref[:, lanes] + back).astype(BF16)
    dc_ref[...] = (inner_dc_ref[...] + dot(gt_ref[...], ent_ref[0], 1, 1)).astype(BF16)
    db_ref[...] = (inner_db_ref[...] + dot(xt_ref[...], ent_ref[1], 1, 1)).astype(BF16)


def swapped(array):
    return lax.ppermute(array, "seq", [(i, i ^ 1) for i in range(lax.axis_size("seq"))])


def from_chip(array, k):
    n = lax.axis_size("seq")
    return lax.ppermute(array, "seq", [(i, (i + 2 * k) % n) for i in range(n)])


def turned(array, k):
    n = lax.axis_size("dp")
    return lax.ppermute(array, "dp", [(i, (i + k) % n) for i in range(n)])


def call(kernel, outs, ins, scratch, microseconds, name):
    return pl.pallas_call(
        kernel,
        out_shape=tuple(jax.ShapeDtypeStruct(*out) for out in outs),
        in_specs=ins,
        out_specs=(VMEM,) * len(outs),
        scratch_shapes=scratch,
        compiler_params=params(),
        cost_estimate=cost(microseconds),
        name=name,
    )


def body(query, key, value, ssm_input, in_b, in_c, step, rate_log, skip, block_mask, grad_out):
    n = lax.axis_size("seq")
    chips = n // 2
    tokens = query.shape[1]
    blocks = block_mask.shape[1]
    most = 3 * blocks // 8
    every = blocks * BLOCK
    q, g, x = query[0], grad_out[0], ssm_input[0]
    b, c, steps = in_b[0], in_c[0], step[0].T

    (kv,) = call(pack_kernel, [((tokens, 2 * LANES), BF16)], [VMEM] * 2, [], 1, "pack_kv")(
        key[0], value[0]
    )
    kv_parts = [kv, swapped(kv)]
    for k in range(1, chips):
        part = from_chip(kv, k)
        kv_parts += [part, swapped(part)]

    half = ((4, HALF, WIDE + LANES), F32)
    keep, give = call(
        local_states_kernel,
        [half, half],
        [VMEM] * 5 + [SMEM],
        [
            pltpu.VMEM((LANES, tokens), F32),
            pltpu.VMEM((tokens, WIDE), BF16),
            pltpu.VMEM((tokens, WIDE), BF16),
            pltpu.VMEM((tokens, WIDE), BF16),
            pltpu.VMEM((4, NS, WIDE), F32),
        ],
        4,
        "local_states",
    )(x, g, b, c, steps, rate_log)
    received = swapped(give)
    messages = call(
        lambda *refs: combine_kernel(chips, *refs),
        [((HALF, WIDE + LANES), BF16)] * (chips - 1),
        [VMEM] * 2,
        [],
        1,
        "combine_states",
    )(keep, received)
    arrived = [from_chip(messages[k - 1], k) for k in range(1, chips)]

    inner_y, inner_dx, inner_db, inner_dc, sums = call(
        inner_kernel,
        [((tokens, WIDE), F32)] * 2 + [((tokens, NS), F32)] * 2 + [((2 * HS, LANES), F32)],
        [VMEM] * 5 + [SMEM] * 2 + [AFTER],
        [
            pltpu.VMEM((LANES, tokens), F32),
            pltpu.VMEM((tokens, tokens), F32),
            pltpu.VMEM((tokens, tokens), F32),
            pltpu.VMEM((tokens, tokens), BF16),
            pltpu.VMEM((LANES, 2 * tokens), F32),
        ],
        5,
        "chunk_inner",
    )(x, g, b, c, steps, rate_log, skip, messages[0])

    entering = ((2, HALF, WIDE), BF16)
    own, give, totals = call(
        lambda *refs: chain_kernel(chips, *refs),
        [entering, entering, ((2 * HS, LANES), F32)],
        [VMEM] * (2 + chips),
        [],
        2,
        "chain_states",
    )(keep, received, sums, *arrived)
    other = swapped(give)
    replicas = lax.axis_size("dp")
    summed = totals + sum(turned(totals, k) for k in range(1, replicas))

    columns = QUERY_HEADS * BLOCK
    split = ((chips, 2 * LANES, tokens), BF16)
    attention, dq, keep, give = call(
        lambda *refs: attention_kernel(chips, most, *refs),
        [((tokens, columns), F32), ((tokens, columns), BF16), split, split],
        [SMEM] + [VMEM] * (2 + n) + [AFTER],
        [
            pltpu.VMEM((every, 2 * LANES), BF16),
            pltpu.VMEM((2 * LANES, every), F32),
            pltpu.VMEM((most * BLOCK, LANES), BF16),
            pltpu.VMEM((most * BLOCK, LANES), BF16),
            pltpu.VMEM((most * BLOCK, 2 * LANES), BF16),
            pltpu.VMEM((LANES, columns), BF16),
            pltpu.VMEM((LANES, columns), BF16),
            pltpu.VMEM((columns, most * BLOCK), BF16),
            pltpu.VMEM((columns, most * BLOCK), BF16),
        ],
        10,
        "attention",
    )(block_mask[0], q, g, *kv_parts, totals)
    partial, summed, *messages = call(
        lambda *refs: pair_sum_kernel(chips, *refs),
        [((2 * LANES, tokens), F32), ((2 * HS, LANES), F32)]
        + [((2 * LANES + 32, tokens), BF16)] * (chips - 1),
        [VMEM] * 4,
        [],
        1,
        "pair_sum",
    )(keep, swapped(give), summed, swapped(summed))
    arrived = [from_chip(messages[k - 1], k) for k in range(1, chips)]

    y, dx, db, dc = call(
        outer_kernel,
        [((tokens, WIDE), BF16)] * 2 + [((tokens, NS), BF16)] * 2,
        [VMEM] * 5 + [SMEM] + [VMEM] * 7 + [AFTER],
        [
            pltpu.VMEM((LANES, tokens), F32),
            pltpu.VMEM((tokens, WIDE), BF16),
            pltpu.VMEM((tokens, WIDE), BF16),
            pltpu.VMEM((2, NS, WIDE), BF16),
        ],
        3,
        "chunk_outer",
    )(
        x, g, b, c, steps, rate_log, own, other, attention,
        inner_y, inner_dx, inner_db, inner_dc, messages[0],
    )

    tokens_all = replicas * n * tokens
    dk, dv, grad_rate_log, grad_skip = call(
        lambda *refs: owner_sum_kernel(chips, tokens_all, *refs),
        [((tokens, LANES), BF16)] * 2 + [((1, HS), F32)] * 2,
        [VMEM] * (chips + 1),
        [],
        1,
        "owner_sum",
    )(partial, summed, *arrived)
    return (
        y[None],
        dq[None],
        dk[None],
        dv[None],
        dx[None],
        db[None],
        dc[None],
        grad_rate_log.reshape(HS),
        grad_skip.reshape(HS),
    )


def solution(mesh):
    split = P("dp", "seq", None)
    in_specs = (split,) * 7 + (P(), P(), P("dp", None, None), split)
    out_specs = (split,) * 7 + (P(), P())
    return jax.shard_map(body, mesh=mesh, in_specs=in_specs, out_specs=out_specs, check_vma=False)
```

time: 79.5 us -> 71.1 us (0.89); the launches traced: 80.1 us -> 70.7 us
  starting transfers between devices: 27.9 us -> 19 us
  Pallas kernels: 32.7 us -> 39.2 us
  waiting for transfers between devices: 11.5 us -> 6.91 us
  other arithmetic: 2.05 us -> 0.01 us
    ppermute x12 -> x9, waiting for transfers between devices: 9.09 us -> 1.31 us  [from_chip(): return lax.ppermute(array, 'seq', [(i, (i + 2 * k) % n) for i in range(n)])]
    pallas_call x5, Pallas kernels: 18.5 us -> 24.2 us  [the longest x1 13.7 us: body(): call(lambda *refs: attention_kernel(chips, most, *refs), [((tokens, colum...]
    ppermute x12 -> x9, starting transfers between devices: 17.6 us -> 12.7 us  [from_chip(): return lax.ppermute(array, 'seq', [(i, (i + 2 * k) % n) for i in range(n)])]
    ppermute x3, starting transfers between devices: 8.85 us -> 4.62 us  [turned(): return lax.ppermute(array, 'dp', [(i, (i + k) % n) for i in range(n)])]
    ppermute x3, waiting for transfers between devices: 1.36 us -> 4.42 us  [turned(): return lax.ppermute(array, 'dp', [(i, (i + k) % n) for i in range(n)])]
    unnamed x34 -> x42, local copies, waits for them, and re-layouts: 5.09 us -> 4.75 us
  transfers between devices with their start and end apart: 23 -> 20, of which waited for: 8 -> 5; matrix products, arithmetic and copies ran while one was open for 3% -> 0% of each run, Pallas kernels for 33% -> 26%
where the time goes in v4:
time: 71.1 us; the launch traced here: 70.7 us
  Pallas kernels  39.2 us (55%)
  starting transfers between devices  19 us (27%)
  waiting for transfers between devices  6.91 us (10%)
  local copies, waits for them, and re-layouts  4.75 us (7%)
  between operations  0.83 us (1%)
    pallas_call x1, Pallas kernels, body(): call(lambda *refs: attention_kernel(chips, most, *refs), [((tokens, colum...  13.7 us
    ppermute x9, starting transfers between devices, from_chip(): return lax.ppermute(array, 'seq', [(i, (i + 2 * k) % n) for i in range(n)])  12.7 us
    pallas_call x1, Pallas kernels, body(): call(local_states_kernel, [half, half], [VMEM] * 5 + [SMEM], [pltpu.VMEM(...  4.93 us
    unnamed x42, local copies, waits for them, and re-layouts  4.75 us
    pallas_call x1, Pallas kernels, body(): call(outer_kernel, [((tokens, WIDE), BF16)] * 2 + [((tokens, NS), BF16)]...  4.64 us
    ppermute x3, starting transfers between devices, turned(): return lax.ppermute(array, 'dp', [(i, (i + k) % n) for i in range(n)])  4.62 us
    pallas_call x1, Pallas kernels, body(): call(inner_kernel, [((tokens, WIDE), F32)] * 2 + [((tokens, NS), F32)] *...  4.61 us
    ppermute x3, waiting for transfers between devices, turned(): return lax.ppermute(array, 'dp', [(i, (i + k) % n) for i in range(n)])  4.42 us
  transfers between devices with their start and end apart: 20, of which 5 were waited for; matrix products, arithmetic and copies ran while one was open for 0% of the time, Pallas kernels for 26%

profile of v4, /device:TPU:0, one launch (start us, length us, event | category | flops | bytes accessed | tf_op | source)
XLA Modules:
  0.0 70.7 jit_solution(14845732438372630931)
XLA Ops:
  0.6 4.9 %local_states.1 = (f32[4,64,1152]{2,1,0:T(8,128)}, f32[4,64,1152]{2,1,0:T(8,128)}) custom-call(bf16[256,1024]{1,0:T(8,128)(2,1)} %bitcast.21, bf16[256,1024]{1,0:T(8,128)(2,1)} %bitcast.24, bf16[256,128]{1,0:T(8,128)(2,1)} %bitcast.30, bf16[256,128]{1,0:T(8,128)(2,1)} %bitcast.33, f32[8,256]{1,0:T(8,128)} %bitcast.37, f32[8]{0:T(128)} %rate_ref.5), custom_call_target="tpu_custom_call" | custom-call | flops 4400000000 | bytes 1048576 | tf_op jit(solution)/shard_map/local_states/pallas_call | solution.py:438
  6.0 1.5 %pack_kv.1.refs_3_ = bf16[256,256]{1,0:T(8,128)(2,1)} custom-call(bf16[256,128]{1,0:T(8,128)(2,1)} %bitcast.28, bf16[256,128]{1,0:T(8,128)(2,1)} %bitcast.29), custom_call_target="tpu_custom_call" | custom-call | flops 1100000000 | bytes 1048576 | tf_op jit(solution)/shard_map/pack_kv/pallas_call | solution.py:429
  7.6 2.5 %collective-permute-start.6 = (bf16[256,256]{1,0:T(8,128)(2,1)}, bf16[256,256]{1,0:T(8,128)(2,1)S(1)}, u32[]{:S(2)}, u32[]{:S(2)}) collective-permute-start(bf16[256,256]{1,0:T(8,128)(2,1)} %pack_kv.1.refs_3_), channel_id=1, source_target_pairs={{0,2},{1,3},{2,4},{3,5},{4,6},{5,7},{6,0},{7,1},{8,10},{9,11},{10,... | collective-permute-start | bytes 393224 | tf_op jit(solution)/shard_map/ppermute | solution.py:398
  10.1 1.5 %collective-permute-start.8 = (bf16[256,256]{1,0:T(8,128)(2,1)}, bf16[256,256]{1,0:T(8,128)(2,1)S(1)}, u32[]{:S(2)}, u32[]{:S(2)}) collective-permute-start(bf16[256,256]{1,0:T(8,128)(2,1)} %pack_kv.1.refs_3_), channel_id=1, source_target_pairs={{0,4},{1,5},{2,6},{3,7},{4,0},{5,1},{6,2},{7,3},{8,12},{9,13},{10,... | collective-permute-start | bytes 393224 | tf_op jit(solution)/shard_map/ppermute | solution.py:398
  11.6 1.4 %collective-permute-start.10 = (bf16[256,256]{1,0:T(8,128)(2,1)}, bf16[256,256]{1,0:T(8,128)(2,1)S(1)}, u32[]{:S(2)}, u32[]{:S(2)}) collective-permute-start(bf16[256,256]{1,0:T(8,128)(2,1)} %pack_kv.1.refs_3_), channel_id=1, source_target_pairs={{0,6},{1,7},{2,0},{3,1},{4,2},{5,3},{6,4},{7,5},{8,14},{9,15},{10,... | collective-permute-start | bytes 393224 | tf_op jit(solution)/shard_map/ppermute | solution.py:398
  13.0 1.0 %copy-done.2 = f32[4,64,1152]{2,1,0:T(8,128)} copy-done((f32[4,64,1152]{2,1,0:T(8,128)}, f32[4,64,1152]{2,1,0:T(8,128)S(1)}, u32[]{:S(2)}) %copy-start.2) | copy-done | bytes 1179672
  14.1 2.6 %combine_states.1 = (bf16[64,1152]{1,0:T(8,128)(2,1)}, bf16[64,1152]{1,0:T(8,128)(2,1)}, bf16[64,1152]{1,0:T(8,128)(2,1)}) custom-call(f32[4,64,1152]{2,1,0:T(8,128)} %get-tuple-element.39.refs_0_, f32[4,64,1152]{2,1,0:T(8,128)} %copy-done.2), custom_call_target="tpu_custom_call" | custom-call | flops 1100000000 | bytes 1048576 | tf_op jit(solution)/shard_map/combine_states/pallas_call | solution.py:453
  17.8 1.9 %collective-permute-start.3 = (bf16[64,1152]{1,0:T(8,128)(2,1)}, bf16[64,1152]{1,0:T(8,128)(2,1)S(1)}, u32[]{:S(2)}, u32[]{:S(2)}) collective-permute-start(bf16[64,1152]{1,0:T(8,128)(2,1)} %get-tuple-element.44), channel_id=1, source_target_pairs={{0,6},{1,7},{2,0},{3,1},{4,2},{5,3},{6,4},{7,5},{8,14},{9,15},{10,... | collective-permute-start | bytes 442376 | tf_op jit(solution)/shard_map/ppermute | solution.py:398
  19.7 4.6 %chunk_inner.1 = (f32[256,1024]{1,0:T(8,128)}, f32[256,1024]{1,0:T(8,128)}, f32[256,128]{1,0:T(8,128)}, f32[256,128]{1,0:T(8,128)}, f32[16,128]{1,0:T(8,128)}) custom-call(bf16[256,1024]{1,0:T(8,128)(2,1)} %bitcast.22, bf16[256,1024]{1,0:T(8,128)(2,1)} %bitcast.25, bf16[256,128]{1,0:T(8,128)(2,1)} %bitcast.31, bf16[256,128]{1,0:T(8,128)(2,1)} %bitcast.34, ...), custom_call_target="tpu_custom_call" | custom-call | flops 5500000256 | bytes 1048576 | tf_op jit(solution)/shard_map/chunk_inner/pallas_call | solution.py:463
  25.0 0.7 %collective-permute-done.2.refs_4_ = bf16[64,1152]{1,0:T(8,128)(2,1)S(1)} collective-permute-done((bf16[64,1152]{1,0:T(8,128)(2,1)}, bf16[64,1152]{1,0:T(8,128)(2,1)S(1)}, u32[]{:S(2)}, u32[]{:S(2)}) %collective-permute-start.2) | collective-permute-done | bytes 147488 | tf_op jit(solution)/shard_map/ppermute | solution.py:398
  25.8 0.6 copy-done.7
  26.5 3.2 %chain_states.1 = (bf16[2,64,1024]{2,1,0:T(8,128)(2,1)}, bf16[2,64,1024]{2,1,0:T(8,128)(2,1)}, f32[16,128]{1,0:T(8,128)}) custom-call(f32[4,64,1152]{2,1,0:T(8,128)} %get-tuple-element.39.refs_0_, f32[4,64,1152]{2,1,0:T(8,128)} %copy-done.2, f32[16,128]{1,0:T(8,128)} %get-tuple-element.42.refs_2_, bf16[64,1152]{1,0:T(8,128)(2,1)} %copy-done.6, ...), custom_call_target="tpu_custom_call" | custom-call | flops 2200000000 | bytes 1048576 | tf_op jit(solution)/shard_map/chain_states/pallas_call | solution.py:479
  30.5 13.7 %attention.1 = (f32[256,1024]{1,0:T(8,128)}, bf16[256,1024]{1,0:T(8,128)(2,1)}, bf16[4,256,256]{2,1,0:T(8,128)(2,1)}, bf16[4,256,256]{2,1,0:T(8,128)(2,1)}) custom-call(s32[16,16]{1,0:T(8,128)} %bitcast.36, bf16[256,1024]{1,0:T(8,128)(2,1)} %bitcast.20, bf16[256,1024]{1,0:T(8,128)(2,1)} %bitcast.26, bf16[256,256]{1,0:T(8,128)(2,1)} %pack_kv.1.refs_3_, ...), custom_call_target="tpu_custom_call" | custom-call | flops 11000000512 | bytes 1048576 | tf_op jit(solution)/shard_map/attention/pallas_call | solution.py:493
  44.6 3.6 %collective-permute-start.15 = (f32[16,128]{1,0:T(8,128)S(1)}, f32[16,128]{1,0:T(8,128)S(1)}, u32[]{:S(2)}, u32[]{:S(2)}) collective-permute-start(f32[16,128]{1,0:T(8,128)S(1)} %copy-done), channel_id=1, source_target_pairs={{0,24},{8,0},{16,8},{24,16},{1,25},{9,1},{17,9},{25,17},{2,26},{10... | collective-permute-start | bytes 24584 | tf_op jit(solution)/shard_map/ppermute | solution.py:403
  48.2 1.0 %collective-permute-start.14 = (f32[16,128]{1,0:T(8,128)S(1)}, f32[16,128]{1,0:T(8,128)S(1)}, u32[]{:S(2)}, u32[]{:S(2)}) collective-permute-start(f32[16,128]{1,0:T(8,128)S(1)} %copy-done), channel_id=1, source_target_pairs={{0,16},{8,24},{16,0},{24,8},{1,17},{9,25},{17,1},{25,9},{2,18},{10... | collective-permute-start | bytes 24584 | tf_op jit(solution)/shard_map/ppermute | solution.py:403
  49.6 4.1 %collective-permute-done.13 = f32[16,128]{1,0:T(8,128)S(1)} collective-permute-done((f32[16,128]{1,0:T(8,128)S(1)}, f32[16,128]{1,0:T(8,128)S(1)}, u32[]{:S(2)}, u32[]{:S(2)}) %collective-permute-start.13) | collective-permute-done | bytes 8224 | tf_op jit(solution)/shard_map/ppermute | solution.py:403
  53.8 1.2 %collective-permute-done.16.refs_3_ = f32[16,128]{1,0:T(8,128)S(1)} collective-permute-done((f32[16,128]{1,0:T(8,128)S(1)}, f32[16,128]{1,0:T(8,128)S(1)}, u32[]{:S(2)}, u32[]{:S(2)}) %collective-permute-start.16) | collective-permute-done | bytes 8224 | tf_op jit(solution)/shard_map/ppermute | solution.py:393
  55.7 2.1 %pair_sum.1 = (f32[256,256]{1,0:T(8,128)}, f32[16,128]{1,0:T(8,128)}, bf16[288,256]{1,0:T(8,128)(2,1)}, bf16[288,256]{1,0:T(8,128)(2,1)}, bf16[288,256]{1,0:T(8,128)(2,1)}) custom-call(bf16[4,256,256]{2,1,0:T(8,128)(2,1)} %get-tuple-element.53.refs_0_, bf16[4,256,256]{2,1,0:T(8,128)(2,1)} %copy-done.3, f32[16,128]{1,0:T(8,128)} %copy-done.1, ...), custom_call_target="tpu_custom_call" | custom-call | flops 1100000000 | bytes 1048576 | tf_op jit(solution)/shard_map/pair_sum/pallas_call | solution.py:511
  57.9 1.4 %collective-permute-start.17 = (bf16[288,256]{1,0:T(8,128)(2,1)}, bf16[288,256]{1,0:T(8,128)(2,1)S(1)}, u32[]{:S(2)}, u32[]{:S(2)}) collective-permute-start(bf16[288,256]{1,0:T(8,128)(2,1)} %get-tuple-element.55._), channel_id=1, source_target_pairs={{0,2},{1,3},{2,4},{3,5},{4,6},{5,7},{6,0},{7,1},{8,10},{9,11},{10,... | collective-permute-start | bytes 442376 | tf_op jit(solution)/shard_map/ppermute | solution.py:398
  59.2 1.7 %collective-permute-start.18 = (bf16[288,256]{1,0:T(8,128)(2,1)}, bf16[288,256]{1,0:T(8,128)(2,1)S(1)}, u32[]{:S(2)}, u32[]{:S(2)}) collective-permute-start(bf16[288,256]{1,0:T(8,128)(2,1)} %get-tuple-element.60), channel_id=1, source_target_pairs={{0,4},{1,5},{2,6},{3,7},{4,0},{5,1},{6,2},{7,3},{8,12},{9,13},{10,... | collective-permute-start | bytes 442376 | tf_op jit(solution)/shard_map/ppermute | solution.py:398
  60.9 1.1 %collective-permute-start.19 = (bf16[288,256]{1,0:T(8,128)(2,1)}, bf16[288,256]{1,0:T(8,128)(2,1)S(1)}, u32[]{:S(2)}, u32[]{:S(2)}) collective-permute-start(bf16[288,256]{1,0:T(8,128)(2,1)} %get-tuple-element.61), channel_id=1, source_target_pairs={{0,6},{1,7},{2,0},{3,1},{4,2},{5,3},{6,4},{7,5},{8,14},{9,15},{10,... | collective-permute-start | bytes 442376 | tf_op jit(solution)/shard_map/ppermute | solution.py:398
  62.1 0.7 %copy-done.5 = bf16[2,64,1024]{2,1,0:T(8,128)(2,1)} copy-done((bf16[2,64,1024]{2,1,0:T(8,128)(2,1)}, bf16[2,64,1024]{2,1,0:T(8,128)(2,1)S(1)}, u32[]{:S(2)}) %copy-start.5) | copy-done | bytes 262168
  62.8 4.6 %chunk_outer.1 = (bf16[256,1024]{1,0:T(8,128)(2,1)}, bf16[256,1024]{1,0:T(8,128)(2,1)}, bf16[256,128]{1,0:T(8,128)(2,1)}, bf16[256,128]{1,0:T(8,128)(2,1)}) custom-call(bf16[256,1024]{1,0:T(8,128)(2,1)} %bitcast.23, bf16[256,1024]{1,0:T(8,128)(2,1)} %bitcast.27, bf16[256,128]{1,0:T(8,128)(2,1)} %bitcast.32, bf16[256,128]{1,0:T(8,128)(2,1)} %bitcast.35, ...), custom_call_target="tpu_custom_call" | custom-call | flops 3300000000 | bytes 1048576 | tf_op jit(solution)/shard_map/chunk_outer/pallas_call | solution.py:522
  68.8 1.9 %owner_sum.1 = (bf16[256,128]{1,0:T(8,128)(2,1)}, bf16[256,128]{1,0:T(8,128)(2,1)}, f32[1,8]{1,0:T(1,128)}, f32[1,8]{1,0:T(1,128)}) custom-call(f32[256,256]{1,0:T(8,128)} %get-tuple-element.58.refs_0_, f32[16,128]{1,0:T(8,128)} %get-tuple-element.59.refs_1_, bf16[288,256]{1,0:T(8,128)(2,1)} %copy-done.9, bf16[288,256]{1,0:T(8,128)(2,1)} %copy-done.10, ...), custom_call_target="tpu_custom_call" | custom-call | flops 1100000000 | bytes 1048576 | tf_op jit(solution)/shard_map/owner_sum/pallas_call | solution.py:540
  (68 shorter events, 6.1 us)
Async XLA Ops:
  5.6 7.4 %collective-permute-start = (f32[4,64,1152]{2,1,0:T(8,128)}, f32[4,64,1152]{2,1,0:T(8,128)S(1)}, u32[]{:S(2)}, u32[]{:S(2)}) collective-permute-start(f32[4,64,1152]{2,1,0:T(8,128)} %get-tuple-element.40), channel_id=1, source_target_pairs={{0,1},{1,0},{2,3},{3,2},{4,5},{5,4},{6,7},{7,6},{8,9},{9,8},{10,11... | collective-permute-start | bytes 3538952 | tf_op jit(solution)/shard_map/ppermute | solution.py:393
  7.6 10.2 %collective-permute-start.6 = (bf16[256,256]{1,0:T(8,128)(2,1)}, bf16[256,256]{1,0:T(8,128)(2,1)S(1)}, u32[]{:S(2)}, u32[]{:S(2)}) collective-permute-start(bf16[256,256]{1,0:T(8,128)(2,1)} %pack_kv.1.refs_3_), channel_id=1, source_target_pairs={{0,2},{1,3},{2,4},{3,5},{4,6},{5,7},{6,0},{7,1},{8,10},{9,11},{10,... | collective-permute-start | bytes 393224 | tf_op jit(solution)/shard_map/ppermute | solution.py:398
  10.1 14.2 %collective-permute-start.8 = (bf16[256,256]{1,0:T(8,128)(2,1)}, bf16[256,256]{1,0:T(8,128)(2,1)S(1)}, u32[]{:S(2)}, u32[]{:S(2)}) collective-permute-start(bf16[256,256]{1,0:T(8,128)(2,1)} %pack_kv.1.refs_3_), channel_id=1, source_target_pairs={{0,4},{1,5},{2,6},{3,7},{4,0},{5,1},{6,2},{7,3},{8,12},{9,13},{10,... | collective-permute-start | bytes 393224 | tf_op jit(solution)/shard_map/ppermute | solution.py:398
  11.6 12.8 %collective-permute-start.10 = (bf16[256,256]{1,0:T(8,128)(2,1)}, bf16[256,256]{1,0:T(8,128)(2,1)S(1)}, u32[]{:S(2)}, u32[]{:S(2)}) collective-permute-start(bf16[256,256]{1,0:T(8,128)(2,1)} %pack_kv.1.refs_3_), channel_id=1, source_target_pairs={{0,6},{1,7},{2,0},{3,1},{4,2},{5,3},{6,4},{7,5},{8,14},{9,15},{10,... | collective-permute-start | bytes 393224 | tf_op jit(solution)/shard_map/ppermute | solution.py:398
  16.7 8.3 %collective-permute-start.1 = (bf16[64,1152]{1,0:T(8,128)(2,1)}, bf16[64,1152]{1,0:T(8,128)(2,1)S(1)}, u32[]{:S(2)}, u32[]{:S(2)}) collective-permute-start(bf16[64,1152]{1,0:T(8,128)(2,1)} %get-tuple-element.41._), channel_id=1, source_target_pairs={{0,2},{1,3},{2,4},{3,5},{4,6},{5,7},{6,0},{7,1},{8,10},{9,11},{10,... | collective-permute-start | bytes 442376 | tf_op jit(solution)/shard_map/ppermute | solution.py:398
  17.2 8.5 %collective-permute-start.2 = (bf16[64,1152]{1,0:T(8,128)(2,1)}, bf16[64,1152]{1,0:T(8,128)(2,1)S(1)}, u32[]{:S(2)}, u32[]{:S(2)}) collective-permute-start(bf16[64,1152]{1,0:T(8,128)(2,1)} %get-tuple-element.43), channel_id=1, source_target_pairs={{0,4},{1,5},{2,6},{3,7},{4,0},{5,1},{6,2},{7,3},{8,12},{9,13},{10,... | collective-permute-start | bytes 442376 | tf_op jit(solution)/shard_map/ppermute | solution.py:398
  17.7 6.6 %copy-start.13 = (bf16[256,256]{1,0:T(8,128)(2,1)}, bf16[256,256]{1,0:T(8,128)(2,1)S(1)}, u32[]{:S(2)}) copy-start(bf16[256,256]{1,0:T(8,128)(2,1)S(1)} %collective-permute-done.6.refs_5_) | copy-start | bytes 393220
  17.7 6.5 %copy-start.12 = (bf16[256,256]{1,0:T(8,128)(2,1)S(1)}, bf16[256,256]{1,0:T(8,128)(2,1)}, u32[]{:S(2)}) copy-start(bf16[256,256]{1,0:T(8,128)(2,1)} %pack_kv.1.refs_3_) | copy-start | bytes 393220
  17.8 8.0 %collective-permute-start.3 = (bf16[64,1152]{1,0:T(8,128)(2,1)}, bf16[64,1152]{1,0:T(8,128)(2,1)S(1)}, u32[]{:S(2)}, u32[]{:S(2)}) collective-permute-start(bf16[64,1152]{1,0:T(8,128)(2,1)} %get-tuple-element.44), channel_id=1, source_target_pairs={{0,6},{1,7},{2,0},{3,1},{4,2},{5,3},{6,4},{7,5},{8,14},{9,15},{10,... | collective-permute-start | bytes 442376 | tf_op jit(solution)/shard_map/ppermute | solution.py:398
  24.3 5.4 %collective-permute-start.5 = (bf16[256,256]{1,0:T(8,128)(2,1)S(1)}, bf16[256,256]{1,0:T(8,128)(2,1)S(1)}, u32[]{:S(2)}, u32[]{:S(2)}) collective-permute-start(bf16[256,256]{1,0:T(8,128)(2,1)S(1)} %copy-done.12), channel_id=1, source_target_pairs={{0,1},{1,0},{2,3},{3,2},{4,5},{5,4},{6,7},{7,6},{8,9},{9,8},{10,11... | collective-permute-start | bytes 393224 | tf_op jit(solution)/shard_map/ppermute | solution.py:393
  24.4 5.3 %collective-permute-start.7 = (bf16[256,256]{1,0:T(8,128)(2,1)S(1)}, bf16[256,256]{1,0:T(8,128)(2,1)S(1)}, u32[]{:S(2)}, u32[]{:S(2)}) collective-permute-start(bf16[256,256]{1,0:T(8,128)(2,1)S(1)} %collective-permute-done.6.refs_5_), channel_id=1, source_target_pairs={{0,1},{1,0},{2,3},{3,2},{4,5},{5,4},{6,7},{7,6},{8,9},{9,8},{10,11... | collective-permute-start | bytes 393224 | tf_op jit(solution)/shard_map/ppermute | solution.py:393
  24.9 4.7 %collective-permute-start.9 = (bf16[256,256]{1,0:T(8,128)(2,1)S(1)}, bf16[256,256]{1,0:T(8,128)(2,1)S(1)}, u32[]{:S(2)}, u32[]{:S(2)}) collective-permute-start(bf16[256,256]{1,0:T(8,128)(2,1)S(1)} %collective-permute-done.8.refs_7_), channel_id=1, source_target_pairs={{0,1},{1,0},{2,3},{3,2},{4,5},{5,4},{6,7},{7,6},{8,9},{9,8},{10,11... | collective-permute-start | bytes 393224 | tf_op jit(solution)/shard_map/ppermute | solution.py:393
  25.8 3.9 %collective-permute-start.11 = (bf16[256,256]{1,0:T(8,128)(2,1)S(1)}, bf16[256,256]{1,0:T(8,128)(2,1)S(1)}, u32[]{:S(2)}, u32[]{:S(2)}) collective-permute-start(bf16[256,256]{1,0:T(8,128)(2,1)S(1)} %collective-permute-done.10.refs_9_), channel_id=1, source_target_pairs={{0,1},{1,0},{2,3},{3,2},{4,5},{5,4},{6,7},{7,6},{8,9},{9,8},{10,11... | collective-permute-start | bytes 393224 | tf_op jit(solution)/shard_map/ppermute | solution.py:393
  30.5 14.2 %copy-start = (f32[16,128]{1,0:T(8,128)S(1)}, f32[16,128]{1,0:T(8,128)}, u32[]{:S(2)}) copy-start(f32[16,128]{1,0:T(8,128)} %get-tuple-element.47.refs_11_) | copy-start | bytes 24580
  30.5 18.8 %copy-start.4 = (bf16[2,64,1024]{2,1,0:T(8,128)(2,1)S(1)}, bf16[2,64,1024]{2,1,0:T(8,128)(2,1)}, u32[]{:S(2)}) copy-start(bf16[2,64,1024]{2,1,0:T(8,128)(2,1)} %get-tuple-element.46) | copy-start | bytes 786436
  44.2 10.8 %collective-permute-start.12 = (bf16[4,256,256]{2,1,0:T(8,128)(2,1)}, bf16[4,256,256]{2,1,0:T(8,128)(2,1)S(1)}, u32[]{:S(2)}, u32[]{:S(2)}) collective-permute-start(bf16[4,256,256]{2,1,0:T(8,128)(2,1)} %get-tuple-element.54), channel_id=1, source_target_pairs={{0,1},{1,0},{2,3},{3,2},{4,5},{5,4},{6,7},{7,6},{8,9},{9,8},{10,11... | collective-permute-start | bytes 1572872 | tf_op jit(solution)/shard_map/ppermute | solution.py:393
  44.6 5.0 %collective-permute-start.15 = (f32[16,128]{1,0:T(8,128)S(1)}, f32[16,128]{1,0:T(8,128)S(1)}, u32[]{:S(2)}, u32[]{:S(2)}) collective-permute-start(f32[16,128]{1,0:T(8,128)S(1)} %copy-done), channel_id=1, source_target_pairs={{0,24},{8,0},{16,8},{24,16},{1,25},{9,1},{17,9},{25,17},{2,26},{10... | collective-permute-start | bytes 24584 | tf_op jit(solution)/shard_map/ppermute | solution.py:403
  48.2 5.4 %collective-permute-start.13 = (f32[16,128]{1,0:T(8,128)S(1)}, f32[16,128]{1,0:T(8,128)S(1)}, u32[]{:S(2)}, u32[]{:S(2)}) collective-permute-start(f32[16,128]{1,0:T(8,128)S(1)} %copy-done), channel_id=1, source_target_pairs={{0,8},{8,16},{16,24},{24,0},{1,9},{9,17},{17,25},{25,1},{2,10},{10... | collective-permute-start | bytes 24584 | tf_op jit(solution)/shard_map/ppermute | solution.py:403
  48.2 5.4 %collective-permute-start.14 = (f32[16,128]{1,0:T(8,128)S(1)}, f32[16,128]{1,0:T(8,128)S(1)}, u32[]{:S(2)}, u32[]{:S(2)}) collective-permute-start(f32[16,128]{1,0:T(8,128)S(1)} %copy-done), channel_id=1, source_target_pairs={{0,16},{8,24},{16,0},{24,8},{1,17},{9,25},{17,1},{25,9},{2,18},{10... | collective-permute-start | bytes 24584 | tf_op jit(solution)/shard_map/ppermute | solution.py:403
  49.3 12.8 %collective-permute-start.4 = (bf16[2,64,1024]{2,1,0:T(8,128)(2,1)S(1)}, bf16[2,64,1024]{2,1,0:T(8,128)(2,1)S(1)}, u32[]{:S(2)}, u32[]{:S(2)}) collective-permute-start(bf16[2,64,1024]{2,1,0:T(8,128)(2,1)S(1)} %copy-done.4), channel_id=1, source_target_pairs={{0,1},{1,0},{2,3},{3,2},{4,5},{5,4},{6,7},{7,6},{8,9},{9,8},{10,11... | collective-permute-start | bytes 786440 | tf_op jit(solution)/shard_map/ppermute | solution.py:393
  53.7 1.2 %collective-permute-start.16 = (f32[16,128]{1,0:T(8,128)S(1)}, f32[16,128]{1,0:T(8,128)S(1)}, u32[]{:S(2)}, u32[]{:S(2)}) collective-permute-start(f32[16,128]{1,0:T(8,128)S(1)} %add_add_fusion.refs_2_), channel_id=1, source_target_pairs={{0,1},{1,0},{2,3},{3,2},{4,5},{5,4},{6,7},{7,6},{8,9},{9,8},{10,11... | collective-permute-start | bytes 24584 | tf_op jit(solution)/shard_map/ppermute | solution.py:393
  57.9 9.6 %collective-permute-start.17 = (bf16[288,256]{1,0:T(8,128)(2,1)}, bf16[288,256]{1,0:T(8,128)(2,1)S(1)}, u32[]{:S(2)}, u32[]{:S(2)}) collective-permute-start(bf16[288,256]{1,0:T(8,128)(2,1)} %get-tuple-element.55._), channel_id=1, source_target_pairs={{0,2},{1,3},{2,4},{3,5},{4,6},{5,7},{6,0},{7,1},{8,10},{9,11},{10,... | collective-permute-start | bytes 442376 | tf_op jit(solution)/shard_map/ppermute | solution.py:398
  59.2 8.8 %collective-permute-start.18 = (bf16[288,256]{1,0:T(8,128)(2,1)}, bf16[288,256]{1,0:T(8,128)(2,1)S(1)}, u32[]{:S(2)}, u32[]{:S(2)}) collective-permute-start(bf16[288,256]{1,0:T(8,128)(2,1)} %get-tuple-element.60), channel_id=1, source_target_pairs={{0,4},{1,5},{2,6},{3,7},{4,0},{5,1},{6,2},{7,3},{8,12},{9,13},{10,... | collective-permute-start | bytes 442376 | tf_op jit(solution)/shard_map/ppermute | solution.py:398
  60.9 7.1 %collective-permute-start.19 = (bf16[288,256]{1,0:T(8,128)(2,1)}, bf16[288,256]{1,0:T(8,128)(2,1)S(1)}, u32[]{:S(2)}, u32[]{:S(2)}) collective-permute-start(bf16[288,256]{1,0:T(8,128)(2,1)} %get-tuple-element.61), channel_id=1, source_target_pairs={{0,6},{1,7},{2,0},{3,1},{4,2},{5,3},{6,4},{7,5},{8,14},{9,15},{10,... | collective-permute-start | bytes 442376 | tf_op jit(solution)/shard_map/ppermute | solution.py:398
  (17 other events, 22.1 us)

commit v5 on v4

--- a/solution.py
+++ b/solution.py
@@ -26,10 +26,6 @@
 AFTER = pl.BlockSpec(memory_space=pl.ANY)
 
 
-def params(limit=56 << 20):
-    return pltpu.CompilerParams(vmem_limit_bytes=limit)
-
-
 def cost(microseconds):
     return pl.CostEstimate(
         flops=int(microseconds * 1.1e9), bytes_accessed=1 << 20, transcendentals=0
@@ -69,11 +65,6 @@
     return me // 2, me % 2
 
 
-def pack_kernel(key_ref, value_ref, out_ref):
-    out_ref[:, :LANES] = key_ref[...]
-    out_ref[:, LANES:] = value_ref[...]
-
-
 def enter_and_tail(run0, run1):
     t0, t1 = run0[BLOCK - 1 :, :], run1[BLOCK - 1 :, :]
     enter = jnp.concatenate([run0, run1 + t0], axis=0)
@@ -82,10 +73,12 @@
 
 
 def local_states_kernel(
-    x_ref, g_ref, b_ref, c_ref, step_ref, rate_ref, keep_ref, give_ref,
+    x_ref, g_ref, b_ref, c_ref, step_ref, rate_ref, key_ref, value_ref, keep_ref, give_ref, kv_ref,
     pad_ref, high_ref, rest_ref, log_ref, state_ref,
 ):
     _, core = chip_and_core()
+    kv_ref[:, :LANES] = key_ref[...]
+    kv_ref[:, LANES:] = value_ref[...]
     _, _, run0, run1 = running_logs(step_ref, rate_ref, pad_ref)
     enter_log, tail_log, total = enter_and_tail(run0, run1)
     enter, tail = jnp.exp(enter_log), jnp.exp(tail_log)
@@ -185,32 +178,35 @@
         give_ref[1, :, head(h)] = jnp.where(is0, l1, l0)
 
 
-def attention_kernel(chips, most, mask_ref, q_ref, g_ref, *refs):
-    kv_parts = refs[: 2 * chips]
+def attention_kernel(
+    chips, most, mask_ref, q_ref, g_ref, stack_ref, other_stack_ref, _, totals_ref, *refs
+):
+    extra = len(refs) - 15
     (
-        _, out_ref, dq_ref, keep_ref, give_ref,
-        kv_ref, acc_ref, k_ref, k_live_ref, v_ref, q_turned_ref, g_turned_ref, ds_ref, pr_ref,
-    ) = refs[2 * chips :]
+        out_ref, dq_ref, keep_ref, give_ref, sums_ref,
+        slot_ref, kv_ref, acc_ref, k_ref, k_live_ref, v_ref, q_turned_ref, g_turned_ref, ds_ref, wb_ref,
+    ) = refs[extra:]
     count = mask_ref.shape[0]
     columns = QUERY_HEADS * BLOCK
     tokens = q_ref.shape[0]
     chip, core = chip_and_core()
     me = 2 * chip + core
     scale = FACTOR * LOG2E
+    sums = totals_ref[...]
+    for ref in refs[:extra]:
+        sums += ref[...]
+    sums_ref[...] = sums
+    high = sums.astype(BF16)
+    middle = (sums - high.astype(F32)).astype(BF16)
+    low = (sums - high.astype(F32) - middle.astype(F32)).astype(BF16)
+    give_ref[chips * tokens : chips * tokens + 16, :] = jnp.concatenate([high, middle], axis=1)
+    give_ref[chips * tokens + 16 :, :] = jnp.concatenate([low, jnp.zeros_like(low)], axis=1)
     acc_ref[...] = jnp.zeros_like(acc_ref)
     for k in range(chips):
-        for other in range(2):
+        for other, ref in enumerate((stack_ref, other_stack_ref)):
             source = 2 * lax.rem(chip + chips - k, chips) + lax.rem(core + other, 2)
             at = pl.ds(pl.multiple_of(source * tokens, tokens), tokens)
-            kv_ref[at, :] = kv_parts[2 * k + other][...]
-
-    def nth(row, slot):
-        def look(j, carry):
-            found, seen = carry
-            hit = (mask_ref[row, j] == 1) & (seen == slot)
-            return jnp.where(hit, j, found), seen + mask_ref[row, j]
-
-        return lax.fori_loop(0, count, look, (row, 0))
+            kv_ref[at, :] = ref[k]
 
     lower, upper = slice(0, LANES), slice(LANES, 2 * LANES)
     for block in range(tokens // BLOCK):
@@ -218,8 +214,20 @@
         row = me * (tokens // BLOCK) + block
         slots = []
         for slot in range(most):
-            index, allowed = nth(row, slot)
-            live = slot < allowed
+            slot_ref[block, slot] = row
+
+        def note(j, seen):
+            hit = mask_ref[row, j]
+
+            @pl.when(hit == 1)
+            def _():
+                slot_ref[block, seen] = j
+
+            return seen + hit
+
+        allowed = lax.fori_loop(0, count, note, 0)
+        for slot in range(most):
+            index, live = slot_ref[block, slot], slot < allowed
             slots.append((index, live))
             source = pl.ds(pl.multiple_of(index * BLOCK, BLOCK), BLOCK)
             target = slice(slot * BLOCK, (slot + 1) * BLOCK)
@@ -228,10 +236,6 @@
             k_live_ref[target, :] = jnp.where(live, k_tile, jnp.zeros_like(k_tile))
             v_ref[target, lower] = jnp.where(live, v_tile, jnp.zeros_like(v_tile))
             v_ref[target, upper] = jnp.full((BLOCK, LANES), jnp.where(live, 1.0, 0.0), F32).astype(BF16)
-        for h in range(QUERY_HEADS):
-            rows = slice(h * BLOCK, (h + 1) * BLOCK)
-            q_turned_ref[:, rows] = q_ref[at, head(h)].T
-            g_turned_ref[:, rows] = g_ref[at, head(h)].T
         group = 2
         for first in range(0, QUERY_HEADS, group):
             heads = range(first, first + group)
@@ -241,22 +245,22 @@
             scores = dot(q, k_ref[...], 1, 1)
             best = jnp.max(scores, axis=1, keepdims=True)
             weights = jnp.exp2((scores - best) * scale)
-            both = dot(weights.astype(BF16), v_ref[...], 1, 0)
+            wb_ref[rows, :] = weights.astype(BF16)
+            both = dot(wb_ref[rows, :], v_ref[...], 1, 0)
             inverse = 1.0 / both[:, upper]
             out = both[:, lower] * inverse
             delta = jnp.sum(out * g.astype(F32), axis=1, keepdims=True)
-            probs = weights * jnp.concatenate([inverse] * most, axis=1)
             dprobs = dot(g, v_ref[:, lower], 1, 1)
-            ds = (probs * (dprobs - delta)).astype(BF16)
-            pr_ref[rows, :] = probs.astype(BF16)
-            ds_ref[rows, :] = ds
-            dq = (dot(ds, k_live_ref[...], 1, 0) * FACTOR).astype(BF16)
+            ds_ref[rows, :] = (weights * (dprobs - delta)).astype(BF16)
+            dq = (dot(ds_ref[rows, :], k_live_ref[...], 1, 0) * (inverse * FACTOR)).astype(BF16)
+            q_turned_ref[:, rows] = (q.astype(F32) * inverse).astype(BF16).T
+            g_turned_ref[:, rows] = (g.astype(F32) * inverse).astype(BF16).T
             for place, h in enumerate(heads):
                 part = slice(place * BLOCK, (place + 1) * BLOCK)
                 out_ref[at, head(h)] = out[part]
                 dq_ref[at, head(h)] = dq[part]
         dk = dot(q_turned_ref[...], ds_ref[...], 1, 0)
-        dv = dot(g_turned_ref[...], pr_ref[...], 1, 0)
+        dv = dot(g_turned_ref[...], wb_ref[...], 1, 0)
         for slot, (index, live) in enumerate(slots):
             source = slice(slot * BLOCK, (slot + 1) * BLOCK)
 
@@ -269,31 +273,32 @@
     for k in range(chips):
         mine = pl.multiple_of((2 * k + core) * tokens, tokens)
         other = pl.multiple_of((2 * k + 1 - core) * tokens, tokens)
-        keep_ref[k] = acc_ref[:, pl.ds(mine, tokens)].astype(BF16)
-        give_ref[k] = acc_ref[:, pl.ds(other, tokens)].astype(BF16)
-
-
-def pair_sum_kernel(chips, keep_ref, recv_ref, sums_ref, other_ref, own_ref, total_ref, *message_refs):
+        rows = slice(k * tokens, (k + 1) * tokens)
+        keep_ref[rows, :] = acc_ref[:, pl.ds(mine, tokens)].astype(BF16)
+        give_ref[rows, :] = acc_ref[:, pl.ds(other, tokens)].astype(BF16)
+
+
+def pair_sum_kernel(chips, keep_ref, recv_ref, sums_ref, own_ref, total_ref, *message_refs):
     chip, _ = chip_and_core()
     rows = own_ref.shape[0]
-    own_ref[...] = keep_ref[chip].astype(F32) + recv_ref[chip].astype(F32)
-    total = sums_ref[...] + other_ref[...]
+    at = pl.ds(pl.multiple_of(chip * rows, rows), rows)
+    own_ref[...] = keep_ref[at, :].astype(F32) + recv_ref[at, :].astype(F32)
+    total = sums_ref[...] + whole_sums(recv_ref[chips * rows :, :])
     total_ref[...] = total
     high = total.astype(BF16)
     middle = (total - high.astype(F32)).astype(BF16)
     low = (total - high.astype(F32) - middle.astype(F32)).astype(BF16)
-    tail = jnp.concatenate(
-        [
-            jnp.concatenate([high, middle], axis=1),
-            jnp.concatenate([low, jnp.zeros_like(low)], axis=1),
-        ],
-        axis=0,
-    )
     for k in range(1, chips):
-        target = lax.rem(chip + k, chips)
-        both = keep_ref[target].astype(F32) + recv_ref[target].astype(F32)
+        target = pl.ds(pl.multiple_of(lax.rem(chip + k, chips) * rows, rows), rows)
+        both = keep_ref[target, :].astype(F32) + recv_ref[target, :].astype(F32)
         message_refs[k - 1][:rows, :] = both.astype(BF16)
-        message_refs[k - 1][rows:, :] = tail
+        message_refs[k - 1][rows : rows + 16, :] = jnp.concatenate([high, middle], axis=1)
+        message_refs[k - 1][rows + 16 :, :] = jnp.concatenate([low, jnp.zeros_like(low)], axis=1)
+
+
+def whole_sums(tail):
+    tail = tail.astype(F32)
+    return tail[:16, :LANES] + tail[:16, LANES:] + tail[16:, :LANES]
 
 
 def owner_sum_kernel(chips, tokens_all, own_ref, sums_ref, *refs):
@@ -303,8 +308,7 @@
     sums = sums_ref[...]
     for part in parts:
         total += part[:rows, :].astype(F32)
-        tail = part[rows:, :].astype(F32)
-        sums += tail[:16, :LANES] + tail[:16, LANES:] + tail[16:, :LANES]
+        sums += whole_sums(part[rows:, :])
     dk_ref[...] = (total[:LANES].T * FACTOR).astype(BF16)
     dv_ref[...] = total[LANES:].T.astype(BF16)
     ones = jnp.ones((8, LANES), F32)
@@ -314,11 +318,13 @@
     skip_ref[...] = skip[0:1, :]
 
 
-def inner_kernel(
-    x_ref, g_ref, b_ref, c_ref, step_ref, rate_ref, skip_ref, _,
-    y_ref, dx_ref, db_ref, dc_ref, sums_ref,
-    pad_ref, inner_ref, dinner_ref, m_ref, runt_ref,
-):
+def inner_kernel(chips, x_ref, g_ref, b_ref, c_ref, step_ref, rate_ref, skip_ref, _, *refs):
+    (
+        stack_ref, y_ref, dx_ref, db_ref, dc_ref, sums_ref,
+        pad_ref, inner_ref, dinner_ref, m_ref, runt_ref,
+    ) = refs[chips:]
+    for k in range(chips):
+        stack_ref[k] = refs[k][...]
     tokens = 2 * BLOCK
     flat0, flat1, run0, run1 = running_logs(step_ref, rate_ref, pad_ref)
     own = jnp.concatenate([run0, run1], axis=0)
@@ -403,14 +409,14 @@
     return lax.ppermute(array, "dp", [(i, (i + k) % n) for i in range(n)])
 
 
-def call(kernel, outs, ins, scratch, microseconds, name):
+def call(kernel, outs, ins, scratch, microseconds, name, limit=16):
     return pl.pallas_call(
         kernel,
         out_shape=tuple(jax.ShapeDtypeStruct(*out) for out in outs),
         in_specs=ins,
         out_specs=(VMEM,) * len(outs),
         scratch_shapes=scratch,
-        compiler_params=params(),
+        compiler_params=pltpu.CompilerParams(vmem_limit_bytes=limit << 20),
         cost_estimate=cost(microseconds),
         name=name,
     )
@@ -419,6 +425,7 @@
 def body(query, key, value, ssm_input, in_b, in_c, step, rate_log, skip, block_mask, grad_out):
     n = lax.axis_size("seq")
     chips = n // 2
+    replicas = lax.axis_size("dp")
     tokens = query.shape[1]
     blocks = block_mask.shape[1]
     most = 3 * blocks // 8
@@ -426,19 +433,11 @@
     q, g, x = query[0], grad_out[0], ssm_input[0]
     b, c, steps = in_b[0], in_c[0], step[0].T
 
-    (kv,) = call(pack_kernel, [((tokens, 2 * LANES), BF16)], [VMEM] * 2, [], 1, "pack_kv")(
-        key[0], value[0]
-    )
-    kv_parts = [kv, swapped(kv)]
-    for k in range(1, chips):
-        part = from_chip(kv, k)
-        kv_parts += [part, swapped(part)]
-
     half = ((4, HALF, WIDE + LANES), F32)
-    keep, give = call(
+    keep, give, kv = call(
         local_states_kernel,
-        [half, half],
-        [VMEM] * 5 + [SMEM],
+        [half, half, ((tokens, 2 * LANES), BF16)],
+        [VMEM] * 5 + [SMEM] + [VMEM] * 2,
         [
             pltpu.VMEM((LANES, tokens), F32),
             pltpu.VMEM((tokens, WIDE), BF16),
@@ -448,8 +447,9 @@
         ],
         4,
         "local_states",
-    )(x, g, b, c, steps, rate_log)
+    )(x, g, b, c, steps, rate_log, key[0], value[0])
     received = swapped(give)
+    kv_parts = [kv] + [from_chip(kv, k) for k in range(1, chips)]
     messages = call(
         lambda *refs: combine_kernel(chips, *refs),
         [((HALF, WIDE + LANES), BF16)] * (chips - 1),
@@ -460,10 +460,13 @@
     )(keep, received)
     arrived = [from_chip(messages[k - 1], k) for k in range(1, chips)]
 
-    inner_y, inner_dx, inner_db, inner_dc, sums = call(
-        inner_kernel,
-        [((tokens, WIDE), F32)] * 2 + [((tokens, NS), F32)] * 2 + [((2 * HS, LANES), F32)],
-        [VMEM] * 5 + [SMEM] * 2 + [AFTER],
+    stack, inner_y, inner_dx, inner_db, inner_dc, sums = call(
+        lambda *refs: inner_kernel(chips, *refs),
+        [((chips, tokens, 2 * LANES), BF16)]
+        + [((tokens, WIDE), F32)] * 2
+        + [((tokens, NS), F32)] * 2
+        + [((2 * HS, LANES), F32)],
+        [VMEM] * 5 + [SMEM] * 2 + [AFTER] + [VMEM] * chips,
         [
             pltpu.VMEM((LANES, tokens), F32),
             pltpu.VMEM((tokens, tokens), F32),
@@ -473,7 +476,8 @@
         ],
         5,
         "chunk_inner",
-    )(x, g, b, c, steps, rate_log, skip, messages[0])
+    )(x, g, b, c, steps, rate_log, skip, messages[0], *kv_parts)
+    other_stack = swapped(stack)
 
     entering = ((2, HALF, WIDE), BF16)
     own, give, totals = call(
@@ -485,16 +489,21 @@
         "chain_states",
     )(keep, received, sums, *arrived)
     other = swapped(give)
-    replicas = lax.axis_size("dp")
-    summed = totals + sum(turned(totals, k) for k in range(1, replicas))
+    replicated = [turned(totals, k) for k in range(1, replicas)]
 
     columns = QUERY_HEADS * BLOCK
-    split = ((chips, 2 * LANES, tokens), BF16)
-    attention, dq, keep, give = call(
+    attention, dq, keep, give, sums = call(
         lambda *refs: attention_kernel(chips, most, *refs),
-        [((tokens, columns), F32), ((tokens, columns), BF16), split, split],
-        [SMEM] + [VMEM] * (2 + n) + [AFTER],
         [
+            ((tokens, columns), F32),
+            ((tokens, columns), BF16),
+            ((chips * 2 * LANES, tokens), BF16),
+            ((chips * 2 * LANES + 32, tokens), BF16),
+            ((2 * HS, LANES), F32),
+        ],
+        [SMEM] + [VMEM] * 4 + [AFTER] + [VMEM] * replicas,
+        [
+            pltpu.SMEM((2, most), jnp.int32),
             pltpu.VMEM((every, 2 * LANES), BF16),
             pltpu.VMEM((2 * LANES, every), F32),
             pltpu.VMEM((most * BLOCK, LANES), BF16),
@@ -507,16 +516,17 @@
         ],
         10,
         "attention",
-    )(block_mask[0], q, g, *kv_parts, totals)
+        18 + most,
+    )(block_mask[0], q, g, stack, other_stack, other, totals, *replicated)
     partial, summed, *messages = call(
         lambda *refs: pair_sum_kernel(chips, *refs),
         [((2 * LANES, tokens), F32), ((2 * HS, LANES), F32)]
         + [((2 * LANES + 32, tokens), BF16)] * (chips - 1),
-        [VMEM] * 4,
+        [VMEM] * 3,
         [],
         1,
         "pair_sum",
-    )(keep, swapped(give), summed, swapped(summed))
+    )(keep, swapped(give), sums)
     arrived = [from_chip(messages[k - 1], k) for k in range(1, chips)]
 
     y, dx, db, dc = call(

time: 71.1 us -> 62.5 us (0.88)
  Pallas kernels: 39.2 us -> 20.1 us
  waiting for transfers between devices: 6.91 us -> 16.9 us
  local copies, waits for them, and re-layouts: 4.75 us -> 6.83 us
  starting transfers between devices: 19 us -> 17.5 us
    ppermute x9, waiting for transfers between devices: 1.31 us -> 10.5 us  [from_chip(): return lax.ppermute(array, 'seq', [(i, (i + 2 * k) % n) for i in range(n)])]
    pallas_call x3 -> x2, Pallas kernels: 11.1 us -> 5.58 us  [the longest x1 2.93 us: body(): call(local_states_kernel, [half, half, ((tokens, 2 * LANES), BF16)], [VME...]
    pallas_call x1, Pallas kernels: 13.7 us -> 9.9 us  [body(): call(lambda *refs: attention_kernel(chips, most, *refs), [((tokens, colum...]
    pallas_call x1, Pallas kernels: 3.17 us -> 0.67 us  [body(): call(lambda *refs: chain_kernel(chips, *refs), [entering, entering, ((2 *...]
    pallas_call x1, Pallas kernels: 2.6 us -> 0.22 us  [body(): call(lambda *refs: combine_kernel(chips, *refs), [((HALF, WIDE + LANES),...]
    unnamed x42 -> x34, local copies, waits for them, and re-layouts: 4.75 us -> 6.83 us
    pallas_call x1, Pallas kernels: 2.12 us -> 0.13 us  [body(): call(lambda *refs: pair_sum_kernel(chips, *refs), [((2 * LANES, tokens),...]
    pallas_call x1, Pallas kernels: 4.64 us -> 2.78 us  [body(): call(outer_kernel, [((tokens, WIDE), BF16)] * 2 + [((tokens, NS), BF16)]...]
  transfers between devices with their start and end apart: 20 -> 16, of which waited for: 5 -> 9; matrix products, arithmetic and copies ran while one was open for 0% -> 0% of each run, Pallas kernels for 26% -> 10%
where the time goes in v5:
time: 62.5 us; the launch traced here: 62.1 us
  Pallas kernels  20.1 us (32%)
  starting transfers between devices  17.5 us (28%)
  waiting for transfers between devices  16.9 us (27%)
  local copies, waits for them, and re-layouts  6.83 us (11%)
  between operations  0.79 us (1%)
    ppermute x9, starting transfers between devices, from_chip(): return lax.ppermute(array, 'seq', [(i, (i + 2 * k) % n) for i in range(n)])  12.2 us
    ppermute x9, waiting for transfers between devices, from_chip(): return lax.ppermute(array, 'seq', [(i, (i + 2 * k) % n) for i in range(n)])  10.5 us
    pallas_call x1, Pallas kernels, body(): call(lambda *refs: attention_kernel(chips, most, *refs), [((tokens, colum...  9.9 us
    unnamed x34, local copies, waits for them, and re-layouts  6.83 us
    ppermute x3, starting transfers between devices, turned(): return lax.ppermute(array, 'dp', [(i, (i + k) % n) for i in range(n)])  4.67 us
    ppermute x3, waiting for transfers between devices, turned(): return lax.ppermute(array, 'dp', [(i, (i + k) % n) for i in range(n)])  4.44 us
    pallas_call x1, Pallas kernels, body(): call(local_states_kernel, [half, half, ((tokens, 2 * LANES), BF16)], [VME...  2.93 us
    pallas_call x1, Pallas kernels, body(): call(outer_kernel, [((tokens, WIDE), BF16)] * 2 + [((tokens, NS), BF16)]...  2.78 us
  transfers between devices with their start and end apart: 16, of which 9 were waited for; matrix products, arithmetic and copies ran while one was open for 0% of the time, Pallas kernels for 10%

profile of v5, /device:TPU:0, one launch (start us, length us, event | category | flops | bytes accessed | tf_op | source)
XLA Modules:
  0.0 62.1 jit_solution(15597827854079234064)
XLA Ops:
  0.7 1.0 %copy-done.1 = bf16[1,256,1024]{2,1,0:T(8,128)(2,1)S(1)} copy-done((bf16[1,256,1024]{2,1,0:T(8,128)(2,1)S(1)}, bf16[1,256,1024]{2,1,0:T(8,128)(2,1)}, u32[]{:S(2)}) %copy-start.1) | copy-done | bytes 524312
  1.7 1.0 %copy-done.3 = bf16[1,256,1024]{2,1,0:T(8,128)(2,1)S(1)} copy-done((bf16[1,256,1024]{2,1,0:T(8,128)(2,1)S(1)}, bf16[1,256,1024]{2,1,0:T(8,128)(2,1)}, u32[]{:S(2)}) %copy-start.3) | copy-done | bytes 524312
  2.7 0.8 %copy-done.5 = bf16[1,256,128]{2,1,0:T(8,128)(2,1)S(1)} copy-done((bf16[1,256,128]{2,1,0:T(8,128)(2,1)S(1)}, bf16[1,256,128]{2,1,0:T(8,128)(2,1)}, u32[]{:S(2)}) %copy-start.5) | copy-done | bytes 65560
  3.6 0.8 %copy-done.6 = bf16[1,256,128]{2,1,0:T(8,128)(2,1)S(1)} copy-done((bf16[1,256,128]{2,1,0:T(8,128)(2,1)S(1)}, bf16[1,256,128]{2,1,0:T(8,128)(2,1)}, u32[]{:S(2)}) %copy-start.6) | copy-done | bytes 65560
  4.4 0.8 %copy-done.7 = bf16[1,256,128]{2,1,0:T(8,128)(2,1)S(1)} copy-done((bf16[1,256,128]{2,1,0:T(8,128)(2,1)S(1)}, bf16[1,256,128]{2,1,0:T(8,128)(2,1)}, u32[]{:S(2)}) %copy-start.7) | copy-done | bytes 65560
  5.3 0.8 %copy-done.9 = bf16[1,256,128]{2,1,0:T(8,128)(2,1)S(1)} copy-done((bf16[1,256,128]{2,1,0:T(8,128)(2,1)S(1)}, bf16[1,256,128]{2,1,0:T(8,128)(2,1)}, u32[]{:S(2)}) %copy-start.9) | copy-done | bytes 65560
  7.4 2.9 %local_states.1 = (f32[4,64,1152]{2,1,0:T(8,128)S(1)}, f32[4,64,1152]{2,1,0:T(8,128)S(1)}, bf16[256,256]{1,0:T(8,128)(2,1)S(1)}) custom-call(bf16[256,1024]{1,0:T(8,128)(2,1)S(1)} %bitcast.21, bf16[256,1024]{1,0:T(8,128)(2,1)S(1)} %bitcast.24, bf16[256,128]{1,0:T(8,128)(2,1)S(1)} %bitcast.30, bf16[256,128]{1,0:T(8,128)(2,1)S(1)} %bitcast.33, ...), custom_call_target="tpu_custom_call" | custom-call | flops 4400000000 | bytes 1048576 | tf_op jit(solution)/shard_map/local_states/pallas_call | solution.py:437
  10.9 3.5 %collective-permute-start.3 = (bf16[256,256]{1,0:T(8,128)(2,1)S(1)}, bf16[256,256]{1,0:T(8,128)(2,1)S(1)}, u32[]{:S(2)}, u32[]{:S(2)}) collective-permute-start(bf16[256,256]{1,0:T(8,128)(2,1)S(1)} %get-tuple-element.45.refs_8_), channel_id=1, source_target_pairs={{0,6},{1,7},{2,0},{3,1},{4,2},{5,3},{6,4},{7,5},{8,14},{9,15},{10,... | collective-permute-start | bytes 393224 | tf_op jit(solution)/shard_map/ppermute | solution.py:404
  15.8 1.0 %collective-permute-start.5 = (bf16[64,1152]{1,0:T(8,128)(2,1)S(1)}, bf16[64,1152]{1,0:T(8,128)(2,1)S(1)}, u32[]{:S(2)}, u32[]{:S(2)}) collective-permute-start(bf16[64,1152]{1,0:T(8,128)(2,1)S(1)} %get-tuple-element.47), channel_id=1, source_target_pairs={{0,4},{1,5},{2,6},{3,7},{4,0},{5,1},{6,2},{7,3},{8,12},{9,13},{10,... | collective-permute-start | bytes 442376 | tf_op jit(solution)/shard_map/ppermute | solution.py:404
  16.8 2.9 %collective-permute-start.6 = (bf16[64,1152]{1,0:T(8,128)(2,1)S(1)}, bf16[64,1152]{1,0:T(8,128)(2,1)S(1)}, u32[]{:S(2)}, u32[]{:S(2)}) collective-permute-start(bf16[64,1152]{1,0:T(8,128)(2,1)S(1)} %get-tuple-element.48), channel_id=1, source_target_pairs={{0,6},{1,7},{2,0},{3,1},{4,2},{5,3},{6,4},{7,5},{8,14},{9,15},{10,... | collective-permute-start | bytes 442376 | tf_op jit(solution)/shard_map/ppermute | solution.py:404
  19.7 1.0 %collective-permute-start.4 = (bf16[64,1152]{1,0:T(8,128)(2,1)S(1)}, bf16[64,1152]{1,0:T(8,128)(2,1)S(1)}, u32[]{:S(2)}, u32[]{:S(2)}) collective-permute-start(bf16[64,1152]{1,0:T(8,128)(2,1)S(1)} %get-tuple-element.44.refs_7_), channel_id=1, source_target_pairs={{0,2},{1,3},{2,4},{3,5},{4,6},{5,7},{6,0},{7,1},{8,10},{9,11},{10,... | collective-permute-start | bytes 442376 | tf_op jit(solution)/shard_map/ppermute | solution.py:404
  20.7 2.9 %collective-permute-done.2.refs_10_ = bf16[256,256]{1,0:T(8,128)(2,1)S(1)} collective-permute-done((bf16[256,256]{1,0:T(8,128)(2,1)S(1)}, bf16[256,256]{1,0:T(8,128)(2,1)S(1)}, u32[]{:S(2)}, u32[]{:S(2)}) %collective-permute-start.2) | collective-permute-done | bytes 131104 | tf_op jit(solution)/shard_map/ppermute | solution.py:404
  23.6 2.6 %chunk_inner.1 = (bf16[4,256,256]{2,1,0:T(8,128)(2,1)S(1)}, f32[256,1024]{1,0:T(8,128)S(1)}, f32[256,1024]{1,0:T(8,128)S(1)}, f32[256,128]{1,0:T(8,128)S(1)}, f3...) custom-call(bf16[256,1024]{1,0:T(8,128)(2,1)S(1)} %bitcast.22, bf16[256,1024]{1,0:T(8,128)(2,1)S(1)} %bitcast.25, ...), custom_call_target="tpu_custom_call" | custom-call | flops 5500000256 | bytes 1048576 | tf_op jit(solution)/shard_map/chunk_inner/pallas_call | solution.py:463
  26.3 2.8 %collective-permute-done.5.refs_4_ = bf16[64,1152]{1,0:T(8,128)(2,1)S(1)} collective-permute-done((bf16[64,1152]{1,0:T(8,128)(2,1)S(1)}, bf16[64,1152]{1,0:T(8,128)(2,1)S(1)}, u32[]{:S(2)}, u32[]{:S(2)}) %collective-permute-start.5) | collective-permute-done | bytes 147488 | tf_op jit(solution)/shard_map/ppermute | solution.py:404
  29.9 3.7 %collective-permute-start.11 = (f32[16,128]{1,0:T(8,128)S(1)}, f32[16,128]{1,0:T(8,128)S(1)}, u32[]{:S(2)}, u32[]{:S(2)}) collective-permute-start(f32[16,128]{1,0:T(8,128)S(1)} %get-tuple-element.52.refs_6_), channel_id=1, source_target_pairs={{0,24},{8,0},{16,8},{24,16},{1,25},{9,1},{17,9},{25,17},{2,26},{10... | collective-permute-start | bytes 24584 | tf_op jit(solution)/shard_map/ppermute | solution.py:409
  33.5 1.0 %collective-permute-start.9 = (f32[16,128]{1,0:T(8,128)S(1)}, f32[16,128]{1,0:T(8,128)S(1)}, u32[]{:S(2)}, u32[]{:S(2)}) collective-permute-start(f32[16,128]{1,0:T(8,128)S(1)} %get-tuple-element.52.refs_6_), channel_id=1, source_target_pairs={{0,8},{8,16},{16,24},{24,0},{1,9},{9,17},{17,25},{25,1},{2,10},{10... | collective-permute-start | bytes 24584 | tf_op jit(solution)/shard_map/ppermute | solution.py:409
  34.9 3.2 %collective-permute-done.10.refs_8_ = f32[16,128]{1,0:T(8,128)S(1)} collective-permute-done((f32[16,128]{1,0:T(8,128)S(1)}, f32[16,128]{1,0:T(8,128)S(1)}, u32[]{:S(2)}, u32[]{:S(2)}) %collective-permute-start.10) | collective-permute-done | bytes 8224 | tf_op jit(solution)/shard_map/ppermute | solution.py:409
  38.1 0.9 %collective-permute-done.9.refs_7_ = f32[16,128]{1,0:T(8,128)S(1)} collective-permute-done((f32[16,128]{1,0:T(8,128)S(1)}, f32[16,128]{1,0:T(8,128)S(1)}, u32[]{:S(2)}, u32[]{:S(2)}) %collective-permute-start.9) | collective-permute-done | bytes 8224 | tf_op jit(solution)/shard_map/ppermute | solution.py:409
  39.0 9.9 %attention.1 = (f32[256,1024]{1,0:T(8,128)S(1)}, bf16[256,1024]{1,0:T(8,128)(2,1)}, bf16[1024,256]{1,0:T(8,128)(2,1)S(1)}, bf16[1056,256]{1,0:T(8,128)(2,1)S(1)}, f32[16,128]{1,0:T(8,128)S(1)}) custom-call(s32[16,16]{1,0:T(8,128)S(1)} %bitcast.36, bf16[256,1024]{1,0:T(8,128)(2,1)S(1)} %bitcast.20, bf16[256,1024]{1,0:T(8,128)(2,1)S(1)} %bitcast.26, ...), custom_call_target="tpu_custom_call" | custom-call | flops 11000000512 | bytes 1048576 | tf_op jit(solution)/shard_map/attention/pallas_call | solution.py:495
  48.9 1.9 %collective-permute-done.12.refs_1_ = bf16[1056,256]{1,0:T(8,128)(2,1)S(1)} collective-permute-done((bf16[1056,256]{1,0:T(8,128)(2,1)S(1)}, bf16[1056,256]{1,0:T(8,128)(2,1)S(1)}, u32[]{:S(2)}, u32[]{:S(2)}) %collective-permute-start.12) | collective-permute-done | bytes 540704 | tf_op jit(solution)/shard_map/ppermute | solution.py:399
  51.6 1.3 %collective-permute-start.15 = (bf16[288,256]{1,0:T(8,128)(2,1)S(1)}, bf16[288,256]{1,0:T(8,128)(2,1)S(1)}, u32[]{:S(2)}, u32[]{:S(2)}) collective-permute-start(bf16[288,256]{1,0:T(8,128)(2,1)S(1)} %get-tuple-element.67), channel_id=1, source_target_pairs={{0,6},{1,7},{2,0},{3,1},{4,2},{5,3},{6,4},{7,5},{8,14},{9,15},{10,... | collective-permute-start | bytes 442376 | tf_op jit(solution)/shard_map/ppermute | solution.py:404
  53.6 2.8 %chunk_outer.1 = (bf16[256,1024]{1,0:T(8,128)(2,1)}, bf16[256,1024]{1,0:T(8,128)(2,1)}, bf16[256,128]{1,0:T(8,128)(2,1)}, bf16[256,128]{1,0:T(8,128)(2,1)}) custom-call(bf16[256,1024]{1,0:T(8,128)(2,1)S(1)} %bitcast.23, bf16[256,1024]{1,0:T(8,128)(2,1)S(1)} %bitcast.27, bf16[256,128]{1,0:T(8,128)(2,1)S(1)} %bitcast.32, bf16[256,128]{1,0:T(8,128)(2,1)S(1)} %bitcast.35, ...), custom_call_target="tpu_custom_call" | custom-call | flops 3300000000 | bytes 1048576 | tf_op jit(solution)/shard_map/chunk_outer/pallas_call | solution.py:532
  56.9 1.4 %collective-permute-done.15.refs_4_ = bf16[288,256]{1,0:T(8,128)(2,1)S(1)} collective-permute-done((bf16[288,256]{1,0:T(8,128)(2,1)S(1)}, bf16[288,256]{1,0:T(8,128)(2,1)S(1)}, u32[]{:S(2)}, u32[]{:S(2)}) %collective-permute-start.15) | collective-permute-done | bytes 147488 | tf_op jit(solution)/shard_map/ppermute | solution.py:404
  58.3 3.0 %collective-permute-done.13.refs_2_ = bf16[288,256]{1,0:T(8,128)(2,1)S(1)} collective-permute-done((bf16[288,256]{1,0:T(8,128)(2,1)S(1)}, bf16[288,256]{1,0:T(8,128)(2,1)S(1)}, u32[]{:S(2)}, u32[]{:S(2)}) %collective-permute-start.13) | collective-permute-done | bytes 147488 | tf_op jit(solution)/shard_map/ppermute | solution.py:404
  (50 shorter events, 7.3 us)
Async XLA Ops:
  10.4 5.1 %collective-permute-start = (f32[4,64,1152]{2,1,0:T(8,128)S(1)}, f32[4,64,1152]{2,1,0:T(8,128)S(1)}, u32[]{:S(2)}, u32[]{:S(2)}) collective-permute-start(f32[4,64,1152]{2,1,0:T(8,128)S(1)} %get-tuple-element.43), channel_id=1, source_target_pairs={{0,1},{1,0},{2,3},{3,2},{4,5},{5,4},{6,7},{7,6},{8,9},{9,8},{10,11... | collective-permute-start | bytes 3538952 | tf_op jit(solution)/shard_map/ppermute | solution.py:399
  10.9 8.8 %collective-permute-start.3 = (bf16[256,256]{1,0:T(8,128)(2,1)S(1)}, bf16[256,256]{1,0:T(8,128)(2,1)S(1)}, u32[]{:S(2)}, u32[]{:S(2)}) collective-permute-start(bf16[256,256]{1,0:T(8,128)(2,1)S(1)} %get-tuple-element.45.refs_8_), channel_id=1, source_target_pairs={{0,6},{1,7},{2,0},{3,1},{4,2},{5,3},{6,4},{7,5},{8,14},{9,15},{10,... | collective-permute-start | bytes 393224 | tf_op jit(solution)/shard_map/ppermute | solution.py:404
  14.4 9.1 %collective-permute-start.2 = (bf16[256,256]{1,0:T(8,128)(2,1)S(1)}, bf16[256,256]{1,0:T(8,128)(2,1)S(1)}, u32[]{:S(2)}, u32[]{:S(2)}) collective-permute-start(bf16[256,256]{1,0:T(8,128)(2,1)S(1)} %get-tuple-element.45.refs_8_), channel_id=1, source_target_pairs={{0,4},{1,5},{2,6},{3,7},{4,0},{5,1},{6,2},{7,3},{8,12},{9,13},{10,... | collective-permute-start | bytes 393224 | tf_op jit(solution)/shard_map/ppermute | solution.py:404
  14.9 8.6 %collective-permute-start.1 = (bf16[256,256]{1,0:T(8,128)(2,1)S(1)}, bf16[256,256]{1,0:T(8,128)(2,1)S(1)}, u32[]{:S(2)}, u32[]{:S(2)}) collective-permute-start(bf16[256,256]{1,0:T(8,128)(2,1)S(1)} %get-tuple-element.45.refs_8_), channel_id=1, source_target_pairs={{0,2},{1,3},{2,4},{3,5},{4,6},{5,7},{6,0},{7,1},{8,10},{9,11},{10,... | collective-permute-start | bytes 393224 | tf_op jit(solution)/shard_map/ppermute | solution.py:404
  15.5 8.1 %copy-start.2 = (bf16[1,256,1024]{2,1,0:T(8,128)(2,1)S(1)}, bf16[1,256,1024]{2,1,0:T(8,128)(2,1)}, u32[]{:S(2)}) copy-start(bf16[1,256,1024]{2,1,0:T(8,128)(2,1)} %param.14) | copy-start | bytes 1572868
  15.5 8.1 %copy-start.4 = (bf16[1,256,1024]{2,1,0:T(8,128)(2,1)S(1)}, bf16[1,256,1024]{2,1,0:T(8,128)(2,1)}, u32[]{:S(2)}) copy-start(bf16[1,256,1024]{2,1,0:T(8,128)(2,1)} %param.21) | copy-start | bytes 1572868
  15.5 8.1 %copy-start.8 = (bf16[1,256,128]{2,1,0:T(8,128)(2,1)S(1)}, bf16[1,256,128]{2,1,0:T(8,128)(2,1)}, u32[]{:S(2)}) copy-start(bf16[1,256,128]{2,1,0:T(8,128)(2,1)} %param.15) | copy-start | bytes 196612
  15.5 8.1 %copy-start.10 = (bf16[1,256,128]{2,1,0:T(8,128)(2,1)S(1)}, bf16[1,256,128]{2,1,0:T(8,128)(2,1)}, u32[]{:S(2)}) copy-start(bf16[1,256,128]{2,1,0:T(8,128)(2,1)} %param.16) | copy-start | bytes 196612
  15.5 8.1 %copy-start.14 = (f32[8]{0:T(128)S(1)}, f32[8]{0:T(128)}, u32[]{:S(2)}) copy-start(f32[8]{0:T(128)} %refs_6_.1) | copy-start | bytes 100
  15.8 13.3 %collective-permute-start.5 = (bf16[64,1152]{1,0:T(8,128)(2,1)S(1)}, bf16[64,1152]{1,0:T(8,128)(2,1)S(1)}, u32[]{:S(2)}, u32[]{:S(2)}) collective-permute-start(bf16[64,1152]{1,0:T(8,128)(2,1)S(1)} %get-tuple-element.47), channel_id=1, source_target_pairs={{0,4},{1,5},{2,6},{3,7},{4,0},{5,1},{6,2},{7,3},{8,12},{9,13},{10,... | collective-permute-start | bytes 442376 | tf_op jit(solution)/shard_map/ppermute | solution.py:404
  16.8 12.3 %collective-permute-start.6 = (bf16[64,1152]{1,0:T(8,128)(2,1)S(1)}, bf16[64,1152]{1,0:T(8,128)(2,1)S(1)}, u32[]{:S(2)}, u32[]{:S(2)}) collective-permute-start(bf16[64,1152]{1,0:T(8,128)(2,1)S(1)} %get-tuple-element.48), channel_id=1, source_target_pairs={{0,6},{1,7},{2,0},{3,1},{4,2},{5,3},{6,4},{7,5},{8,14},{9,15},{10,... | collective-permute-start | bytes 442376 | tf_op jit(solution)/shard_map/ppermute | solution.py:404
  19.7 9.4 %collective-permute-start.4 = (bf16[64,1152]{1,0:T(8,128)(2,1)S(1)}, bf16[64,1152]{1,0:T(8,128)(2,1)S(1)}, u32[]{:S(2)}, u32[]{:S(2)}) collective-permute-start(bf16[64,1152]{1,0:T(8,128)(2,1)S(1)} %get-tuple-element.44.refs_7_), channel_id=1, source_target_pairs={{0,2},{1,3},{2,4},{3,5},{4,6},{5,7},{6,0},{7,1},{8,10},{9,11},{10,... | collective-permute-start | bytes 442376 | tf_op jit(solution)/shard_map/ppermute | solution.py:404
  26.2 12.7 %collective-permute-start.8 = (bf16[4,256,256]{2,1,0:T(8,128)(2,1)S(1)}, bf16[4,256,256]{2,1,0:T(8,128)(2,1)S(1)}, u32[]{:S(2)}, u32[]{:S(2)}) collective-permute-start(bf16[4,256,256]{2,1,0:T(8,128)(2,1)S(1)} %get-tuple-element.51.refs_3_), channel_id=1, source_target_pairs={{0,1},{1,0},{2,3},{3,2},{4,5},{5,4},{6,7},{7,6},{8,9},{9,8},{10,11... | collective-permute-start | bytes 1572872 | tf_op jit(solution)/shard_map/ppermute | solution.py:399
  29.1 9.9 %copy-start = (bf16[1,256,1024]{2,1,0:T(8,128)(2,1)S(1)}, bf16[1,256,1024]{2,1,0:T(8,128)(2,1)}, u32[]{:S(2)}) copy-start(bf16[1,256,1024]{2,1,0:T(8,128)(2,1)} %param.11) | copy-start | bytes 1572868
  29.1 9.9 %copy-start.11 = (s32[1,16,16]{2,1,0:T(8,128)S(1)}, s32[1,16,16]{2,1,0:T(8,128)}, u32[]{:S(2)}) copy-start(s32[1,16,16]{2,1,0:T(8,128)} %param.20) | copy-start | bytes 3076
  29.8 9.2 %collective-permute-start.7 = (bf16[2,64,1024]{2,1,0:T(8,128)(2,1)S(1)}, bf16[2,64,1024]{2,1,0:T(8,128)(2,1)S(1)}, u32[]{:S(2)}, u32[]{:S(2)}) collective-permute-start(bf16[2,64,1024]{2,1,0:T(8,128)(2,1)S(1)} %get-tuple-element.50), channel_id=1, source_target_pairs={{0,1},{1,0},{2,3},{3,2},{4,5},{5,4},{6,7},{7,6},{8,9},{9,8},{10,11... | collective-permute-start | bytes 786440 | tf_op jit(solution)/shard_map/ppermute | solution.py:399
  29.9 5.0 %collective-permute-start.11 = (f32[16,128]{1,0:T(8,128)S(1)}, f32[16,128]{1,0:T(8,128)S(1)}, u32[]{:S(2)}, u32[]{:S(2)}) collective-permute-start(f32[16,128]{1,0:T(8,128)S(1)} %get-tuple-element.52.refs_6_), channel_id=1, source_target_pairs={{0,24},{8,0},{16,8},{24,16},{1,25},{9,1},{17,9},{25,17},{2,26},{10... | collective-permute-start | bytes 24584 | tf_op jit(solution)/shard_map/ppermute | solution.py:409
  33.5 4.5 %collective-permute-start.10 = (f32[16,128]{1,0:T(8,128)S(1)}, f32[16,128]{1,0:T(8,128)S(1)}, u32[]{:S(2)}, u32[]{:S(2)}) collective-permute-start(f32[16,128]{1,0:T(8,128)S(1)} %get-tuple-element.52.refs_6_), channel_id=1, source_target_pairs={{0,16},{8,24},{16,0},{24,8},{1,17},{9,25},{17,1},{25,9},{2,18},{10... | collective-permute-start | bytes 24584 | tf_op jit(solution)/shard_map/ppermute | solution.py:409
  33.5 5.4 %collective-permute-start.9 = (f32[16,128]{1,0:T(8,128)S(1)}, f32[16,128]{1,0:T(8,128)S(1)}, u32[]{:S(2)}, u32[]{:S(2)}) collective-permute-start(f32[16,128]{1,0:T(8,128)S(1)} %get-tuple-element.52.refs_6_), channel_id=1, source_target_pairs={{0,8},{8,16},{16,24},{24,0},{1,9},{9,17},{17,25},{25,1},{2,10},{10... | collective-permute-start | bytes 24584 | tf_op jit(solution)/shard_map/ppermute | solution.py:409
  48.9 1.9 %collective-permute-start.12 = (bf16[1056,256]{1,0:T(8,128)(2,1)S(1)}, bf16[1056,256]{1,0:T(8,128)(2,1)S(1)}, u32[]{:S(2)}, u32[]{:S(2)}) collective-permute-start(bf16[1056,256]{1,0:T(8,128)(2,1)S(1)} %get-tuple-element.59), channel_id=1, source_target_pairs={{0,1},{1,0},{2,3},{3,2},{4,5},{5,4},{6,7},{7,6},{8,9},{9,8},{10,11... | collective-permute-start | bytes 1622024 | tf_op jit(solution)/shard_map/ppermute | solution.py:399
  50.8 2.8 %copy-start.16 = (f32[8]{0:T(128)S(1)}, f32[8]{0:T(128)}, u32[]{:S(2)}) copy-start(f32[8]{0:T(128)} %rate_ref.3) | copy-start | bytes 100
  51.0 6.0 %collective-permute-start.14 = (bf16[288,256]{1,0:T(8,128)(2,1)S(1)}, bf16[288,256]{1,0:T(8,128)(2,1)S(1)}, u32[]{:S(2)}, u32[]{:S(2)}) collective-permute-start(bf16[288,256]{1,0:T(8,128)(2,1)S(1)} %get-tuple-element.66), channel_id=1, source_target_pairs={{0,4},{1,5},{2,6},{3,7},{4,0},{5,1},{6,2},{7,3},{8,12},{9,13},{10,... | collective-permute-start | bytes 442376 | tf_op jit(solution)/shard_map/ppermute | solution.py:404
  51.6 6.7 %collective-permute-start.15 = (bf16[288,256]{1,0:T(8,128)(2,1)S(1)}, bf16[288,256]{1,0:T(8,128)(2,1)S(1)}, u32[]{:S(2)}, u32[]{:S(2)}) collective-permute-start(bf16[288,256]{1,0:T(8,128)(2,1)S(1)} %get-tuple-element.67), channel_id=1, source_target_pairs={{0,6},{1,7},{2,0},{3,1},{4,2},{5,3},{6,4},{7,5},{8,14},{9,15},{10,... | collective-permute-start | bytes 442376 | tf_op jit(solution)/shard_map/ppermute | solution.py:404
  52.9 8.4 %collective-permute-start.13 = (bf16[288,256]{1,0:T(8,128)(2,1)S(1)}, bf16[288,256]{1,0:T(8,128)(2,1)S(1)}, u32[]{:S(2)}, u32[]{:S(2)}) collective-permute-start(bf16[288,256]{1,0:T(8,128)(2,1)S(1)} %get-tuple-element.61._), channel_id=1, source_target_pairs={{0,2},{1,3},{2,4},{3,5},{4,6},{5,7},{6,0},{7,1},{8,10},{9,11},{10,... | collective-permute-start | bytes 442376 | tf_op jit(solution)/shard_map/ppermute | solution.py:404
  (9 other events, 9.6 us)

commit v6 on v5

--- a/solution.py
+++ b/solution.py
@@ -65,6 +65,26 @@
     return me // 2, me % 2
 
 
+def fetch(pairs, sems):
+    copies = [
+        pltpu.make_async_copy(source, target, sems.at[i]) for i, (source, target) in enumerate(pairs)
+    ]
+    for copy in copies:
+        copy.start()
+    return copies
+
+
+def pack_kernel(key_ref, value_ref, out_ref, sems):
+    pairs = [(key_ref, out_ref.at[:, :LANES]), (value_ref, out_ref.at[:, LANES:])]
+    for copy in fetch(pairs, sems):
+        copy.wait()
+
+
+def stack_kernel(*refs):
+    for k, ref in enumerate(refs[:-1]):
+        refs[-1][k] = ref[...]
+
+
 def enter_and_tail(run0, run1):
     t0, t1 = run0[BLOCK - 1 :, :], run1[BLOCK - 1 :, :]
     enter = jnp.concatenate([run0, run1 + t0], axis=0)
@@ -73,20 +93,27 @@
 
 
 def local_states_kernel(
-    x_ref, g_ref, b_ref, c_ref, step_ref, rate_ref, key_ref, value_ref, keep_ref, give_ref, kv_ref,
-    pad_ref, high_ref, rest_ref, log_ref, state_ref,
+    x_hbm, g_hbm, b_hbm, c_hbm, step_hbm, rate_ref, _, keep_ref, give_ref,
+    x_ref, g_ref, b_ref, c_ref, step_ref, sems, pad_ref, high_ref, rest_ref, log_ref, state_ref,
 ):
     _, core = chip_and_core()
-    kv_ref[:, :LANES] = key_ref[...]
-    kv_ref[:, LANES:] = value_ref[...]
+    step_copy, b_copy, x_copy, c_copy, g_copy = fetch(
+        [(step_hbm, step_ref), (b_hbm, b_ref), (x_hbm, x_ref), (c_hbm, c_ref), (g_hbm, g_ref)], sems
+    )
+    step_copy.wait()
     _, _, run0, run1 = running_logs(step_ref, rate_ref, pad_ref)
     enter_log, tail_log, total = enter_and_tail(run0, run1)
     enter, tail = jnp.exp(enter_log), jnp.exp(tail_log)
     logs = jnp.broadcast_to(total, (HALF, LANES))
     mine = pl.ds(pl.multiple_of(core * HALF, HALF), HALF)
     other = pl.ds(pl.multiple_of((1 - core) * HALF, HALF), HALF)
-    cases = ((b_ref, x_ref, tail, tail_log), (c_ref, g_ref, enter, enter_log))
-    for direction, (left, right, factor, weight) in enumerate(cases):
+    cases = (
+        (b_ref, x_ref, tail, tail_log, (b_copy, x_copy)),
+        (c_ref, g_ref, enter, enter_log, (c_copy, g_copy)),
+    )
+    for direction, (left, right, factor, weight, copies) in enumerate(cases):
+        for copy in copies:
+            copy.wait()
         for h in range(HS):
             product = right[:, head(h)].astype(F32) * factor[:, h : h + 1]
             rounded = product.astype(BF16)
@@ -118,7 +145,7 @@
     return jnp.where(is0, mine, other), jnp.where(is0, other, mine)
 
 
-def combine_kernel(chips, keep_ref, recv_ref, *message_refs):
+def combine_kernel(chips, keep_ref, recv_ref, _, *message_refs):
     chip, core = chip_and_core()
     is0 = core == 0
     log0, log1 = pair_logs(keep_ref, recv_ref, is0)
@@ -138,7 +165,7 @@
         message_refs[k - 1][:, WIDE:] = logs
 
 
-def chain_kernel(chips, keep_ref, recv_ref, sums_ref, *refs):
+def chain_kernel(chips, keep_ref, recv_ref, sums_ref, _, *refs):
     message_refs = refs[: chips - 1]
     own_ref, give_ref, total_ref = refs[chips - 1 :]
     chip, core = chip_and_core()
@@ -178,22 +205,103 @@
         give_ref[1, :, head(h)] = jnp.where(is0, l1, l0)
 
 
-def attention_kernel(
-    chips, most, mask_ref, q_ref, g_ref, stack_ref, other_stack_ref, _, totals_ref, *refs
+def block_attention(
+    block, most, mask_ref, q_ref, g_ref, kv_ref, out_ref, dq_ref, acc_ref,
+    slot_ref, k_ref, k_live_ref, v_ref, q_turned_ref, g_turned_ref, ds_ref, wb_ref,
 ):
-    extra = len(refs) - 15
-    (
-        out_ref, dq_ref, keep_ref, give_ref, sums_ref,
-        slot_ref, kv_ref, acc_ref, k_ref, k_live_ref, v_ref, q_turned_ref, g_turned_ref, ds_ref, wb_ref,
-    ) = refs[extra:]
     count = mask_ref.shape[0]
-    columns = QUERY_HEADS * BLOCK
+    scale = FACTOR * LOG2E
+    lower, upper = slice(0, LANES), slice(LANES, 2 * LANES)
+    own = slice(block * BLOCK, (block + 1) * BLOCK)
+    at = slice(block * BLOCK, (block + 1) * BLOCK)
+    row = lax.axis_index("seq") * (q_ref.shape[0] // BLOCK) + block
+    slots = []
+    for slot in range(most):
+        slot_ref[slot] = row
+
+    def note(j, seen):
+        hit = mask_ref[row, j]
+
+        @pl.when(hit == 1)
+        def _():
+            slot_ref[seen] = j
+
+        return seen + hit
+
+    allowed = lax.fori_loop(0, count, note, 0)
+    for slot in range(most):
+        index, live = slot_ref[slot], slot < allowed
+        slots.append((index, live))
+        source = pl.ds(pl.multiple_of(index * BLOCK, BLOCK), BLOCK)
+        target = slice(slot * BLOCK, (slot + 1) * BLOCK)
+        k_tile, v_tile = kv_ref[source, lower], kv_ref[source, upper]
+        k_ref[target, :] = k_tile
+        k_live_ref[target, :] = jnp.where(live, k_tile, jnp.zeros_like(k_tile))
+        v_ref[target, lower] = jnp.where(live, v_tile, jnp.zeros_like(v_tile))
+        v_ref[target, upper] = jnp.full((BLOCK, LANES), jnp.where(live, 1.0, 0.0), F32).astype(BF16)
+    group = 2
+    for first in range(0, QUERY_HEADS, group):
+        heads = range(first, first + group)
+        rows = slice(first * BLOCK, (first + group) * BLOCK)
+        q = jnp.concatenate([q_ref[at, head(h)] for h in heads], axis=0)
+        g = jnp.concatenate([g_ref[at, head(h)] for h in heads], axis=0)
+        scores = dot(q, k_ref[...], 1, 1)
+        best = jnp.max(scores, axis=1, keepdims=True)
+        weights = jnp.exp2((scores - best) * scale)
+        wb_ref[rows, :] = weights.astype(BF16)
+        both = dot(wb_ref[rows, :], v_ref[...], 1, 0)
+        inverse = 1.0 / both[:, upper]
+        out = both[:, lower] * inverse
+        delta = jnp.sum(out * g.astype(F32), axis=1, keepdims=True)
+        dprobs = dot(g, v_ref[:, lower], 1, 1)
+        ds_ref[rows, :] = (weights * (dprobs - delta)).astype(BF16)
+        dq = (dot(ds_ref[rows, :], k_live_ref[...], 1, 0) * (inverse * FACTOR)).astype(BF16)
+        q_turned_ref[:, rows] = (q.astype(F32) * inverse).astype(BF16).T
+        g_turned_ref[:, rows] = (g.astype(F32) * inverse).astype(BF16).T
+        for place, h in enumerate(heads):
+            part = slice(place * BLOCK, (place + 1) * BLOCK)
+            out_ref[:, head(h)] = out[part]
+            dq_ref[own, head(h)] = dq[part]
+    dk = dot(q_turned_ref[...], ds_ref[...], 1, 0)
+    dv = dot(g_turned_ref[...], wb_ref[...], 1, 0)
+    for slot, (index, live) in enumerate(slots):
+        source = slice(slot * BLOCK, (slot + 1) * BLOCK)
+
+        @pl.when(live)
+        def _():
+            target = pl.ds(pl.multiple_of(index * BLOCK, BLOCK), BLOCK)
+            acc_ref[lower, target] += dk[:, source]
+            acc_ref[upper, target] += dv[:, source]
+
+
+def first_attention_kernel(
+    chips, most, mask_ref, q_ref, g_ref, stack_ref, other_stack_ref, _, out_ref, dq_ref, acc_ref, kv_ref, *scratch
+):
     tokens = q_ref.shape[0]
     chip, core = chip_and_core()
-    me = 2 * chip + core
-    scale = FACTOR * LOG2E
-    sums = totals_ref[...]
-    for ref in refs[:extra]:
+    acc_ref[...] = jnp.zeros_like(acc_ref)
+    for k in range(chips):
+        for other, ref in enumerate((stack_ref, other_stack_ref)):
+            source = 2 * lax.rem(chip + chips - k, chips) + lax.rem(core + other, 2)
+            at = pl.ds(pl.multiple_of(source * tokens, tokens), tokens)
+            kv_ref[at, :] = ref[k]
+    block_attention(0, most, mask_ref, q_ref, g_ref, kv_ref, out_ref, dq_ref, acc_ref, *scratch)
+
+
+def second_attention_kernel(
+    most, mask_ref, q_ref, g_ref, kv_ref, first_dq_ref, first_acc_ref, _, out_ref, dq_ref, acc_ref, *scratch
+):
+    acc_ref[...] = first_acc_ref[...]
+    dq_ref[:BLOCK, :] = first_dq_ref[...]
+    block_attention(1, most, mask_ref, q_ref, g_ref, kv_ref, out_ref, dq_ref, acc_ref, *scratch)
+
+
+def share_kernel(chips, acc_ref, *refs):
+    keep_ref, give_ref, sums_ref = refs[-3:]
+    tokens = keep_ref.shape[1]
+    _, core = chip_and_core()
+    sums = refs[0][...]
+    for ref in refs[1:-3]:
         sums += ref[...]
     sums_ref[...] = sums
     high = sums.astype(BF16)
@@ -201,75 +309,6 @@
     low = (sums - high.astype(F32) - middle.astype(F32)).astype(BF16)
     give_ref[chips * tokens : chips * tokens + 16, :] = jnp.concatenate([high, middle], axis=1)
     give_ref[chips * tokens + 16 :, :] = jnp.concatenate([low, jnp.zeros_like(low)], axis=1)
-    acc_ref[...] = jnp.zeros_like(acc_ref)
-    for k in range(chips):
-        for other, ref in enumerate((stack_ref, other_stack_ref)):
-            source = 2 * lax.rem(chip + chips - k, chips) + lax.rem(core + other, 2)
-            at = pl.ds(pl.multiple_of(source * tokens, tokens), tokens)
-            kv_ref[at, :] = ref[k]
-
-    lower, upper = slice(0, LANES), slice(LANES, 2 * LANES)
-    for block in range(tokens // BLOCK):
-        at = slice(block * BLOCK, (block + 1) * BLOCK)
-        row = me * (tokens // BLOCK) + block
-        slots = []
-        for slot in range(most):
-            slot_ref[block, slot] = row
-
-        def note(j, seen):
-            hit = mask_ref[row, j]
-
-            @pl.when(hit == 1)
-            def _():
-                slot_ref[block, seen] = j
-
-            return seen + hit
-
-        allowed = lax.fori_loop(0, count, note, 0)
-        for slot in range(most):
-            index, live = slot_ref[block, slot], slot < allowed
-            slots.append((index, live))
-            source = pl.ds(pl.multiple_of(index * BLOCK, BLOCK), BLOCK)
-            target = slice(slot * BLOCK, (slot + 1) * BLOCK)
-            k_tile, v_tile = kv_ref[source, lower], kv_ref[source, upper]
-            k_ref[target, :] = k_tile
-            k_live_ref[target, :] = jnp.where(live, k_tile, jnp.zeros_like(k_tile))
-            v_ref[target, lower] = jnp.where(live, v_tile, jnp.zeros_like(v_tile))
-            v_ref[target, upper] = jnp.full((BLOCK, LANES), jnp.where(live, 1.0, 0.0), F32).astype(BF16)
-        group = 2
-        for first in range(0, QUERY_HEADS, group):
-            heads = range(first, first + group)
-            rows = slice(first * BLOCK, (first + group) * BLOCK)
-            q = jnp.concatenate([q_ref[at, head(h)] for h in heads], axis=0)
-            g = jnp.concatenate([g_ref[at, head(h)] for h in heads], axis=0)
-            scores = dot(q, k_ref[...], 1, 1)
-            best = jnp.max(scores, axis=1, keepdims=True)
-            weights = jnp.exp2((scores - best) * scale)
-            wb_ref[rows, :] = weights.astype(BF16)
-            both = dot(wb_ref[rows, :], v_ref[...], 1, 0)
-            inverse = 1.0 / both[:, upper]
-            out = both[:, lower] * inverse
-            delta = jnp.sum(out * g.astype(F32), axis=1, keepdims=True)
-            dprobs = dot(g, v_ref[:, lower], 1, 1)
-            ds_ref[rows, :] = (weights * (dprobs - delta)).astype(BF16)
-            dq = (dot(ds_ref[rows, :], k_live_ref[...], 1, 0) * (inverse * FACTOR)).astype(BF16)
-            q_turned_ref[:, rows] = (q.astype(F32) * inverse).astype(BF16).T
-            g_turned_ref[:, rows] = (g.astype(F32) * inverse).astype(BF16).T
-            for place, h in enumerate(heads):
-                part = slice(place * BLOCK, (place + 1) * BLOCK)
-                out_ref[at, head(h)] = out[part]
-                dq_ref[at, head(h)] = dq[part]
-        dk = dot(q_turned_ref[...], ds_ref[...], 1, 0)
-        dv = dot(g_turned_ref[...], wb_ref[...], 1, 0)
-        for slot, (index, live) in enumerate(slots):
-            source = slice(slot * BLOCK, (slot + 1) * BLOCK)
-
-            @pl.when(live)
-            def _():
-                target = pl.ds(pl.multiple_of(index * BLOCK, BLOCK), BLOCK)
-                acc_ref[lower, target] += dk[:, source]
-                acc_ref[upper, target] += dv[:, source]
-
     for k in range(chips):
         mine = pl.multiple_of((2 * k + core) * tokens, tokens)
         other = pl.multiple_of((2 * k + 1 - core) * tokens, tokens)
@@ -318,13 +357,11 @@
     skip_ref[...] = skip[0:1, :]
 
 
-def inner_kernel(chips, x_ref, g_ref, b_ref, c_ref, step_ref, rate_ref, skip_ref, _, *refs):
-    (
-        stack_ref, y_ref, dx_ref, db_ref, dc_ref, sums_ref,
-        pad_ref, inner_ref, dinner_ref, m_ref, runt_ref,
-    ) = refs[chips:]
-    for k in range(chips):
-        stack_ref[k] = refs[k][...]
+def inner_kernel(
+    x_ref, g_ref, b_ref, c_ref, step_ref, rate_ref, skip_ref, _,
+    y_ref, dx_ref, db_ref, dc_ref, sums_ref,
+    pad_ref, inner_ref, dinner_ref, m_ref, runt_ref,
+):
     tokens = 2 * BLOCK
     flat0, flat1, run0, run1 = running_logs(step_ref, rate_ref, pad_ref)
     own = jnp.concatenate([run0, run1], axis=0)
@@ -370,7 +407,7 @@
 
 
 def outer_kernel(
-    x_ref, g_ref, b_ref, c_ref, step_ref, rate_ref, own_ref, other_ref, att_ref,
+    x_ref, g_ref, b_ref, c_ref, step_ref, rate_ref, own_ref, other_ref, first_ref, second_ref,
     inner_y_ref, inner_dx_ref, inner_db_ref, inner_dc_ref, _,
     y_ref, dx_ref, db_ref, dc_ref,
     pad_ref, xt_ref, gt_ref, ent_ref,
@@ -389,7 +426,9 @@
         lanes = head(h)
         carried = dot(c, ent_ref[0, :, lanes], 1, 0) * enter[:, h : h + 1]
         back = dot(b, ent_ref[1, :, lanes], 1, 0) * tail[:, h : h + 1]
-        y_ref[:, lanes] = (inner_y_ref[:, lanes] + carried + att_ref[:, lanes]).astype(BF16)
+        y = inner_y_ref[:, lanes] + carried
+        y_ref[:BLOCK, lanes] = (y[:BLOCK] + first_ref[:, lanes]).astype(BF16)
+        y_ref[BLOCK:, lanes] = (y[BLOCK:] + second_ref[:, lanes]).astype(BF16)
         dx_ref[:, lanes] = (inner_dx_ref[:, lanes] + back).astype(BF16)
     dc_ref[...] = (inner_dc_ref[...] + dot(gt_ref[...], ent_ref[0], 1, 1)).astype(BF16)
     db_ref[...] = (inner_db_ref[...] + dot(xt_ref[...], ent_ref[1], 1, 1)).astype(BF16)
@@ -433,40 +472,45 @@
     q, g, x = query[0], grad_out[0], ssm_input[0]
     b, c, steps = in_b[0], in_c[0], step[0].T
 
+    (kv,) = call(
+        pack_kernel,
+        [((tokens, 2 * LANES), BF16)],
+        [AFTER] * 2,
+        [pltpu.SemaphoreType.DMA((2,))],
+        1,
+        "pack_kv",
+        60,
+    )(key[0], value[0])
+    kv_parts = [kv] + [from_chip(kv, k) for k in range(1, chips)]
+
     half = ((4, HALF, WIDE + LANES), F32)
-    keep, give, kv = call(
+    keep, give = call(
         local_states_kernel,
-        [half, half, ((tokens, 2 * LANES), BF16)],
-        [VMEM] * 5 + [SMEM] + [VMEM] * 2,
+        [half, half],
+        [AFTER] * 5 + [SMEM, AFTER],
         [
+            pltpu.VMEM((tokens, WIDE), BF16),
+            pltpu.VMEM((tokens, WIDE), BF16),
+            pltpu.VMEM((tokens, NS), BF16),
+            pltpu.VMEM((tokens, NS), BF16),
+            pltpu.VMEM((HS, tokens), F32),
+            pltpu.SemaphoreType.DMA((5,)),
             pltpu.VMEM((LANES, tokens), F32),
             pltpu.VMEM((tokens, WIDE), BF16),
             pltpu.VMEM((tokens, WIDE), BF16),
             pltpu.VMEM((tokens, WIDE), BF16),
             pltpu.VMEM((4, NS, WIDE), F32),
         ],
-        4,
+        20,
         "local_states",
-    )(x, g, b, c, steps, rate_log, key[0], value[0])
+        60,
+    )(x, g, b, c, steps, rate_log, kv)
     received = swapped(give)
-    kv_parts = [kv] + [from_chip(kv, k) for k in range(1, chips)]
-    messages = call(
-        lambda *refs: combine_kernel(chips, *refs),
-        [((HALF, WIDE + LANES), BF16)] * (chips - 1),
-        [VMEM] * 2,
-        [],
-        1,
-        "combine_states",
-    )(keep, received)
-    arrived = [from_chip(messages[k - 1], k) for k in range(1, chips)]
-
-    stack, inner_y, inner_dx, inner_db, inner_dc, sums = call(
-        lambda *refs: inner_kernel(chips, *refs),
-        [((chips, tokens, 2 * LANES), BF16)]
-        + [((tokens, WIDE), F32)] * 2
-        + [((tokens, NS), F32)] * 2
-        + [((2 * HS, LANES), F32)],
-        [VMEM] * 5 + [SMEM] * 2 + [AFTER] + [VMEM] * chips,
+
+    inner_y, inner_dx, inner_db, inner_dc, sums = call(
+        inner_kernel,
+        [((tokens, WIDE), F32)] * 2 + [((tokens, NS), F32)] * 2 + [((2 * HS, LANES), F32)],
+        [VMEM] * 5 + [SMEM] * 2 + [AFTER],
         [
             pltpu.VMEM((LANES, tokens), F32),
             pltpu.VMEM((tokens, tokens), F32),
@@ -474,50 +518,87 @@
             pltpu.VMEM((tokens, tokens), BF16),
             pltpu.VMEM((LANES, 2 * tokens), F32),
         ],
+        0.3,
+        "chunk_inner",
+    )(x, g, b, c, steps, rate_log, skip, keep)
+
+    messages = call(
+        lambda *refs: combine_kernel(chips, *refs),
+        [((HALF, WIDE + LANES), BF16)] * (chips - 1),
+        [VMEM] * 2 + [AFTER],
+        [],
+        1,
+        "combine_states",
+    )(keep, received, sums)
+    arrived = [from_chip(messages[k - 1], k) for k in range(1, chips)]
+    (stack,) = call(
+        lambda _, *refs: stack_kernel(*refs),
+        [((chips, tokens, 2 * LANES), BF16)],
+        [AFTER] + [VMEM] * chips,
+        [],
+        1,
+        "stack_kv",
+    )(messages[0], *kv_parts)
+    other_stack = swapped(stack)
+
+    columns = QUERY_HEADS * BLOCK
+    scratch = [
+        pltpu.SMEM((most,), jnp.int32),
+        pltpu.VMEM((most * BLOCK, LANES), BF16),
+        pltpu.VMEM((most * BLOCK, LANES), BF16),
+        pltpu.VMEM((most * BLOCK, 2 * LANES), BF16),
+        pltpu.VMEM((LANES, columns), BF16),
+        pltpu.VMEM((LANES, columns), BF16),
+        pltpu.VMEM((columns, most * BLOCK), BF16),
+        pltpu.VMEM((columns, most * BLOCK), BF16),
+    ]
+    first_out, first_dq, first_acc, kv_all = call(
+        lambda *refs: first_attention_kernel(chips, most, *refs),
+        [
+            ((BLOCK, columns), F32),
+            ((BLOCK, columns), BF16),
+            ((2 * LANES, every), F32),
+            ((every, 2 * LANES), BF16),
+        ],
+        [SMEM] + [VMEM] * 4 + [AFTER],
+        scratch,
         5,
-        "chunk_inner",
-    )(x, g, b, c, steps, rate_log, skip, messages[0], *kv_parts)
-    other_stack = swapped(stack)
-
+        "first_attention",
+        18 + most,
+    )(block_mask[0], q, g, stack, other_stack, messages[0])
     entering = ((2, HALF, WIDE), BF16)
     own, give, totals = call(
         lambda *refs: chain_kernel(chips, *refs),
         [entering, entering, ((2 * HS, LANES), F32)],
-        [VMEM] * (2 + chips),
+        [VMEM] * 3 + [AFTER] + [VMEM] * (chips - 1),
         [],
         2,
         "chain_states",
-    )(keep, received, sums, *arrived)
+    )(keep, received, sums, first_dq, *arrived)
     other = swapped(give)
     replicated = [turned(totals, k) for k in range(1, replicas)]
 
-    columns = QUERY_HEADS * BLOCK
-    attention, dq, keep, give, sums = call(
-        lambda *refs: attention_kernel(chips, most, *refs),
+    second_out, dq, acc = call(
+        lambda *refs: second_attention_kernel(most, *refs),
+        [((BLOCK, columns), F32), ((tokens, columns), BF16), ((2 * LANES, every), F32)],
+        [SMEM] + [VMEM] * 5 + [AFTER],
+        scratch,
+        5,
+        "second_attention",
+        18 + most,
+    )(block_mask[0], q, g, kv_all, first_dq, first_acc, totals)
+    keep, give, sums = call(
+        lambda *refs: share_kernel(chips, *refs),
         [
-            ((tokens, columns), F32),
-            ((tokens, columns), BF16),
             ((chips * 2 * LANES, tokens), BF16),
             ((chips * 2 * LANES + 32, tokens), BF16),
             ((2 * HS, LANES), F32),
         ],
-        [SMEM] + [VMEM] * 4 + [AFTER] + [VMEM] * replicas,
-        [
-            pltpu.SMEM((2, most), jnp.int32),
-            pltpu.VMEM((every, 2 * LANES), BF16),
-            pltpu.VMEM((2 * LANES, every), F32),
-            pltpu.VMEM((most * BLOCK, LANES), BF16),
-            pltpu.VMEM((most * BLOCK, LANES), BF16),
-            pltpu.VMEM((most * BLOCK, 2 * LANES), BF16),
-            pltpu.VMEM((LANES, columns), BF16),
-            pltpu.VMEM((LANES, columns), BF16),
-            pltpu.VMEM((columns, most * BLOCK), BF16),
-            pltpu.VMEM((columns, most * BLOCK), BF16),
-        ],
-        10,
-        "attention",
-        18 + most,
-    )(block_mask[0], q, g, stack, other_stack, other, totals, *replicated)
+        [VMEM] * (1 + replicas),
+        [],
+        1,
+        "share_key_gradients",
+    )(acc, totals, *replicated)
     partial, summed, *messages = call(
         lambda *refs: pair_sum_kernel(chips, *refs),
         [((2 * LANES, tokens), F32), ((2 * HS, LANES), F32)]
@@ -532,7 +613,7 @@
     y, dx, db, dc = call(
         outer_kernel,
         [((tokens, WIDE), BF16)] * 2 + [((tokens, NS), BF16)] * 2,
-        [VMEM] * 5 + [SMEM] + [VMEM] * 7 + [AFTER],
+        [VMEM] * 5 + [SMEM] + [VMEM] * 8 + [AFTER],
         [
             pltpu.VMEM((LANES, tokens), F32),
             pltpu.VMEM((tokens, WIDE), BF16),
@@ -542,7 +623,7 @@
         3,
         "chunk_outer",
     )(
-        x, g, b, c, steps, rate_log, own, other, attention,
+        x, g, b, c, steps, rate_log, own, other, first_out, second_out,
         inner_y, inner_dx, inner_db, inner_dc, messages[0],
     )
 

time: 62.5 us -> 53.7 us (0.86)
  waiting for transfers between devices: 16.9 us -> 6.82 us
  local copies, waits for them, and re-layouts: 6.83 us -> 1.33 us
  Pallas kernels: 20.1 us -> 24.7 us
  starting transfers between devices: 17.5 us -> 19.7 us
    unnamed x34 -> x24, local copies, waits for them, and re-layouts: 6.83 us -> 1.33 us
    ppermute x9, waiting for transfers between devices: 10.5 us -> 5.38 us  [from_chip(): return lax.ppermute(array, 'seq', [(i, (i + 2 * k) % n) for i in range(n)])]
    pallas_call x3 -> x7, Pallas kernels: 15.5 us -> 20 us  [the longest x1 5.55 us: body(): call(local_states_kernel, [half, half], [AFTER] * 5 + [SMEM, AFTER], [plt...]
    ppermute x3, waiting for transfers between devices: 4.44 us -> 0.01 us  [turned(): return lax.ppermute(array, 'dp', [(i, (i + k) % n) for i in range(n)])]
    ppermute x9, starting transfers between devices: 12.2 us -> 13.9 us  [from_chip(): return lax.ppermute(array, 'seq', [(i, (i + 2 * k) % n) for i in range(n)])]
  transfers between devices with their start and end apart: 16 -> 16, of which waited for: 9 -> 6; matrix products, arithmetic and copies ran while one was open for 0% -> 0% of each run, Pallas kernels for 10% -> 30%
where the time goes in v6:
time: 53.7 us; the launch traced here: 53.4 us
  Pallas kernels  24.7 us (46%)
  starting transfers between devices  19.7 us (37%)
  waiting for transfers between devices  6.82 us (13%)
  local copies, waits for them, and re-layouts  1.33 us (2%)
  between operations  0.86 us (2%)
    ppermute x9, starting transfers between devices, from_chip(): return lax.ppermute(array, 'seq', [(i, (i + 2 * k) % n) for i in range(n)])  13.9 us
    pallas_call x1, Pallas kernels, body(): call(local_states_kernel, [half, half], [AFTER] * 5 + [SMEM, AFTER], [plt...  5.55 us
    pallas_call x1, Pallas kernels, body(): call(lambda *refs: second_attention_kernel(most, *refs), [((BLOCK, column...  5.45 us
    ppermute x9, waiting for transfers between devices, from_chip(): return lax.ppermute(array, 'seq', [(i, (i + 2 * k) % n) for i in range(n)])  5.38 us
    pallas_call x1, Pallas kernels, body(): call(lambda *refs: first_attention_kernel(chips, most, *refs), [((BLOCK,...  4.7 us
    ppermute x3, starting transfers between devices, turned(): return lax.ppermute(array, 'dp', [(i, (i + k) % n) for i in range(n)])  4.68 us
    pallas_call x1, Pallas kernels, body(): call(outer_kernel, [((tokens, WIDE), BF16)] * 2 + [((tokens, NS), BF16)]...  2.81 us
    pallas_call x1, Pallas kernels, body(): call(inner_kernel, [((tokens, WIDE), F32)] * 2 + [((tokens, NS), F32)] *...  2.62 us
  transfers between devices with their start and end apart: 16, of which 6 were waited for; matrix products, arithmetic and copies ran while one was open for 0% of the time, Pallas kernels for 30%

profile of v6, /device:TPU:0, one launch (start us, length us, event | category | flops | bytes accessed | tf_op | source)
XLA Modules:
  0.0 53.4 jit_solution(11149561491485684105)
XLA Ops:
  0.6 1.5 %pack_kv.1._.refs_0_ = bf16[256,256]{1,0:T(8,128)(2,1)} custom-call(bf16[256,128]{1,0:T(8,128)(2,1)} %bitcast.41, bf16[256,128]{1,0:T(8,128)(2,1)} %bitcast.42), custom_call_target="tpu_custom_call" | custom-call | flops 1100000000 | bytes 1048576 | tf_op jit(solution)/shard_map/pack_kv/pallas_call | solution.py:475
  2.3 5.6 %local_states.1 = (f32[4,64,1152]{2,1,0:T(8,128)}, f32[4,64,1152]{2,1,0:T(8,128)}) custom-call(bf16[256,1024]{1,0:T(8,128)(2,1)} %bitcast.20, bf16[256,1024]{1,0:T(8,128)(2,1)} %bitcast.23, bf16[256,128]{1,0:T(8,128)(2,1)} %bitcast.28, bf16[256,128]{1,0:T(8,128)(2,1)} %bitcast.31, f32[8,256]{1,0:T(8,128)} %bitcast.34, f32[8]{0:T(128)} %rate_ref.5, ...), custom_call_target="tpu_custom_call" | custom-call | flops 22000001024 | bytes 1048576 | tf_op jit(solution)/shard_map/local_states/pallas_call | solution.py:487
  8.4 2.6 %collective-permute-start.1 = (bf16[256,256]{1,0:T(8,128)(2,1)S(1)}, bf16[256,256]{1,0:T(8,128)(2,1)S(1)}, u32[]{:S(2)}, u32[]{:S(2)}) collective-permute-start(bf16[256,256]{1,0:T(8,128)(2,1)S(1)} %copy-done.10), channel_id=1, source_target_pairs={{0,2},{1,3},{2,4},{3,5},{4,6},{5,7},{6,0},{7,1},{8,10},{9,11},{10,... | collective-permute-start | bytes 393224 | tf_op jit(solution)/shard_map/ppermute | solution.py:443
  10.9 1.5 %collective-permute-start.2 = (bf16[256,256]{1,0:T(8,128)(2,1)S(1)}, bf16[256,256]{1,0:T(8,128)(2,1)S(1)}, u32[]{:S(2)}, u32[]{:S(2)}) collective-permute-start(bf16[256,256]{1,0:T(8,128)(2,1)S(1)} %copy-done.10), channel_id=1, source_target_pairs={{0,4},{1,5},{2,6},{3,7},{4,0},{5,1},{6,2},{7,3},{8,12},{9,13},{10,... | collective-permute-start | bytes 393224 | tf_op jit(solution)/shard_map/ppermute | solution.py:443
  12.4 1.4 %collective-permute-start.3 = (bf16[256,256]{1,0:T(8,128)(2,1)S(1)}, bf16[256,256]{1,0:T(8,128)(2,1)S(1)}, u32[]{:S(2)}, u32[]{:S(2)}) collective-permute-start(bf16[256,256]{1,0:T(8,128)(2,1)S(1)} %copy-done.10), channel_id=1, source_target_pairs={{0,6},{1,7},{2,0},{3,1},{4,2},{5,3},{6,4},{7,5},{8,14},{9,15},{10,... | collective-permute-start | bytes 393224 | tf_op jit(solution)/shard_map/ppermute | solution.py:443
  13.9 1.3 %copy-done = f32[4,64,1152]{2,1,0:T(8,128)S(1)} copy-done((f32[4,64,1152]{2,1,0:T(8,128)S(1)}, f32[4,64,1152]{2,1,0:T(8,128)}, u32[]{:S(2)}) %copy-start) | copy-done | bytes 1179672
  15.2 2.6 %chunk_inner.1 = (f32[256,1024]{1,0:T(8,128)S(1)}, f32[256,1024]{1,0:T(8,128)S(1)}, f32[256,128]{1,0:T(8,128)S(1)}, f32[256,128]{1,0:T(8,128)S(1)}, f32[16,128]{1,0:T(8,128)S(1)}) custom-call(bf16[256,1024]{1,0:T(8,128)(2,1)S(1)} %bitcast.21, bf16[256,1024]{1,0:T(8,128)(2,1)S(1)} %bitcast.24, bf16[256,128]{1,0:T(8,128)(2,1)S(1)} %bitcast.29, ...), custom_call_target="tpu_custom_call" | custom-call | flops 330000000 | bytes 1048576 | tf_op jit(solution)/shard_map/chunk_inner/pallas_call | solution.py:510
  18.1 0.7 %collective-permute-done.2.refs_2_ = bf16[256,256]{1,0:T(8,128)(2,1)S(1)} collective-permute-done((bf16[256,256]{1,0:T(8,128)(2,1)S(1)}, bf16[256,256]{1,0:T(8,128)(2,1)S(1)}, u32[]{:S(2)}, u32[]{:S(2)}) %collective-permute-start.2) | collective-permute-done | bytes 131104 | tf_op jit(solution)/shard_map/ppermute | solution.py:443
  19.2 1.8 %collective-permute-start.5 = (bf16[64,1152]{1,0:T(8,128)(2,1)S(1)}, bf16[64,1152]{1,0:T(8,128)(2,1)S(1)}, u32[]{:S(2)}, u32[]{:S(2)}) collective-permute-start(bf16[64,1152]{1,0:T(8,128)(2,1)S(1)} %get-tuple-element.48._.refs_5_), channel_id=1, source_target_pairs={{0,2},{1,3},{2,4},{3,5},{4,6},{5,7},{6,0},{7,1},{8,10},{9,11},{10,... | collective-permute-start | bytes 442376 | tf_op jit(solution)/shard_map/ppermute | solution.py:443
  21.3 2.3 %collective-permute-start.7 = (bf16[64,1152]{1,0:T(8,128)(2,1)S(1)}, bf16[64,1152]{1,0:T(8,128)(2,1)S(1)}, u32[]{:S(2)}, u32[]{:S(2)}) collective-permute-start(bf16[64,1152]{1,0:T(8,128)(2,1)S(1)} %get-tuple-element.51), channel_id=1, source_target_pairs={{0,6},{1,7},{2,0},{3,1},{4,2},{5,3},{6,4},{7,5},{8,14},{9,15},{10,... | collective-permute-start | bytes 442376 | tf_op jit(solution)/shard_map/ppermute | solution.py:443
  23.6 4.7 %first_attention.1 = (f32[128,1024]{1,0:T(8,128)S(1)}, bf16[128,1024]{1,0:T(8,128)(2,1)S(1)}, f32[256,2048]{1,0:T(8,128)S(1)}, bf16[2048,256]{1,0:T(8,128)(2,1)S(1)}) custom-call(s32[16,16]{1,0:T(8,128)S(1)} %bitcast.39, bf16[256,1024]{1,0:T(8,128)(2,1)S(1)} %bitcast.37, bf16[256,1024]{1,0:T(8,128)(2,1)S(1)} %bitcast.25, ...), custom_call_target="tpu_custom_call" | custom-call | flops 5500000256 | bytes 1048576 | tf_op jit(solution)/shard_map/first_attention/pallas_call | solution.py:555
  28.3 1.2 %collective-permute-done.6.refs_5_ = bf16[64,1152]{1,0:T(8,128)(2,1)S(1)} collective-permute-done((bf16[64,1152]{1,0:T(8,128)(2,1)S(1)}, bf16[64,1152]{1,0:T(8,128)(2,1)S(1)}, u32[]{:S(2)}, u32[]{:S(2)}) %collective-permute-start.6) | collective-permute-done | bytes 147488 | tf_op jit(solution)/shard_map/ppermute | solution.py:443
  29.5 0.7 %chain_states.1 = (bf16[2,64,1024]{2,1,0:T(8,128)(2,1)S(1)}, bf16[2,64,1024]{2,1,0:T(8,128)(2,1)S(1)}, f32[16,128]{1,0:T(8,128)S(1)}) custom-call(f32[4,64,1152]{2,1,0:T(8,128)S(1)} %copy-done.1, f32[4,64,1152]{2,1,0:T(8,128)S(1)} %collective-permute-done.refs_1_, f32[16,128]{1,0:T(8,128)S(1)} %get-tuple-element.47.refs_2_, ...), custom_call_target="tpu_custom_call" | custom-call | flops 2200000000 | bytes 1048576 | tf_op jit(solution)/shard_map/chain_states/pallas_call | solution.py:570
  30.2 2.7 %collective-permute-start.10 = (f32[16,128]{1,0:T(8,128)S(1)}, f32[16,128]{1,0:T(8,128)S(1)}, u32[]{:S(2)}, u32[]{:S(2)}) collective-permute-start(f32[16,128]{1,0:T(8,128)S(1)} %get-tuple-element.57.refs_6_.refs_1_), channel_id=1, source_target_pairs={{0,16},{8,24},{16,0},{24,8},{1,17},{9,25},{17,1},{25,9},{2,18},{10... | collective-permute-start | bytes 24584 | tf_op jit(solution)/shard_map/ppermute | solution.py:448
  32.8 1.3 %collective-permute-start.11 = (f32[16,128]{1,0:T(8,128)S(1)}, f32[16,128]{1,0:T(8,128)S(1)}, u32[]{:S(2)}, u32[]{:S(2)}) collective-permute-start(f32[16,128]{1,0:T(8,128)S(1)} %get-tuple-element.57.refs_6_.refs_1_), channel_id=1, source_target_pairs={{0,24},{8,0},{16,8},{24,16},{1,25},{9,1},{17,9},{25,17},{2,26},{10... | collective-permute-start | bytes 24584 | tf_op jit(solution)/shard_map/ppermute | solution.py:448
  34.2 0.7 %collective-permute-start.9 = (f32[16,128]{1,0:T(8,128)S(1)}, f32[16,128]{1,0:T(8,128)S(1)}, u32[]{:S(2)}, u32[]{:S(2)}) collective-permute-start(f32[16,128]{1,0:T(8,128)S(1)} %get-tuple-element.57.refs_6_.refs_1_), channel_id=1, source_target_pairs={{0,8},{8,16},{16,24},{24,0},{1,9},{9,17},{17,25},{25,1},{2,10},{10... | collective-permute-start | bytes 24584 | tf_op jit(solution)/shard_map/ppermute | solution.py:448
  34.9 5.4 %second_attention.1 = (f32[128,1024]{1,0:T(8,128)S(1)}, bf16[256,1024]{1,0:T(8,128)(2,1)}, f32[256,2048]{1,0:T(8,128)S(1)}) custom-call(s32[16,16]{1,0:T(8,128)S(1)} %bitcast.40, bf16[256,1024]{1,0:T(8,128)(2,1)S(1)} %bitcast.38, bf16[256,1024]{1,0:T(8,128)(2,1)S(1)} %bitcast.26, bf16[2048,256]{1,0:T(8,128)(2,1)S(1)} %get-tuple-element.55.refs_3_, ...), custom_call_target="tpu_custom_call" | custom-call | flops 5500000256 | bytes 1048576 | tf_op jit(solution)/shard_map/second_attention/pallas_call | solution.py:581
  41.1 1.4 %collective-permute-done.12.refs_1_ = bf16[1056,256]{1,0:T(8,128)(2,1)S(1)} collective-permute-done((bf16[1056,256]{1,0:T(8,128)(2,1)S(1)}, bf16[1056,256]{1,0:T(8,128)(2,1)S(1)}, u32[]{:S(2)}, u32[]{:S(2)}) %collective-permute-start.12) | collective-permute-done | bytes 540704 | tf_op jit(solution)/shard_map/ppermute | solution.py:438
  42.6 1.8 %collective-permute-start.13 = (bf16[288,256]{1,0:T(8,128)(2,1)S(1)}, bf16[288,256]{1,0:T(8,128)(2,1)S(1)}, u32[]{:S(2)}, u32[]{:S(2)}) collective-permute-start(bf16[288,256]{1,0:T(8,128)(2,1)S(1)} %get-tuple-element.67._), channel_id=1, source_target_pairs={{0,2},{1,3},{2,4},{3,5},{4,6},{5,7},{6,0},{7,1},{8,10},{9,11},{10,... | collective-permute-start | bytes 442376 | tf_op jit(solution)/shard_map/ppermute | solution.py:443
  45.0 1.6 %collective-permute-start.15 = (bf16[288,256]{1,0:T(8,128)(2,1)S(1)}, bf16[288,256]{1,0:T(8,128)(2,1)S(1)}, u32[]{:S(2)}, u32[]{:S(2)}) collective-permute-start(bf16[288,256]{1,0:T(8,128)(2,1)S(1)} %get-tuple-element.73), channel_id=1, source_target_pairs={{0,6},{1,7},{2,0},{3,1},{4,2},{5,3},{6,4},{7,5},{8,14},{9,15},{10,... | collective-permute-start | bytes 442376 | tf_op jit(solution)/shard_map/ppermute | solution.py:443
  46.6 2.8 %chunk_outer.1 = (bf16[256,1024]{1,0:T(8,128)(2,1)}, bf16[256,1024]{1,0:T(8,128)(2,1)}, bf16[256,128]{1,0:T(8,128)(2,1)}, bf16[256,128]{1,0:T(8,128)(2,1)}) custom-call(bf16[256,1024]{1,0:T(8,128)(2,1)S(1)} %bitcast.22, bf16[256,1024]{1,0:T(8,128)(2,1)S(1)} %bitcast.27, bf16[256,128]{1,0:T(8,128)(2,1)S(1)} %bitcast.30, bf16[256,128]{1,0:T(8,128)(2,1)S(1)} %bitcast.33, ...), custom_call_target="tpu_custom_call" | custom-call | flops 3300000000 | bytes 1048576 | tf_op jit(solution)/shard_map/chunk_outer/pallas_call | solution.py:613
  49.4 0.9 %collective-permute-done.13.refs_2_ = bf16[288,256]{1,0:T(8,128)(2,1)S(1)} collective-permute-done((bf16[288,256]{1,0:T(8,128)(2,1)S(1)}, bf16[288,256]{1,0:T(8,128)(2,1)S(1)}, u32[]{:S(2)}, u32[]{:S(2)}) %collective-permute-start.13) | collective-permute-done | bytes 147488 | tf_op jit(solution)/shard_map/ppermute | solution.py:443
  50.3 2.3 %collective-permute-done.14.refs_3_ = bf16[288,256]{1,0:T(8,128)(2,1)S(1)} collective-permute-done((bf16[288,256]{1,0:T(8,128)(2,1)S(1)}, bf16[288,256]{1,0:T(8,128)(2,1)S(1)}, u32[]{:S(2)}, u32[]{:S(2)}) %collective-permute-start.14) | collective-permute-done | bytes 147488 | tf_op jit(solution)/shard_map/ppermute | solution.py:443
  52.6 0.8 %owner_sum.1 = (bf16[256,128]{1,0:T(8,128)(2,1)}, bf16[256,128]{1,0:T(8,128)(2,1)}, f32[1,8]{1,0:T(1,128)}, f32[1,8]{1,0:T(1,128)}) custom-call(f32[256,256]{1,0:T(8,128)S(1)} %get-tuple-element.70.refs_0_, f32[16,128]{1,0:T(8,128)S(1)} %get-tuple-element.71.refs_1_, bf16[288,256]{1,0:T(8,128)(2,1)S(1)} %collective-permute-done.13.refs_2_, ...), custom_call_target="tpu_custom_call" | custom-call | flops 1100000000 | bytes 1048576 | tf_op jit(solution)/shard_map/owner_sum/pallas_call | solution.py:631
  (44 shorter events, 3.0 us)
Async XLA Ops:
  2.2 6.2 %copy-start.10 = (bf16[256,256]{1,0:T(8,128)(2,1)S(1)}, bf16[256,256]{1,0:T(8,128)(2,1)}, u32[]{:S(2)}) copy-start(bf16[256,256]{1,0:T(8,128)(2,1)} %pack_kv.1._.refs_0_) | copy-start | bytes 393220
  2.2 11.7 %copy-start.2 = (bf16[1,256,1024]{2,1,0:T(8,128)(2,1)S(1)}, bf16[1,256,1024]{2,1,0:T(8,128)(2,1)}, u32[]{:S(2)}) copy-start(bf16[1,256,1024]{2,1,0:T(8,128)(2,1)} %param.14) | copy-start | bytes 1572868
  2.2 11.7 %copy-start.3 = (bf16[1,256,1024]{2,1,0:T(8,128)(2,1)S(1)}, bf16[1,256,1024]{2,1,0:T(8,128)(2,1)}, u32[]{:S(2)}) copy-start(bf16[1,256,1024]{2,1,0:T(8,128)(2,1)} %param.21) | copy-start | bytes 1572868
  2.2 11.7 %copy-start.4 = (bf16[1,256,128]{2,1,0:T(8,128)(2,1)S(1)}, bf16[1,256,128]{2,1,0:T(8,128)(2,1)}, u32[]{:S(2)}) copy-start(bf16[1,256,128]{2,1,0:T(8,128)(2,1)} %param.15) | copy-start | bytes 196612
  2.2 11.7 %copy-start.5 = (bf16[1,256,128]{2,1,0:T(8,128)(2,1)S(1)}, bf16[1,256,128]{2,1,0:T(8,128)(2,1)}, u32[]{:S(2)}) copy-start(bf16[1,256,128]{2,1,0:T(8,128)(2,1)} %param.16) | copy-start | bytes 196612
  2.3 11.6 %copy-start.6 = (f32[1,256,8]{1,2,0:T(8,128)S(1)}, f32[1,256,8]{1,2,0:T(8,128)}, u32[]{:S(2)}) copy-start(f32[1,256,8]{1,2,0:T(8,128)} %param.17) | copy-start | bytes 24580
  2.3 11.6 %copy-start.7 = (f32[8]{0:T(128)S(1)}, f32[8]{0:T(128)}, u32[]{:S(2)}) copy-start(f32[8]{0:T(128)} %skip_ref.1) | copy-start | bytes 100
  2.3 11.6 %copy-start.8 = (f32[8]{0:T(128)S(1)}, f32[8]{0:T(128)}, u32[]{:S(2)}) copy-start(f32[8]{0:T(128)} %rate_ref.5) | copy-start | bytes 100
  7.8 10.0 %collective-permute-start = (f32[4,64,1152]{2,1,0:T(8,128)}, f32[4,64,1152]{2,1,0:T(8,128)S(1)}, u32[]{:S(2)}, u32[]{:S(2)}) collective-permute-start(f32[4,64,1152]{2,1,0:T(8,128)} %get-tuple-element.46), channel_id=1, source_target_pairs={{0,1},{1,0},{2,3},{3,2},{4,5},{5,4},{6,7},{7,6},{8,9},{9,8},{10,11... | collective-permute-start | bytes 3538952 | tf_op jit(solution)/shard_map/ppermute | solution.py:438
  8.4 9.7 %collective-permute-start.1 = (bf16[256,256]{1,0:T(8,128)(2,1)S(1)}, bf16[256,256]{1,0:T(8,128)(2,1)S(1)}, u32[]{:S(2)}, u32[]{:S(2)}) collective-permute-start(bf16[256,256]{1,0:T(8,128)(2,1)S(1)} %copy-done.10), channel_id=1, source_target_pairs={{0,2},{1,3},{2,4},{3,5},{4,6},{5,7},{6,0},{7,1},{8,10},{9,11},{10,... | collective-permute-start | bytes 393224 | tf_op jit(solution)/shard_map/ppermute | solution.py:443
  10.9 7.9 %collective-permute-start.2 = (bf16[256,256]{1,0:T(8,128)(2,1)S(1)}, bf16[256,256]{1,0:T(8,128)(2,1)S(1)}, u32[]{:S(2)}, u32[]{:S(2)}) collective-permute-start(bf16[256,256]{1,0:T(8,128)(2,1)S(1)} %copy-done.10), channel_id=1, source_target_pairs={{0,4},{1,5},{2,6},{3,7},{4,0},{5,1},{6,2},{7,3},{8,12},{9,13},{10,... | collective-permute-start | bytes 393224 | tf_op jit(solution)/shard_map/ppermute | solution.py:443
  12.4 6.6 %collective-permute-start.3 = (bf16[256,256]{1,0:T(8,128)(2,1)S(1)}, bf16[256,256]{1,0:T(8,128)(2,1)S(1)}, u32[]{:S(2)}, u32[]{:S(2)}) collective-permute-start(bf16[256,256]{1,0:T(8,128)(2,1)S(1)} %copy-done.10), channel_id=1, source_target_pairs={{0,6},{1,7},{2,0},{3,1},{4,2},{5,3},{6,4},{7,5},{8,14},{9,15},{10,... | collective-permute-start | bytes 393224 | tf_op jit(solution)/shard_map/ppermute | solution.py:443
  19.1 4.5 %collective-permute-start.4 = (bf16[4,256,256]{2,1,0:T(8,128)(2,1)S(1)}, bf16[4,256,256]{2,1,0:T(8,128)(2,1)S(1)}, u32[]{:S(2)}, u32[]{:S(2)}) collective-permute-start(bf16[4,256,256]{2,1,0:T(8,128)(2,1)S(1)} %stack_kv.1.refs_3_), channel_id=1, source_target_pairs={{0,1},{1,0},{2,3},{3,2},{4,5},{5,4},{6,7},{7,6},{8,9},{9,8},{10,11... | collective-permute-start | bytes 1572872 | tf_op jit(solution)/shard_map/ppermute | solution.py:438
  19.2 9.1 %collective-permute-start.5 = (bf16[64,1152]{1,0:T(8,128)(2,1)S(1)}, bf16[64,1152]{1,0:T(8,128)(2,1)S(1)}, u32[]{:S(2)}, u32[]{:S(2)}) collective-permute-start(bf16[64,1152]{1,0:T(8,128)(2,1)S(1)} %get-tuple-element.48._.refs_5_), channel_id=1, source_target_pairs={{0,2},{1,3},{2,4},{3,5},{4,6},{5,7},{6,0},{7,1},{8,10},{9,11},{10,... | collective-permute-start | bytes 442376 | tf_op jit(solution)/shard_map/ppermute | solution.py:443
  21.0 8.5 %collective-permute-start.6 = (bf16[64,1152]{1,0:T(8,128)(2,1)S(1)}, bf16[64,1152]{1,0:T(8,128)(2,1)S(1)}, u32[]{:S(2)}, u32[]{:S(2)}) collective-permute-start(bf16[64,1152]{1,0:T(8,128)(2,1)S(1)} %get-tuple-element.50), channel_id=1, source_target_pairs={{0,4},{1,5},{2,6},{3,7},{4,0},{5,1},{6,2},{7,3},{8,12},{9,13},{10,... | collective-permute-start | bytes 442376 | tf_op jit(solution)/shard_map/ppermute | solution.py:443
  21.3 8.3 %collective-permute-start.7 = (bf16[64,1152]{1,0:T(8,128)(2,1)S(1)}, bf16[64,1152]{1,0:T(8,128)(2,1)S(1)}, u32[]{:S(2)}, u32[]{:S(2)}) collective-permute-start(bf16[64,1152]{1,0:T(8,128)(2,1)S(1)} %get-tuple-element.51), channel_id=1, source_target_pairs={{0,6},{1,7},{2,0},{3,1},{4,2},{5,3},{6,4},{7,5},{8,14},{9,15},{10,... | collective-permute-start | bytes 442376 | tf_op jit(solution)/shard_map/ppermute | solution.py:443
  30.2 10.1 %collective-permute-start.10 = (f32[16,128]{1,0:T(8,128)S(1)}, f32[16,128]{1,0:T(8,128)S(1)}, u32[]{:S(2)}, u32[]{:S(2)}) collective-permute-start(f32[16,128]{1,0:T(8,128)S(1)} %get-tuple-element.57.refs_6_.refs_1_), channel_id=1, source_target_pairs={{0,16},{8,24},{16,0},{24,8},{1,17},{9,25},{17,1},{25,9},{2,18},{10... | collective-permute-start | bytes 24584 | tf_op jit(solution)/shard_map/ppermute | solution.py:448
  32.8 7.5 %collective-permute-start.11 = (f32[16,128]{1,0:T(8,128)S(1)}, f32[16,128]{1,0:T(8,128)S(1)}, u32[]{:S(2)}, u32[]{:S(2)}) collective-permute-start(f32[16,128]{1,0:T(8,128)S(1)} %get-tuple-element.57.refs_6_.refs_1_), channel_id=1, source_target_pairs={{0,24},{8,0},{16,8},{24,16},{1,25},{9,1},{17,9},{25,17},{2,26},{10... | collective-permute-start | bytes 24584 | tf_op jit(solution)/shard_map/ppermute | solution.py:448
  34.2 6.1 %collective-permute-start.9 = (f32[16,128]{1,0:T(8,128)S(1)}, f32[16,128]{1,0:T(8,128)S(1)}, u32[]{:S(2)}, u32[]{:S(2)}) collective-permute-start(f32[16,128]{1,0:T(8,128)S(1)} %get-tuple-element.57.refs_6_.refs_1_), channel_id=1, source_target_pairs={{0,8},{8,16},{16,24},{24,0},{1,9},{9,17},{17,25},{25,1},{2,10},{10... | collective-permute-start | bytes 24584 | tf_op jit(solution)/shard_map/ppermute | solution.py:448
  40.5 2.0 %collective-permute-start.12 = (bf16[1056,256]{1,0:T(8,128)(2,1)S(1)}, bf16[1056,256]{1,0:T(8,128)(2,1)S(1)}, u32[]{:S(2)}, u32[]{:S(2)}) collective-permute-start(bf16[1056,256]{1,0:T(8,128)(2,1)S(1)} %get-tuple-element.65), channel_id=1, source_target_pairs={{0,1},{1,0},{2,3},{3,2},{4,5},{5,4},{6,7},{7,6},{8,9},{9,8},{10,11... | collective-permute-start | bytes 1622024 | tf_op jit(solution)/shard_map/ppermute | solution.py:438
  40.6 6.1 %collective-permute-start.8 = (bf16[2,64,1024]{2,1,0:T(8,128)(2,1)S(1)}, bf16[2,64,1024]{2,1,0:T(8,128)(2,1)S(1)}, u32[]{:S(2)}, u32[]{:S(2)}) collective-permute-start(bf16[2,64,1024]{2,1,0:T(8,128)(2,1)S(1)} %get-tuple-element.53), channel_id=1, source_target_pairs={{0,1},{1,0},{2,3},{3,2},{4,5},{5,4},{6,7},{7,6},{8,9},{9,8},{10,11... | collective-permute-start | bytes 786440 | tf_op jit(solution)/shard_map/ppermute | solution.py:438
  42.6 7.7 %collective-permute-start.13 = (bf16[288,256]{1,0:T(8,128)(2,1)S(1)}, bf16[288,256]{1,0:T(8,128)(2,1)S(1)}, u32[]{:S(2)}, u32[]{:S(2)}) collective-permute-start(bf16[288,256]{1,0:T(8,128)(2,1)S(1)} %get-tuple-element.67._), channel_id=1, source_target_pairs={{0,2},{1,3},{2,4},{3,5},{4,6},{5,7},{6,0},{7,1},{8,10},{9,11},{10,... | collective-permute-start | bytes 442376 | tf_op jit(solution)/shard_map/ppermute | solution.py:443
  44.4 8.2 %collective-permute-start.14 = (bf16[288,256]{1,0:T(8,128)(2,1)S(1)}, bf16[288,256]{1,0:T(8,128)(2,1)S(1)}, u32[]{:S(2)}, u32[]{:S(2)}) collective-permute-start(bf16[288,256]{1,0:T(8,128)(2,1)S(1)} %get-tuple-element.72), channel_id=1, source_target_pairs={{0,4},{1,5},{2,6},{3,7},{4,0},{5,1},{6,2},{7,3},{8,12},{9,13},{10,... | collective-permute-start | bytes 442376 | tf_op jit(solution)/shard_map/ppermute | solution.py:443
  45.0 7.6 %collective-permute-start.15 = (bf16[288,256]{1,0:T(8,128)(2,1)S(1)}, bf16[288,256]{1,0:T(8,128)(2,1)S(1)}, u32[]{:S(2)}, u32[]{:S(2)}) collective-permute-start(bf16[288,256]{1,0:T(8,128)(2,1)S(1)} %get-tuple-element.73), channel_id=1, source_target_pairs={{0,6},{1,7},{2,0},{3,1},{4,2},{5,3},{6,4},{7,5},{8,14},{9,15},{10,... | collective-permute-start | bytes 442376 | tf_op jit(solution)/shard_map/ppermute | solution.py:443
  (4 other events, 13.0 us)

commit v7 on v6

--- a/solution.py
+++ b/solution.py
@@ -80,9 +80,13 @@
         copy.wait()
 
 
-def stack_kernel(*refs):
-    for k, ref in enumerate(refs[:-1]):
-        refs[-1][k] = ref[...]
+def split_kernel(states_ref, *refs):
+    keep_ref, give_ref, stack_ref = refs[-3:]
+    _, core = chip_and_core()
+    keep_ref[...] = states_ref[:, pl.ds(pl.multiple_of(core * HALF, HALF), HALF), :]
+    give_ref[...] = states_ref[:, pl.ds(pl.multiple_of((1 - core) * HALF, HALF), HALF), :]
+    for k, ref in enumerate(refs[:-3]):
+        stack_ref[k] = ref[...]
 
 
 def enter_and_tail(run0, run1):
@@ -93,27 +97,14 @@
 
 
 def local_states_kernel(
-    x_hbm, g_hbm, b_hbm, c_hbm, step_hbm, rate_ref, _, keep_ref, give_ref,
-    x_ref, g_ref, b_ref, c_ref, step_ref, sems, pad_ref, high_ref, rest_ref, log_ref, state_ref,
+    x_ref, g_ref, b_ref, c_ref, step_ref, rate_ref, state_ref, pad_ref, high_ref, rest_ref, log_ref
 ):
-    _, core = chip_and_core()
-    step_copy, b_copy, x_copy, c_copy, g_copy = fetch(
-        [(step_hbm, step_ref), (b_hbm, b_ref), (x_hbm, x_ref), (c_hbm, c_ref), (g_hbm, g_ref)], sems
-    )
-    step_copy.wait()
     _, _, run0, run1 = running_logs(step_ref, rate_ref, pad_ref)
     enter_log, tail_log, total = enter_and_tail(run0, run1)
     enter, tail = jnp.exp(enter_log), jnp.exp(tail_log)
-    logs = jnp.broadcast_to(total, (HALF, LANES))
-    mine = pl.ds(pl.multiple_of(core * HALF, HALF), HALF)
-    other = pl.ds(pl.multiple_of((1 - core) * HALF, HALF), HALF)
-    cases = (
-        (b_ref, x_ref, tail, tail_log, (b_copy, x_copy)),
-        (c_ref, g_ref, enter, enter_log, (c_copy, g_copy)),
-    )
-    for direction, (left, right, factor, weight, copies) in enumerate(cases):
-        for copy in copies:
-            copy.wait()
+    state_ref[:, :, WIDE:] = jnp.broadcast_to(total, (4, NS, LANES))
+    cases = ((b_ref, x_ref, tail, tail_log), (c_ref, g_ref, enter, enter_log))
+    for direction, (left, right, factor, weight) in enumerate(cases):
         for h in range(HS):
             product = right[:, head(h)].astype(F32) * factor[:, h : h + 1]
             rounded = product.astype(BF16)
@@ -121,15 +112,10 @@
             rest_ref[:, head(h)] = (product - rounded.astype(F32)).astype(BF16)
             log_ref[:, head(h)] = (product * weight[:, h : h + 1]).astype(BF16)
         turned_left = left[...].astype(F32).T.astype(BF16)
-        state_ref[direction] = dot(turned_left, high_ref[...], 1, 0) + dot(
+        state_ref[direction, :, :WIDE] = dot(turned_left, high_ref[...], 1, 0) + dot(
             turned_left, rest_ref[...], 1, 0
         )
-        state_ref[3 - direction] = dot(turned_left, log_ref[...], 1, 0)
-    for kind in range(4):
-        keep_ref[kind, :, :WIDE] = state_ref[kind, mine, :]
-        keep_ref[kind, :, WIDE:] = logs
-        give_ref[kind, :, :WIDE] = state_ref[kind, other, :]
-        give_ref[kind, :, WIDE:] = logs
+        state_ref[3 - direction, :, :WIDE] = dot(turned_left, log_ref[...], 1, 0)
 
 
 def three_parts(value, rows):
@@ -240,12 +226,20 @@
         v_ref[target, lower] = jnp.where(live, v_tile, jnp.zeros_like(v_tile))
         v_ref[target, upper] = jnp.full((BLOCK, LANES), jnp.where(live, 1.0, 0.0), F32).astype(BF16)
     group = 2
-    for first in range(0, QUERY_HEADS, group):
+    firsts = range(0, QUERY_HEADS, group)
+
+    def stacked(ref, first):
+        return jnp.concatenate([ref[at, head(h)] for h in range(first, first + group)], axis=0)
+
+    upcoming = dot(stacked(q_ref, 0), k_ref[...], 1, 1)
+    for first in firsts:
         heads = range(first, first + group)
         rows = slice(first * BLOCK, (first + group) * BLOCK)
-        q = jnp.concatenate([q_ref[at, head(h)] for h in heads], axis=0)
-        g = jnp.concatenate([g_ref[at, head(h)] for h in heads], axis=0)
-        scores = dot(q, k_ref[...], 1, 1)
+        q, g = stacked(q_ref, first), stacked(g_ref, first)
+        scores = upcoming
+        dprobs = dot(g, v_ref[:, lower], 1, 1)
+        if first + group < QUERY_HEADS:
+            upcoming = dot(stacked(q_ref, first + group), k_ref[...], 1, 1)
         best = jnp.max(scores, axis=1, keepdims=True)
         weights = jnp.exp2((scores - best) * scale)
         wb_ref[rows, :] = weights.astype(BF16)
@@ -253,7 +247,6 @@
         inverse = 1.0 / both[:, upper]
         out = both[:, lower] * inverse
         delta = jnp.sum(out * g.astype(F32), axis=1, keepdims=True)
-        dprobs = dot(g, v_ref[:, lower], 1, 1)
         ds_ref[rows, :] = (weights * (dprobs - delta)).astype(BF16)
         dq = (dot(ds_ref[rows, :], k_live_ref[...], 1, 0) * (inverse * FACTOR)).astype(BF16)
         q_turned_ref[:, rows] = (q.astype(F32) * inverse).astype(BF16).T
@@ -358,7 +351,7 @@
 
 
 def inner_kernel(
-    x_ref, g_ref, b_ref, c_ref, step_ref, rate_ref, skip_ref, _,
+    x_ref, g_ref, b_ref, c_ref, step_ref, rate_ref, skip_ref,
     y_ref, dx_ref, db_ref, dc_ref, sums_ref,
     pad_ref, inner_ref, dinner_ref, m_ref, runt_ref,
 ):
@@ -406,6 +399,15 @@
     db_ref[...] = dot(dinner, c, 0, 0)
 
 
+def chunk_kernel(
+    x_ref, g_ref, b_ref, c_ref, step_ref, rate_ref, skip_ref, _,
+    state_ref, y_ref, dx_ref, db_ref, dc_ref, sums_ref, pad_ref, *scratch
+):
+    operands = (x_ref, g_ref, b_ref, c_ref, step_ref, rate_ref)
+    local_states_kernel(*operands, state_ref, pad_ref, *scratch[:3])
+    inner_kernel(*operands, skip_ref, y_ref, dx_ref, db_ref, dc_ref, sums_ref, pad_ref, *scratch[3:])
+
+
 def outer_kernel(
     x_ref, g_ref, b_ref, c_ref, step_ref, rate_ref, own_ref, other_ref, first_ref, second_ref,
     inner_y_ref, inner_dx_ref, inner_db_ref, inner_dc_ref, _,
@@ -483,44 +485,38 @@
     )(key[0], value[0])
     kv_parts = [kv] + [from_chip(kv, k) for k in range(1, chips)]
 
-    half = ((4, HALF, WIDE + LANES), F32)
-    keep, give = call(
-        local_states_kernel,
-        [half, half],
-        [AFTER] * 5 + [SMEM, AFTER],
+    states, inner_y, inner_dx, inner_db, inner_dc, sums = call(
+        chunk_kernel,
+        [((4, NS, WIDE + LANES), F32)]
+        + [((tokens, WIDE), F32)] * 2
+        + [((tokens, NS), F32)] * 2
+        + [((2 * HS, LANES), F32)],
+        [VMEM] * 5 + [SMEM] * 2 + [AFTER],
         [
-            pltpu.VMEM((tokens, WIDE), BF16),
-            pltpu.VMEM((tokens, WIDE), BF16),
-            pltpu.VMEM((tokens, NS), BF16),
-            pltpu.VMEM((tokens, NS), BF16),
-            pltpu.VMEM((HS, tokens), F32),
-            pltpu.SemaphoreType.DMA((5,)),
             pltpu.VMEM((LANES, tokens), F32),
             pltpu.VMEM((tokens, WIDE), BF16),
             pltpu.VMEM((tokens, WIDE), BF16),
             pltpu.VMEM((tokens, WIDE), BF16),
-            pltpu.VMEM((4, NS, WIDE), F32),
-        ],
-        20,
-        "local_states",
-        60,
-    )(x, g, b, c, steps, rate_log, kv)
-    received = swapped(give)
-
-    inner_y, inner_dx, inner_db, inner_dc, sums = call(
-        inner_kernel,
-        [((tokens, WIDE), F32)] * 2 + [((tokens, NS), F32)] * 2 + [((2 * HS, LANES), F32)],
-        [VMEM] * 5 + [SMEM] * 2 + [AFTER],
-        [
-            pltpu.VMEM((LANES, tokens), F32),
             pltpu.VMEM((tokens, tokens), F32),
             pltpu.VMEM((tokens, tokens), F32),
             pltpu.VMEM((tokens, tokens), BF16),
             pltpu.VMEM((LANES, 2 * tokens), F32),
         ],
-        0.3,
-        "chunk_inner",
-    )(x, g, b, c, steps, rate_log, skip, keep)
+        6,
+        "chunk_alone",
+        20,
+    )(x, g, b, c, steps, rate_log, skip, kv)
+    half = ((4, HALF, WIDE + LANES), F32)
+    keep, give, stack = call(
+        split_kernel,
+        [half, half, ((chips, tokens, 2 * LANES), BF16)],
+        [VMEM] * (1 + chips),
+        [],
+        1,
+        "split_states",
+    )(states, *kv_parts)
+    received = swapped(give)
+    other_stack = swapped(stack)
 
     messages = call(
         lambda *refs: combine_kernel(chips, *refs),
@@ -531,15 +527,6 @@
         "combine_states",
     )(keep, received, sums)
     arrived = [from_chip(messages[k - 1], k) for k in range(1, chips)]
-    (stack,) = call(
-        lambda _, *refs: stack_kernel(*refs),
-        [((chips, tokens, 2 * LANES), BF16)],
-        [AFTER] + [VMEM] * chips,
-        [],
-        1,
-        "stack_kv",
-    )(messages[0], *kv_parts)
-    other_stack = swapped(stack)
 
     columns = QUERY_HEADS * BLOCK
     scratch = [

time: 53.7 us -> 50.6 us (0.942)
  Pallas kernels: 24.7 us -> 20.3 us
  waiting for transfers between devices: 6.82 us -> 9.07 us
    pallas_call x3 -> x2, Pallas kernels: 8.2 us -> 4.73 us  [the longest x1 4.53 us: body(): call(chunk_kernel, [((4, NS, WIDE + LANES), F32)] + [((tokens, WIDE), F32...]
    ppermute x4, waiting for transfers between devices: 1.43 us -> 3.77 us  [swapped(): lax.ppermute(array, 'seq', [(i, i ^ 1) for i in range(lax.axis_size('seq'...]
    unnamed x24 -> x20, local copies, waits for them, and re-layouts: 1.33 us -> 0.97 us
  transfers between devices with their start and end apart: 16 -> 16, of which waited for: 6 -> 5; matrix products, arithmetic and copies ran while one was open for 0% -> 0% of each run, Pallas kernels for 30% -> 33%
where the time goes in v7:
time: 50.6 us; the launch traced here: 50.4 us
  Pallas kernels  20.3 us (40%)
  starting transfers between devices  19.2 us (38%)
  waiting for transfers between devices  9.07 us (18%)
  local copies, waits for them, and re-layouts  0.97 us (2%)
  between operations  0.87 us (2%)
    ppermute x9, starting transfers between devices, from_chip(): return lax.ppermute(array, 'seq', [(i, (i + 2 * k) % n) for i in range(n)])  13.4 us
    ppermute x9, waiting for transfers between devices, from_chip(): return lax.ppermute(array, 'seq', [(i, (i + 2 * k) % n) for i in range(n)])  5.3 us
    pallas_call x1, Pallas kernels, body(): call(lambda *refs: second_attention_kernel(most, *refs), [((BLOCK, column...  4.92 us
    ppermute x3, starting transfers between devices, turned(): return lax.ppermute(array, 'dp', [(i, (i + k) % n) for i in range(n)])  4.68 us
    pallas_call x1, Pallas kernels, body(): call(chunk_kernel, [((4, NS, WIDE + LANES), F32)] + [((tokens, WIDE), F32...  4.53 us
    pallas_call x1, Pallas kernels, body(): call(lambda *refs: first_attention_kernel(chips, most, *refs), [((BLOCK,...  4.18 us
    ppermute x4, waiting for transfers between devices, swapped(): lax.ppermute(array, 'seq', [(i, i ^ 1) for i in range(lax.axis_size('seq'...  3.77 us
    pallas_call x1, Pallas kernels, body(): call(outer_kernel, [((tokens, WIDE), BF16)] * 2 + [((tokens, NS), BF16)]...  2.81 us
  transfers between devices with their start and end apart: 16, of which 5 were waited for; matrix products, arithmetic and copies ran while one was open for 0% of the time, Pallas kernels for 33%

profile of v7, /device:TPU:0, one launch (start us, length us, event | category | flops | bytes accessed | tf_op | source)
XLA Modules:
  0.0 50.4 jit_solution(10565437661485278003)
XLA Ops:
  0.7 1.6 %pack_kv.1._.refs_0_ = bf16[256,256]{1,0:T(8,128)(2,1)} custom-call(bf16[256,128]{1,0:T(8,128)(2,1)} %bitcast.36, bf16[256,128]{1,0:T(8,128)(2,1)} %bitcast.37), custom_call_target="tpu_custom_call" | custom-call | flops 1100000000 | bytes 1048576 | tf_op jit(solution)/shard_map/pack_kv/pallas_call | solution.py:477
  2.3 3.0 %collective-permute-start = (bf16[256,256]{1,0:T(8,128)(2,1)}, bf16[256,256]{1,0:T(8,128)(2,1)S(1)}, u32[]{:S(2)}, u32[]{:S(2)}) collective-permute-start(bf16[256,256]{1,0:T(8,128)(2,1)} %pack_kv.1._.refs_0_), channel_id=1, source_target_pairs={{0,2},{1,3},{2,4},{3,5},{4,6},{5,7},{6,0},{7,1},{8,10},{9,11},{10,... | collective-permute-start | bytes 393224 | tf_op jit(solution)/shard_map/ppermute | solution.py:445
  5.3 1.5 %collective-permute-start.1 = (bf16[256,256]{1,0:T(8,128)(2,1)}, bf16[256,256]{1,0:T(8,128)(2,1)S(1)}, u32[]{:S(2)}, u32[]{:S(2)}) collective-permute-start(bf16[256,256]{1,0:T(8,128)(2,1)} %pack_kv.1._.refs_0_), channel_id=1, source_target_pairs={{0,4},{1,5},{2,6},{3,7},{4,0},{5,1},{6,2},{7,3},{8,12},{9,13},{10,... | collective-permute-start | bytes 393224 | tf_op jit(solution)/shard_map/ppermute | solution.py:445
  6.9 1.4 %collective-permute-start.2 = (bf16[256,256]{1,0:T(8,128)(2,1)}, bf16[256,256]{1,0:T(8,128)(2,1)S(1)}, u32[]{:S(2)}, u32[]{:S(2)}) collective-permute-start(bf16[256,256]{1,0:T(8,128)(2,1)} %pack_kv.1._.refs_0_), channel_id=1, source_target_pairs={{0,6},{1,7},{2,0},{3,1},{4,2},{5,3},{6,4},{7,5},{8,14},{9,15},{10,... | collective-permute-start | bytes 393224 | tf_op jit(solution)/shard_map/ppermute | solution.py:445
  8.3 0.9 %copy-done.3 = bf16[256,256]{1,0:T(8,128)(2,1)S(1)} copy-done((bf16[256,256]{1,0:T(8,128)(2,1)S(1)}, bf16[256,256]{1,0:T(8,128)(2,1)}, u32[]{:S(2)}) %copy-start.3) | copy-done | bytes 131096
  9.3 4.5 %chunk_alone.1 = (f32[4,128,1152]{2,1,0:T(8,128)S(1)}, f32[256,1024]{1,0:T(8,128)S(1)}, f32[256,1024]{1,0:T(8,128)S(1)}, f32[256,128]{1,0:T(8,128)S(1)}, f32[256,128]{1,0:T(8,128)S(1)}, /*index=5*/f32[16,128]{1,0:T(8,128)S(1)}) custom-call(bf16[256,1024]{1,0:T(8,128)(2,1)S(1)} %bitcast.22, bf16[256,1024]{1,0:T(8,128)(2,1)S(1)} %bitcast.24, ...), custom_call_target="tpu_custom_call" | custom-call | flops 6600000000 | bytes 1048576 | tf_op jit(solution)/shard_map/chunk_alone/pallas_call | solution.py:488
  14.6 2.3 %collective-permute-done.3.refs_1_ = f32[4,64,1152]{2,1,0:T(8,128)S(1)} collective-permute-done((f32[4,64,1152]{2,1,0:T(8,128)S(1)}, f32[4,64,1152]{2,1,0:T(8,128)S(1)}, u32[]{:S(2)}, u32[]{:S(2)}) %collective-permute-start.3) | collective-permute-done | bytes 1179680 | tf_op jit(solution)/shard_map/ppermute | solution.py:440
  17.2 1.0 %collective-permute-start.5 = (bf16[64,1152]{1,0:T(8,128)(2,1)S(1)}, bf16[64,1152]{1,0:T(8,128)(2,1)S(1)}, u32[]{:S(2)}, u32[]{:S(2)}) collective-permute-start(bf16[64,1152]{1,0:T(8,128)(2,1)S(1)} %get-tuple-element.52.refs_5_), channel_id=1, source_target_pairs={{0,2},{1,3},{2,4},{3,5},{4,6},{5,7},{6,0},{7,1},{8,10},{9,11},{10,... | collective-permute-start | bytes 442376 | tf_op jit(solution)/shard_map/ppermute | solution.py:445
  18.6 2.3 %collective-permute-start.7 = (bf16[64,1152]{1,0:T(8,128)(2,1)S(1)}, bf16[64,1152]{1,0:T(8,128)(2,1)S(1)}, u32[]{:S(2)}, u32[]{:S(2)}) collective-permute-start(bf16[64,1152]{1,0:T(8,128)(2,1)S(1)} %get-tuple-element.55), channel_id=1, source_target_pairs={{0,6},{1,7},{2,0},{3,1},{4,2},{5,3},{6,4},{7,5},{8,14},{9,15},{10,... | collective-permute-start | bytes 442376 | tf_op jit(solution)/shard_map/ppermute | solution.py:445
  20.9 4.2 %first_attention.1 = (f32[128,1024]{1,0:T(8,128)S(1)}, bf16[128,1024]{1,0:T(8,128)(2,1)S(1)}, f32[256,2048]{1,0:T(8,128)S(1)}, bf16[2048,256]{1,0:T(8,128)(2,1)S(1)}) custom-call(s32[16,16]{1,0:T(8,128)S(1)} %bitcast.32, bf16[256,1024]{1,0:T(8,128)(2,1)S(1)} %bitcast.20, bf16[256,1024]{1,0:T(8,128)(2,1)S(1)} %bitcast.25, ...), custom_call_target="tpu_custom_call" | custom-call | flops 5500000256 | bytes 1048576 | tf_op jit(solution)/shard_map/first_attention/pallas_call | solution.py:542
  25.1 1.9 %collective-permute-done.6.refs_5_ = bf16[64,1152]{1,0:T(8,128)(2,1)S(1)} collective-permute-done((bf16[64,1152]{1,0:T(8,128)(2,1)S(1)}, bf16[64,1152]{1,0:T(8,128)(2,1)S(1)}, u32[]{:S(2)}, u32[]{:S(2)}) %collective-permute-start.6) | collective-permute-done | bytes 147488 | tf_op jit(solution)/shard_map/ppermute | solution.py:445
  27.0 0.7 %chain_states.1 = (bf16[2,64,1024]{2,1,0:T(8,128)(2,1)S(1)}, bf16[2,64,1024]{2,1,0:T(8,128)(2,1)S(1)}, f32[16,128]{1,0:T(8,128)S(1)}) custom-call(f32[4,64,1152]{2,1,0:T(8,128)S(1)} %get-tuple-element.48.refs_0_, f32[4,64,1152]{2,1,0:T(8,128)S(1)} %collective-permute-done.3.refs_1_, f32[16,128]{1,0:T(8,128)S(1)} %get-tuple-element.50.refs_2_, ...), custom_call_target="tpu_custom_call" | custom-call | flops 2200000000 | bytes 1048576 | tf_op jit(solution)/shard_map/chain_states/pallas_call | solution.py:557
  27.7 2.7 %collective-permute-start.10 = (f32[16,128]{1,0:T(8,128)S(1)}, f32[16,128]{1,0:T(8,128)S(1)}, u32[]{:S(2)}, u32[]{:S(2)}) collective-permute-start(f32[16,128]{1,0:T(8,128)S(1)} %get-tuple-element.61.refs_6_.refs_1_), channel_id=1, source_target_pairs={{0,16},{8,24},{16,0},{24,8},{1,17},{9,25},{17,1},{25,9},{2,18},{10... | collective-permute-start | bytes 24584 | tf_op jit(solution)/shard_map/ppermute | solution.py:450
  30.4 1.3 %collective-permute-start.11 = (f32[16,128]{1,0:T(8,128)S(1)}, f32[16,128]{1,0:T(8,128)S(1)}, u32[]{:S(2)}, u32[]{:S(2)}) collective-permute-start(f32[16,128]{1,0:T(8,128)S(1)} %get-tuple-element.61.refs_6_.refs_1_), channel_id=1, source_target_pairs={{0,24},{8,0},{16,8},{24,16},{1,25},{9,1},{17,9},{25,17},{2,26},{10... | collective-permute-start | bytes 24584 | tf_op jit(solution)/shard_map/ppermute | solution.py:450
  31.7 0.7 %collective-permute-start.9 = (f32[16,128]{1,0:T(8,128)S(1)}, f32[16,128]{1,0:T(8,128)S(1)}, u32[]{:S(2)}, u32[]{:S(2)}) collective-permute-start(f32[16,128]{1,0:T(8,128)S(1)} %get-tuple-element.61.refs_6_.refs_1_), channel_id=1, source_target_pairs={{0,8},{8,16},{16,24},{24,0},{1,9},{9,17},{17,25},{25,1},{2,10},{10... | collective-permute-start | bytes 24584 | tf_op jit(solution)/shard_map/ppermute | solution.py:450
  32.4 4.9 %second_attention.1 = (f32[128,1024]{1,0:T(8,128)S(1)}, bf16[256,1024]{1,0:T(8,128)(2,1)}, f32[256,2048]{1,0:T(8,128)S(1)}) custom-call(s32[16,16]{1,0:T(8,128)S(1)} %bitcast.33, bf16[256,1024]{1,0:T(8,128)(2,1)S(1)} %bitcast.21, bf16[256,1024]{1,0:T(8,128)(2,1)S(1)} %bitcast.26, bf16[2048,256]{1,0:T(8,128)(2,1)S(1)} %get-tuple-element.59.refs_3_, ...), custom_call_target="tpu_custom_call" | custom-call | flops 5500000256 | bytes 1048576 | tf_op jit(solution)/shard_map/second_attention/pallas_call | solution.py:568
  38.0 1.4 %collective-permute-done.12.refs_1_ = bf16[1056,256]{1,0:T(8,128)(2,1)S(1)} collective-permute-done((bf16[1056,256]{1,0:T(8,128)(2,1)S(1)}, bf16[1056,256]{1,0:T(8,128)(2,1)S(1)}, u32[]{:S(2)}, u32[]{:S(2)}) %collective-permute-start.12) | collective-permute-done | bytes 540704 | tf_op jit(solution)/shard_map/ppermute | solution.py:440
  39.6 1.2 %collective-permute-start.13 = (bf16[288,256]{1,0:T(8,128)(2,1)S(1)}, bf16[288,256]{1,0:T(8,128)(2,1)S(1)}, u32[]{:S(2)}, u32[]{:S(2)}) collective-permute-start(bf16[288,256]{1,0:T(8,128)(2,1)S(1)} %get-tuple-element.71._), channel_id=1, source_target_pairs={{0,2},{1,3},{2,4},{3,5},{4,6},{5,7},{6,0},{7,1},{8,10},{9,11},{10,... | collective-permute-start | bytes 442376 | tf_op jit(solution)/shard_map/ppermute | solution.py:445
  40.8 1.4 %collective-permute-start.14 = (bf16[288,256]{1,0:T(8,128)(2,1)S(1)}, bf16[288,256]{1,0:T(8,128)(2,1)S(1)}, u32[]{:S(2)}, u32[]{:S(2)}) collective-permute-start(bf16[288,256]{1,0:T(8,128)(2,1)S(1)} %get-tuple-element.76), channel_id=1, source_target_pairs={{0,4},{1,5},{2,6},{3,7},{4,0},{5,1},{6,2},{7,3},{8,12},{9,13},{10,... | collective-permute-start | bytes 442376 | tf_op jit(solution)/shard_map/ppermute | solution.py:445
  42.2 1.2 %collective-permute-start.15 = (bf16[288,256]{1,0:T(8,128)(2,1)S(1)}, bf16[288,256]{1,0:T(8,128)(2,1)S(1)}, u32[]{:S(2)}, u32[]{:S(2)}) collective-permute-start(bf16[288,256]{1,0:T(8,128)(2,1)S(1)} %get-tuple-element.77), channel_id=1, source_target_pairs={{0,6},{1,7},{2,0},{3,1},{4,2},{5,3},{6,4},{7,5},{8,14},{9,15},{10,... | collective-permute-start | bytes 442376 | tf_op jit(solution)/shard_map/ppermute | solution.py:445
  43.4 2.8 %chunk_outer.1 = (bf16[256,1024]{1,0:T(8,128)(2,1)}, bf16[256,1024]{1,0:T(8,128)(2,1)}, bf16[256,128]{1,0:T(8,128)(2,1)}, bf16[256,128]{1,0:T(8,128)(2,1)}) custom-call(bf16[256,1024]{1,0:T(8,128)(2,1)S(1)} %bitcast.23, bf16[256,1024]{1,0:T(8,128)(2,1)S(1)} %bitcast.27, bf16[256,128]{1,0:T(8,128)(2,1)S(1)} %bitcast.29, bf16[256,128]{1,0:T(8,128)(2,1)S(1)} %bitcast.31, ...), custom_call_target="tpu_custom_call" | custom-call | flops 3300000000 | bytes 1048576 | tf_op jit(solution)/shard_map/chunk_outer/pallas_call | solution.py:600
  46.2 1.1 %collective-permute-done.13.refs_2_ = bf16[288,256]{1,0:T(8,128)(2,1)S(1)} collective-permute-done((bf16[288,256]{1,0:T(8,128)(2,1)S(1)}, bf16[288,256]{1,0:T(8,128)(2,1)S(1)}, u32[]{:S(2)}, u32[]{:S(2)}) %collective-permute-start.13) | collective-permute-done | bytes 147488 | tf_op jit(solution)/shard_map/ppermute | solution.py:445
  47.3 2.3 %collective-permute-done.14.refs_3_ = bf16[288,256]{1,0:T(8,128)(2,1)S(1)} collective-permute-done((bf16[288,256]{1,0:T(8,128)(2,1)S(1)}, bf16[288,256]{1,0:T(8,128)(2,1)S(1)}, u32[]{:S(2)}, u32[]{:S(2)}) %collective-permute-start.14) | collective-permute-done | bytes 147488 | tf_op jit(solution)/shard_map/ppermute | solution.py:445
  49.6 0.8 %owner_sum.1 = (bf16[256,128]{1,0:T(8,128)(2,1)}, bf16[256,128]{1,0:T(8,128)(2,1)}, f32[1,8]{1,0:T(1,128)}, f32[1,8]{1,0:T(1,128)}) custom-call(f32[256,256]{1,0:T(8,128)S(1)} %get-tuple-element.74.refs_0_, f32[16,128]{1,0:T(8,128)S(1)} %get-tuple-element.75.refs_1_, bf16[288,256]{1,0:T(8,128)(2,1)S(1)} %collective-permute-done.13.refs_2_, ...), custom_call_target="tpu_custom_call" | custom-call | flops 1100000000 | bytes 1048576 | tf_op jit(solution)/shard_map/owner_sum/pallas_call | solution.py:618
  (39 shorter events, 2.3 us)
Async XLA Ops:
  0.6 7.7 %copy-start.2 = (bf16[1,256,1024]{2,1,0:T(8,128)(2,1)S(1)}, bf16[1,256,1024]{2,1,0:T(8,128)(2,1)}, u32[]{:S(2)}) copy-start(bf16[1,256,1024]{2,1,0:T(8,128)(2,1)} %param.21) | copy-start | bytes 1572868
  0.7 7.6 %copy-start.1 = (bf16[1,256,1024]{2,1,0:T(8,128)(2,1)S(1)}, bf16[1,256,1024]{2,1,0:T(8,128)(2,1)}, u32[]{:S(2)}) copy-start(bf16[1,256,1024]{2,1,0:T(8,128)(2,1)} %param.14) | copy-start | bytes 1572868
  0.7 7.6 %copy-start.4 = (bf16[1,256,128]{2,1,0:T(8,128)(2,1)S(1)}, bf16[1,256,128]{2,1,0:T(8,128)(2,1)}, u32[]{:S(2)}) copy-start(bf16[1,256,128]{2,1,0:T(8,128)(2,1)} %param.15) | copy-start | bytes 196612
  0.7 7.6 %copy-start.5 = (bf16[1,256,128]{2,1,0:T(8,128)(2,1)S(1)}, bf16[1,256,128]{2,1,0:T(8,128)(2,1)}, u32[]{:S(2)}) copy-start(bf16[1,256,128]{2,1,0:T(8,128)(2,1)} %param.16) | copy-start | bytes 196612
  0.7 7.6 %copy-start.7 = (f32[1,256,8]{1,2,0:T(8,128)S(1)}, f32[1,256,8]{1,2,0:T(8,128)}, u32[]{:S(2)}) copy-start(f32[1,256,8]{1,2,0:T(8,128)} %param.17) | copy-start | bytes 24580
  0.7 7.6 %copy-start.9 = (f32[8]{0:T(128)S(1)}, f32[8]{0:T(128)}, u32[]{:S(2)}) copy-start(f32[8]{0:T(128)} %rate_ref.3) | copy-start | bytes 100
  0.7 7.6 %copy-start.8 = (f32[8]{0:T(128)S(1)}, f32[8]{0:T(128)}, u32[]{:S(2)}) copy-start(f32[8]{0:T(128)} %skip_ref.1) | copy-start | bytes 100
  2.3 11.5 %collective-permute-start = (bf16[256,256]{1,0:T(8,128)(2,1)}, bf16[256,256]{1,0:T(8,128)(2,1)S(1)}, u32[]{:S(2)}, u32[]{:S(2)}) collective-permute-start(bf16[256,256]{1,0:T(8,128)(2,1)} %pack_kv.1._.refs_0_), channel_id=1, source_target_pairs={{0,2},{1,3},{2,4},{3,5},{4,6},{5,7},{6,0},{7,1},{8,10},{9,11},{10,... | collective-permute-start | bytes 393224 | tf_op jit(solution)/shard_map/ppermute | solution.py:445
  5.3 8.5 %collective-permute-start.1 = (bf16[256,256]{1,0:T(8,128)(2,1)}, bf16[256,256]{1,0:T(8,128)(2,1)S(1)}, u32[]{:S(2)}, u32[]{:S(2)}) collective-permute-start(bf16[256,256]{1,0:T(8,128)(2,1)} %pack_kv.1._.refs_0_), channel_id=1, source_target_pairs={{0,4},{1,5},{2,6},{3,7},{4,0},{5,1},{6,2},{7,3},{8,12},{9,13},{10,... | collective-permute-start | bytes 393224 | tf_op jit(solution)/shard_map/ppermute | solution.py:445
  6.9 7.0 %collective-permute-start.2 = (bf16[256,256]{1,0:T(8,128)(2,1)}, bf16[256,256]{1,0:T(8,128)(2,1)S(1)}, u32[]{:S(2)}, u32[]{:S(2)}) collective-permute-start(bf16[256,256]{1,0:T(8,128)(2,1)} %pack_kv.1._.refs_0_), channel_id=1, source_target_pairs={{0,6},{1,7},{2,0},{3,1},{4,2},{5,3},{6,4},{7,5},{8,14},{9,15},{10,... | collective-permute-start | bytes 393224 | tf_op jit(solution)/shard_map/ppermute | solution.py:445
  14.0 6.8 %copy-start = (bf16[1,256,1024]{2,1,0:T(8,128)(2,1)S(1)}, bf16[1,256,1024]{2,1,0:T(8,128)(2,1)}, u32[]{:S(2)}) copy-start(bf16[1,256,1024]{2,1,0:T(8,128)(2,1)} %param.11) | copy-start | bytes 1572868
  14.1 2.9 %collective-permute-start.3 = (f32[4,64,1152]{2,1,0:T(8,128)S(1)}, f32[4,64,1152]{2,1,0:T(8,128)S(1)}, u32[]{:S(2)}, u32[]{:S(2)}) collective-permute-start(f32[4,64,1152]{2,1,0:T(8,128)S(1)} %get-tuple-element.49), channel_id=1, source_target_pairs={{0,1},{1,0},{2,3},{3,2},{4,5},{5,4},{6,7},{7,6},{8,9},{9,8},{10,11... | collective-permute-start | bytes 3538952 | tf_op jit(solution)/shard_map/ppermute | solution.py:440
  14.1 6.7 %collective-permute-start.4 = (bf16[4,256,256]{2,1,0:T(8,128)(2,1)S(1)}, bf16[4,256,256]{2,1,0:T(8,128)(2,1)S(1)}, u32[]{:S(2)}, u32[]{:S(2)}) collective-permute-start(bf16[4,256,256]{2,1,0:T(8,128)(2,1)S(1)} %get-tuple-element.51.refs_3_), channel_id=1, source_target_pairs={{0,1},{1,0},{2,3},{3,2},{4,5},{5,4},{6,7},{7,6},{8,9},{9,8},{10,11... | collective-permute-start | bytes 1572872 | tf_op jit(solution)/shard_map/ppermute | solution.py:440
  17.2 7.8 %collective-permute-start.5 = (bf16[64,1152]{1,0:T(8,128)(2,1)S(1)}, bf16[64,1152]{1,0:T(8,128)(2,1)S(1)}, u32[]{:S(2)}, u32[]{:S(2)}) collective-permute-start(bf16[64,1152]{1,0:T(8,128)(2,1)S(1)} %get-tuple-element.52.refs_5_), channel_id=1, source_target_pairs={{0,2},{1,3},{2,4},{3,5},{4,6},{5,7},{6,0},{7,1},{8,10},{9,11},{10,... | collective-permute-start | bytes 442376 | tf_op jit(solution)/shard_map/ppermute | solution.py:445
  18.2 8.8 %collective-permute-start.6 = (bf16[64,1152]{1,0:T(8,128)(2,1)S(1)}, bf16[64,1152]{1,0:T(8,128)(2,1)S(1)}, u32[]{:S(2)}, u32[]{:S(2)}) collective-permute-start(bf16[64,1152]{1,0:T(8,128)(2,1)S(1)} %get-tuple-element.54), channel_id=1, source_target_pairs={{0,4},{1,5},{2,6},{3,7},{4,0},{5,1},{6,2},{7,3},{8,12},{9,13},{10,... | collective-permute-start | bytes 442376 | tf_op jit(solution)/shard_map/ppermute | solution.py:445
  18.6 8.4 %collective-permute-start.7 = (bf16[64,1152]{1,0:T(8,128)(2,1)S(1)}, bf16[64,1152]{1,0:T(8,128)(2,1)S(1)}, u32[]{:S(2)}, u32[]{:S(2)}) collective-permute-start(bf16[64,1152]{1,0:T(8,128)(2,1)S(1)} %get-tuple-element.55), channel_id=1, source_target_pairs={{0,6},{1,7},{2,0},{3,1},{4,2},{5,3},{6,4},{7,5},{8,14},{9,15},{10,... | collective-permute-start | bytes 442376 | tf_op jit(solution)/shard_map/ppermute | solution.py:445
  27.7 9.6 %collective-permute-start.10 = (f32[16,128]{1,0:T(8,128)S(1)}, f32[16,128]{1,0:T(8,128)S(1)}, u32[]{:S(2)}, u32[]{:S(2)}) collective-permute-start(f32[16,128]{1,0:T(8,128)S(1)} %get-tuple-element.61.refs_6_.refs_1_), channel_id=1, source_target_pairs={{0,16},{8,24},{16,0},{24,8},{1,17},{9,25},{17,1},{25,9},{2,18},{10... | collective-permute-start | bytes 24584 | tf_op jit(solution)/shard_map/ppermute | solution.py:450
  30.4 7.0 %collective-permute-start.11 = (f32[16,128]{1,0:T(8,128)S(1)}, f32[16,128]{1,0:T(8,128)S(1)}, u32[]{:S(2)}, u32[]{:S(2)}) collective-permute-start(f32[16,128]{1,0:T(8,128)S(1)} %get-tuple-element.61.refs_6_.refs_1_), channel_id=1, source_target_pairs={{0,24},{8,0},{16,8},{24,16},{1,25},{9,1},{17,9},{25,17},{2,26},{10... | collective-permute-start | bytes 24584 | tf_op jit(solution)/shard_map/ppermute | solution.py:450
  31.7 5.6 %collective-permute-start.9 = (f32[16,128]{1,0:T(8,128)S(1)}, f32[16,128]{1,0:T(8,128)S(1)}, u32[]{:S(2)}, u32[]{:S(2)}) collective-permute-start(f32[16,128]{1,0:T(8,128)S(1)} %get-tuple-element.61.refs_6_.refs_1_), channel_id=1, source_target_pairs={{0,8},{8,16},{16,24},{24,0},{1,9},{9,17},{17,25},{25,1},{2,10},{10... | collective-permute-start | bytes 24584 | tf_op jit(solution)/shard_map/ppermute | solution.py:450
  37.5 2.0 %collective-permute-start.12 = (bf16[1056,256]{1,0:T(8,128)(2,1)S(1)}, bf16[1056,256]{1,0:T(8,128)(2,1)S(1)}, u32[]{:S(2)}, u32[]{:S(2)}) collective-permute-start(bf16[1056,256]{1,0:T(8,128)(2,1)S(1)} %get-tuple-element.69), channel_id=1, source_target_pairs={{0,1},{1,0},{2,3},{3,2},{4,5},{5,4},{6,7},{7,6},{8,9},{9,8},{10,11... | collective-permute-start | bytes 1622024 | tf_op jit(solution)/shard_map/ppermute | solution.py:440
  37.5 5.9 %collective-permute-start.8 = (bf16[2,64,1024]{2,1,0:T(8,128)(2,1)S(1)}, bf16[2,64,1024]{2,1,0:T(8,128)(2,1)S(1)}, u32[]{:S(2)}, u32[]{:S(2)}) collective-permute-start(bf16[2,64,1024]{2,1,0:T(8,128)(2,1)S(1)} %get-tuple-element.57), channel_id=1, source_target_pairs={{0,1},{1,0},{2,3},{3,2},{4,5},{5,4},{6,7},{7,6},{8,9},{9,8},{10,11... | collective-permute-start | bytes 786440 | tf_op jit(solution)/shard_map/ppermute | solution.py:440
  39.6 7.7 %collective-permute-start.13 = (bf16[288,256]{1,0:T(8,128)(2,1)S(1)}, bf16[288,256]{1,0:T(8,128)(2,1)S(1)}, u32[]{:S(2)}, u32[]{:S(2)}) collective-permute-start(bf16[288,256]{1,0:T(8,128)(2,1)S(1)} %get-tuple-element.71._), channel_id=1, source_target_pairs={{0,2},{1,3},{2,4},{3,5},{4,6},{5,7},{6,0},{7,1},{8,10},{9,11},{10,... | collective-permute-start | bytes 442376 | tf_op jit(solution)/shard_map/ppermute | solution.py:445
  40.8 8.8 %collective-permute-start.14 = (bf16[288,256]{1,0:T(8,128)(2,1)S(1)}, bf16[288,256]{1,0:T(8,128)(2,1)S(1)}, u32[]{:S(2)}, u32[]{:S(2)}) collective-permute-start(bf16[288,256]{1,0:T(8,128)(2,1)S(1)} %get-tuple-element.76), channel_id=1, source_target_pairs={{0,4},{1,5},{2,6},{3,7},{4,0},{5,1},{6,2},{7,3},{8,12},{9,13},{10,... | collective-permute-start | bytes 442376 | tf_op jit(solution)/shard_map/ppermute | solution.py:445
  42.2 7.4 %collective-permute-start.15 = (bf16[288,256]{1,0:T(8,128)(2,1)S(1)}, bf16[288,256]{1,0:T(8,128)(2,1)S(1)}, u32[]{:S(2)}, u32[]{:S(2)}) collective-permute-start(bf16[288,256]{1,0:T(8,128)(2,1)S(1)} %get-tuple-element.77), channel_id=1, source_target_pairs={{0,6},{1,7},{2,0},{3,1},{4,2},{5,3},{6,4},{7,5},{8,14},{9,15},{10,... | collective-permute-start | bytes 442376 | tf_op jit(solution)/shard_map/ppermute | solution.py:445
  (2 other events, 7.7 us)

commit v8 on v7

--- a/solution.py
+++ b/solution.py
@@ -17,6 +17,7 @@
 LOG2E = 1.4426950408889634
 NEG = -1e30
 HALF = NS // 2
+EARLY_HEADS = 4
 HIGH = lax.Precision.HIGHEST
 F32 = jnp.float32
 BF16 = jnp.bfloat16
@@ -192,7 +193,7 @@
 
 
 def block_attention(
-    block, most, mask_ref, q_ref, g_ref, kv_ref, out_ref, dq_ref, acc_ref,
+    block, chosen, most, mask_ref, q_ref, g_ref, kv_ref, out_ref, dq_ref, acc_ref,
     slot_ref, k_ref, k_live_ref, v_ref, q_turned_ref, g_turned_ref, ds_ref, wb_ref,
 ):
     count = mask_ref.shape[0]
@@ -226,19 +227,20 @@
         v_ref[target, lower] = jnp.where(live, v_tile, jnp.zeros_like(v_tile))
         v_ref[target, upper] = jnp.full((BLOCK, LANES), jnp.where(live, 1.0, 0.0), F32).astype(BF16)
     group = 2
-    firsts = range(0, QUERY_HEADS, group)
+    firsts = range(chosen[0], chosen[1], group)
+    used = slice(chosen[0] * BLOCK, chosen[1] * BLOCK)
 
     def stacked(ref, first):
         return jnp.concatenate([ref[at, head(h)] for h in range(first, first + group)], axis=0)
 
-    upcoming = dot(stacked(q_ref, 0), k_ref[...], 1, 1)
+    upcoming = dot(stacked(q_ref, chosen[0]), k_ref[...], 1, 1)
     for first in firsts:
         heads = range(first, first + group)
         rows = slice(first * BLOCK, (first + group) * BLOCK)
         q, g = stacked(q_ref, first), stacked(g_ref, first)
         scores = upcoming
         dprobs = dot(g, v_ref[:, lower], 1, 1)
-        if first + group < QUERY_HEADS:
+        if first + group < chosen[1]:
             upcoming = dot(stacked(q_ref, first + group), k_ref[...], 1, 1)
         best = jnp.max(scores, axis=1, keepdims=True)
         weights = jnp.exp2((scores - best) * scale)
@@ -253,10 +255,10 @@
         g_turned_ref[:, rows] = (g.astype(F32) * inverse).astype(BF16).T
         for place, h in enumerate(heads):
             part = slice(place * BLOCK, (place + 1) * BLOCK)
-            out_ref[:, head(h)] = out[part]
+            out_ref[own, head(h)] = out[part]
             dq_ref[own, head(h)] = dq[part]
-    dk = dot(q_turned_ref[...], ds_ref[...], 1, 0)
-    dv = dot(g_turned_ref[...], wb_ref[...], 1, 0)
+    dk = dot(q_turned_ref[:, used], ds_ref[used, :], 1, 0)
+    dv = dot(g_turned_ref[:, used], wb_ref[used, :], 1, 0)
     for slot, (index, live) in enumerate(slots):
         source = slice(slot * BLOCK, (slot + 1) * BLOCK)
 
@@ -278,15 +280,23 @@
             source = 2 * lax.rem(chip + chips - k, chips) + lax.rem(core + other, 2)
             at = pl.ds(pl.multiple_of(source * tokens, tokens), tokens)
             kv_ref[at, :] = ref[k]
-    block_attention(0, most, mask_ref, q_ref, g_ref, kv_ref, out_ref, dq_ref, acc_ref, *scratch)
+    shared = (most, mask_ref, q_ref, g_ref, kv_ref, out_ref, dq_ref, acc_ref, *scratch)
+    block_attention(0, (0, QUERY_HEADS), *shared)
+    block_attention(1, (0, EARLY_HEADS), *shared)
 
 
 def second_attention_kernel(
-    most, mask_ref, q_ref, g_ref, kv_ref, first_dq_ref, first_acc_ref, _, out_ref, dq_ref, acc_ref, *scratch
+    most, mask_ref, q_ref, g_ref, kv_ref, first_out_ref, first_dq_ref, first_acc_ref, _,
+    out_ref, dq_ref, acc_ref, *scratch
 ):
     acc_ref[...] = first_acc_ref[...]
-    dq_ref[:BLOCK, :] = first_dq_ref[...]
-    block_attention(1, most, mask_ref, q_ref, g_ref, kv_ref, out_ref, dq_ref, acc_ref, *scratch)
+    early = EARLY_HEADS * HEAD_WIDTH
+    dq_ref[:BLOCK, :] = first_dq_ref[:BLOCK, :]
+    dq_ref[BLOCK:, :early] = first_dq_ref[BLOCK:, :early]
+    out_ref[:BLOCK, :] = first_out_ref[:BLOCK, :]
+    out_ref[BLOCK:, :early] = first_out_ref[BLOCK:, :early]
+    shared = (most, mask_ref, q_ref, g_ref, kv_ref, out_ref, dq_ref, acc_ref, *scratch)
+    block_attention(1, (EARLY_HEADS, QUERY_HEADS), *shared)
 
 
 def share_kernel(chips, acc_ref, *refs):
@@ -310,12 +320,17 @@
         give_ref[rows, :] = acc_ref[:, pl.ds(other, tokens)].astype(BF16)
 
 
-def pair_sum_kernel(chips, keep_ref, recv_ref, sums_ref, own_ref, total_ref, *message_refs):
+def pair_sum_kernel(chips, keep_ref, recv_ref, sums_ref, *refs):
+    farther_refs, (own_ref, total_ref), message_refs = (
+        refs[: -chips - 1], refs[-chips - 1 : -chips + 1], refs[-chips + 1 :]
+    )
     chip, _ = chip_and_core()
     rows = own_ref.shape[0]
     at = pl.ds(pl.multiple_of(chip * rows, rows), rows)
     own_ref[...] = keep_ref[at, :].astype(F32) + recv_ref[at, :].astype(F32)
     total = sums_ref[...] + whole_sums(recv_ref[chips * rows :, :])
+    for ref in farther_refs:
+        total += ref[...]
     total_ref[...] = total
     high = total.astype(BF16)
     middle = (total - high.astype(F32)).astype(BF16)
@@ -400,7 +415,7 @@
 
 
 def chunk_kernel(
-    x_ref, g_ref, b_ref, c_ref, step_ref, rate_ref, skip_ref, _,
+    x_ref, g_ref, b_ref, c_ref, step_ref, rate_ref, skip_ref,
     state_ref, y_ref, dx_ref, db_ref, dc_ref, sums_ref, pad_ref, *scratch
 ):
     operands = (x_ref, g_ref, b_ref, c_ref, step_ref, rate_ref)
@@ -409,7 +424,7 @@
 
 
 def outer_kernel(
-    x_ref, g_ref, b_ref, c_ref, step_ref, rate_ref, own_ref, other_ref, first_ref, second_ref,
+    x_ref, g_ref, b_ref, c_ref, step_ref, rate_ref, own_ref, other_ref, att_ref,
     inner_y_ref, inner_dx_ref, inner_db_ref, inner_dc_ref, _,
     y_ref, dx_ref, db_ref, dc_ref,
     pad_ref, xt_ref, gt_ref, ent_ref,
@@ -428,9 +443,7 @@
         lanes = head(h)
         carried = dot(c, ent_ref[0, :, lanes], 1, 0) * enter[:, h : h + 1]
         back = dot(b, ent_ref[1, :, lanes], 1, 0) * tail[:, h : h + 1]
-        y = inner_y_ref[:, lanes] + carried
-        y_ref[:BLOCK, lanes] = (y[:BLOCK] + first_ref[:, lanes]).astype(BF16)
-        y_ref[BLOCK:, lanes] = (y[BLOCK:] + second_ref[:, lanes]).astype(BF16)
+        y_ref[:, lanes] = (inner_y_ref[:, lanes] + carried + att_ref[:, lanes]).astype(BF16)
         dx_ref[:, lanes] = (inner_dx_ref[:, lanes] + back).astype(BF16)
     dc_ref[...] = (inner_dc_ref[...] + dot(gt_ref[...], ent_ref[0], 1, 1)).astype(BF16)
     db_ref[...] = (inner_db_ref[...] + dot(xt_ref[...], ent_ref[1], 1, 1)).astype(BF16)
@@ -445,9 +458,12 @@
     return lax.ppermute(array, "seq", [(i, (i + 2 * k) % n) for i in range(n)])
 
 
-def turned(array, k):
-    n = lax.axis_size("dp")
-    return lax.ppermute(array, "dp", [(i, (i + k) % n) for i in range(n)])
+def from_replica(array, distance, flip):
+    replicas, n = lax.axis_size("dp"), lax.axis_size("seq")
+    pairs = [
+        (r * n + i, (r ^ distance) * n + (i ^ flip)) for r in range(replicas) for i in range(n)
+    ]
+    return lax.ppermute(array, ("dp", "seq"), pairs)
 
 
 def call(kernel, outs, ins, scratch, microseconds, name, limit=16):
@@ -491,7 +507,7 @@
         + [((tokens, WIDE), F32)] * 2
         + [((tokens, NS), F32)] * 2
         + [((2 * HS, LANES), F32)],
-        [VMEM] * 5 + [SMEM] * 2 + [AFTER],
+        [VMEM] * 5 + [SMEM] * 2,
         [
             pltpu.VMEM((LANES, tokens), F32),
             pltpu.VMEM((tokens, WIDE), BF16),
@@ -505,7 +521,7 @@
         6,
         "chunk_alone",
         20,
-    )(x, g, b, c, steps, rate_log, skip, kv)
+    )(x, g, b, c, steps, rate_log, skip)
     half = ((4, HALF, WIDE + LANES), F32)
     keep, give, stack = call(
         split_kernel,
@@ -542,8 +558,8 @@
     first_out, first_dq, first_acc, kv_all = call(
         lambda *refs: first_attention_kernel(chips, most, *refs),
         [
-            ((BLOCK, columns), F32),
-            ((BLOCK, columns), BF16),
+            ((tokens, columns), F32),
+            ((tokens, columns), BF16),
             ((2 * LANES, every), F32),
             ((every, 2 * LANES), BF16),
         ],
@@ -563,17 +579,17 @@
         "chain_states",
     )(keep, received, sums, first_dq, *arrived)
     other = swapped(give)
-    replicated = [turned(totals, k) for k in range(1, replicas)]
-
-    second_out, dq, acc = call(
+    neighbour = from_replica(totals, 1, 0)
+
+    attention, dq, acc = call(
         lambda *refs: second_attention_kernel(most, *refs),
-        [((BLOCK, columns), F32), ((tokens, columns), BF16), ((2 * LANES, every), F32)],
-        [SMEM] + [VMEM] * 5 + [AFTER],
+        [((tokens, columns), F32), ((tokens, columns), BF16), ((2 * LANES, every), F32)],
+        [SMEM] + [VMEM] * 6 + [AFTER],
         scratch,
         5,
         "second_attention",
         18 + most,
-    )(block_mask[0], q, g, kv_all, first_dq, first_acc, totals)
+    )(block_mask[0], q, g, kv_all, first_out, first_dq, first_acc, totals)
     keep, give, sums = call(
         lambda *refs: share_kernel(chips, *refs),
         [
@@ -581,26 +597,27 @@
             ((chips * 2 * LANES + 32, tokens), BF16),
             ((2 * HS, LANES), F32),
         ],
-        [VMEM] * (1 + replicas),
+        [VMEM] * 3,
         [],
         1,
         "share_key_gradients",
-    )(acc, totals, *replicated)
+    )(acc, totals, neighbour)
+    farther = [from_replica(sums, d, flip) for d in range(2, replicas, 2) for flip in (0, 1)]
     partial, summed, *messages = call(
         lambda *refs: pair_sum_kernel(chips, *refs),
         [((2 * LANES, tokens), F32), ((2 * HS, LANES), F32)]
         + [((2 * LANES + 32, tokens), BF16)] * (chips - 1),
-        [VMEM] * 3,
+        [VMEM] * (3 + len(farther)),
         [],
         1,
         "pair_sum",
-    )(keep, swapped(give), sums)
+    )(keep, swapped(give), sums, *farther)
     arrived = [from_chip(messages[k - 1], k) for k in range(1, chips)]
 
     y, dx, db, dc = call(
         outer_kernel,
         [((tokens, WIDE), BF16)] * 2 + [((tokens, NS), BF16)] * 2,
-        [VMEM] * 5 + [SMEM] + [VMEM] * 8 + [AFTER],
+        [VMEM] * 5 + [SMEM] + [VMEM] * 7 + [AFTER],
         [
             pltpu.VMEM((LANES, tokens), F32),
             pltpu.VMEM((tokens, WIDE), BF16),
@@ -610,7 +627,7 @@
         3,
         "chunk_outer",
     )(
-        x, g, b, c, steps, rate_log, own, other, first_out, second_out,
+        x, g, b, c, steps, rate_log, own, other, attention,
         inner_y, inner_dx, inner_db, inner_dc, messages[0],
     )
 

time: 50.6 us -> 52.2 us (1.032)
  waiting for transfers between devices: 9.07 us -> 13.5 us
  starting transfers between devices: 19.2 us -> 15.8 us
  Pallas kernels: 20.3 us -> 21.8 us
  local copies, waits for them, and re-layouts: 0.97 us -> 0.05 us
    ppermute x3, waiting for transfers between devices: 0.01 us -> 4.2 us  [from_replica(): return lax.ppermute(array, ('dp', 'seq'), pairs)]
    ppermute x9, starting transfers between devices: 13.4 us -> 10.4 us  [from_chip(): return lax.ppermute(array, 'seq', [(i, (i + 2 * k) % n) for i in range(n)])]
    ppermute x9, waiting for transfers between devices: 5.3 us -> 6.99 us  [from_chip(): return lax.ppermute(array, 'seq', [(i, (i + 2 * k) % n) for i in range(n)])]
    pallas_call x2, Pallas kernels: 9.09 us -> 10.6 us  [the longest x1 6.78 us: body(): call(lambda *refs: first_attention_kernel(chips, most, *refs), [((tokens,...]
    ppermute x4, waiting for transfers between devices: 3.77 us -> 2.34 us  [swapped(): lax.ppermute(array, 'seq', [(i, i ^ 1) for i in range(lax.axis_size('seq'...]
    unnamed x20, local copies, waits for them, and re-layouts: 0.97 us -> 0.05 us
  transfers between devices with their start and end apart: 16 -> 16, of which waited for: 5 -> 8; matrix products, arithmetic and copies ran while one was open for 0% -> 0% of each run, Pallas kernels for 33% -> 35%
where the time goes in v8:
time: 52.2 us; the launch traced here: 52 us
  Pallas kernels  21.8 us (42%)
  starting transfers between devices  15.8 us (30%)
  waiting for transfers between devices  13.5 us (26%)
  between operations  0.86 us (2%)
    ppermute x9, starting transfers between devices, from_chip(): return lax.ppermute(array, 'seq', [(i, (i + 2 * k) % n) for i in range(n)])  10.4 us
    ppermute x9, waiting for transfers between devices, from_chip(): return lax.ppermute(array, 'seq', [(i, (i + 2 * k) % n) for i in range(n)])  6.99 us
    pallas_call x1, Pallas kernels, body(): call(lambda *refs: first_attention_kernel(chips, most, *refs), [((tokens,...  6.78 us
    pallas_call x1, Pallas kernels, body(): call(chunk_kernel, [((4, NS, WIDE + LANES), F32)] + [((tokens, WIDE), F32...  4.53 us
    ppermute x3, starting transfers between devices, from_replica(): return lax.ppermute(array, ('dp', 'seq'), pairs)  4.26 us
    ppermute x3, waiting for transfers between devices, from_replica(): return lax.ppermute(array, ('dp', 'seq'), pairs)  4.2 us
    pallas_call x1, Pallas kernels, body(): call(lambda *refs: second_attention_kernel(most, *refs), [((tokens, colum...  3.8 us
    pallas_call x1, Pallas kernels, body(): call(outer_kernel, [((tokens, WIDE), BF16)] * 2 + [((tokens, NS), BF16)]...  2.83 us
  transfers between devices with their start and end apart: 16, of which 8 were waited for; matrix products, arithmetic and copies ran while one was open for 0% of the time, Pallas kernels for 35%

profile of v8, /device:TPU:0, one launch (start us, length us, event | category | flops | bytes accessed | tf_op | source)
XLA Modules:
  0.0 52.0 jit_solution(11060863995718195978)
XLA Ops:
  0.7 1.6 %pack_kv.1.refs_0_ = bf16[256,256]{1,0:T(8,128)(2,1)} custom-call(bf16[256,128]{1,0:T(8,128)(2,1)} %bitcast.36, bf16[256,128]{1,0:T(8,128)(2,1)} %bitcast.37), custom_call_target="tpu_custom_call" | custom-call | flops 1100000000 | bytes 1048576 | tf_op jit(solution)/shard_map/pack_kv/pallas_call | solution.py:493
  2.4 3.9 %collective-permute-start.2 = (bf16[256,256]{1,0:T(8,128)(2,1)}, bf16[256,256]{1,0:T(8,128)(2,1)S(1)}, u32[]{:S(2)}, u32[]{:S(2)}) collective-permute-start(bf16[256,256]{1,0:T(8,128)(2,1)} %pack_kv.1.refs_0_), channel_id=1, source_target_pairs={{0,6},{1,7},{2,0},{3,1},{4,2},{5,3},{6,4},{7,5},{8,14},{9,15},{10,... | collective-permute-start | bytes 393224 | tf_op jit(solution)/shard_map/ppermute | solution.py:458
  6.8 0.6 %collective-permute-start = (bf16[256,256]{1,0:T(8,128)(2,1)}, bf16[256,256]{1,0:T(8,128)(2,1)S(1)}, u32[]{:S(2)}, u32[]{:S(2)}) collective-permute-start(bf16[256,256]{1,0:T(8,128)(2,1)} %pack_kv.1.refs_0_), channel_id=1, source_target_pairs={{0,2},{1,3},{2,4},{3,5},{4,6},{5,7},{6,0},{7,1},{8,10},{9,11},{10,... | collective-permute-start | bytes 393224 | tf_op jit(solution)/shard_map/ppermute | solution.py:458
  7.5 4.5 %chunk_alone.1 = (f32[4,128,1152]{2,1,0:T(8,128)S(1)}, f32[256,1024]{1,0:T(8,128)S(1)}, f32[256,1024]{1,0:T(8,128)S(1)}, f32[256,128]{1,0:T(8,128)S(1)}, f32[256,128]{1,0:T(8,128)S(1)}, /*index=5*/f32[16,128]{1,0:T(8,128)S(1)}) custom-call(bf16[256,1024]{1,0:T(8,128)(2,1)S(1)} %bitcast.22, bf16[256,1024]{1,0:T(8,128)(2,1)S(1)} %bitcast.24, ...), custom_call_target="tpu_custom_call" | custom-call | flops 6600000000 | bytes 1048576 | tf_op jit(solution)/shard_map/chunk_alone/pallas_call | solution.py:504
  12.0 2.3 %collective-permute-done.1.refs_2_ = bf16[256,256]{1,0:T(8,128)(2,1)S(1)} collective-permute-done((bf16[256,256]{1,0:T(8,128)(2,1)}, bf16[256,256]{1,0:T(8,128)(2,1)S(1)}, u32[]{:S(2)}, u32[]{:S(2)}) %collective-permute-start.1) | collective-permute-done | bytes 131104 | tf_op jit(solution)/shard_map/ppermute | solution.py:458
  15.1 2.3 %collective-permute-done.3.refs_1_ = f32[4,64,1152]{2,1,0:T(8,128)S(1)} collective-permute-done((f32[4,64,1152]{2,1,0:T(8,128)S(1)}, f32[4,64,1152]{2,1,0:T(8,128)S(1)}, u32[]{:S(2)}, u32[]{:S(2)}) %collective-permute-start.3) | collective-permute-done | bytes 1179680 | tf_op jit(solution)/shard_map/ppermute | solution.py:453
  17.6 0.6 %collective-permute-start.6 = (bf16[64,1152]{1,0:T(8,128)(2,1)S(1)}, bf16[64,1152]{1,0:T(8,128)(2,1)S(1)}, u32[]{:S(2)}, u32[]{:S(2)}) collective-permute-start(bf16[64,1152]{1,0:T(8,128)(2,1)S(1)} %get-tuple-element.54), channel_id=1, source_target_pairs={{0,4},{1,5},{2,6},{3,7},{4,0},{5,1},{6,2},{7,3},{8,12},{9,13},{10,... | collective-permute-start | bytes 442376 | tf_op jit(solution)/shard_map/ppermute | solution.py:458
  18.2 1.3 %collective-permute-start.7 = (bf16[64,1152]{1,0:T(8,128)(2,1)S(1)}, bf16[64,1152]{1,0:T(8,128)(2,1)S(1)}, u32[]{:S(2)}, u32[]{:S(2)}) collective-permute-start(bf16[64,1152]{1,0:T(8,128)(2,1)S(1)} %get-tuple-element.55), channel_id=1, source_target_pairs={{0,6},{1,7},{2,0},{3,1},{4,2},{5,3},{6,4},{7,5},{8,14},{9,15},{10,... | collective-permute-start | bytes 442376 | tf_op jit(solution)/shard_map/ppermute | solution.py:458
  19.5 0.8 %collective-permute-start.5 = (bf16[64,1152]{1,0:T(8,128)(2,1)S(1)}, bf16[64,1152]{1,0:T(8,128)(2,1)S(1)}, u32[]{:S(2)}, u32[]{:S(2)}) collective-permute-start(bf16[64,1152]{1,0:T(8,128)(2,1)S(1)} %get-tuple-element.52.refs_5_), channel_id=1, source_target_pairs={{0,2},{1,3},{2,4},{3,5},{4,6},{5,7},{6,0},{7,1},{8,10},{9,11},{10,... | collective-permute-start | bytes 442376 | tf_op jit(solution)/shard_map/ppermute | solution.py:458
  20.3 6.8 %first_attention.1 = (f32[256,1024]{1,0:T(8,128)S(1)}, bf16[256,1024]{1,0:T(8,128)(2,1)S(1)}, f32[256,2048]{1,0:T(8,128)S(1)}, bf16[2048,256]{1,0:T(8,128)(2,1)S(1)}) custom-call(s32[16,16]{1,0:T(8,128)S(1)} %bitcast.32, bf16[256,1024]{1,0:T(8,128)(2,1)S(1)} %bitcast.20, bf16[256,1024]{1,0:T(8,128)(2,1)S(1)} %bitcast.25, ...), custom_call_target="tpu_custom_call" | custom-call | flops 5500000256 | bytes 1048576 | tf_op jit(solution)/shard_map/first_attention/pallas_call | solution.py:558
  27.1 0.9 %collective-permute-done.5.refs_4_ = bf16[64,1152]{1,0:T(8,128)(2,1)S(1)} collective-permute-done((bf16[64,1152]{1,0:T(8,128)(2,1)S(1)}, bf16[64,1152]{1,0:T(8,128)(2,1)S(1)}, u32[]{:S(2)}, u32[]{:S(2)}) %collective-permute-start.5) | collective-permute-done | bytes 147488 | tf_op jit(solution)/shard_map/ppermute | solution.py:458
  27.9 0.7 %chain_states.1 = (bf16[2,64,1024]{2,1,0:T(8,128)(2,1)S(1)}, bf16[2,64,1024]{2,1,0:T(8,128)(2,1)S(1)}, f32[16,128]{1,0:T(8,128)S(1)}) custom-call(f32[4,64,1152]{2,1,0:T(8,128)S(1)} %get-tuple-element.48.refs_0_, f32[4,64,1152]{2,1,0:T(8,128)S(1)} %collective-permute-done.3.refs_1_, f32[16,128]{1,0:T(8,128)S(1)} %get-tuple-element.50.refs_2_, ...), custom_call_target="tpu_custom_call" | custom-call | flops 2200000000 | bytes 1048576 | tf_op jit(solution)/shard_map/chain_states/pallas_call | solution.py:573
  28.6 1.6 %collective-permute-start.9 = (f32[16,128]{1,0:T(8,128)S(1)}, f32[16,128]{1,0:T(8,128)S(1)}, u32[]{:S(2)}, u32[]{:S(2)}) collective-permute-start(f32[16,128]{1,0:T(8,128)S(1)} %get-tuple-element.61.refs_7_.refs_1_), channel_id=1, source_target_pairs={{0,8},{1,9},{2,10},{3,11},{4,12},{5,13},{6,14},{7,15},{8,0},{9,1},... | collective-permute-start | bytes 24584 | tf_op jit(solution)/shard_map/ppermute | solution.py:466
  30.3 3.8 %second_attention.1 = (f32[256,1024]{1,0:T(8,128)S(1)}, bf16[256,1024]{1,0:T(8,128)(2,1)}, f32[256,2048]{1,0:T(8,128)S(1)}) custom-call(s32[16,16]{1,0:T(8,128)S(1)} %bitcast.33, bf16[256,1024]{1,0:T(8,128)(2,1)S(1)} %bitcast.21, bf16[256,1024]{1,0:T(8,128)(2,1)S(1)} %bitcast.26, bf16[2048,256]{1,0:T(8,128)(2,1)S(1)} %get-tuple-element.58.refs_3_, ...), custom_call_target="tpu_custom_call" | custom-call | flops 5500000256 | bytes 1048576 | tf_op jit(solution)/shard_map/second_attention/pallas_call | solution.py:584
  34.8 2.3 %collective-permute-start.12 = (f32[16,128]{1,0:T(8,128)S(1)}, f32[16,128]{1,0:T(8,128)S(1)}, u32[]{:S(2)}, u32[]{:S(2)}) collective-permute-start(f32[16,128]{1,0:T(8,128)S(1)} %get-tuple-element.70.refs_2_), channel_id=1, source_target_pairs={{0,17},{1,16},{2,19},{3,18},{4,21},{5,20},{6,23},{7,22},{8,25},{9,... | collective-permute-start | bytes 24584 | tf_op jit(solution)/shard_map/ppermute | solution.py:466
  37.4 1.4 %collective-permute-done.12.refs_4_ = f32[16,128]{1,0:T(8,128)S(1)} collective-permute-done((f32[16,128]{1,0:T(8,128)S(1)}, f32[16,128]{1,0:T(8,128)S(1)}, u32[]{:S(2)}, u32[]{:S(2)}) %collective-permute-start.12) | collective-permute-done | bytes 8224 | tf_op jit(solution)/shard_map/ppermute | solution.py:466
  38.8 2.8 %collective-permute-done.11.refs_3_ = f32[16,128]{1,0:T(8,128)S(1)} collective-permute-done((f32[16,128]{1,0:T(8,128)S(1)}, f32[16,128]{1,0:T(8,128)S(1)}, u32[]{:S(2)}, u32[]{:S(2)}) %collective-permute-start.11) | collective-permute-done | bytes 8224 | tf_op jit(solution)/shard_map/ppermute | solution.py:466
  41.8 0.8 %collective-permute-start.14 = (bf16[288,256]{1,0:T(8,128)(2,1)S(1)}, bf16[288,256]{1,0:T(8,128)(2,1)S(1)}, u32[]{:S(2)}, u32[]{:S(2)}) collective-permute-start(bf16[288,256]{1,0:T(8,128)(2,1)S(1)} %get-tuple-element.76), channel_id=1, source_target_pairs={{0,4},{1,5},{2,6},{3,7},{4,0},{5,1},{6,2},{7,3},{8,12},{9,13},{10,... | collective-permute-start | bytes 442376 | tf_op jit(solution)/shard_map/ppermute | solution.py:458
  42.5 1.4 %collective-permute-start.15 = (bf16[288,256]{1,0:T(8,128)(2,1)S(1)}, bf16[288,256]{1,0:T(8,128)(2,1)S(1)}, u32[]{:S(2)}, u32[]{:S(2)}) collective-permute-start(bf16[288,256]{1,0:T(8,128)(2,1)S(1)} %get-tuple-element.77), channel_id=1, source_target_pairs={{0,6},{1,7},{2,0},{3,1},{4,2},{5,3},{6,4},{7,5},{8,14},{9,15},{10,... | collective-permute-start | bytes 442376 | tf_op jit(solution)/shard_map/ppermute | solution.py:458
  43.9 0.6 %collective-permute-start.13 = (bf16[288,256]{1,0:T(8,128)(2,1)S(1)}, bf16[288,256]{1,0:T(8,128)(2,1)S(1)}, u32[]{:S(2)}, u32[]{:S(2)}) collective-permute-start(bf16[288,256]{1,0:T(8,128)(2,1)S(1)} %get-tuple-element.71._), channel_id=1, source_target_pairs={{0,2},{1,3},{2,4},{3,5},{4,6},{5,7},{6,0},{7,1},{8,10},{9,11},{10,... | collective-permute-start | bytes 442376 | tf_op jit(solution)/shard_map/ppermute | solution.py:458
  44.6 2.8 %chunk_outer.1 = (bf16[256,1024]{1,0:T(8,128)(2,1)}, bf16[256,1024]{1,0:T(8,128)(2,1)}, bf16[256,128]{1,0:T(8,128)(2,1)}, bf16[256,128]{1,0:T(8,128)(2,1)}) custom-call(bf16[256,1024]{1,0:T(8,128)(2,1)S(1)} %bitcast.23, bf16[256,1024]{1,0:T(8,128)(2,1)S(1)} %bitcast.27, bf16[256,128]{1,0:T(8,128)(2,1)S(1)} %bitcast.29, bf16[256,128]{1,0:T(8,128)(2,1)S(1)} %bitcast.31, ...), custom_call_target="tpu_custom_call" | custom-call | flops 3300000000 | bytes 1048576 | tf_op jit(solution)/shard_map/chunk_outer/pallas_call | solution.py:617
  47.9 1.3 %collective-permute-done.15.refs_4_ = bf16[288,256]{1,0:T(8,128)(2,1)S(1)} collective-permute-done((bf16[288,256]{1,0:T(8,128)(2,1)S(1)}, bf16[288,256]{1,0:T(8,128)(2,1)S(1)}, u32[]{:S(2)}, u32[]{:S(2)}) %collective-permute-start.15) | collective-permute-done | bytes 147488 | tf_op jit(solution)/shard_map/ppermute | solution.py:458
  49.3 2.0 %collective-permute-done.13.refs_2_ = bf16[288,256]{1,0:T(8,128)(2,1)S(1)} collective-permute-done((bf16[288,256]{1,0:T(8,128)(2,1)S(1)}, bf16[288,256]{1,0:T(8,128)(2,1)S(1)}, u32[]{:S(2)}, u32[]{:S(2)}) %collective-permute-start.13) | collective-permute-done | bytes 147488 | tf_op jit(solution)/shard_map/ppermute | solution.py:458
  51.2 0.8 %owner_sum.1 = (bf16[256,128]{1,0:T(8,128)(2,1)}, bf16[256,128]{1,0:T(8,128)(2,1)}, f32[1,8]{1,0:T(1,128)}, f32[1,8]{1,0:T(1,128)}) custom-call(f32[256,256]{1,0:T(8,128)S(1)} %get-tuple-element.74.refs_0_, f32[16,128]{1,0:T(8,128)S(1)} %get-tuple-element.75.refs_1_, bf16[288,256]{1,0:T(8,128)(2,1)S(1)} %collective-permute-done.13.refs_2_, ...), custom_call_target="tpu_custom_call" | custom-call | flops 1100000000 | bytes 1048576 | tf_op jit(solution)/shard_map/owner_sum/pallas_call | solution.py:635
  (39 shorter events, 3.3 us)
Async XLA Ops:
  0.6 6.8 %copy-start.9 = (f32[8]{0:T(128)S(1)}, f32[8]{0:T(128)}, u32[]{:S(2)}) copy-start(f32[8]{0:T(128)} %rate_ref.3) | copy-start | bytes 100
  0.7 6.7 %copy-start.2 = (bf16[1,256,1024]{2,1,0:T(8,128)(2,1)S(1)}, bf16[1,256,1024]{2,1,0:T(8,128)(2,1)}, u32[]{:S(2)}) copy-start(bf16[1,256,1024]{2,1,0:T(8,128)(2,1)} %param.21) | copy-start | bytes 1572868
  0.7 6.7 %copy-start.8 = (f32[8]{0:T(128)S(1)}, f32[8]{0:T(128)}, u32[]{:S(2)}) copy-start(f32[8]{0:T(128)} %skip_ref.1) | copy-start | bytes 100
  0.7 6.7 %copy-start.7 = (f32[1,256,8]{1,2,0:T(8,128)S(1)}, f32[1,256,8]{1,2,0:T(8,128)}, u32[]{:S(2)}) copy-start(f32[1,256,8]{1,2,0:T(8,128)} %param.17) | copy-start | bytes 24580
  0.7 6.7 %copy-start.5 = (bf16[1,256,128]{2,1,0:T(8,128)(2,1)S(1)}, bf16[1,256,128]{2,1,0:T(8,128)(2,1)}, u32[]{:S(2)}) copy-start(bf16[1,256,128]{2,1,0:T(8,128)(2,1)} %param.16) | copy-start | bytes 196612
  0.7 6.7 %copy-start.4 = (bf16[1,256,128]{2,1,0:T(8,128)(2,1)S(1)}, bf16[1,256,128]{2,1,0:T(8,128)(2,1)}, u32[]{:S(2)}) copy-start(bf16[1,256,128]{2,1,0:T(8,128)(2,1)} %param.15) | copy-start | bytes 196612
  0.7 6.7 %copy-start.1 = (bf16[1,256,1024]{2,1,0:T(8,128)(2,1)S(1)}, bf16[1,256,1024]{2,1,0:T(8,128)(2,1)}, u32[]{:S(2)}) copy-start(bf16[1,256,1024]{2,1,0:T(8,128)(2,1)} %param.14) | copy-start | bytes 1572868
  2.4 9.6 %collective-permute-start.2 = (bf16[256,256]{1,0:T(8,128)(2,1)}, bf16[256,256]{1,0:T(8,128)(2,1)S(1)}, u32[]{:S(2)}, u32[]{:S(2)}) collective-permute-start(bf16[256,256]{1,0:T(8,128)(2,1)} %pack_kv.1.refs_0_), channel_id=1, source_target_pairs={{0,6},{1,7},{2,0},{3,1},{4,2},{5,3},{6,4},{7,5},{8,14},{9,15},{10,... | collective-permute-start | bytes 393224 | tf_op jit(solution)/shard_map/ppermute | solution.py:458
  6.3 8.0 %collective-permute-start.1 = (bf16[256,256]{1,0:T(8,128)(2,1)}, bf16[256,256]{1,0:T(8,128)(2,1)S(1)}, u32[]{:S(2)}, u32[]{:S(2)}) collective-permute-start(bf16[256,256]{1,0:T(8,128)(2,1)} %pack_kv.1.refs_0_), channel_id=1, source_target_pairs={{0,4},{1,5},{2,6},{3,7},{4,0},{5,1},{6,2},{7,3},{8,12},{9,13},{10,... | collective-permute-start | bytes 393224 | tf_op jit(solution)/shard_map/ppermute | solution.py:458
  6.8 7.5 %collective-permute-start = (bf16[256,256]{1,0:T(8,128)(2,1)}, bf16[256,256]{1,0:T(8,128)(2,1)S(1)}, u32[]{:S(2)}, u32[]{:S(2)}) collective-permute-start(bf16[256,256]{1,0:T(8,128)(2,1)} %pack_kv.1.refs_0_), channel_id=1, source_target_pairs={{0,2},{1,3},{2,4},{3,5},{4,6},{5,7},{6,0},{7,1},{8,10},{9,11},{10,... | collective-permute-start | bytes 393224 | tf_op jit(solution)/shard_map/ppermute | solution.py:458
  7.4 6.8 %copy-start.3 = (bf16[256,256]{1,0:T(8,128)(2,1)S(1)}, bf16[256,256]{1,0:T(8,128)(2,1)}, u32[]{:S(2)}) copy-start(bf16[256,256]{1,0:T(8,128)(2,1)} %pack_kv.1.refs_0_) | copy-start | bytes 393220
  14.5 2.9 %collective-permute-start.3 = (f32[4,64,1152]{2,1,0:T(8,128)S(1)}, f32[4,64,1152]{2,1,0:T(8,128)S(1)}, u32[]{:S(2)}, u32[]{:S(2)}) collective-permute-start(f32[4,64,1152]{2,1,0:T(8,128)S(1)} %get-tuple-element.49), channel_id=1, source_target_pairs={{0,1},{1,0},{2,3},{3,2},{4,5},{5,4},{6,7},{7,6},{8,9},{9,8},{10,11... | collective-permute-start | bytes 3538952 | tf_op jit(solution)/shard_map/ppermute | solution.py:453
  14.6 5.7 %collective-permute-start.4 = (bf16[4,256,256]{2,1,0:T(8,128)(2,1)S(1)}, bf16[4,256,256]{2,1,0:T(8,128)(2,1)S(1)}, u32[]{:S(2)}, u32[]{:S(2)}) collective-permute-start(bf16[4,256,256]{2,1,0:T(8,128)(2,1)S(1)} %get-tuple-element.51.refs_3_), channel_id=1, source_target_pairs={{0,1},{1,0},{2,3},{3,2},{4,5},{5,4},{6,7},{7,6},{8,9},{9,8},{10,11... | collective-permute-start | bytes 1572872 | tf_op jit(solution)/shard_map/ppermute | solution.py:453
  17.6 9.4 %collective-permute-start.6 = (bf16[64,1152]{1,0:T(8,128)(2,1)S(1)}, bf16[64,1152]{1,0:T(8,128)(2,1)S(1)}, u32[]{:S(2)}, u32[]{:S(2)}) collective-permute-start(bf16[64,1152]{1,0:T(8,128)(2,1)S(1)} %get-tuple-element.54), channel_id=1, source_target_pairs={{0,4},{1,5},{2,6},{3,7},{4,0},{5,1},{6,2},{7,3},{8,12},{9,13},{10,... | collective-permute-start | bytes 442376 | tf_op jit(solution)/shard_map/ppermute | solution.py:458
  18.2 8.8 %collective-permute-start.7 = (bf16[64,1152]{1,0:T(8,128)(2,1)S(1)}, bf16[64,1152]{1,0:T(8,128)(2,1)S(1)}, u32[]{:S(2)}, u32[]{:S(2)}) collective-permute-start(bf16[64,1152]{1,0:T(8,128)(2,1)S(1)} %get-tuple-element.55), channel_id=1, source_target_pairs={{0,6},{1,7},{2,0},{3,1},{4,2},{5,3},{6,4},{7,5},{8,14},{9,15},{10,... | collective-permute-start | bytes 442376 | tf_op jit(solution)/shard_map/ppermute | solution.py:458
  19.5 8.4 %collective-permute-start.5 = (bf16[64,1152]{1,0:T(8,128)(2,1)S(1)}, bf16[64,1152]{1,0:T(8,128)(2,1)S(1)}, u32[]{:S(2)}, u32[]{:S(2)}) collective-permute-start(bf16[64,1152]{1,0:T(8,128)(2,1)S(1)} %get-tuple-element.52.refs_5_), channel_id=1, source_target_pairs={{0,2},{1,3},{2,4},{3,5},{4,6},{5,7},{6,0},{7,1},{8,10},{9,11},{10,... | collective-permute-start | bytes 442376 | tf_op jit(solution)/shard_map/ppermute | solution.py:458
  28.6 5.5 %collective-permute-start.9 = (f32[16,128]{1,0:T(8,128)S(1)}, f32[16,128]{1,0:T(8,128)S(1)}, u32[]{:S(2)}, u32[]{:S(2)}) collective-permute-start(f32[16,128]{1,0:T(8,128)S(1)} %get-tuple-element.61.refs_7_.refs_1_), channel_id=1, source_target_pairs={{0,8},{1,9},{2,10},{3,11},{4,12},{5,13},{6,14},{7,15},{8,0},{9,1},... | collective-permute-start | bytes 24584 | tf_op jit(solution)/shard_map/ppermute | solution.py:466
  34.2 7.4 %collective-permute-start.10 = (bf16[1056,256]{1,0:T(8,128)(2,1)S(1)}, bf16[1056,256]{1,0:T(8,128)(2,1)S(1)}, u32[]{:S(2)}, u32[]{:S(2)}) collective-permute-start(bf16[1056,256]{1,0:T(8,128)(2,1)S(1)} %get-tuple-element.69), channel_id=1, source_target_pairs={{0,1},{1,0},{2,3},{3,2},{4,5},{5,4},{6,7},{7,6},{8,9},{9,8},{10,11... | collective-permute-start | bytes 1622024 | tf_op jit(solution)/shard_map/ppermute | solution.py:453
  34.3 10.3 %collective-permute-start.8 = (bf16[2,64,1024]{2,1,0:T(8,128)(2,1)S(1)}, bf16[2,64,1024]{2,1,0:T(8,128)(2,1)S(1)}, u32[]{:S(2)}, u32[]{:S(2)}) collective-permute-start(bf16[2,64,1024]{2,1,0:T(8,128)(2,1)S(1)} %get-tuple-element.57), channel_id=1, source_target_pairs={{0,1},{1,0},{2,3},{3,2},{4,5},{5,4},{6,7},{7,6},{8,9},{9,8},{10,11... | collective-permute-start | bytes 786440 | tf_op jit(solution)/shard_map/ppermute | solution.py:453
  34.8 4.0 %collective-permute-start.12 = (f32[16,128]{1,0:T(8,128)S(1)}, f32[16,128]{1,0:T(8,128)S(1)}, u32[]{:S(2)}, u32[]{:S(2)}) collective-permute-start(f32[16,128]{1,0:T(8,128)S(1)} %get-tuple-element.70.refs_2_), channel_id=1, source_target_pairs={{0,17},{1,16},{2,19},{3,18},{4,21},{5,20},{6,23},{7,22},{8,25},{9,... | collective-permute-start | bytes 24584 | tf_op jit(solution)/shard_map/ppermute | solution.py:466
  37.1 4.5 %collective-permute-start.11 = (f32[16,128]{1,0:T(8,128)S(1)}, f32[16,128]{1,0:T(8,128)S(1)}, u32[]{:S(2)}, u32[]{:S(2)}) collective-permute-start(f32[16,128]{1,0:T(8,128)S(1)} %get-tuple-element.70.refs_2_), channel_id=1, source_target_pairs={{0,16},{1,17},{2,18},{3,19},{4,20},{5,21},{6,22},{7,23},{8,24},{9,... | collective-permute-start | bytes 24584 | tf_op jit(solution)/shard_map/ppermute | solution.py:466
  41.8 6.1 %collective-permute-start.14 = (bf16[288,256]{1,0:T(8,128)(2,1)S(1)}, bf16[288,256]{1,0:T(8,128)(2,1)S(1)}, u32[]{:S(2)}, u32[]{:S(2)}) collective-permute-start(bf16[288,256]{1,0:T(8,128)(2,1)S(1)} %get-tuple-element.76), channel_id=1, source_target_pairs={{0,4},{1,5},{2,6},{3,7},{4,0},{5,1},{6,2},{7,3},{8,12},{9,13},{10,... | collective-permute-start | bytes 442376 | tf_op jit(solution)/shard_map/ppermute | solution.py:458
  42.5 6.7 %collective-permute-start.15 = (bf16[288,256]{1,0:T(8,128)(2,1)S(1)}, bf16[288,256]{1,0:T(8,128)(2,1)S(1)}, u32[]{:S(2)}, u32[]{:S(2)}) collective-permute-start(bf16[288,256]{1,0:T(8,128)(2,1)S(1)} %get-tuple-element.77), channel_id=1, source_target_pairs={{0,6},{1,7},{2,0},{3,1},{4,2},{5,3},{6,4},{7,5},{8,14},{9,15},{10,... | collective-permute-start | bytes 442376 | tf_op jit(solution)/shard_map/ppermute | solution.py:458
  43.9 7.3 %collective-permute-start.13 = (bf16[288,256]{1,0:T(8,128)(2,1)S(1)}, bf16[288,256]{1,0:T(8,128)(2,1)S(1)}, u32[]{:S(2)}, u32[]{:S(2)}) collective-permute-start(bf16[288,256]{1,0:T(8,128)(2,1)S(1)} %get-tuple-element.71._), channel_id=1, source_target_pairs={{0,2},{1,3},{2,4},{3,5},{4,6},{5,7},{6,0},{7,1},{8,10},{9,11},{10,... | collective-permute-start | bytes 442376 | tf_op jit(solution)/shard_map/ppermute | solution.py:458
  (2 other events, 11.5 us)

commit v9 on v7

--- a/solution.py
+++ b/solution.py
@@ -334,13 +334,17 @@
 
 
 def owner_sum_kernel(chips, tokens_all, own_ref, sums_ref, *refs):
-    parts, (dk_ref, dv_ref, rate_ref, skip_ref) = refs[: chips - 1], refs[chips - 1 :]
+    parts, farther_refs, (dk_ref, dv_ref, rate_ref, skip_ref) = (
+        refs[: chips - 1], refs[chips - 1 : -4], refs[-4:]
+    )
     rows = own_ref.shape[0]
     total = own_ref[...]
     sums = sums_ref[...]
     for part in parts:
         total += part[:rows, :].astype(F32)
         sums += whole_sums(part[rows:, :])
+    for ref in farther_refs:
+        sums += ref[...]
     dk_ref[...] = (total[:LANES].T * FACTOR).astype(BF16)
     dv_ref[...] = total[LANES:].T.astype(BF16)
     ones = jnp.ones((8, LANES), F32)
@@ -400,7 +404,7 @@
 
 
 def chunk_kernel(
-    x_ref, g_ref, b_ref, c_ref, step_ref, rate_ref, skip_ref, _,
+    x_ref, g_ref, b_ref, c_ref, step_ref, rate_ref, skip_ref,
     state_ref, y_ref, dx_ref, db_ref, dc_ref, sums_ref, pad_ref, *scratch
 ):
     operands = (x_ref, g_ref, b_ref, c_ref, step_ref, rate_ref)
@@ -410,10 +414,11 @@
 
 def outer_kernel(
     x_ref, g_ref, b_ref, c_ref, step_ref, rate_ref, own_ref, other_ref, first_ref, second_ref,
-    inner_y_ref, inner_dx_ref, inner_db_ref, inner_dc_ref, _,
-    y_ref, dx_ref, db_ref, dc_ref,
+    inner_y_ref, inner_dx_ref, inner_db_ref, inner_dc_ref, sums_ref,
+    y_ref, dx_ref, db_ref, dc_ref, passed_ref,
     pad_ref, xt_ref, gt_ref, ent_ref,
 ):
+    passed_ref[...] = sums_ref[...]
     _, core = chip_and_core()
     ent_ref[:, pl.ds(pl.multiple_of(core * HALF, HALF), HALF), :] = own_ref[...]
     ent_ref[:, pl.ds(pl.multiple_of((1 - core) * HALF, HALF), HALF), :] = other_ref[...]
@@ -445,9 +450,12 @@
     return lax.ppermute(array, "seq", [(i, (i + 2 * k) % n) for i in range(n)])
 
 
-def turned(array, k):
-    n = lax.axis_size("dp")
-    return lax.ppermute(array, "dp", [(i, (i + k) % n) for i in range(n)])
+def from_replica(array, distance, k):
+    replicas, n = lax.axis_size("dp"), lax.axis_size("seq")
+    pairs = [
+        (r * n + i, (r ^ distance) * n + (i + 2 * k) % n) for r in range(replicas) for i in range(n)
+    ]
+    return lax.ppermute(array, ("dp", "seq"), pairs)
 
 
 def call(kernel, outs, ins, scratch, microseconds, name, limit=16):
@@ -491,7 +499,7 @@
         + [((tokens, WIDE), F32)] * 2
         + [((tokens, NS), F32)] * 2
         + [((2 * HS, LANES), F32)],
-        [VMEM] * 5 + [SMEM] * 2 + [AFTER],
+        [VMEM] * 5 + [SMEM] * 2,
         [
             pltpu.VMEM((LANES, tokens), F32),
             pltpu.VMEM((tokens, WIDE), BF16),
@@ -505,7 +513,7 @@
         6,
         "chunk_alone",
         20,
-    )(x, g, b, c, steps, rate_log, skip, kv)
+    )(x, g, b, c, steps, rate_log, skip)
     half = ((4, HALF, WIDE + LANES), F32)
     keep, give, stack = call(
         split_kernel,
@@ -563,7 +571,7 @@
         "chain_states",
     )(keep, received, sums, first_dq, *arrived)
     other = swapped(give)
-    replicated = [turned(totals, k) for k in range(1, replicas)]
+    neighbour = from_replica(totals, 1, 0)
 
     second_out, dq, acc = call(
         lambda *refs: second_attention_kernel(most, *refs),
@@ -581,11 +589,11 @@
             ((chips * 2 * LANES + 32, tokens), BF16),
             ((2 * HS, LANES), F32),
         ],
-        [VMEM] * (1 + replicas),
+        [VMEM] * 3,
         [],
         1,
         "share_key_gradients",
-    )(acc, totals, *replicated)
+    )(acc, totals, neighbour)
     partial, summed, *messages = call(
         lambda *refs: pair_sum_kernel(chips, *refs),
         [((2 * LANES, tokens), F32), ((2 * HS, LANES), F32)]
@@ -596,11 +604,10 @@
         "pair_sum",
     )(keep, swapped(give), sums)
     arrived = [from_chip(messages[k - 1], k) for k in range(1, chips)]
-
-    y, dx, db, dc = call(
+    y, dx, db, dc, passed = call(
         outer_kernel,
-        [((tokens, WIDE), BF16)] * 2 + [((tokens, NS), BF16)] * 2,
-        [VMEM] * 5 + [SMEM] + [VMEM] * 8 + [AFTER],
+        [((tokens, WIDE), BF16)] * 2 + [((tokens, NS), BF16)] * 2 + [((2 * HS, LANES), F32)],
+        [VMEM] * 5 + [SMEM] + [VMEM] * 9,
         [
             pltpu.VMEM((LANES, tokens), F32),
             pltpu.VMEM((tokens, WIDE), BF16),
@@ -611,18 +618,19 @@
         "chunk_outer",
     )(
         x, g, b, c, steps, rate_log, own, other, first_out, second_out,
-        inner_y, inner_dx, inner_db, inner_dc, messages[0],
+        inner_y, inner_dx, inner_db, inner_dc, summed,
     )
+    farther = [from_replica(passed, d, k) for d in range(2, replicas, 2) for k in range(chips)]
 
     tokens_all = replicas * n * tokens
     dk, dv, grad_rate_log, grad_skip = call(
         lambda *refs: owner_sum_kernel(chips, tokens_all, *refs),
         [((tokens, LANES), BF16)] * 2 + [((1, HS), F32)] * 2,
-        [VMEM] * (chips + 1),
+        [VMEM] * (chips + 1 + len(farther)),
         [],
         1,
         "owner_sum",
-    )(partial, summed, *arrived)
+    )(partial, summed, *arrived, *farther)
     return (
         y[None],
         dq[None],

time: 50.6 us -> 58.4 us (1.15)
  waiting for transfers between devices: 9.07 us -> 13.9 us
  starting transfers between devices: 19.2 us -> 23 us
  local copies, waits for them, and re-layouts: 0.97 us -> 0.05 us
    ppermute x3 -> x5, waiting for transfers between devices: 0.01 us -> 8.53 us  [from_replica(): return lax.ppermute(array, ('dp', 'seq'), pairs)]
    ppermute x9, waiting for transfers between devices: 5.3 us -> 1.57 us  [from_chip(): return lax.ppermute(array, 'seq', [(i, (i + 2 * k) % n) for i in range(n)])]
    ppermute x3 -> x5, starting transfers between devices: 4.68 us -> 7.5 us  [from_replica(): return lax.ppermute(array, ('dp', 'seq'), pairs)]
    ppermute x9, starting transfers between devices: 13.4 us -> 14.4 us  [from_chip(): return lax.ppermute(array, 'seq', [(i, (i + 2 * k) % n) for i in range(n)])]
    unnamed x20, local copies, waits for them, and re-layouts: 0.97 us -> 0.05 us
  transfers between devices with their start and end apart: 16 -> 18, of which waited for: 5 -> 8; matrix products, arithmetic and copies ran while one was open for 0% -> 0% of each run, Pallas kernels for 33% -> 29%
where the time goes in v9:
time: 58.4 us; the launch traced here: 58.3 us
  starting transfers between devices  23 us (39%)
  Pallas kernels  20.4 us (35%)
  waiting for transfers between devices  13.9 us (24%)
  between operations  0.86 us (1%)
    ppermute x9, starting transfers between devices, from_chip(): return lax.ppermute(array, 'seq', [(i, (i + 2 * k) % n) for i in range(n)])  14.4 us
    ppermute x5, waiting for transfers between devices, from_replica(): return lax.ppermute(array, ('dp', 'seq'), pairs)  8.53 us
    ppermute x5, starting transfers between devices, from_replica(): return lax.ppermute(array, ('dp', 'seq'), pairs)  7.5 us
    pallas_call x1, Pallas kernels, body(): call(lambda *refs: second_attention_kernel(most, *refs), [((BLOCK, column...  5.1 us
    pallas_call x1, Pallas kernels, body(): call(chunk_kernel, [((4, NS, WIDE + LANES), F32)] + [((tokens, WIDE), F32...  4.53 us
    pallas_call x1, Pallas kernels, body(): call(lambda *refs: first_attention_kernel(chips, most, *refs), [((BLOCK,...  4.17 us
    ppermute x4, waiting for transfers between devices, swapped(): lax.ppermute(array, 'seq', [(i, i ^ 1) for i in range(lax.axis_size('seq'...  3.77 us
    pallas_call x1, Pallas kernels, body(): call(outer_kernel, [((tokens, WIDE), BF16)] * 2 + [((tokens, NS), BF16)]...  2.81 us
  transfers between devices with their start and end apart: 18, of which 8 were waited for; matrix products, arithmetic and copies ran while one was open for 0% of the time, Pallas kernels for 29%

profile of v9, /device:TPU:0, one launch (start us, length us, event | category | flops | bytes accessed | tf_op | source)
XLA Modules:
  0.0 58.3 jit_solution(18248747206357819805)
XLA Ops:
  0.7 1.6 %pack_kv.1.refs_0_ = bf16[256,256]{1,0:T(8,128)(2,1)} custom-call(bf16[256,128]{1,0:T(8,128)(2,1)} %bitcast.36, bf16[256,128]{1,0:T(8,128)(2,1)} %bitcast.37), custom_call_target="tpu_custom_call" | custom-call | flops 1100000000 | bytes 1048576 | tf_op jit(solution)/shard_map/pack_kv/pallas_call | solution.py:485
  2.3 3.0 %collective-permute-start = (bf16[256,256]{1,0:T(8,128)(2,1)}, bf16[256,256]{1,0:T(8,128)(2,1)S(1)}, u32[]{:S(2)}, u32[]{:S(2)}) collective-permute-start(bf16[256,256]{1,0:T(8,128)(2,1)} %pack_kv.1.refs_0_), channel_id=1, source_target_pairs={{0,2},{1,3},{2,4},{3,5},{4,6},{5,7},{6,0},{7,1},{8,10},{9,11},{10,... | collective-permute-start | bytes 393224 | tf_op jit(solution)/shard_map/ppermute | solution.py:450
  5.3 1.5 %collective-permute-start.1 = (bf16[256,256]{1,0:T(8,128)(2,1)}, bf16[256,256]{1,0:T(8,128)(2,1)S(1)}, u32[]{:S(2)}, u32[]{:S(2)}) collective-permute-start(bf16[256,256]{1,0:T(8,128)(2,1)} %pack_kv.1.refs_0_), channel_id=1, source_target_pairs={{0,4},{1,5},{2,6},{3,7},{4,0},{5,1},{6,2},{7,3},{8,12},{9,13},{10,... | collective-permute-start | bytes 393224 | tf_op jit(solution)/shard_map/ppermute | solution.py:450
  6.9 1.4 %collective-permute-start.2 = (bf16[256,256]{1,0:T(8,128)(2,1)}, bf16[256,256]{1,0:T(8,128)(2,1)S(1)}, u32[]{:S(2)}, u32[]{:S(2)}) collective-permute-start(bf16[256,256]{1,0:T(8,128)(2,1)} %pack_kv.1.refs_0_), channel_id=1, source_target_pairs={{0,6},{1,7},{2,0},{3,1},{4,2},{5,3},{6,4},{7,5},{8,14},{9,15},{10,... | collective-permute-start | bytes 393224 | tf_op jit(solution)/shard_map/ppermute | solution.py:450
  8.3 4.5 %chunk_alone.1 = (f32[4,128,1152]{2,1,0:T(8,128)S(1)}, f32[256,1024]{1,0:T(8,128)S(1)}, f32[256,1024]{1,0:T(8,128)S(1)}, f32[256,128]{1,0:T(8,128)S(1)}, f32[256,128]{1,0:T(8,128)S(1)}, /*index=5*/f32[16,128]{1,0:T(8,128)S(1)}) custom-call(bf16[256,1024]{1,0:T(8,128)(2,1)S(1)} %bitcast.22, bf16[256,1024]{1,0:T(8,128)(2,1)S(1)} %bitcast.24, ...), custom_call_target="tpu_custom_call" | custom-call | flops 6600000000 | bytes 1048576 | tf_op jit(solution)/shard_map/chunk_alone/pallas_call | solution.py:496
  13.9 2.3 %collective-permute-done.3.refs_1_ = f32[4,64,1152]{2,1,0:T(8,128)S(1)} collective-permute-done((f32[4,64,1152]{2,1,0:T(8,128)S(1)}, f32[4,64,1152]{2,1,0:T(8,128)S(1)}, u32[]{:S(2)}, u32[]{:S(2)}) %collective-permute-start.3) | collective-permute-done | bytes 1179680 | tf_op jit(solution)/shard_map/ppermute | solution.py:445
  16.4 1.8 %collective-permute-start.5 = (bf16[64,1152]{1,0:T(8,128)(2,1)S(1)}, bf16[64,1152]{1,0:T(8,128)(2,1)S(1)}, u32[]{:S(2)}, u32[]{:S(2)}) collective-permute-start(bf16[64,1152]{1,0:T(8,128)(2,1)S(1)} %get-tuple-element.53.refs_5_), channel_id=1, source_target_pairs={{0,2},{1,3},{2,4},{3,5},{4,6},{5,7},{6,0},{7,1},{8,10},{9,11},{10,... | collective-permute-start | bytes 442376 | tf_op jit(solution)/shard_map/ppermute | solution.py:450
  18.6 2.3 %collective-permute-start.7 = (bf16[64,1152]{1,0:T(8,128)(2,1)S(1)}, bf16[64,1152]{1,0:T(8,128)(2,1)S(1)}, u32[]{:S(2)}, u32[]{:S(2)}) collective-permute-start(bf16[64,1152]{1,0:T(8,128)(2,1)S(1)} %get-tuple-element.56), channel_id=1, source_target_pairs={{0,6},{1,7},{2,0},{3,1},{4,2},{5,3},{6,4},{7,5},{8,14},{9,15},{10,... | collective-permute-start | bytes 442376 | tf_op jit(solution)/shard_map/ppermute | solution.py:450
  20.9 4.2 %first_attention.1 = (f32[128,1024]{1,0:T(8,128)S(1)}, bf16[128,1024]{1,0:T(8,128)(2,1)S(1)}, f32[256,2048]{1,0:T(8,128)S(1)}, bf16[2048,256]{1,0:T(8,128)(2,1)S(1)}) custom-call(s32[16,16]{1,0:T(8,128)S(1)} %bitcast.32, bf16[256,1024]{1,0:T(8,128)(2,1)S(1)} %bitcast.20, bf16[256,1024]{1,0:T(8,128)(2,1)S(1)} %bitcast.25, ...), custom_call_target="tpu_custom_call" | custom-call | flops 5500000256 | bytes 1048576 | tf_op jit(solution)/shard_map/first_attention/pallas_call | solution.py:550
  25.1 1.4 %collective-permute-done.6.refs_5_ = bf16[64,1152]{1,0:T(8,128)(2,1)S(1)} collective-permute-done((bf16[64,1152]{1,0:T(8,128)(2,1)S(1)}, bf16[64,1152]{1,0:T(8,128)(2,1)S(1)}, u32[]{:S(2)}, u32[]{:S(2)}) %collective-permute-start.6) | collective-permute-done | bytes 147488 | tf_op jit(solution)/shard_map/ppermute | solution.py:450
  26.5 0.7 %chain_states.1 = (bf16[2,64,1024]{2,1,0:T(8,128)(2,1)S(1)}, bf16[2,64,1024]{2,1,0:T(8,128)(2,1)S(1)}, f32[16,128]{1,0:T(8,128)S(1)}) custom-call(f32[4,64,1152]{2,1,0:T(8,128)S(1)} %get-tuple-element.49.refs_0_, f32[4,64,1152]{2,1,0:T(8,128)S(1)} %collective-permute-done.3.refs_1_, f32[16,128]{1,0:T(8,128)S(1)} %get-tuple-element.51.refs_2_, ...), custom_call_target="tpu_custom_call" | custom-call | flops 2200000000 | bytes 1048576 | tf_op jit(solution)/shard_map/chain_states/pallas_call | solution.py:565
  27.2 1.6 %collective-permute-start.9 = (f32[16,128]{1,0:T(8,128)S(1)}, f32[16,128]{1,0:T(8,128)S(1)}, u32[]{:S(2)}, u32[]{:S(2)}) collective-permute-start(f32[16,128]{1,0:T(8,128)S(1)} %get-tuple-element.62.refs_6_.refs_1_), channel_id=1, source_target_pairs={{0,8},{1,9},{2,10},{3,11},{4,12},{5,13},{6,14},{7,15},{8,0},{9,1},... | collective-permute-start | bytes 24584 | tf_op jit(solution)/shard_map/ppermute | solution.py:458
  28.8 5.1 %second_attention.1 = (f32[128,1024]{1,0:T(8,128)S(1)}, bf16[256,1024]{1,0:T(8,128)(2,1)}, f32[256,2048]{1,0:T(8,128)S(1)}) custom-call(s32[16,16]{1,0:T(8,128)S(1)} %bitcast.33, bf16[256,1024]{1,0:T(8,128)(2,1)S(1)} %bitcast.21, bf16[256,1024]{1,0:T(8,128)(2,1)S(1)} %bitcast.26, bf16[2048,256]{1,0:T(8,128)(2,1)S(1)} %get-tuple-element.60.refs_3_, ...), custom_call_target="tpu_custom_call" | custom-call | flops 5500000256 | bytes 1048576 | tf_op jit(solution)/shard_map/second_attention/pallas_call | solution.py:576
  34.6 1.4 %collective-permute-done.10.refs_1_ = bf16[1056,256]{1,0:T(8,128)(2,1)S(1)} collective-permute-done((bf16[1056,256]{1,0:T(8,128)(2,1)S(1)}, bf16[1056,256]{1,0:T(8,128)(2,1)S(1)}, u32[]{:S(2)}, u32[]{:S(2)}) %collective-permute-start.10) | collective-permute-done | bytes 540704 | tf_op jit(solution)/shard_map/ppermute | solution.py:445
  36.2 1.8 %collective-permute-start.11 = (bf16[288,256]{1,0:T(8,128)(2,1)S(1)}, bf16[288,256]{1,0:T(8,128)(2,1)S(1)}, u32[]{:S(2)}, u32[]{:S(2)}) collective-permute-start(bf16[288,256]{1,0:T(8,128)(2,1)S(1)} %get-tuple-element.76), channel_id=1, source_target_pairs={{0,2},{1,3},{2,4},{3,5},{4,6},{5,7},{6,0},{7,1},{8,10},{9,11},{10,... | collective-permute-start | bytes 442376 | tf_op jit(solution)/shard_map/ppermute | solution.py:450
  38.6 1.6 %collective-permute-start.13 = (bf16[288,256]{1,0:T(8,128)(2,1)S(1)}, bf16[288,256]{1,0:T(8,128)(2,1)S(1)}, u32[]{:S(2)}, u32[]{:S(2)}) collective-permute-start(bf16[288,256]{1,0:T(8,128)(2,1)S(1)} %get-tuple-element.78), channel_id=1, source_target_pairs={{0,6},{1,7},{2,0},{3,1},{4,2},{5,3},{6,4},{7,5},{8,14},{9,15},{10,... | collective-permute-start | bytes 442376 | tf_op jit(solution)/shard_map/ppermute | solution.py:450
  40.2 2.8 %chunk_outer.1 = (bf16[256,1024]{1,0:T(8,128)(2,1)}, bf16[256,1024]{1,0:T(8,128)(2,1)}, bf16[256,128]{1,0:T(8,128)(2,1)}, bf16[256,128]{1,0:T(8,128)(2,1)}, f32[16,128]{1,0:T(8,128)S(1)}) custom-call(bf16[256,1024]{1,0:T(8,128)(2,1)S(1)} %bitcast.23, bf16[256,1024]{1,0:T(8,128)(2,1)S(1)} %bitcast.27, bf16[256,128]{1,0:T(8,128)(2,1)S(1)} %bitcast.29, ...), custom_call_target="tpu_custom_call" | custom-call | flops 3300000000 | bytes 1048576 | tf_op jit(solution)/shard_map/chunk_outer/pallas_call | solution.py:607
  43.0 2.6 %collective-permute-start.14 = (f32[16,128]{1,0:T(8,128)S(1)}, f32[16,128]{1,0:T(8,128)S(1)}, u32[]{:S(2)}, u32[]{:S(2)}) collective-permute-start(f32[16,128]{1,0:T(8,128)S(1)} %get-tuple-element.79), channel_id=1, source_target_pairs={{0,16},{1,17},{2,18},{3,19},{4,20},{5,21},{6,22},{7,23},{8,24},{9,... | collective-permute-start | bytes 24584 | tf_op jit(solution)/shard_map/ppermute | solution.py:458
  45.8 1.8 %collective-permute-done.14.refs_5_ = f32[16,128]{1,0:T(8,128)S(1)} collective-permute-done((f32[16,128]{1,0:T(8,128)S(1)}, f32[16,128]{1,0:T(8,128)S(1)}, u32[]{:S(2)}, u32[]{:S(2)}) %collective-permute-start.14) | collective-permute-done | bytes 8224 | tf_op jit(solution)/shard_map/ppermute | solution.py:458
  47.6 3.0 %collective-permute-start.16 = (f32[16,128]{1,0:T(8,128)S(1)}, f32[16,128]{1,0:T(8,128)S(1)}, u32[]{:S(2)}, u32[]{:S(2)}) collective-permute-start(f32[16,128]{1,0:T(8,128)S(1)} %get-tuple-element.79), channel_id=1, source_target_pairs={{0,20},{1,21},{2,22},{3,23},{4,16},{5,17},{6,18},{7,19},{8,28},{9,... | collective-permute-start | bytes 24584 | tf_op jit(solution)/shard_map/ppermute | solution.py:458
  50.6 1.4 %collective-permute-done.15.refs_6_ = f32[16,128]{1,0:T(8,128)S(1)} collective-permute-done((f32[16,128]{1,0:T(8,128)S(1)}, f32[16,128]{1,0:T(8,128)S(1)}, u32[]{:S(2)}, u32[]{:S(2)}) %collective-permute-start.15) | collective-permute-done | bytes 8224 | tf_op jit(solution)/shard_map/ppermute | solution.py:458
  52.1 1.0 %collective-permute-done.16.refs_7_ = f32[16,128]{1,0:T(8,128)S(1)} collective-permute-done((f32[16,128]{1,0:T(8,128)S(1)}, f32[16,128]{1,0:T(8,128)S(1)}, u32[]{:S(2)}, u32[]{:S(2)}) %collective-permute-start.16) | collective-permute-done | bytes 8224 | tf_op jit(solution)/shard_map/ppermute | solution.py:458
  53.0 4.4 %collective-permute-done.17.refs_8_ = f32[16,128]{1,0:T(8,128)S(1)} collective-permute-done((f32[16,128]{1,0:T(8,128)S(1)}, f32[16,128]{1,0:T(8,128)S(1)}, u32[]{:S(2)}, u32[]{:S(2)}) %collective-permute-start.17) | collective-permute-done | bytes 8224 | tf_op jit(solution)/shard_map/ppermute | solution.py:458
  57.4 0.8 %owner_sum.1 = (bf16[256,128]{1,0:T(8,128)(2,1)}, bf16[256,128]{1,0:T(8,128)(2,1)}, f32[1,8]{1,0:T(1,128)}, f32[1,8]{1,0:T(1,128)}) custom-call(f32[256,256]{1,0:T(8,128)S(1)} %get-tuple-element.75.refs_0_, f32[16,128]{1,0:T(8,128)S(1)} %get-tuple-element.72.sums_ref.refs_1_, bf16[288,256]{1,0:T(8,128)(2,1)S(1)} %collective-permute-done.11.refs_2_, ...), custom_call_target="tpu_custom_call" | custom-call | flops 1100000000 | bytes 1048576 | tf_op jit(solution)/shard_map/owner_sum/pallas_call | solution.py:626
  (43 shorter events, 3.4 us)
Async XLA Ops:
  0.6 7.7 %copy-start.2 = (bf16[1,256,1024]{2,1,0:T(8,128)(2,1)S(1)}, bf16[1,256,1024]{2,1,0:T(8,128)(2,1)}, u32[]{:S(2)}) copy-start(bf16[1,256,1024]{2,1,0:T(8,128)(2,1)} %param.21) | copy-start | bytes 1572868
  0.7 7.6 %copy-start.1 = (bf16[1,256,1024]{2,1,0:T(8,128)(2,1)S(1)}, bf16[1,256,1024]{2,1,0:T(8,128)(2,1)}, u32[]{:S(2)}) copy-start(bf16[1,256,1024]{2,1,0:T(8,128)(2,1)} %param.14) | copy-start | bytes 1572868
  0.7 7.6 %copy-start.4 = (bf16[1,256,128]{2,1,0:T(8,128)(2,1)S(1)}, bf16[1,256,128]{2,1,0:T(8,128)(2,1)}, u32[]{:S(2)}) copy-start(bf16[1,256,128]{2,1,0:T(8,128)(2,1)} %param.15) | copy-start | bytes 196612
  0.7 7.6 %copy-start.5 = (bf16[1,256,128]{2,1,0:T(8,128)(2,1)S(1)}, bf16[1,256,128]{2,1,0:T(8,128)(2,1)}, u32[]{:S(2)}) copy-start(bf16[1,256,128]{2,1,0:T(8,128)(2,1)} %param.16) | copy-start | bytes 196612
  0.7 7.6 %copy-start.7 = (f32[1,256,8]{1,2,0:T(8,128)S(1)}, f32[1,256,8]{1,2,0:T(8,128)}, u32[]{:S(2)}) copy-start(f32[1,256,8]{1,2,0:T(8,128)} %param.17) | copy-start | bytes 24580
  0.7 7.6 %copy-start.9 = (f32[8]{0:T(128)S(1)}, f32[8]{0:T(128)}, u32[]{:S(2)}) copy-start(f32[8]{0:T(128)} %rate_ref.3) | copy-start | bytes 100
  2.3 10.5 %collective-permute-start = (bf16[256,256]{1,0:T(8,128)(2,1)}, bf16[256,256]{1,0:T(8,128)(2,1)S(1)}, u32[]{:S(2)}, u32[]{:S(2)}) collective-permute-start(bf16[256,256]{1,0:T(8,128)(2,1)} %pack_kv.1.refs_0_), channel_id=1, source_target_pairs={{0,2},{1,3},{2,4},{3,5},{4,6},{5,7},{6,0},{7,1},{8,10},{9,11},{10,... | collective-permute-start | bytes 393224 | tf_op jit(solution)/shard_map/ppermute | solution.py:450
  5.3 7.6 %collective-permute-start.1 = (bf16[256,256]{1,0:T(8,128)(2,1)}, bf16[256,256]{1,0:T(8,128)(2,1)S(1)}, u32[]{:S(2)}, u32[]{:S(2)}) collective-permute-start(bf16[256,256]{1,0:T(8,128)(2,1)} %pack_kv.1.refs_0_), channel_id=1, source_target_pairs={{0,4},{1,5},{2,6},{3,7},{4,0},{5,1},{6,2},{7,3},{8,12},{9,13},{10,... | collective-permute-start | bytes 393224 | tf_op jit(solution)/shard_map/ppermute | solution.py:450
  6.9 6.2 %collective-permute-start.2 = (bf16[256,256]{1,0:T(8,128)(2,1)}, bf16[256,256]{1,0:T(8,128)(2,1)S(1)}, u32[]{:S(2)}, u32[]{:S(2)}) collective-permute-start(bf16[256,256]{1,0:T(8,128)(2,1)} %pack_kv.1.refs_0_), channel_id=1, source_target_pairs={{0,6},{1,7},{2,0},{3,1},{4,2},{5,3},{6,4},{7,5},{8,14},{9,15},{10,... | collective-permute-start | bytes 393224 | tf_op jit(solution)/shard_map/ppermute | solution.py:450
  13.3 2.9 %collective-permute-start.3 = (f32[4,64,1152]{2,1,0:T(8,128)S(1)}, f32[4,64,1152]{2,1,0:T(8,128)S(1)}, u32[]{:S(2)}, u32[]{:S(2)}) collective-permute-start(f32[4,64,1152]{2,1,0:T(8,128)S(1)} %get-tuple-element.50), channel_id=1, source_target_pairs={{0,1},{1,0},{2,3},{3,2},{4,5},{5,4},{6,7},{7,6},{8,9},{9,8},{10,11... | collective-permute-start | bytes 3538952 | tf_op jit(solution)/shard_map/ppermute | solution.py:445
  13.4 7.5 %collective-permute-start.4 = (bf16[4,256,256]{2,1,0:T(8,128)(2,1)S(1)}, bf16[4,256,256]{2,1,0:T(8,128)(2,1)S(1)}, u32[]{:S(2)}, u32[]{:S(2)}) collective-permute-start(bf16[4,256,256]{2,1,0:T(8,128)(2,1)S(1)} %get-tuple-element.52.refs_3_), channel_id=1, source_target_pairs={{0,1},{1,0},{2,3},{3,2},{4,5},{5,4},{6,7},{7,6},{8,9},{9,8},{10,11... | collective-permute-start | bytes 1572872 | tf_op jit(solution)/shard_map/ppermute | solution.py:445
  16.4 8.6 %collective-permute-start.5 = (bf16[64,1152]{1,0:T(8,128)(2,1)S(1)}, bf16[64,1152]{1,0:T(8,128)(2,1)S(1)}, u32[]{:S(2)}, u32[]{:S(2)}) collective-permute-start(bf16[64,1152]{1,0:T(8,128)(2,1)S(1)} %get-tuple-element.53.refs_5_), channel_id=1, source_target_pairs={{0,2},{1,3},{2,4},{3,5},{4,6},{5,7},{6,0},{7,1},{8,10},{9,11},{10,... | collective-permute-start | bytes 442376 | tf_op jit(solution)/shard_map/ppermute | solution.py:450
  18.2 8.2 %collective-permute-start.6 = (bf16[64,1152]{1,0:T(8,128)(2,1)S(1)}, bf16[64,1152]{1,0:T(8,128)(2,1)S(1)}, u32[]{:S(2)}, u32[]{:S(2)}) collective-permute-start(bf16[64,1152]{1,0:T(8,128)(2,1)S(1)} %get-tuple-element.55), channel_id=1, source_target_pairs={{0,4},{1,5},{2,6},{3,7},{4,0},{5,1},{6,2},{7,3},{8,12},{9,13},{10,... | collective-permute-start | bytes 442376 | tf_op jit(solution)/shard_map/ppermute | solution.py:450
  18.6 7.9 %collective-permute-start.7 = (bf16[64,1152]{1,0:T(8,128)(2,1)S(1)}, bf16[64,1152]{1,0:T(8,128)(2,1)S(1)}, u32[]{:S(2)}, u32[]{:S(2)}) collective-permute-start(bf16[64,1152]{1,0:T(8,128)(2,1)S(1)} %get-tuple-element.56), channel_id=1, source_target_pairs={{0,6},{1,7},{2,0},{3,1},{4,2},{5,3},{6,4},{7,5},{8,14},{9,15},{10,... | collective-permute-start | bytes 442376 | tf_op jit(solution)/shard_map/ppermute | solution.py:450
  27.2 6.7 %collective-permute-start.9 = (f32[16,128]{1,0:T(8,128)S(1)}, f32[16,128]{1,0:T(8,128)S(1)}, u32[]{:S(2)}, u32[]{:S(2)}) collective-permute-start(f32[16,128]{1,0:T(8,128)S(1)} %get-tuple-element.62.refs_6_.refs_1_), channel_id=1, source_target_pairs={{0,8},{1,9},{2,10},{3,11},{4,12},{5,13},{6,14},{7,15},{8,0},{9,1},... | collective-permute-start | bytes 24584 | tf_op jit(solution)/shard_map/ppermute | solution.py:458
  34.1 2.0 %collective-permute-start.10 = (bf16[1056,256]{1,0:T(8,128)(2,1)S(1)}, bf16[1056,256]{1,0:T(8,128)(2,1)S(1)}, u32[]{:S(2)}, u32[]{:S(2)}) collective-permute-start(bf16[1056,256]{1,0:T(8,128)(2,1)S(1)} %get-tuple-element.70), channel_id=1, source_target_pairs={{0,1},{1,0},{2,3},{3,2},{4,5},{5,4},{6,7},{7,6},{8,9},{9,8},{10,11... | collective-permute-start | bytes 1622024 | tf_op jit(solution)/shard_map/ppermute | solution.py:445
  34.1 6.1 %collective-permute-start.8 = (bf16[2,64,1024]{2,1,0:T(8,128)(2,1)S(1)}, bf16[2,64,1024]{2,1,0:T(8,128)(2,1)S(1)}, u32[]{:S(2)}, u32[]{:S(2)}) collective-permute-start(bf16[2,64,1024]{2,1,0:T(8,128)(2,1)S(1)} %get-tuple-element.58), channel_id=1, source_target_pairs={{0,1},{1,0},{2,3},{3,2},{4,5},{5,4},{6,7},{7,6},{8,9},{9,8},{10,11... | collective-permute-start | bytes 786440 | tf_op jit(solution)/shard_map/ppermute | solution.py:445
  36.2 21.2 %collective-permute-start.11 = (bf16[288,256]{1,0:T(8,128)(2,1)S(1)}, bf16[288,256]{1,0:T(8,128)(2,1)S(1)}, u32[]{:S(2)}, u32[]{:S(2)}) collective-permute-start(bf16[288,256]{1,0:T(8,128)(2,1)S(1)} %get-tuple-element.76), channel_id=1, source_target_pairs={{0,2},{1,3},{2,4},{3,5},{4,6},{5,7},{6,0},{7,1},{8,10},{9,11},{10,... | collective-permute-start | bytes 442376 | tf_op jit(solution)/shard_map/ppermute | solution.py:450
  38.0 19.5 %collective-permute-start.12 = (bf16[288,256]{1,0:T(8,128)(2,1)S(1)}, bf16[288,256]{1,0:T(8,128)(2,1)S(1)}, u32[]{:S(2)}, u32[]{:S(2)}) collective-permute-start(bf16[288,256]{1,0:T(8,128)(2,1)S(1)} %get-tuple-element.77), channel_id=1, source_target_pairs={{0,4},{1,5},{2,6},{3,7},{4,0},{5,1},{6,2},{7,3},{8,12},{9,13},{10,... | collective-permute-start | bytes 442376 | tf_op jit(solution)/shard_map/ppermute | solution.py:450
  38.6 18.8 %collective-permute-start.13 = (bf16[288,256]{1,0:T(8,128)(2,1)S(1)}, bf16[288,256]{1,0:T(8,128)(2,1)S(1)}, u32[]{:S(2)}, u32[]{:S(2)}) collective-permute-start(bf16[288,256]{1,0:T(8,128)(2,1)S(1)} %get-tuple-element.78), channel_id=1, source_target_pairs={{0,6},{1,7},{2,0},{3,1},{4,2},{5,3},{6,4},{7,5},{8,14},{9,15},{10,... | collective-permute-start | bytes 442376 | tf_op jit(solution)/shard_map/ppermute | solution.py:450
  43.0 4.5 %collective-permute-start.14 = (f32[16,128]{1,0:T(8,128)S(1)}, f32[16,128]{1,0:T(8,128)S(1)}, u32[]{:S(2)}, u32[]{:S(2)}) collective-permute-start(f32[16,128]{1,0:T(8,128)S(1)} %get-tuple-element.79), channel_id=1, source_target_pairs={{0,16},{1,17},{2,18},{3,19},{4,20},{5,21},{6,22},{7,23},{8,24},{9,... | collective-permute-start | bytes 24584 | tf_op jit(solution)/shard_map/ppermute | solution.py:458
  45.6 6.3 %collective-permute-start.15 = (f32[16,128]{1,0:T(8,128)S(1)}, f32[16,128]{1,0:T(8,128)S(1)}, u32[]{:S(2)}, u32[]{:S(2)}) collective-permute-start(f32[16,128]{1,0:T(8,128)S(1)} %get-tuple-element.79), channel_id=1, source_target_pairs={{0,18},{1,19},{2,20},{3,21},{4,22},{5,23},{6,16},{7,17},{8,26},{9,... | collective-permute-start | bytes 24584 | tf_op jit(solution)/shard_map/ppermute | solution.py:458
  47.6 5.4 %collective-permute-start.16 = (f32[16,128]{1,0:T(8,128)S(1)}, f32[16,128]{1,0:T(8,128)S(1)}, u32[]{:S(2)}, u32[]{:S(2)}) collective-permute-start(f32[16,128]{1,0:T(8,128)S(1)} %get-tuple-element.79), channel_id=1, source_target_pairs={{0,20},{1,21},{2,22},{3,23},{4,16},{5,17},{6,18},{7,19},{8,28},{9,... | collective-permute-start | bytes 24584 | tf_op jit(solution)/shard_map/ppermute | solution.py:458
  52.0 5.4 %collective-permute-start.17 = (f32[16,128]{1,0:T(8,128)S(1)}, f32[16,128]{1,0:T(8,128)S(1)}, u32[]{:S(2)}, u32[]{:S(2)}) collective-permute-start(f32[16,128]{1,0:T(8,128)S(1)} %get-tuple-element.79), channel_id=1, source_target_pairs={{0,22},{1,23},{2,16},{3,17},{4,18},{5,19},{6,20},{7,21},{8,30},{9,... | collective-permute-start | bytes 24584 | tf_op jit(solution)/shard_map/ppermute | solution.py:458
  (4 other events, 27.6 us)

commit v10 on v7

--- a/solution.py
+++ b/solution.py
@@ -191,33 +191,32 @@
         give_ref[1, :, head(h)] = jnp.where(is0, l1, l0)
 
 
+def find_slots(row, most, mask_ref, slot_ref):
+    for slot in range(most):
+        slot_ref[slot] = row
+
+    def note(j, seen):
+        hit = mask_ref[row, j]
+
+        @pl.when(hit == 1)
+        def _():
+            slot_ref[seen] = j
+
+        return seen + hit
+
+    allowed = lax.fori_loop(0, mask_ref.shape[0], note, 0)
+    return [(slot_ref[slot], slot < allowed) for slot in range(most)]
+
+
 def block_attention(
-    block, most, mask_ref, q_ref, g_ref, kv_ref, out_ref, dq_ref, acc_ref,
-    slot_ref, k_ref, k_live_ref, v_ref, q_turned_ref, g_turned_ref, ds_ref, wb_ref,
+    block, slots, q_ref, g_ref, kv_ref, out_ref, dq_ref,
+    k_ref, k_live_ref, v_ref, q_turned_ref, g_turned_ref, ds_ref, wb_ref,
 ):
-    count = mask_ref.shape[0]
     scale = FACTOR * LOG2E
     lower, upper = slice(0, LANES), slice(LANES, 2 * LANES)
     own = slice(block * BLOCK, (block + 1) * BLOCK)
     at = slice(block * BLOCK, (block + 1) * BLOCK)
-    row = lax.axis_index("seq") * (q_ref.shape[0] // BLOCK) + block
-    slots = []
-    for slot in range(most):
-        slot_ref[slot] = row
-
-    def note(j, seen):
-        hit = mask_ref[row, j]
-
-        @pl.when(hit == 1)
-        def _():
-            slot_ref[seen] = j
-
-        return seen + hit
-
-    allowed = lax.fori_loop(0, count, note, 0)
-    for slot in range(most):
-        index, live = slot_ref[slot], slot < allowed
-        slots.append((index, live))
+    for slot, (index, live) in enumerate(slots):
         source = pl.ds(pl.multiple_of(index * BLOCK, BLOCK), BLOCK)
         target = slice(slot * BLOCK, (slot + 1) * BLOCK)
         k_tile, v_tile = kv_ref[source, lower], kv_ref[source, upper]
@@ -255,6 +254,10 @@
             part = slice(place * BLOCK, (place + 1) * BLOCK)
             out_ref[:, head(h)] = out[part]
             dq_ref[own, head(h)] = dq[part]
+
+
+def add_key_terms(slots, acc_ref, q_turned_ref, g_turned_ref, ds_ref, wb_ref):
+    lower, upper = slice(0, LANES), slice(LANES, 2 * LANES)
     dk = dot(q_turned_ref[...], ds_ref[...], 1, 0)
     dv = dot(g_turned_ref[...], wb_ref[...], 1, 0)
     for slot, (index, live) in enumerate(slots):
@@ -268,7 +271,7 @@
 
 
 def first_attention_kernel(
-    chips, most, mask_ref, q_ref, g_ref, stack_ref, other_stack_ref, _, out_ref, dq_ref, acc_ref, kv_ref, *scratch
+    chips, most, mask_ref, q_ref, g_ref, stack_ref, other_stack_ref, _, out_ref, dq_ref, acc_ref, kv_ref, slot_ref, *scratch
 ):
     tokens = q_ref.shape[0]
     chip, core = chip_and_core()
@@ -278,15 +281,26 @@
             source = 2 * lax.rem(chip + chips - k, chips) + lax.rem(core + other, 2)
             at = pl.ds(pl.multiple_of(source * tokens, tokens), tokens)
             kv_ref[at, :] = ref[k]
-    block_attention(0, most, mask_ref, q_ref, g_ref, kv_ref, out_ref, dq_ref, acc_ref, *scratch)
+    slots = find_slots(2 * lax.axis_index("seq"), most, mask_ref, slot_ref)
+    block_attention(0, slots, q_ref, g_ref, kv_ref, out_ref, dq_ref, *scratch)
+    add_key_terms(slots, acc_ref, *scratch[3:])
 
 
 def second_attention_kernel(
-    most, mask_ref, q_ref, g_ref, kv_ref, first_dq_ref, first_acc_ref, _, out_ref, dq_ref, acc_ref, *scratch
+    most, mask_ref, q_ref, g_ref, kv_ref, first_dq_ref, _, out_ref, dq_ref,
+    q_turned_ref, g_turned_ref, ds_ref, wb_ref, slot_ref, *scratch
 ):
+    dq_ref[:BLOCK, :] = first_dq_ref[...]
+    slots = find_slots(2 * lax.axis_index("seq") + 1, most, mask_ref, slot_ref)
+    products = (q_turned_ref, g_turned_ref, ds_ref, wb_ref)
+    block_attention(1, slots, q_ref, g_ref, kv_ref, out_ref, dq_ref, *scratch, *products)
+
+
+def key_terms_kernel(most, mask_ref, first_acc_ref, *refs):
+    products, acc_ref, slot_ref = refs[:4], refs[4], refs[5]
     acc_ref[...] = first_acc_ref[...]
-    dq_ref[:BLOCK, :] = first_dq_ref[...]
-    block_attention(1, most, mask_ref, q_ref, g_ref, kv_ref, out_ref, dq_ref, acc_ref, *scratch)
+    slots = find_slots(2 * lax.axis_index("seq") + 1, most, mask_ref, slot_ref)
+    add_key_terms(slots, acc_ref, *products)
 
 
 def share_kernel(chips, acc_ref, *refs):
@@ -400,7 +414,7 @@
 
 
 def chunk_kernel(
-    x_ref, g_ref, b_ref, c_ref, step_ref, rate_ref, skip_ref, _,
+    x_ref, g_ref, b_ref, c_ref, step_ref, rate_ref, skip_ref,
     state_ref, y_ref, dx_ref, db_ref, dc_ref, sums_ref, pad_ref, *scratch
 ):
     operands = (x_ref, g_ref, b_ref, c_ref, step_ref, rate_ref)
@@ -445,9 +459,9 @@
     return lax.ppermute(array, "seq", [(i, (i + 2 * k) % n) for i in range(n)])
 
 
-def turned(array, k):
-    n = lax.axis_size("dp")
-    return lax.ppermute(array, "dp", [(i, (i + k) % n) for i in range(n)])
+def from_replica(array, distance):
+    pairs = [(r, r ^ distance) for r in range(lax.axis_size("dp"))]
+    return lax.ppermute(array, "dp", pairs)
 
 
 def call(kernel, outs, ins, scratch, microseconds, name, limit=16):
@@ -491,7 +505,7 @@
         + [((tokens, WIDE), F32)] * 2
         + [((tokens, NS), F32)] * 2
         + [((2 * HS, LANES), F32)],
-        [VMEM] * 5 + [SMEM] * 2 + [AFTER],
+        [VMEM] * 5 + [SMEM] * 2,
         [
             pltpu.VMEM((LANES, tokens), F32),
             pltpu.VMEM((tokens, WIDE), BF16),
@@ -505,7 +519,7 @@
         6,
         "chunk_alone",
         20,
-    )(x, g, b, c, steps, rate_log, skip, kv)
+    )(x, g, b, c, steps, rate_log, skip)
     half = ((4, HALF, WIDE + LANES), F32)
     keep, give, stack = call(
         split_kernel,
@@ -563,17 +577,37 @@
         "chain_states",
     )(keep, received, sums, first_dq, *arrived)
     other = swapped(give)
-    replicated = [turned(totals, k) for k in range(1, replicas)]
-
-    second_out, dq, acc = call(
+    rounds = [1 << bit for bit in range((replicas - 1).bit_length())]
+    replicated = totals
+    for distance in rounds[:-1]:
+        replicated = replicated + from_replica(replicated, distance)
+    last_round = from_replica(replicated, rounds[-1])
+
+    second_out, dq, *products = call(
         lambda *refs: second_attention_kernel(most, *refs),
-        [((BLOCK, columns), F32), ((tokens, columns), BF16), ((2 * LANES, every), F32)],
-        [SMEM] + [VMEM] * 5 + [AFTER],
-        scratch,
-        5,
+        [
+            ((BLOCK, columns), F32),
+            ((tokens, columns), BF16),
+            ((LANES, columns), BF16),
+            ((LANES, columns), BF16),
+            ((columns, most * BLOCK), BF16),
+            ((columns, most * BLOCK), BF16),
+        ],
+        [SMEM] + [VMEM] * 4 + [AFTER],
+        scratch[:4],
+        4,
         "second_attention",
         18 + most,
-    )(block_mask[0], q, g, kv_all, first_dq, first_acc, totals)
+    )(block_mask[0], q, g, kv_all, first_dq, totals)
+    (acc,) = call(
+        lambda *refs: key_terms_kernel(most, *refs),
+        [((2 * LANES, every), F32)],
+        [SMEM] + [VMEM] * 5,
+        scratch[:1],
+        2,
+        "key_terms",
+        18 + most,
+    )(block_mask[0], first_acc, *products)
     keep, give, sums = call(
         lambda *refs: share_kernel(chips, *refs),
         [
@@ -581,11 +615,11 @@
             ((chips * 2 * LANES + 32, tokens), BF16),
             ((2 * HS, LANES), F32),
         ],
-        [VMEM] * (1 + replicas),
+        [VMEM] * 3,
         [],
         1,
         "share_key_gradients",
-    )(acc, totals, *replicated)
+    )(acc, replicated, last_round)
     partial, summed, *messages = call(
         lambda *refs: pair_sum_kernel(chips, *refs),
         [((2 * LANES, tokens), F32), ((2 * HS, LANES), F32)]

time: 50.6 us -> 51.2 us (1.012)
  Pallas kernels: 20.3 us -> 21.7 us
  local copies, waits for them, and re-layouts: 0.97 us -> 0.04 us
  starting transfers between devices: 19.2 us -> 19.8 us
    pallas_call x0 -> x1, Pallas kernels: none -> 1.63 us  [body(): call(lambda *refs: key_terms_kernel(most, *refs), [((2 * LANES, every), F...]
    ppermute x9, starting transfers between devices: 13.4 us -> 14.4 us  [from_chip(): return lax.ppermute(array, 'seq', [(i, (i + 2 * k) % n) for i in range(n)])]
    unnamed x20, local copies, waits for them, and re-layouts: 0.97 us -> 0.04 us
    ppermute x9, waiting for transfers between devices: 5.3 us -> 4.54 us  [from_chip(): return lax.ppermute(array, 'seq', [(i, (i + 2 * k) % n) for i in range(n)])]
    ppermute x3 -> x2, starting transfers between devices: 4.68 us -> 4.23 us  [from_replica(): return lax.ppermute(array, 'dp', pairs)]
  transfers between devices with their start and end apart: 16 -> 15, of which waited for: 5 -> 7; matrix products, arithmetic and copies ran while one was open for 0% -> 0% of each run, Pallas kernels for 33% -> 36%
where the time goes in v10:
time: 51.2 us; the launch traced here: 51 us
  Pallas kernels  21.7 us (42%)
  starting transfers between devices  19.8 us (39%)
  waiting for transfers between devices  8.63 us (17%)
  between operations  0.85 us (2%)
    ppermute x9, starting transfers between devices, from_chip(): return lax.ppermute(array, 'seq', [(i, (i + 2 * k) % n) for i in range(n)])  14.4 us
    pallas_call x1, Pallas kernels, body(): call(lambda *refs: second_attention_kernel(most, *refs), [((BLOCK, column...  4.59 us
    ppermute x9, waiting for transfers between devices, from_chip(): return lax.ppermute(array, 'seq', [(i, (i + 2 * k) % n) for i in range(n)])  4.54 us
    pallas_call x1, Pallas kernels, body(): call(chunk_kernel, [((4, NS, WIDE + LANES), F32)] + [((tokens, WIDE), F32...  4.53 us
    pallas_call x1, Pallas kernels, body(): call(lambda *refs: first_attention_kernel(chips, most, *refs), [((BLOCK,...  4.36 us
    ppermute x2, starting transfers between devices, from_replica(): return lax.ppermute(array, 'dp', pairs)  4.23 us
    ppermute x4, waiting for transfers between devices, swapped(): lax.ppermute(array, 'seq', [(i, i ^ 1) for i in range(lax.axis_size('seq'...  3.77 us
    pallas_call x1, Pallas kernels, body(): call(outer_kernel, [((tokens, WIDE), BF16)] * 2 + [((tokens, NS), BF16)]...  2.82 us
  transfers between devices with their start and end apart: 15, of which 7 were waited for; matrix products, arithmetic and copies ran while one was open for 0% of the time, Pallas kernels for 36%

profile of v10, /device:TPU:0, one launch (start us, length us, event | category | flops | bytes accessed | tf_op | source)
XLA Modules:
  0.0 51.0 jit_solution(5352157032711338958)
XLA Ops:
  0.7 1.6 %pack_kv.1.refs_0_ = bf16[256,256]{1,0:T(8,128)(2,1)} custom-call(bf16[256,128]{1,0:T(8,128)(2,1)} %bitcast.37, bf16[256,128]{1,0:T(8,128)(2,1)} %bitcast.38), custom_call_target="tpu_custom_call" | custom-call | flops 1100000000 | bytes 1048576 | tf_op jit(solution)/shard_map/pack_kv/pallas_call | solution.py:491
  2.3 3.0 %collective-permute-start = (bf16[256,256]{1,0:T(8,128)(2,1)}, bf16[256,256]{1,0:T(8,128)(2,1)S(1)}, u32[]{:S(2)}, u32[]{:S(2)}) collective-permute-start(bf16[256,256]{1,0:T(8,128)(2,1)} %pack_kv.1.refs_0_), channel_id=1, source_target_pairs={{0,2},{1,3},{2,4},{3,5},{4,6},{5,7},{6,0},{7,1},{8,10},{9,11},{10,... | collective-permute-start | bytes 393224 | tf_op jit(solution)/shard_map/ppermute | solution.py:459
  5.3 1.5 %collective-permute-start.1 = (bf16[256,256]{1,0:T(8,128)(2,1)}, bf16[256,256]{1,0:T(8,128)(2,1)S(1)}, u32[]{:S(2)}, u32[]{:S(2)}) collective-permute-start(bf16[256,256]{1,0:T(8,128)(2,1)} %pack_kv.1.refs_0_), channel_id=1, source_target_pairs={{0,4},{1,5},{2,6},{3,7},{4,0},{5,1},{6,2},{7,3},{8,12},{9,13},{10,... | collective-permute-start | bytes 393224 | tf_op jit(solution)/shard_map/ppermute | solution.py:459
  6.9 1.4 %collective-permute-start.2 = (bf16[256,256]{1,0:T(8,128)(2,1)}, bf16[256,256]{1,0:T(8,128)(2,1)S(1)}, u32[]{:S(2)}, u32[]{:S(2)}) collective-permute-start(bf16[256,256]{1,0:T(8,128)(2,1)} %pack_kv.1.refs_0_), channel_id=1, source_target_pairs={{0,6},{1,7},{2,0},{3,1},{4,2},{5,3},{6,4},{7,5},{8,14},{9,15},{10,... | collective-permute-start | bytes 393224 | tf_op jit(solution)/shard_map/ppermute | solution.py:459
  8.3 4.5 %chunk_alone.1 = (f32[4,128,1152]{2,1,0:T(8,128)S(1)}, f32[256,1024]{1,0:T(8,128)S(1)}, f32[256,1024]{1,0:T(8,128)S(1)}, f32[256,128]{1,0:T(8,128)S(1)}, f32[256,128]{1,0:T(8,128)S(1)}, /*index=5*/f32[16,128]{1,0:T(8,128)S(1)}) custom-call(bf16[256,1024]{1,0:T(8,128)(2,1)S(1)} %bitcast.22, bf16[256,1024]{1,0:T(8,128)(2,1)S(1)} %bitcast.24, ...), custom_call_target="tpu_custom_call" | custom-call | flops 6600000000 | bytes 1048576 | tf_op jit(solution)/shard_map/chunk_alone/pallas_call | solution.py:502
  13.8 2.3 %collective-permute-done.3.refs_1_ = f32[4,64,1152]{2,1,0:T(8,128)S(1)} collective-permute-done((f32[4,64,1152]{2,1,0:T(8,128)S(1)}, f32[4,64,1152]{2,1,0:T(8,128)S(1)}, u32[]{:S(2)}, u32[]{:S(2)}) %collective-permute-start.3) | collective-permute-done | bytes 1179680 | tf_op jit(solution)/shard_map/ppermute | solution.py:454
  16.4 1.8 %collective-permute-start.5 = (bf16[64,1152]{1,0:T(8,128)(2,1)S(1)}, bf16[64,1152]{1,0:T(8,128)(2,1)S(1)}, u32[]{:S(2)}, u32[]{:S(2)}) collective-permute-start(bf16[64,1152]{1,0:T(8,128)(2,1)S(1)} %get-tuple-element.55.refs_5_), channel_id=1, source_target_pairs={{0,2},{1,3},{2,4},{3,5},{4,6},{5,7},{6,0},{7,1},{8,10},{9,11},{10,... | collective-permute-start | bytes 442376 | tf_op jit(solution)/shard_map/ppermute | solution.py:459
  18.6 2.3 %collective-permute-start.7 = (bf16[64,1152]{1,0:T(8,128)(2,1)S(1)}, bf16[64,1152]{1,0:T(8,128)(2,1)S(1)}, u32[]{:S(2)}, u32[]{:S(2)}) collective-permute-start(bf16[64,1152]{1,0:T(8,128)(2,1)S(1)} %get-tuple-element.58), channel_id=1, source_target_pairs={{0,6},{1,7},{2,0},{3,1},{4,2},{5,3},{6,4},{7,5},{8,14},{9,15},{10,... | collective-permute-start | bytes 442376 | tf_op jit(solution)/shard_map/ppermute | solution.py:459
  20.9 4.4 %first_attention.1 = (f32[128,1024]{1,0:T(8,128)S(1)}, bf16[128,1024]{1,0:T(8,128)(2,1)S(1)}, f32[256,2048]{1,0:T(8,128)S(1)}, bf16[2048,256]{1,0:T(8,128)(2,1)S(1)}) custom-call(s32[16,16]{1,0:T(8,128)S(1)} %bitcast.32, bf16[256,1024]{1,0:T(8,128)(2,1)S(1)} %bitcast.20, bf16[256,1024]{1,0:T(8,128)(2,1)S(1)} %bitcast.25, ...), custom_call_target="tpu_custom_call" | custom-call | flops 5500000256 | bytes 1048576 | tf_op jit(solution)/shard_map/first_attention/pallas_call | solution.py:556
  25.2 1.2 %collective-permute-done.6.refs_5_ = bf16[64,1152]{1,0:T(8,128)(2,1)S(1)} collective-permute-done((bf16[64,1152]{1,0:T(8,128)(2,1)S(1)}, bf16[64,1152]{1,0:T(8,128)(2,1)S(1)}, u32[]{:S(2)}, u32[]{:S(2)}) %collective-permute-start.6) | collective-permute-done | bytes 147488 | tf_op jit(solution)/shard_map/ppermute | solution.py:459
  26.5 0.7 %chain_states.1 = (bf16[2,64,1024]{2,1,0:T(8,128)(2,1)S(1)}, bf16[2,64,1024]{2,1,0:T(8,128)(2,1)S(1)}, f32[16,128]{1,0:T(8,128)S(1)}) custom-call(f32[4,64,1152]{2,1,0:T(8,128)S(1)} %get-tuple-element.51.refs_0_, f32[4,64,1152]{2,1,0:T(8,128)S(1)} %collective-permute-done.3.refs_1_, f32[16,128]{1,0:T(8,128)S(1)} %get-tuple-element.53.refs_2_, ...), custom_call_target="tpu_custom_call" | custom-call | flops 2200000000 | bytes 1048576 | tf_op jit(solution)/shard_map/chain_states/pallas_call | solution.py:571
  27.1 1.6 %collective-permute-start.9 = (f32[16,128]{1,0:T(8,128)S(1)}, f32[16,128]{1,0:T(8,128)S(1)}, u32[]{:S(2)}, u32[]{:S(2)}) collective-permute-start(f32[16,128]{1,0:T(8,128)S(1)} %get-tuple-element.63.refs_5_), channel_id=1, source_target_pairs={{0,8},{8,0},{16,24},{24,16},{1,9},{9,1},{17,25},{25,17},{2,10},{10... | collective-permute-start | bytes 24584 | tf_op jit(solution)/shard_map/ppermute | solution.py:464
  28.8 4.6 %second_attention.1 = (f32[128,1024]{1,0:T(8,128)S(1)}, bf16[256,1024]{1,0:T(8,128)(2,1)}, bf16[128,1024]{1,0:T(8,128)(2,1)S(1)}, bf16[128,1024]{1,0:T(8,128)(2,...) custom-call(s32[16,16]{1,0:T(8,128)S(1)} %bitcast.33, bf16[256,1024]{1,0:T(8,128)(2,1)S(1)} %bitcast.21, ...), custom_call_target="tpu_custom_call" | custom-call | flops 4400000000 | bytes 1048576 | tf_op jit(solution)/shard_map/second_attention/pallas_call | solution.py:586
  33.4 2.6 %collective-permute-start.10 = (f32[16,128]{1,0:T(8,128)S(1)}, f32[16,128]{1,0:T(8,128)S(1)}, u32[]{:S(2)}, u32[]{:S(2)}) collective-permute-start(f32[16,128]{1,0:T(8,128)S(1)} %add.3.refs_1_), channel_id=1, source_target_pairs={{0,16},{8,24},{16,0},{24,8},{1,17},{9,25},{17,1},{25,9},{2,18},{10... | collective-permute-start | bytes 24584 | tf_op jit(solution)/shard_map/ppermute | solution.py:464
  35.9 1.6 %key_terms.1.refs_0_ = f32[256,2048]{1,0:T(8,128)S(1)} custom-call(s32[16,16]{1,0:T(8,128)S(1)} %bitcast.34, f32[256,2048]{1,0:T(8,128)S(1)} %get-tuple-element.69.refs_1_, bf16[128,1024]{1,0:T(8,128)(2,1)S(1)} %get-tuple-element.70.refs_2_, bf16[128,1024]{1,0:T(8,128)(2,1)S(1)} %get-tuple-element.71.refs_3_, ...), custom_call_target="tpu_custom_call" | custom-call | flops 2200000000 | bytes 1048576 | tf_op jit(solution)/shard_map/key_terms/pallas_call | solution.py:602
  38.1 0.5 collective-permute-start.8
  38.6 1.4 %collective-permute-done.11.refs_1_ = bf16[1056,256]{1,0:T(8,128)(2,1)S(1)} collective-permute-done((bf16[1056,256]{1,0:T(8,128)(2,1)S(1)}, bf16[1056,256]{1,0:T(8,128)(2,1)S(1)}, u32[]{:S(2)}, u32[]{:S(2)}) %collective-permute-start.11) | collective-permute-done | bytes 540704 | tf_op jit(solution)/shard_map/ppermute | solution.py:454
  40.2 1.8 %collective-permute-start.12 = (bf16[288,256]{1,0:T(8,128)(2,1)S(1)}, bf16[288,256]{1,0:T(8,128)(2,1)S(1)}, u32[]{:S(2)}, u32[]{:S(2)}) collective-permute-start(bf16[288,256]{1,0:T(8,128)(2,1)S(1)} %get-tuple-element.77._), channel_id=1, source_target_pairs={{0,2},{1,3},{2,4},{3,5},{4,6},{5,7},{6,0},{7,1},{8,10},{9,11},{10,... | collective-permute-start | bytes 442376 | tf_op jit(solution)/shard_map/ppermute | solution.py:459
  42.0 0.6 %collective-permute-start.13 = (bf16[288,256]{1,0:T(8,128)(2,1)S(1)}, bf16[288,256]{1,0:T(8,128)(2,1)S(1)}, u32[]{:S(2)}, u32[]{:S(2)}) collective-permute-start(bf16[288,256]{1,0:T(8,128)(2,1)S(1)} %get-tuple-element.82), channel_id=1, source_target_pairs={{0,4},{1,5},{2,6},{3,7},{4,0},{5,1},{6,2},{7,3},{8,12},{9,13},{10,... | collective-permute-start | bytes 442376 | tf_op jit(solution)/shard_map/ppermute | solution.py:459
  42.5 1.7 %collective-permute-start.14 = (bf16[288,256]{1,0:T(8,128)(2,1)S(1)}, bf16[288,256]{1,0:T(8,128)(2,1)S(1)}, u32[]{:S(2)}, u32[]{:S(2)}) collective-permute-start(bf16[288,256]{1,0:T(8,128)(2,1)S(1)} %get-tuple-element.83), channel_id=1, source_target_pairs={{0,6},{1,7},{2,0},{3,1},{4,2},{5,3},{6,4},{7,5},{8,14},{9,15},{10,... | collective-permute-start | bytes 442376 | tf_op jit(solution)/shard_map/ppermute | solution.py:459
  44.2 2.8 %chunk_outer.1 = (bf16[256,1024]{1,0:T(8,128)(2,1)}, bf16[256,1024]{1,0:T(8,128)(2,1)}, bf16[256,128]{1,0:T(8,128)(2,1)}, bf16[256,128]{1,0:T(8,128)(2,1)}) custom-call(bf16[256,1024]{1,0:T(8,128)(2,1)S(1)} %bitcast.23, bf16[256,1024]{1,0:T(8,128)(2,1)S(1)} %bitcast.27, bf16[256,128]{1,0:T(8,128)(2,1)S(1)} %bitcast.29, bf16[256,128]{1,0:T(8,128)(2,1)S(1)} %bitcast.31, ...), custom_call_target="tpu_custom_call" | custom-call | flops 3300000000 | bytes 1048576 | tf_op jit(solution)/shard_map/chunk_outer/pallas_call | solution.py:634
  47.0 0.8 %collective-permute-done.12.refs_2_ = bf16[288,256]{1,0:T(8,128)(2,1)S(1)} collective-permute-done((bf16[288,256]{1,0:T(8,128)(2,1)S(1)}, bf16[288,256]{1,0:T(8,128)(2,1)S(1)}, u32[]{:S(2)}, u32[]{:S(2)}) %collective-permute-start.12) | collective-permute-done | bytes 147488 | tf_op jit(solution)/shard_map/ppermute | solution.py:459
  47.9 2.3 %collective-permute-done.13.refs_3_ = bf16[288,256]{1,0:T(8,128)(2,1)S(1)} collective-permute-done((bf16[288,256]{1,0:T(8,128)(2,1)S(1)}, bf16[288,256]{1,0:T(8,128)(2,1)S(1)}, u32[]{:S(2)}, u32[]{:S(2)}) %collective-permute-start.13) | collective-permute-done | bytes 147488 | tf_op jit(solution)/shard_map/ppermute | solution.py:459
  50.2 0.8 %owner_sum.1 = (bf16[256,128]{1,0:T(8,128)(2,1)}, bf16[256,128]{1,0:T(8,128)(2,1)}, f32[1,8]{1,0:T(1,128)}, f32[1,8]{1,0:T(1,128)}) custom-call(f32[256,256]{1,0:T(8,128)S(1)} %get-tuple-element.80.refs_0_, f32[16,128]{1,0:T(8,128)S(1)} %get-tuple-element.81.refs_1_, bf16[288,256]{1,0:T(8,128)(2,1)S(1)} %collective-permute-done.12.refs_2_, ...), custom_call_target="tpu_custom_call" | custom-call | flops 1100000000 | bytes 1048576 | tf_op jit(solution)/shard_map/owner_sum/pallas_call | solution.py:652
  (39 shorter events, 2.3 us)
Async XLA Ops:
  0.6 7.7 %copy-start.1 = (bf16[1,256,1024]{2,1,0:T(8,128)(2,1)S(1)}, bf16[1,256,1024]{2,1,0:T(8,128)(2,1)}, u32[]{:S(2)}) copy-start(bf16[1,256,1024]{2,1,0:T(8,128)(2,1)} %param.14) | copy-start | bytes 1572868
  0.7 7.6 %copy-start.2 = (bf16[1,256,1024]{2,1,0:T(8,128)(2,1)S(1)}, bf16[1,256,1024]{2,1,0:T(8,128)(2,1)}, u32[]{:S(2)}) copy-start(bf16[1,256,1024]{2,1,0:T(8,128)(2,1)} %param.21) | copy-start | bytes 1572868
  0.7 7.6 %copy-start.4 = (bf16[1,256,128]{2,1,0:T(8,128)(2,1)S(1)}, bf16[1,256,128]{2,1,0:T(8,128)(2,1)}, u32[]{:S(2)}) copy-start(bf16[1,256,128]{2,1,0:T(8,128)(2,1)} %param.15) | copy-start | bytes 196612
  0.7 7.6 %copy-start.5 = (bf16[1,256,128]{2,1,0:T(8,128)(2,1)S(1)}, bf16[1,256,128]{2,1,0:T(8,128)(2,1)}, u32[]{:S(2)}) copy-start(bf16[1,256,128]{2,1,0:T(8,128)(2,1)} %param.16) | copy-start | bytes 196612
  0.7 7.6 %copy-start.7 = (f32[1,256,8]{1,2,0:T(8,128)S(1)}, f32[1,256,8]{1,2,0:T(8,128)}, u32[]{:S(2)}) copy-start(f32[1,256,8]{1,2,0:T(8,128)} %param.17) | copy-start | bytes 24580
  0.7 7.6 %copy-start.8 = (f32[8]{0:T(128)S(1)}, f32[8]{0:T(128)}, u32[]{:S(2)}) copy-start(f32[8]{0:T(128)} %skip_ref.1) | copy-start | bytes 100
  0.7 7.6 %copy-start.9 = (f32[8]{0:T(128)S(1)}, f32[8]{0:T(128)}, u32[]{:S(2)}) copy-start(f32[8]{0:T(128)} %rate_ref.3) | copy-start | bytes 100
  2.3 10.5 %collective-permute-start = (bf16[256,256]{1,0:T(8,128)(2,1)}, bf16[256,256]{1,0:T(8,128)(2,1)S(1)}, u32[]{:S(2)}, u32[]{:S(2)}) collective-permute-start(bf16[256,256]{1,0:T(8,128)(2,1)} %pack_kv.1.refs_0_), channel_id=1, source_target_pairs={{0,2},{1,3},{2,4},{3,5},{4,6},{5,7},{6,0},{7,1},{8,10},{9,11},{10,... | collective-permute-start | bytes 393224 | tf_op jit(solution)/shard_map/ppermute | solution.py:459
  5.3 7.6 %collective-permute-start.1 = (bf16[256,256]{1,0:T(8,128)(2,1)}, bf16[256,256]{1,0:T(8,128)(2,1)S(1)}, u32[]{:S(2)}, u32[]{:S(2)}) collective-permute-start(bf16[256,256]{1,0:T(8,128)(2,1)} %pack_kv.1.refs_0_), channel_id=1, source_target_pairs={{0,4},{1,5},{2,6},{3,7},{4,0},{5,1},{6,2},{7,3},{8,12},{9,13},{10,... | collective-permute-start | bytes 393224 | tf_op jit(solution)/shard_map/ppermute | solution.py:459
  6.9 6.2 %collective-permute-start.2 = (bf16[256,256]{1,0:T(8,128)(2,1)}, bf16[256,256]{1,0:T(8,128)(2,1)S(1)}, u32[]{:S(2)}, u32[]{:S(2)}) collective-permute-start(bf16[256,256]{1,0:T(8,128)(2,1)} %pack_kv.1.refs_0_), channel_id=1, source_target_pairs={{0,6},{1,7},{2,0},{3,1},{4,2},{5,3},{6,4},{7,5},{8,14},{9,15},{10,... | collective-permute-start | bytes 393224 | tf_op jit(solution)/shard_map/ppermute | solution.py:459
  8.3 4.7 %copy-start.3 = (bf16[256,256]{1,0:T(8,128)(2,1)S(1)}, bf16[256,256]{1,0:T(8,128)(2,1)}, u32[]{:S(2)}) copy-start(bf16[256,256]{1,0:T(8,128)(2,1)} %pack_kv.1.refs_0_) | copy-start | bytes 393220
  13.3 2.9 %collective-permute-start.3 = (f32[4,64,1152]{2,1,0:T(8,128)S(1)}, f32[4,64,1152]{2,1,0:T(8,128)S(1)}, u32[]{:S(2)}, u32[]{:S(2)}) collective-permute-start(f32[4,64,1152]{2,1,0:T(8,128)S(1)} %get-tuple-element.52), channel_id=1, source_target_pairs={{0,1},{1,0},{2,3},{3,2},{4,5},{5,4},{6,7},{7,6},{8,9},{9,8},{10,11... | collective-permute-start | bytes 3538952 | tf_op jit(solution)/shard_map/ppermute | solution.py:454
  13.3 7.5 %collective-permute-start.4 = (bf16[4,256,256]{2,1,0:T(8,128)(2,1)S(1)}, bf16[4,256,256]{2,1,0:T(8,128)(2,1)S(1)}, u32[]{:S(2)}, u32[]{:S(2)}) collective-permute-start(bf16[4,256,256]{2,1,0:T(8,128)(2,1)S(1)} %get-tuple-element.54.refs_3_), channel_id=1, source_target_pairs={{0,1},{1,0},{2,3},{3,2},{4,5},{5,4},{6,7},{7,6},{8,9},{9,8},{10,11... | collective-permute-start | bytes 1572872 | tf_op jit(solution)/shard_map/ppermute | solution.py:454
  16.2 4.7 %copy-start.6 = (s32[1,16,16]{2,1,0:T(8,128)S(1)}, s32[1,16,16]{2,1,0:T(8,128)}, u32[]{:S(2)}) copy-start(s32[1,16,16]{2,1,0:T(8,128)} %param.20) | copy-start | bytes 3076
  16.4 8.8 %collective-permute-start.5 = (bf16[64,1152]{1,0:T(8,128)(2,1)S(1)}, bf16[64,1152]{1,0:T(8,128)(2,1)S(1)}, u32[]{:S(2)}, u32[]{:S(2)}) collective-permute-start(bf16[64,1152]{1,0:T(8,128)(2,1)S(1)} %get-tuple-element.55.refs_5_), channel_id=1, source_target_pairs={{0,2},{1,3},{2,4},{3,5},{4,6},{5,7},{6,0},{7,1},{8,10},{9,11},{10,... | collective-permute-start | bytes 442376 | tf_op jit(solution)/shard_map/ppermute | solution.py:459
  18.2 8.2 %collective-permute-start.6 = (bf16[64,1152]{1,0:T(8,128)(2,1)S(1)}, bf16[64,1152]{1,0:T(8,128)(2,1)S(1)}, u32[]{:S(2)}, u32[]{:S(2)}) collective-permute-start(bf16[64,1152]{1,0:T(8,128)(2,1)S(1)} %get-tuple-element.57), channel_id=1, source_target_pairs={{0,4},{1,5},{2,6},{3,7},{4,0},{5,1},{6,2},{7,3},{8,12},{9,13},{10,... | collective-permute-start | bytes 442376 | tf_op jit(solution)/shard_map/ppermute | solution.py:459
  18.6 7.9 %collective-permute-start.7 = (bf16[64,1152]{1,0:T(8,128)(2,1)S(1)}, bf16[64,1152]{1,0:T(8,128)(2,1)S(1)}, u32[]{:S(2)}, u32[]{:S(2)}) collective-permute-start(bf16[64,1152]{1,0:T(8,128)(2,1)S(1)} %get-tuple-element.58), channel_id=1, source_target_pairs={{0,6},{1,7},{2,0},{3,1},{4,2},{5,3},{6,4},{7,5},{8,14},{9,15},{10,... | collective-permute-start | bytes 442376 | tf_op jit(solution)/shard_map/ppermute | solution.py:459
  27.1 6.2 %collective-permute-start.9 = (f32[16,128]{1,0:T(8,128)S(1)}, f32[16,128]{1,0:T(8,128)S(1)}, u32[]{:S(2)}, u32[]{:S(2)}) collective-permute-start(f32[16,128]{1,0:T(8,128)S(1)} %get-tuple-element.63.refs_5_), channel_id=1, source_target_pairs={{0,8},{8,0},{16,24},{24,16},{1,9},{9,1},{17,25},{25,17},{2,10},{10... | collective-permute-start | bytes 24584 | tf_op jit(solution)/shard_map/ppermute | solution.py:464
  33.4 4.6 %collective-permute-start.10 = (f32[16,128]{1,0:T(8,128)S(1)}, f32[16,128]{1,0:T(8,128)S(1)}, u32[]{:S(2)}, u32[]{:S(2)}) collective-permute-start(f32[16,128]{1,0:T(8,128)S(1)} %add.3.refs_1_), channel_id=1, source_target_pairs={{0,16},{8,24},{16,0},{24,8},{1,17},{9,25},{17,1},{25,9},{2,18},{10... | collective-permute-start | bytes 24584 | tf_op jit(solution)/shard_map/ppermute | solution.py:464
  38.1 2.0 %collective-permute-start.11 = (bf16[1056,256]{1,0:T(8,128)(2,1)S(1)}, bf16[1056,256]{1,0:T(8,128)(2,1)S(1)}, u32[]{:S(2)}, u32[]{:S(2)}) collective-permute-start(bf16[1056,256]{1,0:T(8,128)(2,1)S(1)} %get-tuple-element.75), channel_id=1, source_target_pairs={{0,1},{1,0},{2,3},{3,2},{4,5},{5,4},{6,7},{7,6},{8,9},{9,8},{10,11... | collective-permute-start | bytes 1622024 | tf_op jit(solution)/shard_map/ppermute | solution.py:454
  38.1 6.1 %collective-permute-start.8 = (bf16[2,64,1024]{2,1,0:T(8,128)(2,1)S(1)}, bf16[2,64,1024]{2,1,0:T(8,128)(2,1)S(1)}, u32[]{:S(2)}, u32[]{:S(2)}) collective-permute-start(bf16[2,64,1024]{2,1,0:T(8,128)(2,1)S(1)} %get-tuple-element.60), channel_id=1, source_target_pairs={{0,1},{1,0},{2,3},{3,2},{4,5},{5,4},{6,7},{7,6},{8,9},{9,8},{10,11... | collective-permute-start | bytes 786440 | tf_op jit(solution)/shard_map/ppermute | solution.py:454
  40.2 7.7 %collective-permute-start.12 = (bf16[288,256]{1,0:T(8,128)(2,1)S(1)}, bf16[288,256]{1,0:T(8,128)(2,1)S(1)}, u32[]{:S(2)}, u32[]{:S(2)}) collective-permute-start(bf16[288,256]{1,0:T(8,128)(2,1)S(1)} %get-tuple-element.77._), channel_id=1, source_target_pairs={{0,2},{1,3},{2,4},{3,5},{4,6},{5,7},{6,0},{7,1},{8,10},{9,11},{10,... | collective-permute-start | bytes 442376 | tf_op jit(solution)/shard_map/ppermute | solution.py:459
  42.0 8.2 %collective-permute-start.13 = (bf16[288,256]{1,0:T(8,128)(2,1)S(1)}, bf16[288,256]{1,0:T(8,128)(2,1)S(1)}, u32[]{:S(2)}, u32[]{:S(2)}) collective-permute-start(bf16[288,256]{1,0:T(8,128)(2,1)S(1)} %get-tuple-element.82), channel_id=1, source_target_pairs={{0,4},{1,5},{2,6},{3,7},{4,0},{5,1},{6,2},{7,3},{8,12},{9,13},{10,... | collective-permute-start | bytes 442376 | tf_op jit(solution)/shard_map/ppermute | solution.py:459
  42.5 7.7 %collective-permute-start.14 = (bf16[288,256]{1,0:T(8,128)(2,1)S(1)}, bf16[288,256]{1,0:T(8,128)(2,1)S(1)}, u32[]{:S(2)}, u32[]{:S(2)}) collective-permute-start(bf16[288,256]{1,0:T(8,128)(2,1)S(1)} %get-tuple-element.83), channel_id=1, source_target_pairs={{0,6},{1,7},{2,0},{3,1},{4,2},{5,3},{6,4},{7,5},{8,14},{9,15},{10,... | collective-permute-start | bytes 442376 | tf_op jit(solution)/shard_map/ppermute | solution.py:459
  (1 other events, 4.7 us)

commit v11 on v10

--- a/solution.py
+++ b/solution.py
@@ -17,6 +17,7 @@
 LOG2E = 1.4426950408889634
 NEG = -1e30
 HALF = NS // 2
+HALF_HEADS = QUERY_HEADS // 2
 HIGH = lax.Precision.HIGHEST
 F32 = jnp.float32
 BF16 = jnp.bfloat16
@@ -209,12 +210,12 @@
 
 
 def block_attention(
-    block, slots, q_ref, g_ref, kv_ref, out_ref, dq_ref,
+    block, chosen, slots, q_ref, g_ref, kv_ref, out_ref, dq_ref, dq_rows,
     k_ref, k_live_ref, v_ref, q_turned_ref, g_turned_ref, ds_ref, wb_ref,
 ):
     scale = FACTOR * LOG2E
     lower, upper = slice(0, LANES), slice(LANES, 2 * LANES)
-    own = slice(block * BLOCK, (block + 1) * BLOCK)
+    start, stop = chosen
     at = slice(block * BLOCK, (block + 1) * BLOCK)
     for slot, (index, live) in enumerate(slots):
         source = pl.ds(pl.multiple_of(index * BLOCK, BLOCK), BLOCK)
@@ -225,19 +226,19 @@
         v_ref[target, lower] = jnp.where(live, v_tile, jnp.zeros_like(v_tile))
         v_ref[target, upper] = jnp.full((BLOCK, LANES), jnp.where(live, 1.0, 0.0), F32).astype(BF16)
     group = 2
-    firsts = range(0, QUERY_HEADS, group)
+    firsts = range(start, stop, group)
 
     def stacked(ref, first):
         return jnp.concatenate([ref[at, head(h)] for h in range(first, first + group)], axis=0)
 
-    upcoming = dot(stacked(q_ref, 0), k_ref[...], 1, 1)
+    upcoming = dot(stacked(q_ref, start), k_ref[...], 1, 1)
     for first in firsts:
         heads = range(first, first + group)
-        rows = slice(first * BLOCK, (first + group) * BLOCK)
+        rows = slice((first - start) * BLOCK, (first - start + group) * BLOCK)
         q, g = stacked(q_ref, first), stacked(g_ref, first)
         scores = upcoming
         dprobs = dot(g, v_ref[:, lower], 1, 1)
-        if first + group < QUERY_HEADS:
+        if first + group < stop:
             upcoming = dot(stacked(q_ref, first + group), k_ref[...], 1, 1)
         best = jnp.max(scores, axis=1, keepdims=True)
         weights = jnp.exp2((scores - best) * scale)
@@ -252,14 +253,14 @@
         g_turned_ref[:, rows] = (g.astype(F32) * inverse).astype(BF16).T
         for place, h in enumerate(heads):
             part = slice(place * BLOCK, (place + 1) * BLOCK)
-            out_ref[:, head(h)] = out[part]
-            dq_ref[own, head(h)] = dq[part]
-
-
-def add_key_terms(slots, acc_ref, q_turned_ref, g_turned_ref, ds_ref, wb_ref):
+            out_ref[:, head(h - start)] = out[part]
+            dq_ref[dq_rows, head(h - start)] = dq[part]
+
+
+def add_key_terms(slots, acc_ref, *parts):
     lower, upper = slice(0, LANES), slice(LANES, 2 * LANES)
-    dk = dot(q_turned_ref[...], ds_ref[...], 1, 0)
-    dv = dot(g_turned_ref[...], wb_ref[...], 1, 0)
+    dk = sum(dot(q_turned_ref[...], ds_ref[...], 1, 0) for q_turned_ref, _, ds_ref, _ in parts)
+    dv = sum(dot(g_turned_ref[...], wb_ref[...], 1, 0) for _, g_turned_ref, _, wb_ref in parts)
     for slot, (index, live) in enumerate(slots):
         source = slice(slot * BLOCK, (slot + 1) * BLOCK)
 
@@ -282,25 +283,36 @@
             at = pl.ds(pl.multiple_of(source * tokens, tokens), tokens)
             kv_ref[at, :] = ref[k]
     slots = find_slots(2 * lax.axis_index("seq"), most, mask_ref, slot_ref)
-    block_attention(0, slots, q_ref, g_ref, kv_ref, out_ref, dq_ref, *scratch)
-    add_key_terms(slots, acc_ref, *scratch[3:])
-
-
-def second_attention_kernel(
-    most, mask_ref, q_ref, g_ref, kv_ref, first_dq_ref, _, out_ref, dq_ref,
+    every_row = slice(0, BLOCK)
+    block_attention(
+        0, (0, QUERY_HEADS), slots, q_ref, g_ref, kv_ref, out_ref, dq_ref, every_row, *scratch
+    )
+    add_key_terms(slots, acc_ref, scratch[3:])
+
+
+def half_attention_kernel(
+    chosen, most, mask_ref, q_ref, g_ref, kv_ref, _, out_ref, dq_ref,
     q_turned_ref, g_turned_ref, ds_ref, wb_ref, slot_ref, *scratch
 ):
-    dq_ref[:BLOCK, :] = first_dq_ref[...]
     slots = find_slots(2 * lax.axis_index("seq") + 1, most, mask_ref, slot_ref)
     products = (q_turned_ref, g_turned_ref, ds_ref, wb_ref)
-    block_attention(1, slots, q_ref, g_ref, kv_ref, out_ref, dq_ref, *scratch, *products)
-
-
-def key_terms_kernel(most, mask_ref, first_acc_ref, *refs):
-    products, acc_ref, slot_ref = refs[:4], refs[4], refs[5]
+    every_row = slice(0, BLOCK)
+    block_attention(
+        1, chosen, slots, q_ref, g_ref, kv_ref, out_ref, dq_ref, every_row, *scratch, *products
+    )
+
+
+def key_terms_kernel(
+    most, mask_ref, first_acc_ref, first_dq_ref, early_dq_ref, late_dq_ref, *refs
+):
+    early, late, (acc_ref, dq_ref, slot_ref) = refs[:4], refs[4:8], refs[8:]
+    middle = HALF_HEADS * HEAD_WIDTH
+    dq_ref[:BLOCK, :] = first_dq_ref[...]
+    dq_ref[BLOCK:, :middle] = early_dq_ref[...]
+    dq_ref[BLOCK:, middle:] = late_dq_ref[...]
     acc_ref[...] = first_acc_ref[...]
     slots = find_slots(2 * lax.axis_index("seq") + 1, most, mask_ref, slot_ref)
-    add_key_terms(slots, acc_ref, *products)
+    add_key_terms(slots, acc_ref, early, late)
 
 
 def share_kernel(chips, acc_ref, *refs):
@@ -423,7 +435,7 @@
 
 
 def outer_kernel(
-    x_ref, g_ref, b_ref, c_ref, step_ref, rate_ref, own_ref, other_ref, first_ref, second_ref,
+    x_ref, g_ref, b_ref, c_ref, step_ref, rate_ref, own_ref, other_ref, first_ref, early_ref, late_ref,
     inner_y_ref, inner_dx_ref, inner_db_ref, inner_dc_ref, _,
     y_ref, dx_ref, db_ref, dc_ref,
     pad_ref, xt_ref, gt_ref, ent_ref,
@@ -444,7 +456,8 @@
         back = dot(b, ent_ref[1, :, lanes], 1, 0) * tail[:, h : h + 1]
         y = inner_y_ref[:, lanes] + carried
         y_ref[:BLOCK, lanes] = (y[:BLOCK] + first_ref[:, lanes]).astype(BF16)
-        y_ref[BLOCK:, lanes] = (y[BLOCK:] + second_ref[:, lanes]).astype(BF16)
+        second_ref, place = (early_ref, h) if h < HALF_HEADS else (late_ref, h - HALF_HEADS)
+        y_ref[BLOCK:, lanes] = (y[BLOCK:] + second_ref[:, head(place)]).astype(BF16)
         dx_ref[:, lanes] = (inner_dx_ref[:, lanes] + back).astype(BF16)
     dc_ref[...] = (inner_dc_ref[...] + dot(gt_ref[...], ent_ref[0], 1, 1)).astype(BF16)
     db_ref[...] = (inner_db_ref[...] + dot(xt_ref[...], ent_ref[1], 1, 1)).astype(BF16)
@@ -567,6 +580,29 @@
         "first_attention",
         18 + most,
     )(block_mask[0], q, g, stack, other_stack, messages[0])
+    part = columns // 2
+    half_outs = [
+        ((BLOCK, part), F32),
+        ((BLOCK, part), BF16),
+        ((LANES, part), BF16),
+        ((LANES, part), BF16),
+        ((part, most * BLOCK), BF16),
+        ((part, most * BLOCK), BF16),
+    ]
+
+    def half_attention(chosen, after, name):
+        return call(
+            lambda *refs: half_attention_kernel(chosen, most, *refs),
+            half_outs,
+            [SMEM] + [VMEM] * 3 + [AFTER],
+            scratch[:4],
+            2,
+            name,
+            18 + most,
+        )(block_mask[0], q, g, kv_all, after)
+
+    early_out, early_dq, *early = half_attention((0, HALF_HEADS), first_dq, "early_attention")
+
     entering = ((2, HALF, WIDE), BF16)
     own, give, totals = call(
         lambda *refs: chain_kernel(chips, *refs),
@@ -575,7 +611,7 @@
         [],
         2,
         "chain_states",
-    )(keep, received, sums, first_dq, *arrived)
+    )(keep, received, sums, early_dq, *arrived)
     other = swapped(give)
     rounds = [1 << bit for bit in range((replicas - 1).bit_length())]
     replicated = totals
@@ -583,31 +619,16 @@
         replicated = replicated + from_replica(replicated, distance)
     last_round = from_replica(replicated, rounds[-1])
 
-    second_out, dq, *products = call(
-        lambda *refs: second_attention_kernel(most, *refs),
-        [
-            ((BLOCK, columns), F32),
-            ((tokens, columns), BF16),
-            ((LANES, columns), BF16),
-            ((LANES, columns), BF16),
-            ((columns, most * BLOCK), BF16),
-            ((columns, most * BLOCK), BF16),
-        ],
-        [SMEM] + [VMEM] * 4 + [AFTER],
-        scratch[:4],
-        4,
-        "second_attention",
-        18 + most,
-    )(block_mask[0], q, g, kv_all, first_dq, totals)
-    (acc,) = call(
+    late_out, late_dq, *late = half_attention((HALF_HEADS, QUERY_HEADS), totals, "late_attention")
+    acc, dq = call(
         lambda *refs: key_terms_kernel(most, *refs),
-        [((2 * LANES, every), F32)],
-        [SMEM] + [VMEM] * 5,
+        [((2 * LANES, every), F32), ((tokens, columns), BF16)],
+        [SMEM] + [VMEM] * 12,
         scratch[:1],
         2,
         "key_terms",
         18 + most,
-    )(block_mask[0], first_acc, *products)
+    )(block_mask[0], first_acc, first_dq, early_dq, late_dq, *early, *late)
     keep, give, sums = call(
         lambda *refs: share_kernel(chips, *refs),
         [
@@ -634,7 +655,7 @@
     y, dx, db, dc = call(
         outer_kernel,
         [((tokens, WIDE), BF16)] * 2 + [((tokens, NS), BF16)] * 2,
-        [VMEM] * 5 + [SMEM] + [VMEM] * 8 + [AFTER],
+        [VMEM] * 5 + [SMEM] + [VMEM] * 9 + [AFTER],
         [
             pltpu.VMEM((LANES, tokens), F32),
             pltpu.VMEM((tokens, WIDE), BF16),
@@ -644,7 +665,7 @@
         3,
         "chunk_outer",
     )(
-        x, g, b, c, steps, rate_log, own, other, first_out, second_out,
+        x, g, b, c, steps, rate_log, own, other, first_out, early_out, late_out,
         inner_y, inner_dx, inner_db, inner_dc, messages[0],
     )
 

time: 51.2 us -> 50.5 us (0.986)
  waiting for transfers between devices: 8.63 us -> 6.74 us
  Pallas kernels: 21.7 us -> 23.3 us
    ppermute x9, waiting for transfers between devices: 4.54 us -> 2.97 us  [from_chip(): return lax.ppermute(array, 'seq', [(i, (i + 2 * k) % n) for i in range(n)])]
    pallas_call x1, Pallas kernels: 1.63 us -> 2.44 us  [body(): call(lambda *refs: key_terms_kernel(most, *refs), [((2 * LANES, every), F...]
    pallas_call x1 -> x2, Pallas kernels: 4.59 us -> 5.33 us  [half_attention(): call(lambda *refs: half_attention_kernel(chosen, most, *refs), half_outs,...]
  transfers between devices with their start and end apart: 15 -> 15, of which waited for: 7 -> 5; matrix products, arithmetic and copies ran while one was open for 0% -> 0% of each run, Pallas kernels for 36% -> 39%
where the time goes in v11:
time: 50.5 us; the launch traced here: 50.3 us
  Pallas kernels  23.3 us (46%)
  starting transfers between devices  19.4 us (38%)
  waiting for transfers between devices  6.74 us (13%)
  between operations  0.89 us (2%)
    ppermute x9, starting transfers between devices, from_chip(): return lax.ppermute(array, 'seq', [(i, (i + 2 * k) % n) for i in range(n)])  13.9 us
    pallas_call x2, Pallas kernels, half_attention(): call(lambda *refs: half_attention_kernel(chosen, most, *refs), half_outs,...  5.33 us
    pallas_call x1, Pallas kernels, body(): call(chunk_kernel, [((4, NS, WIDE + LANES), F32)] + [((tokens, WIDE), F32...  4.53 us
    pallas_call x1, Pallas kernels, body(): call(lambda *refs: first_attention_kernel(chips, most, *refs), [((BLOCK,...  4.36 us
    ppermute x2, starting transfers between devices, from_replica(): return lax.ppermute(array, 'dp', pairs)  4.29 us
    ppermute x4, waiting for transfers between devices, swapped(): lax.ppermute(array, 'seq', [(i, i ^ 1) for i in range(lax.axis_size('seq'...  3.77 us
    ppermute x9, waiting for transfers between devices, from_chip(): return lax.ppermute(array, 'seq', [(i, (i + 2 * k) % n) for i in range(n)])  2.97 us
    pallas_call x1, Pallas kernels, body(): call(outer_kernel, [((tokens, WIDE), BF16)] * 2 + [((tokens, NS), BF16)]...  2.83 us
  transfers between devices with their start and end apart: 15, of which 5 were waited for; matrix products, arithmetic and copies ran while one was open for 0% of the time, Pallas kernels for 39%

profile of v11, /device:TPU:0, one launch (start us, length us, event | category | flops | bytes accessed | tf_op | source)
XLA Modules:
  0.0 50.3 jit_solution(14549044381162588000)
XLA Ops:
  0.7 1.6 %pack_kv.1.refs_0_ = bf16[256,256]{1,0:T(8,128)(2,1)} custom-call(bf16[256,128]{1,0:T(8,128)(2,1)} %bitcast.40, bf16[256,128]{1,0:T(8,128)(2,1)} %bitcast.41), custom_call_target="tpu_custom_call" | custom-call | flops 1100000000 | bytes 1048576 | tf_op jit(solution)/shard_map/pack_kv/pallas_call | solution.py:504
  2.3 3.0 %collective-permute-start = (bf16[256,256]{1,0:T(8,128)(2,1)}, bf16[256,256]{1,0:T(8,128)(2,1)S(1)}, u32[]{:S(2)}, u32[]{:S(2)}) collective-permute-start(bf16[256,256]{1,0:T(8,128)(2,1)} %pack_kv.1.refs_0_), channel_id=1, source_target_pairs={{0,2},{1,3},{2,4},{3,5},{4,6},{5,7},{6,0},{7,1},{8,10},{9,11},{10,... | collective-permute-start | bytes 393224 | tf_op jit(solution)/shard_map/ppermute | solution.py:472
  5.3 1.5 %collective-permute-start.1 = (bf16[256,256]{1,0:T(8,128)(2,1)}, bf16[256,256]{1,0:T(8,128)(2,1)S(1)}, u32[]{:S(2)}, u32[]{:S(2)}) collective-permute-start(bf16[256,256]{1,0:T(8,128)(2,1)} %pack_kv.1.refs_0_), channel_id=1, source_target_pairs={{0,4},{1,5},{2,6},{3,7},{4,0},{5,1},{6,2},{7,3},{8,12},{9,13},{10,... | collective-permute-start | bytes 393224 | tf_op jit(solution)/shard_map/ppermute | solution.py:472
  6.9 1.4 %collective-permute-start.2 = (bf16[256,256]{1,0:T(8,128)(2,1)}, bf16[256,256]{1,0:T(8,128)(2,1)S(1)}, u32[]{:S(2)}, u32[]{:S(2)}) collective-permute-start(bf16[256,256]{1,0:T(8,128)(2,1)} %pack_kv.1.refs_0_), channel_id=1, source_target_pairs={{0,6},{1,7},{2,0},{3,1},{4,2},{5,3},{6,4},{7,5},{8,14},{9,15},{10,... | collective-permute-start | bytes 393224 | tf_op jit(solution)/shard_map/ppermute | solution.py:472
  8.3 4.5 %chunk_alone.1 = (f32[4,128,1152]{2,1,0:T(8,128)S(1)}, f32[256,1024]{1,0:T(8,128)S(1)}, f32[256,1024]{1,0:T(8,128)S(1)}, f32[256,128]{1,0:T(8,128)S(1)}, f32[256,128]{1,0:T(8,128)S(1)}, /*index=5*/f32[16,128]{1,0:T(8,128)S(1)}) custom-call(bf16[256,1024]{1,0:T(8,128)(2,1)S(1)} %bitcast.23, bf16[256,1024]{1,0:T(8,128)(2,1)S(1)} %bitcast.25, ...), custom_call_target="tpu_custom_call" | custom-call | flops 6600000000 | bytes 1048576 | tf_op jit(solution)/shard_map/chunk_alone/pallas_call | solution.py:515
  13.4 0.5 collective-permute-start.4
  13.9 2.3 %collective-permute-done.3.refs_1_ = f32[4,64,1152]{2,1,0:T(8,128)S(1)} collective-permute-done((f32[4,64,1152]{2,1,0:T(8,128)S(1)}, f32[4,64,1152]{2,1,0:T(8,128)S(1)}, u32[]{:S(2)}, u32[]{:S(2)}) %collective-permute-start.3) | collective-permute-done | bytes 1179680 | tf_op jit(solution)/shard_map/ppermute | solution.py:467
  16.4 1.8 %collective-permute-start.5 = (bf16[64,1152]{1,0:T(8,128)(2,1)S(1)}, bf16[64,1152]{1,0:T(8,128)(2,1)S(1)}, u32[]{:S(2)}, u32[]{:S(2)}) collective-permute-start(bf16[64,1152]{1,0:T(8,128)(2,1)S(1)} %get-tuple-element.63.refs_5_), channel_id=1, source_target_pairs={{0,2},{1,3},{2,4},{3,5},{4,6},{5,7},{6,0},{7,1},{8,10},{9,11},{10,... | collective-permute-start | bytes 442376 | tf_op jit(solution)/shard_map/ppermute | solution.py:472
  18.6 2.3 %collective-permute-start.7 = (bf16[64,1152]{1,0:T(8,128)(2,1)S(1)}, bf16[64,1152]{1,0:T(8,128)(2,1)S(1)}, u32[]{:S(2)}, u32[]{:S(2)}) collective-permute-start(bf16[64,1152]{1,0:T(8,128)(2,1)S(1)} %get-tuple-element.68), channel_id=1, source_target_pairs={{0,6},{1,7},{2,0},{3,1},{4,2},{5,3},{6,4},{7,5},{8,14},{9,15},{10,... | collective-permute-start | bytes 442376 | tf_op jit(solution)/shard_map/ppermute | solution.py:472
  20.9 4.4 %first_attention.1 = (f32[128,1024]{1,0:T(8,128)S(1)}, bf16[128,1024]{1,0:T(8,128)(2,1)S(1)}, f32[256,2048]{1,0:T(8,128)S(1)}, bf16[2048,256]{1,0:T(8,128)(2,1)S(1)}) custom-call(s32[16,16]{1,0:T(8,128)S(1)} %bitcast.34, bf16[256,1024]{1,0:T(8,128)(2,1)S(1)} %bitcast.20, bf16[256,1024]{1,0:T(8,128)(2,1)S(1)} %bitcast.26, ...), custom_call_target="tpu_custom_call" | custom-call | flops 5500000256 | bytes 1048576 | tf_op jit(solution)/shard_map/first_attention/pallas_call | solution.py:569
  25.2 2.7 %early_attention.1 = (f32[128,512]{1,0:T(8,128)S(1)}, bf16[128,512]{1,0:T(8,128)(2,1)S(1)}, bf16[128,512]{1,0:T(8,128)(2,1)S(1)}, bf16[128,512]{1,0:T(8,128)(2,1...) custom-call(s32[16,16]{1,0:T(8,128)S(1)} %bitcast.35, bf16[256,1024]{1,0:T(8,128)(2,1)S(1)} %bitcast.21, ...), custom_call_target="tpu_custom_call" | custom-call | flops 2200000000 | bytes 1048576 | tf_op jit(solution)/shard_map/early_attention/pallas_call | solution.py:594
  27.9 0.7 %chain_states.1 = (bf16[2,64,1024]{2,1,0:T(8,128)(2,1)S(1)}, bf16[2,64,1024]{2,1,0:T(8,128)(2,1)S(1)}, f32[16,128]{1,0:T(8,128)S(1)}) custom-call(f32[4,64,1152]{2,1,0:T(8,128)S(1)} %get-tuple-element.59.refs_0_, f32[4,64,1152]{2,1,0:T(8,128)S(1)} %collective-permute-done.3.refs_1_, f32[16,128]{1,0:T(8,128)S(1)} %get-tuple-element.61.refs_2_, ...), custom_call_target="tpu_custom_call" | custom-call | flops 2200000000 | bytes 1048576 | tf_op jit(solution)/shard_map/chain_states/pallas_call | solution.py:607
  28.6 1.6 %collective-permute-start.9 = (f32[16,128]{1,0:T(8,128)S(1)}, f32[16,128]{1,0:T(8,128)S(1)}, u32[]{:S(2)}, u32[]{:S(2)}) collective-permute-start(f32[16,128]{1,0:T(8,128)S(1)} %get-tuple-element.73.refs_4_), channel_id=1, source_target_pairs={{0,8},{8,0},{16,24},{24,16},{1,9},{9,1},{17,25},{25,17},{2,10},{10... | collective-permute-start | bytes 24584 | tf_op jit(solution)/shard_map/ppermute | solution.py:477
  30.3 2.7 %late_attention.1 = (f32[128,512]{1,0:T(8,128)S(1)}, bf16[128,512]{1,0:T(8,128)(2,1)S(1)}, bf16[128,512]{1,0:T(8,128)(2,1)S(1)}, bf16[128,512]{1,0:T(8,128)(2,1)...) custom-call(s32[16,16]{1,0:T(8,128)S(1)} %bitcast.36, bf16[256,1024]{1,0:T(8,128)(2,1)S(1)} %bitcast.22, ...), custom_call_target="tpu_custom_call" | custom-call | flops 2200000000 | bytes 1048576 | tf_op jit(solution)/shard_map/late_attention/pallas_call | solution.py:594
  32.9 2.6 %collective-permute-start.10 = (f32[16,128]{1,0:T(8,128)S(1)}, f32[16,128]{1,0:T(8,128)S(1)}, u32[]{:S(2)}, u32[]{:S(2)}) collective-permute-start(f32[16,128]{1,0:T(8,128)S(1)} %add.3.refs_1_), channel_id=1, source_target_pairs={{0,16},{8,24},{16,0},{24,8},{1,17},{9,25},{17,1},{25,9},{2,18},{10... | collective-permute-start | bytes 24584 | tf_op jit(solution)/shard_map/ppermute | solution.py:477
  35.6 2.4 %key_terms.1 = (f32[256,2048]{1,0:T(8,128)S(1)}, bf16[256,1024]{1,0:T(8,128)(2,1)}) custom-call(s32[16,16]{1,0:T(8,128)S(1)} %bitcast.37, f32[256,2048]{1,0:T(8,128)S(1)} %get-tuple-element.79.refs_1_, bf16[128,1024]{1,0:T(8,128)(2,1)S(1)} %get-tuple-element.65.refs_4_.refs_2_, bf16[128,512]{1,0:T(8,128)(2,1)S(1)} %get-tuple-element.66.refs_3_, ...), custom_call_target="tpu_custom_call" | custom-call | flops 2200000000 | bytes 1048576 | tf_op jit(solution)/shard_map/key_terms/pallas_call | solution.py:623
  38.3 0.5 collective-permute-start.8
  38.8 1.4 %collective-permute-done.11.refs_1_ = bf16[1056,256]{1,0:T(8,128)(2,1)S(1)} collective-permute-done((bf16[1056,256]{1,0:T(8,128)(2,1)S(1)}, bf16[1056,256]{1,0:T(8,128)(2,1)S(1)}, u32[]{:S(2)}, u32[]{:S(2)}) %collective-permute-start.11) | collective-permute-done | bytes 540704 | tf_op jit(solution)/shard_map/ppermute | solution.py:467
  40.6 1.3 %collective-permute-start.13 = (bf16[288,256]{1,0:T(8,128)(2,1)S(1)}, bf16[288,256]{1,0:T(8,128)(2,1)S(1)}, u32[]{:S(2)}, u32[]{:S(2)}) collective-permute-start(bf16[288,256]{1,0:T(8,128)(2,1)S(1)} %get-tuple-element.98), channel_id=1, source_target_pairs={{0,4},{1,5},{2,6},{3,7},{4,0},{5,1},{6,2},{7,3},{8,12},{9,13},{10,... | collective-permute-start | bytes 442376 | tf_op jit(solution)/shard_map/ppermute | solution.py:472
  41.9 2.0 %collective-permute-start.14 = (bf16[288,256]{1,0:T(8,128)(2,1)S(1)}, bf16[288,256]{1,0:T(8,128)(2,1)S(1)}, u32[]{:S(2)}, u32[]{:S(2)}) collective-permute-start(bf16[288,256]{1,0:T(8,128)(2,1)S(1)} %get-tuple-element.99), channel_id=1, source_target_pairs={{0,6},{1,7},{2,0},{3,1},{4,2},{5,3},{6,4},{7,5},{8,14},{9,15},{10,... | collective-permute-start | bytes 442376 | tf_op jit(solution)/shard_map/ppermute | solution.py:472
  43.9 2.8 %chunk_outer.1 = (bf16[256,1024]{1,0:T(8,128)(2,1)}, bf16[256,1024]{1,0:T(8,128)(2,1)}, bf16[256,128]{1,0:T(8,128)(2,1)}, bf16[256,128]{1,0:T(8,128)(2,1)}) custom-call(bf16[256,1024]{1,0:T(8,128)(2,1)S(1)} %bitcast.24, bf16[256,1024]{1,0:T(8,128)(2,1)S(1)} %bitcast.29, bf16[256,128]{1,0:T(8,128)(2,1)S(1)} %bitcast.31, bf16[256,128]{1,0:T(8,128)(2,1)S(1)} %bitcast.33, ...), custom_call_target="tpu_custom_call" | custom-call | flops 3300000000 | bytes 1048576 | tf_op jit(solution)/shard_map/chunk_outer/pallas_call | solution.py:655
  46.7 1.3 %collective-permute-done.12.refs_2_ = bf16[288,256]{1,0:T(8,128)(2,1)S(1)} collective-permute-done((bf16[288,256]{1,0:T(8,128)(2,1)S(1)}, bf16[288,256]{1,0:T(8,128)(2,1)S(1)}, u32[]{:S(2)}, u32[]{:S(2)}) %collective-permute-start.12) | collective-permute-done | bytes 147488 | tf_op jit(solution)/shard_map/ppermute | solution.py:472
  48.0 1.5 %collective-permute-done.13.refs_3_ = bf16[288,256]{1,0:T(8,128)(2,1)S(1)} collective-permute-done((bf16[288,256]{1,0:T(8,128)(2,1)S(1)}, bf16[288,256]{1,0:T(8,128)(2,1)S(1)}, u32[]{:S(2)}, u32[]{:S(2)}) %collective-permute-start.13) | collective-permute-done | bytes 147488 | tf_op jit(solution)/shard_map/ppermute | solution.py:472
  49.5 0.8 %owner_sum.1 = (bf16[256,128]{1,0:T(8,128)(2,1)}, bf16[256,128]{1,0:T(8,128)(2,1)}, f32[1,8]{1,0:T(1,128)}, f32[1,8]{1,0:T(1,128)}) custom-call(f32[256,256]{1,0:T(8,128)S(1)} %get-tuple-element.96.refs_0_, f32[16,128]{1,0:T(8,128)S(1)} %get-tuple-element.97.refs_1_, bf16[288,256]{1,0:T(8,128)(2,1)S(1)} %collective-permute-done.12.refs_2_, ...), custom_call_target="tpu_custom_call" | custom-call | flops 1100000000 | bytes 1048576 | tf_op jit(solution)/shard_map/owner_sum/pallas_call | solution.py:673
  (40 shorter events, 1.7 us)
Async XLA Ops:
  0.6 7.7 %copy-start.1 = (bf16[1,256,1024]{2,1,0:T(8,128)(2,1)S(1)}, bf16[1,256,1024]{2,1,0:T(8,128)(2,1)}, u32[]{:S(2)}) copy-start(bf16[1,256,1024]{2,1,0:T(8,128)(2,1)} %param.14) | copy-start | bytes 1572868
  0.7 7.6 %copy-start.2 = (bf16[1,256,1024]{2,1,0:T(8,128)(2,1)S(1)}, bf16[1,256,1024]{2,1,0:T(8,128)(2,1)}, u32[]{:S(2)}) copy-start(bf16[1,256,1024]{2,1,0:T(8,128)(2,1)} %param.21) | copy-start | bytes 1572868
  0.7 7.6 %copy-start.4 = (bf16[1,256,128]{2,1,0:T(8,128)(2,1)S(1)}, bf16[1,256,128]{2,1,0:T(8,128)(2,1)}, u32[]{:S(2)}) copy-start(bf16[1,256,128]{2,1,0:T(8,128)(2,1)} %param.15) | copy-start | bytes 196612
  0.7 7.6 %copy-start.5 = (bf16[1,256,128]{2,1,0:T(8,128)(2,1)S(1)}, bf16[1,256,128]{2,1,0:T(8,128)(2,1)}, u32[]{:S(2)}) copy-start(bf16[1,256,128]{2,1,0:T(8,128)(2,1)} %param.16) | copy-start | bytes 196612
  0.7 7.6 %copy-start.7 = (f32[1,256,8]{1,2,0:T(8,128)S(1)}, f32[1,256,8]{1,2,0:T(8,128)}, u32[]{:S(2)}) copy-start(f32[1,256,8]{1,2,0:T(8,128)} %param.17) | copy-start | bytes 24580
  0.7 7.6 %copy-start.9 = (f32[8]{0:T(128)S(1)}, f32[8]{0:T(128)}, u32[]{:S(2)}) copy-start(f32[8]{0:T(128)} %rate_ref.3) | copy-start | bytes 100
  0.7 7.6 %copy-start.8 = (f32[8]{0:T(128)S(1)}, f32[8]{0:T(128)}, u32[]{:S(2)}) copy-start(f32[8]{0:T(128)} %skip_ref.1) | copy-start | bytes 100
  2.3 10.5 %collective-permute-start = (bf16[256,256]{1,0:T(8,128)(2,1)}, bf16[256,256]{1,0:T(8,128)(2,1)S(1)}, u32[]{:S(2)}, u32[]{:S(2)}) collective-permute-start(bf16[256,256]{1,0:T(8,128)(2,1)} %pack_kv.1.refs_0_), channel_id=1, source_target_pairs={{0,2},{1,3},{2,4},{3,5},{4,6},{5,7},{6,0},{7,1},{8,10},{9,11},{10,... | collective-permute-start | bytes 393224 | tf_op jit(solution)/shard_map/ppermute | solution.py:472
  5.3 7.6 %collective-permute-start.1 = (bf16[256,256]{1,0:T(8,128)(2,1)}, bf16[256,256]{1,0:T(8,128)(2,1)S(1)}, u32[]{:S(2)}, u32[]{:S(2)}) collective-permute-start(bf16[256,256]{1,0:T(8,128)(2,1)} %pack_kv.1.refs_0_), channel_id=1, source_target_pairs={{0,4},{1,5},{2,6},{3,7},{4,0},{5,1},{6,2},{7,3},{8,12},{9,13},{10,... | collective-permute-start | bytes 393224 | tf_op jit(solution)/shard_map/ppermute | solution.py:472
  6.9 6.2 %collective-permute-start.2 = (bf16[256,256]{1,0:T(8,128)(2,1)}, bf16[256,256]{1,0:T(8,128)(2,1)S(1)}, u32[]{:S(2)}, u32[]{:S(2)}) collective-permute-start(bf16[256,256]{1,0:T(8,128)(2,1)} %pack_kv.1.refs_0_), channel_id=1, source_target_pairs={{0,6},{1,7},{2,0},{3,1},{4,2},{5,3},{6,4},{7,5},{8,14},{9,15},{10,... | collective-permute-start | bytes 393224 | tf_op jit(solution)/shard_map/ppermute | solution.py:472
  13.3 7.6 %copy-start = (bf16[1,256,1024]{2,1,0:T(8,128)(2,1)S(1)}, bf16[1,256,1024]{2,1,0:T(8,128)(2,1)}, u32[]{:S(2)}) copy-start(bf16[1,256,1024]{2,1,0:T(8,128)(2,1)} %param.11) | copy-start | bytes 1572868
  13.3 7.6 %copy-start.6 = (s32[1,16,16]{2,1,0:T(8,128)S(1)}, s32[1,16,16]{2,1,0:T(8,128)}, u32[]{:S(2)}) copy-start(s32[1,16,16]{2,1,0:T(8,128)} %param.20) | copy-start | bytes 3076
  13.3 2.9 %collective-permute-start.3 = (f32[4,64,1152]{2,1,0:T(8,128)S(1)}, f32[4,64,1152]{2,1,0:T(8,128)S(1)}, u32[]{:S(2)}, u32[]{:S(2)}) collective-permute-start(f32[4,64,1152]{2,1,0:T(8,128)S(1)} %get-tuple-element.60), channel_id=1, source_target_pairs={{0,1},{1,0},{2,3},{3,2},{4,5},{5,4},{6,7},{7,6},{8,9},{9,8},{10,11... | collective-permute-start | bytes 3538952 | tf_op jit(solution)/shard_map/ppermute | solution.py:467
  13.4 7.5 %collective-permute-start.4 = (bf16[4,256,256]{2,1,0:T(8,128)(2,1)S(1)}, bf16[4,256,256]{2,1,0:T(8,128)(2,1)S(1)}, u32[]{:S(2)}, u32[]{:S(2)}) collective-permute-start(bf16[4,256,256]{2,1,0:T(8,128)(2,1)S(1)} %get-tuple-element.62.refs_3_), channel_id=1, source_target_pairs={{0,1},{1,0},{2,3},{3,2},{4,5},{5,4},{6,7},{7,6},{8,9},{9,8},{10,11... | collective-permute-start | bytes 1572872 | tf_op jit(solution)/shard_map/ppermute | solution.py:467
  16.4 11.5 %collective-permute-start.5 = (bf16[64,1152]{1,0:T(8,128)(2,1)S(1)}, bf16[64,1152]{1,0:T(8,128)(2,1)S(1)}, u32[]{:S(2)}, u32[]{:S(2)}) collective-permute-start(bf16[64,1152]{1,0:T(8,128)(2,1)S(1)} %get-tuple-element.63.refs_5_), channel_id=1, source_target_pairs={{0,2},{1,3},{2,4},{3,5},{4,6},{5,7},{6,0},{7,1},{8,10},{9,11},{10,... | collective-permute-start | bytes 442376 | tf_op jit(solution)/shard_map/ppermute | solution.py:472
  18.2 9.7 %collective-permute-start.6 = (bf16[64,1152]{1,0:T(8,128)(2,1)S(1)}, bf16[64,1152]{1,0:T(8,128)(2,1)S(1)}, u32[]{:S(2)}, u32[]{:S(2)}) collective-permute-start(bf16[64,1152]{1,0:T(8,128)(2,1)S(1)} %get-tuple-element.67), channel_id=1, source_target_pairs={{0,4},{1,5},{2,6},{3,7},{4,0},{5,1},{6,2},{7,3},{8,12},{9,13},{10,... | collective-permute-start | bytes 442376 | tf_op jit(solution)/shard_map/ppermute | solution.py:472
  18.6 9.3 %collective-permute-start.7 = (bf16[64,1152]{1,0:T(8,128)(2,1)S(1)}, bf16[64,1152]{1,0:T(8,128)(2,1)S(1)}, u32[]{:S(2)}, u32[]{:S(2)}) collective-permute-start(bf16[64,1152]{1,0:T(8,128)(2,1)S(1)} %get-tuple-element.68), channel_id=1, source_target_pairs={{0,6},{1,7},{2,0},{3,1},{4,2},{5,3},{6,4},{7,5},{8,14},{9,15},{10,... | collective-permute-start | bytes 442376 | tf_op jit(solution)/shard_map/ppermute | solution.py:472
  28.6 4.3 %collective-permute-start.9 = (f32[16,128]{1,0:T(8,128)S(1)}, f32[16,128]{1,0:T(8,128)S(1)}, u32[]{:S(2)}, u32[]{:S(2)}) collective-permute-start(f32[16,128]{1,0:T(8,128)S(1)} %get-tuple-element.73.refs_4_), channel_id=1, source_target_pairs={{0,8},{8,0},{16,24},{24,16},{1,9},{9,1},{17,25},{25,17},{2,10},{10... | collective-permute-start | bytes 24584 | tf_op jit(solution)/shard_map/ppermute | solution.py:477
  32.9 5.1 %collective-permute-start.10 = (f32[16,128]{1,0:T(8,128)S(1)}, f32[16,128]{1,0:T(8,128)S(1)}, u32[]{:S(2)}, u32[]{:S(2)}) collective-permute-start(f32[16,128]{1,0:T(8,128)S(1)} %add.3.refs_1_), channel_id=1, source_target_pairs={{0,16},{8,24},{16,0},{24,8},{1,17},{9,25},{17,1},{25,9},{2,18},{10... | collective-permute-start | bytes 24584 | tf_op jit(solution)/shard_map/ppermute | solution.py:477
  38.2 2.0 %collective-permute-start.11 = (bf16[1056,256]{1,0:T(8,128)(2,1)S(1)}, bf16[1056,256]{1,0:T(8,128)(2,1)S(1)}, u32[]{:S(2)}, u32[]{:S(2)}) collective-permute-start(bf16[1056,256]{1,0:T(8,128)(2,1)S(1)} %get-tuple-element.91), channel_id=1, source_target_pairs={{0,1},{1,0},{2,3},{3,2},{4,5},{5,4},{6,7},{7,6},{8,9},{9,8},{10,11... | collective-permute-start | bytes 1622024 | tf_op jit(solution)/shard_map/ppermute | solution.py:467
  38.3 5.6 %collective-permute-start.8 = (bf16[2,64,1024]{2,1,0:T(8,128)(2,1)S(1)}, bf16[2,64,1024]{2,1,0:T(8,128)(2,1)S(1)}, u32[]{:S(2)}, u32[]{:S(2)}) collective-permute-start(bf16[2,64,1024]{2,1,0:T(8,128)(2,1)S(1)} %get-tuple-element.70), channel_id=1, source_target_pairs={{0,1},{1,0},{2,3},{3,2},{4,5},{5,4},{6,7},{7,6},{8,9},{9,8},{10,11... | collective-permute-start | bytes 786440 | tf_op jit(solution)/shard_map/ppermute | solution.py:467
  40.3 7.7 %collective-permute-start.12 = (bf16[288,256]{1,0:T(8,128)(2,1)S(1)}, bf16[288,256]{1,0:T(8,128)(2,1)S(1)}, u32[]{:S(2)}, u32[]{:S(2)}) collective-permute-start(bf16[288,256]{1,0:T(8,128)(2,1)S(1)} %get-tuple-element.93._), channel_id=1, source_target_pairs={{0,2},{1,3},{2,4},{3,5},{4,6},{5,7},{6,0},{7,1},{8,10},{9,11},{10,... | collective-permute-start | bytes 442376 | tf_op jit(solution)/shard_map/ppermute | solution.py:472
  40.6 8.9 %collective-permute-start.13 = (bf16[288,256]{1,0:T(8,128)(2,1)S(1)}, bf16[288,256]{1,0:T(8,128)(2,1)S(1)}, u32[]{:S(2)}, u32[]{:S(2)}) collective-permute-start(bf16[288,256]{1,0:T(8,128)(2,1)S(1)} %get-tuple-element.98), channel_id=1, source_target_pairs={{0,4},{1,5},{2,6},{3,7},{4,0},{5,1},{6,2},{7,3},{8,12},{9,13},{10,... | collective-permute-start | bytes 442376 | tf_op jit(solution)/shard_map/ppermute | solution.py:472
  41.9 7.6 %collective-permute-start.14 = (bf16[288,256]{1,0:T(8,128)(2,1)S(1)}, bf16[288,256]{1,0:T(8,128)(2,1)S(1)}, u32[]{:S(2)}, u32[]{:S(2)}) collective-permute-start(bf16[288,256]{1,0:T(8,128)(2,1)S(1)} %get-tuple-element.99), channel_id=1, source_target_pairs={{0,6},{1,7},{2,0},{3,1},{4,2},{5,3},{6,4},{7,5},{8,14},{9,15},{10,... | collective-permute-start | bytes 442376 | tf_op jit(solution)/shard_map/ppermute | solution.py:472
  (1 other events, 4.7 us)
